TPU v7x, 32 devices: a whole 2x2x4 slice. The times are simulated.
32 devices in a mesh: grp: 4 (over y, core), dev: 8 (over z, x).
Axes of the slice: x: 2, y: 2, z: 4, core: 2. Of those that a mesh axis runs over, the one named last changes fastest.
Arguments:
- wave: bfloat16 [1024, 384], P(('grp', 'dev')), may hold values from -6 to 6
- lengths: int32 [1024], P('grp'), may hold values from 288 to 384, as said below
- order: int32 [32, 32], P('grp'), may hold values from 0 to 31, each once within a row
- w_first: bfloat16 [10, 512], replicated, may hold values from -2 to 2
- norm_gain: float32 [512], replicated, may hold values from 0.1 to 1.9
- norm_bias: float32 [512], replicated, may hold values from -3 to 3
- w_second: bfloat16 [3, 512, 512], replicated, may hold values from -0.15625 to 0.15625
- cot: bfloat16 [1024, 37, 512], P(('grp', 'dev')), may hold values from -0.0234375 to 0.0234375
Outputs:
- features: bfloat16 [1024, 37, 512], P(('grp', 'dev'))
- grad_second: float32 [3, 512, 512], P(None, None, 'dev')
- grad_first: float32 [10, 512], P(None, 'dev')
- grad_gain: float32 [512], P('dev')
- grad_bias: float32 [512], P('dev')
Inputs may be any that keep to these rules, and one draw needn't show every extreme that they name: `lengths`: every aligned block of 32 rows (the rows of one device) holds a row of exactly 384 valid samples. Each row of order is a permutation of 0 .. 31.
All inputs are finite; a program needn't handle non-finite values.
Results may differ from a plain program's by a relative error of at most 0.0054.
Values may be sent and summed in bfloat16 or wider, within the bound.
No kernel may reach another device: no remote copies, remote signals or barrier semaphores. Data moves between devices by JAX's collectives and lax.ppermute only.
A program may use at most 64 MiB of HBM per device.

v0:
```python
import jax
import jax.numpy as jnp
from jax import lax
from jax.sharding import PartitionSpec as P


def gelu_slope(value):
    return (
        0.5 * (1.0 + lax.erf(value * 0.7071067811865476))
        + value * jnp.exp(-0.5 * value * value) * 0.3989422804014327
    )


def local_pass(wave, lens, w_first, norm_gain, norm_bias, w_second, cot):
    rows, samp = wave.shape
    ker_first = w_first.shape[0]
    stride_first = ker_first // 2
    chans = w_first.shape[1]
    taps_second = w_second.shape[0]
    frames0 = (samp - ker_first) // stride_first + 1
    frames1 = (frames0 - taps_second) // 2 + 1
    blocks = wave[:, : stride_first * (frames0 + 1)].reshape(rows, frames0 + 1, stride_first)
    patches = jnp.concatenate([blocks[:, :-1], blocks[:, 1:]], axis=2).reshape(
        rows * frames0, ker_first
    )
    pre0 = jnp.dot(patches, w_first, preferred_element_type=jnp.float32).reshape(
        rows, frames0, chans
    )
    valid0 = (lens - ker_first) // stride_first + 1
    mask0 = (jnp.arange(frames0, dtype=jnp.int32)[None, :] < valid0[:, None]).astype(jnp.float32)[
        :, :, None
    ]
    count0 = valid0.astype(jnp.float32)[:, None, None]
    mean0 = jnp.sum(pre0 * mask0, axis=1, keepdims=True) / count0
    centred = (pre0 - mean0) * mask0
    var0 = jnp.sum(centred * centred, axis=1, keepdims=True) / count0
    inv_std = lax.rsqrt(var0 + 1e-05)
    normed = centred * inv_std
    lifted = normed * norm_gain + norm_bias
    act0 = (jax.nn.gelu(lifted, approximate=False) * mask0).astype(jnp.bfloat16)
    span = 2 * frames1
    taps = jnp.concatenate(
        [act0[:, 0:span:2], act0[:, 1:span:2], act0[:, 2 : span + 1 : 2]], axis=2
    )
    taps = taps.reshape(rows * frames1, taps_second * chans)
    kernel = w_second.reshape(taps_second * chans, chans)
    pre1 = jnp.dot(taps, kernel, preferred_element_type=jnp.float32).reshape(rows, frames1, chans)
    valid1 = (valid0 - taps_second) // 2 + 1
    mask1 = (jnp.arange(frames1, dtype=jnp.int32)[None, :] < valid1[:, None]).astype(jnp.float32)[
        :, :, None
    ]
    features = (jax.nn.gelu(pre1, approximate=False) * mask1).astype(jnp.bfloat16)
    grad1 = (
        (cot.astype(jnp.float32) * gelu_slope(pre1) * mask1)
        .astype(jnp.bfloat16)
        .reshape(rows * frames1, chans)
    )
    grad_kernel = lax.dot_general(
        taps, grad1, (((0,), (0,)), ((), ())), preferred_element_type=jnp.float32
    )
    back = lax.dot_general(
        grad1, kernel, (((1,), (1,)), ((), ())), preferred_element_type=jnp.float32
    )
    back = back.reshape(rows, frames1, taps_second, chans)
    zero_row = jnp.zeros((rows, 1, chans), jnp.float32)
    even = back[:, :, 0] + jnp.concatenate([zero_row, back[:, :-1, 2]], axis=1)
    odd = back[:, :, 1]
    pieces = [jnp.stack([even, odd], axis=2).reshape(rows, span, chans), back[:, -1:, 2]]
    dact0 = jnp.concatenate(pieces, axis=1)
    dlift = dact0 * gelu_slope(lifted) * mask0
    grad_gain = jnp.sum(dlift * normed, axis=(0, 1))
    grad_bias = jnp.sum(dlift, axis=(0, 1))
    dnorm = dlift * norm_gain
    first_mean = jnp.sum(dnorm, axis=1, keepdims=True) / count0
    second_mean = jnp.sum(dnorm * normed, axis=1, keepdims=True) / count0
    dpre0 = inv_std * (dnorm - first_mean - normed * second_mean) * mask0
    grad_filter = lax.dot_general(
        patches.astype(jnp.float32),
        dpre0.reshape(rows * frames0, chans),
        (((0,), (0,)), ((), ())),
        precision=lax.Precision.HIGHEST,
        preferred_element_type=jnp.float32,
    )
    grads = jnp.concatenate(
        [grad_kernel, grad_filter, grad_gain[None, :], grad_bias[None, :]], axis=0
    )
    return (features, grads)


def shards(wave, lengths, order, w_first, norm_gain, norm_bias, w_second, cot):
    members = lax.axis_size("dev")
    member = lax.axis_index("dev")
    rows = wave.shape[0]
    share = rows // members
    own_order = lax.dynamic_index_in_dim(order, member, 0, keepdims=False)
    dealt = own_order.reshape(share, members).T.reshape(rows)
    outgoing = jnp.take(wave, dealt, axis=0)
    arrived = lax.all_to_all(outgoing, "dev", split_axis=0, concat_axis=0, tiled=True)
    group_lens = jnp.take_along_axis(lengths.reshape(members, rows), order, axis=1)
    group_lens = group_lens.reshape(members, share, members)
    lens = lax.dynamic_index_in_dim(group_lens, member, 2, keepdims=False).reshape(rows)
    features, grads = local_pass(arrived, lens, w_first, norm_gain, norm_bias, w_second, cot)
    chans = grads.shape[1]
    width = chans // members
    totals = lax.psum(grads, ("grp", "dev"))
    owned = lax.dynamic_slice_in_dim(totals, member * width, width, 1)
    taps_second = w_second.shape[0]
    ker_first = w_first.shape[0]
    in_chans = w_second.shape[1]
    grad_second = owned[: taps_second * in_chans].reshape(taps_second, in_chans, width)
    grad_first = owned[taps_second * in_chans : taps_second * in_chans + ker_first]
    grad_gain = owned[taps_second * in_chans + ker_first]
    grad_bias = owned[taps_second * in_chans + ker_first + 1]
    return (features, grad_second, grad_first, grad_gain, grad_bias)


def solution(mesh):
    placed = (
        P(("grp", "dev"), None),
        P("grp"),
        P("grp", None),
        P(),
        P(),
        P(),
        P(),
        P(("grp", "dev"), None, None),
    )
    return jax.shard_map(
        shards,
        mesh=mesh,
        in_specs=placed,
        out_specs=(
            P(("grp", "dev"), None, None),
            P(None, None, "dev"),
            P(None, "dev"),
            P("dev"),
            P("dev"),
        ),
        check_vma=False,
    )
```

profile of v0, /device:TPU:0, one launch (start us, length us, event | category | flops | bytes accessed | tf_op | source)
XLA Modules:
  0.0 265.5 jit_solution(12610484514627122667)
XLA Ops:
  7.2 0.0 copy-start
  7.2 0.8 fusion.63
  8.0 0.1 reshape.279
  8.1 0.1 copy.36
  8.2 0.1 reshape.280
  8.3 1.4 gather_fusion
  9.7 0.1 copy.35
  9.8 0.7 broadcast_select_fusion
  10.5 7.3 %all-to-all-start = ((bf16[8,4,384]{2,1,0:T(4,128)(2,1)}), bf16[8,4,384]{2,1,0:T(4,128)(2,1)S(1)}, u32[]{:S(2)}, u32[]{:S(2)}) async-start(bf16[8,4,384]{2,1,0:T(4,128)(2,1)} %broadcast_select_fusion), calls=%async_computation | async-start | bytes 49152 | tf_op jit(solution)/shard_map/all_to_all | solution.py:98
  17.7 0.0 all-reduce.3.cloned.1.call-start
  17.8 0.7 bitcast_or_fusion
  18.5 0.8 reshape.282
  19.2 0.1 reshape.295
  19.3 1.4 gather_fusion.1
  20.7 0.1 reshape.298
  20.8 0.7 and_select_fusion
  21.5 0.1 select_n.71
  21.6 0.1 constant_dynamic-slice_fusion.1
  21.7 0.1 copy.51
  21.8 0.1 and.47
  21.9 0.1 div.75
  22.0 0.1 fusion.61
  22.1 0.1 fusion.60
  22.2 2.2 all-to-all-done
  24.4 0.1 copy.37
  24.5 0.1 reshape.281
  24.6 0.2 copy.50
  24.8 0.2 copy.49
  25.0 0.0 copy-done.5
  25.0 0.0 copy-start.6
  25.0 0.0 copy-start.7
  25.0 0.9 multiply_reduce_fusion.3
  25.9 0.1 broadcast_divide_fusion.2
  26.0 1.1 multiply_reduce_fusion.2
  27.2 0.1 add_rsqrt_fusion
  27.3 1.0 copy-done.1
  28.2 0.0 copy-done.7
  28.2 14.2 %fusion.3 = bf16[32,75,512]{2,1,0:T(8,128)(2,1)} fusion(f32[512]{0:T(512)S(1)} %copy-done.6, f32[512]{0:T(512)S(1)} %copy-done.7, f32[32,75]{1,0:T(8,128)S(1)} %fusion.60, f32[32,512]{1,0:T(8,128)S(1)} %add_rsqrt_fusion, f32[32,75,512]{2,1,0:T(8,128)S(1)} %get-tuple-element.37, f32[32,512]{1,0:T(8,128)S(1)} %broadcast_divide_fusion.2), kind=kLoop, calls=%fused_computation.7 | loop fusion | flops 87244800 | bytes 7517568 | tf_op jit(solution)/shard_map/convert_element_type | solution.py:40
  42.4 9.9 %slice.47 = bf16[32,37,512]{2,1,0:T(8,128)(2,1)} slice(bf16[32,75,512]{2,1,0:T(8,128)(2,1)} %fusion.3), slice={[0:32:1], [2:75:2], [0:512:1]} | slice | bytes 2424832 | tf_op jit(solution)/shard_map/slice | solution.py:43
  52.3 9.8 %slice.46 = bf16[32,37,512]{2,1,0:T(8,128)(2,1)} slice(bf16[32,75,512]{2,1,0:T(8,128)(2,1)} %fusion.3), slice={[0:32:1], [1:74:2], [0:512:1]} | slice | bytes 2424832 | tf_op jit(solution)/shard_map/slice | solution.py:43
  62.1 9.7 %slice.45 = bf16[32,37,512]{2,1,0:T(8,128)(2,1)} slice(bf16[32,75,512]{2,1,0:T(8,128)(2,1)} %fusion.3), slice={[0:32:1], [0:74:2], [0:512:1]} | slice | bytes 2424832 | tf_op jit(solution)/shard_map/slice | solution.py:43
  71.8 11.5 %fusion.35 = (bf16[32,37,512]{2,1,0:T(8,128)(2,1)S(1)}, bf16[32,37,512]{2,1,0:T(8,128)(2,1)S(1)}) fusion(bf16[32,37,512]{2,0,1:T(8,128)(2,1)} %param.15, f32[32,37]{1,0:T(8,128)S(1)} %fusion.61, bf16[1536,512,1]{1,0,2:T(8,128)(2,1)S(1)} %bitcast.61, bf16[32,37,512]{2,1,0:T(8,128)(2,1)} %slice.47, bf16[32,37,512]{2,1,0:T(8,128)(2,1)} %slice.46, ...), kind=kOutput, calls=%fused_computation.59 | convolution fusion | flops 1920466944 | bytes 8852096 | tf_op jit(solution)/shard_map/dot_general | solution.py:47
  83.4 3.9 %convolution_bitcast_fusion = f32[1536,512]{1,0:T(8,128)} fusion(bf16[32,37,512]{2,1,0:T(8,128)(2,1)S(1)} %get-tuple-element.29, bf16[32,37,512]{2,1,0:T(8,128)(2,1)S(1)} %copy-done.2, bf16[32,37,512]{2,1,0:T(8,128)(2,1)S(1)} %copy-done.3, bf16[32,37,512]{2,1,0:T(8,128)(2,1)S(1)} %copy-done.4), kind=kOutput, calls=%fused_computation.48 | convolution fusion | flops 1873182720 | bytes 7995392 | tf_op jit(solution)/shard_map/dot_general | solution.py:58
  87.3 2.2 fusion.51
  89.5 0.1 slice_bitcast_fusion.2
  89.6 0.2 slice.65
  89.8 0.2 slice_bitcast_fusion
  90.1 0.6 fusion.37
  90.7 0.6 pad_maximum_fusion
  91.4 2.8 %copy.44 = f32[32,37,2,512]{3,0,2,1:T(8,128)S(1)} copy(f32[32,37,2,512]{3,1,2,0:T(8,128)S(1)} %pad_maximum_fusion) | data formatting | bytes 9699328 | tf_op jit(solution)/shard_map/stack | solution.py:68
  94.2 0.0 slice-start
  94.2 0.0 slice-start.1
  94.2 2.8 %copy.45 = f32[32,74,512]{2,1,0:T(8,128)S(1)} copy(f32[32,74,512]{2,0,1:T(8,128)S(1)} %bitcast.64) | data formatting | bytes 9699328 | tf_op jit(solution)/shard_map/reshape | solution.py:68
  97.1 5.9 %multiply_reduce_fusion = (f32[512]{0:T(512)S(1)}, f32[32,512]{1,0:T(8,128)S(1)}, f32[32,512]{1,0:T(8,128)S(1)}, f32[512]{0:T(512)S(1)}, f32[32,75,512]{2,1,0:T(8,128)S(1)}) fusion(f32[32,512]{1,0:T(8,128)S(1)} %add_rsqrt_fusion, f32[32,75]{1,0:T(8,128)S(1)} %fusion.60, f32[32,75,512]{2,1,0:T(8,128)S(1)} %bitcast.63, ...), kind=kLoop, calls=%fused_computation.15 | loop fusion | flops 28228608 | bytes 15025536 | tf_op jit(solution)/shard_map/reduce_sum | solution.py:71
  103.0 0.1 broadcast_divide_fusion.1
  103.1 3.5 %fusion.55 = f32[10,512]{1,0:T(8,128)S(1)} fusion(f32[32,75,512]{2,1,0:T(8,128)S(1)} %get-tuple-element.24, f32[32,512]{1,0:T(8,128)S(1)} %get-tuple-element.35, f32[32,512]{1,0:T(8,128)S(1)} %get-tuple-element.34, f32[512]{0:T(512)S(1)} %copy-done.7, f32[32,512]{1,0:T(8,128)S(1)} %add_rsqrt_fusion, f32[32,75]{1,0:T(8,128)S(1)} %fusion.60, ...), kind=kOutput, calls=%fused_computation.88 | convolution fusion | flops 158611200 | bytes 10172672 | tf_op jit(solution)/shard_map/dot_general | solution.py:77
  106.5 9.9 %concatenate.19 = f32[1548,512]{1,0:T(8,128)} concatenate(f32[1536,512]{1,0:T(8,128)} %convolution_bitcast_fusion, f32[10,512]{1,0:T(8,128)S(1)} %fusion.55, f32[1,512]{1,0:T(1,128)S(1)} %bitcast.68, f32[1,512]{1,0:T(1,128)S(1)} %bitcast.69), dimensions={0} | concatenate | bytes 6340608 | tf_op jit(solution)/shard_map/concatenate | solution.py:84
  116.4 0.0 all-reduce.3.cloned.1.call-update
  116.5 1.4 copy.46
  117.9 135.7 %all-reduce.3.cloned.1.call-done = f32[1548,512]{1,0:T(8,128)} async-done(((f32[1548,512]{1,0:T(8,128)}), f32[1548,512]{1,0:T(8,128)}) %all-reduce.3.cloned.1.call-update) | async-done | bytes 3170320 | tf_op jit(solution)/shard_map/psum | solution.py:105
  253.6 1.4 constant_dynamic-slice_fusion
  254.9 1.0 copy.47
  256.0 1.4 dynamic-slice.1
  257.3 1.3 dynamic-slice_bitcast_fusion
  (22 shorter events, 0.1 us)
Async XLA Ops:
  7.2 64.6 %copy-start = (bf16[3,512,512]{2,1,0:T(8,128)(2,1)S(1)}, bf16[3,512,512]{2,1,0:T(8,128)(2,1)}, u32[]{:S(2)}) copy-start(bf16[3,512,512]{2,1,0:T(8,128)(2,1)} %param.14) | copy-start | bytes 4718596
  7.2 17.8 %copy-start.5 = (bf16[10,512]{1,0:T(8,128)(2,1)S(1)}, bf16[10,512]{1,0:T(8,128)(2,1)}, u32[]{:S(2)}) copy-start(bf16[10,512]{1,0:T(8,128)(2,1)} %param.11) | copy-start | bytes 30724
  10.5 13.9 %all-to-all-start = ((bf16[8,4,384]{2,1,0:T(4,128)(2,1)}), bf16[8,4,384]{2,1,0:T(4,128)(2,1)S(1)}, u32[]{:S(2)}, u32[]{:S(2)}) async-start(bf16[8,4,384]{2,1,0:T(4,128)(2,1)} %broadcast_select_fusion), calls=%async_computation | async-start | bytes 49152 | tf_op jit(solution)/shard_map/all_to_all | solution.py:98
  17.7 235.8 %all-reduce.3.cloned.1.call-start = ((), (), s32[]{:S(2)}) async-start(), calls=%async_computation.1 | async-start | bytes 6356992 | tf_op jit(solution)/shard_map/psum | solution.py:105
  25.0 3.3 %copy-start.6 = (f32[512]{0:T(512)S(1)}, f32[512]{0:T(512)}, u32[]{:S(2)}) copy-start(f32[512]{0:T(512)} %param.13) | copy-start | bytes 6148
  25.0 3.3 %copy-start.7 = (f32[512]{0:T(512)S(1)}, f32[512]{0:T(512)}, u32[]{:S(2)}) copy-start(f32[512]{0:T(512)} %param.12) | copy-start | bytes 6148
  25.9 2.3 copy-start.1
  71.8 11.5 %copy-start.2 = (bf16[32,37,512]{2,1,0:T(8,128)(2,1)S(1)}, bf16[32,37,512]{2,1,0:T(8,128)(2,1)}, u32[]{:S(2)}) copy-start(bf16[32,37,512]{2,1,0:T(8,128)(2,1)} %slice.47) | copy-start | bytes 3637252
  71.8 11.5 %copy-start.3 = (bf16[32,37,512]{2,1,0:T(8,128)(2,1)S(1)}, bf16[32,37,512]{2,1,0:T(8,128)(2,1)}, u32[]{:S(2)}) copy-start(bf16[32,37,512]{2,1,0:T(8,128)(2,1)} %slice.46) | copy-start | bytes 3637252
  71.8 11.6 %copy-start.4 = (bf16[32,37,512]{2,1,0:T(8,128)(2,1)S(1)}, bf16[32,37,512]{2,1,0:T(8,128)(2,1)}, u32[]{:S(2)}) copy-start(bf16[32,37,512]{2,1,0:T(8,128)(2,1)} %slice.45) | copy-start | bytes 3637252
  94.2 2.9 %slice-start = ((s8[5242880]{0:T(1024)(128)(4,1)}), s8[4194304]{0:T(1024)(128)(4,1)S(1)}, s32[]{:S(2)}) async-start(s8[5242880]{0:T(1024)(128)(4,1)} %bitcast.62), calls=%async_computation.2 | async-start | bytes 8388608
  94.2 2.9 %slice-start.1 = ((s8[5242880]{0:T(1024)(128)(4,1)}), s8[1048576]{0:T(1024)(128)(4,1)S(1)}, s32[]{:S(2)}) async-start(s8[5242880]{0:T(1024)(128)(4,1)} %bitcast.62), calls=%async_computation.3 | async-start | bytes 2097152
Sparse Core Ops, SparseCore 0:
  116.6 136.9 all-reduce.2
where the time goes:
time: 267 us; the launch traced here: 266 us
  waiting for transfers between devices  138 us (52%)
  local copies, waits for them, and re-layouts  58.9 us (22%)
  other arithmetic  25 us (9%)
  matrix products  22.1 us (8%)
  between operations  14.3 us (5%)
  starting transfers between devices  7.29 us (3%)
    psum x1, waiting for transfers between devices, shards(): totals = lax.psum(grads, ('grp', 'dev'))  136 us
    convert_element_type x1, other arithmetic, local_pass(): act0 = (jax.nn.gelu(lifted, approximate=False) * mask0).astype(jnp.bfloat16)  14.2 us
    dot_general x1, matrix products, local_pass(): jnp.dot(taps, kernel, preferred_element_type=jnp.float32)  11.5 us
    concatenate x1, local copies, waits for them, and re-layouts, local_pass(): jnp.concatenate([grad_kernel, grad_filter, grad_gain[None, :], grad_bias[...  9.9 us
    slice x1, local copies, waits for them, and re-layouts, local_pass(): act0[:, 2:span + 1:2]  9.88 us
    slice x1, local copies, waits for them, and re-layouts, local_pass(): act0[:, 1:span:2]  9.77 us
    slice x1, local copies, waits for them, and re-layouts, local_pass(): act0[:, 0:span:2]  9.75 us
    all_to_all x1, starting transfers between devices, shards(): lax.all_to_all(outgoing, 'dev', split_axis=0, concat_axis=0, tiled=True)  7.25 us
  transfers between devices with their start and end apart: 2, of which 2 were waited for; matrix products, arithmetic and copies ran while one was open for 2% of the time, Pallas kernels for 0%

commit v1 on v0

v1 whole, which is shorter than its diff:
```python
import functools

import jax
import jax.numpy as jnp
from jax import lax
from jax.experimental import pallas as pl
from jax.experimental.pallas import tpu as pltpu
from jax.sharding import PartitionSpec as P

F32 = jnp.float32
BF16 = jnp.bfloat16
GROUP = 8
MIN_SAMPLES = 288
MIB = 1 << 20


def gelu_and_slope(value):
    size = jnp.abs(value)
    bell = jnp.exp(value * value * -0.5)
    base = 1.0 + size * (0.3275911 * 0.7071067811865476)
    frac = pl.reciprocal(base, approx=True)
    frac = frac * (2.0 - base * frac)
    poly = 0.5 * 1.061405429
    for coef in (-1.453152027, 1.421413741, -0.284496736, 0.254829592):
        poly = poly * frac + 0.5 * coef
    tail = poly * frac * bell
    gelu = jnp.maximum(value, 0.0) - size * tail
    phi = jnp.where(value < 0.0, tail, 1.0 - tail)
    return gelu, phi + value * bell * 0.3989422804014327


def rows_first(a, b):
    return lax.dot_general(a, b, (((0,), (0,)), ((), ())), preferred_element_type=F32)


def cols_both(a, b):
    return lax.dot_general(a, b, (((1,), (1,)), ((), ())), preferred_element_type=F32)


def dot(a, b):
    return jnp.dot(a, b, preferred_element_type=F32)


def iota(shape, dim):
    return lax.broadcasted_iota(jnp.int32, shape, dim)


def onehot(mask):
    return mask.astype(F32).astype(BF16)


def deal_kernel(members, order_ref, wave_ref, out_ref):
    rows = wave_ref.shape[0]
    share = rows // members
    own = order_ref[pl.ds(lax.axis_index("dev"), 1), :]
    picks = onehot(iota((rows, rows), 0) == own)
    row = iota((rows, rows), 0)
    column = iota((rows, rows), 1)
    swap = onehot(column == lax.rem(row, share) * members + row // share)
    choose = cols_both(swap, picks).astype(BF16)
    out_ref[...] = dot(choose, wave_ref[...]).astype(BF16)


def setup_kernel(members, frames0, order_ref, len_ref, w_ref, valid_ref, band_ref):
    rows = order_ref.shape[1]
    share = rows // members
    taps, chans = w_ref.shape
    stride = taps // 2
    dealt = iota((rows, members), 0)
    owner = onehot(dealt // share == iota((rows, members), 1))
    order_of = dot(owner, order_ref[...].astype(F32).astype(BF16))
    high = len_ref[...] // 16
    low = len_ref[...] - high * 16
    lens_of = dot(owner, high.astype(F32).astype(BF16)) * 16.0 + dot(owner, low.astype(F32).astype(BF16))
    row = iota((rows, rows), 0)
    column = iota((rows, rows), 1)
    mine = column == lax.rem(row, share) * members + lax.axis_index("dev")
    index = jnp.sum(jnp.where(mine, order_of, 0.0), axis=1, keepdims=True)
    picked = column == index.astype(jnp.int32)
    lens = jnp.sum(jnp.where(picked, lens_of, 0.0), axis=1, keepdims=True).astype(jnp.int32)
    valid = (lens - taps) // stride + 1
    valid_ref[...] = jnp.broadcast_to(valid, valid_ref.shape)
    depth = band_ref.shape[0]
    for f in range(GROUP):
        spread = onehot(iota((depth, taps), 0) == iota((depth, taps), 1) + stride * f)
        band_ref[:, f * chans : (f + 1) * chans] = dot(spread, w_ref[...]).astype(BF16)


def forward_kernel(
    frames0,
    frames1,
    taps,
    reverse,
    wave_ref,
    valid_ref,
    band_ref,
    gain_ref,
    bias_ref,
    w_ref,
    cot_ref,
    feat_ref,
    even_ref,
    odd_ref,
    normed_ref,
    slope_ref,
    inv_ref,
    patch_ref,
    grad_ref,
    grad_t_ref,
    pre0,
    pre1,
):
    rows, samp = wave_ref.shape
    chans = gain_ref.shape[1]
    stride = taps // 2
    depth = band_ref.shape[0]
    groups = pre0.shape[0]
    width = pre0.shape[2] // GROUP
    min_valid = (MIN_SAMPLES - taps) // stride + 1
    free_groups = min(min_valid // GROUP, frames0 // GROUP)
    full_groups = frames0 // GROUP
    wave = wave_ref[...]
    for g in range(groups):
        pick = onehot(iota((samp, depth), 0) == iota((samp, depth), 1) + GROUP * stride * g)
        patch_ref[g] = dot(wave, pick).astype(BF16)
    patches = patch_ref[...].reshape(groups * rows, depth)

    for block in range(chans // width):
        lanes = slice(block * width, (block + 1) * width)
        for f in range(GROUP):
            cols = slice(f * chans + block * width, f * chans + (block + 1) * width)
            pre0[:, :, f * width : (f + 1) * width] = dot(patches, band_ref[:, cols]).reshape(groups, rows, width)
        valid = jnp.broadcast_to(valid_ref[:, :1], (rows, width))
        count = valid.astype(F32)

        def frame(g, f):
            return pre0[g, :, f * width : (f + 1) * width]

        def over_frames(body, init):
            def step(masked, g, carry):
                for f in range(GROUP):
                    carry = body(carry, g, f, masked)
                return carry

            carry = lax.fori_loop(0, free_groups, functools.partial(step, False), init)
            carry = lax.fori_loop(free_groups, full_groups, functools.partial(step, True), carry)
            for f in range(frames0 - full_groups * GROUP):
                carry = body(carry, full_groups, f, True)
            return carry

        def masked_to(value, g, f, masked):
            return jnp.where(valid > g * GROUP + f, value, 0.0) if masked else value

        def add_mean(total, g, f, masked):
            return total + masked_to(frame(g, f), g, f, masked)

        mean = over_frames(add_mean, jnp.zeros((rows, width), F32)) / count

        def add_var(total, g, f, masked):
            centred = masked_to(frame(g, f) - mean, g, f, masked)
            return total + centred * centred

        var = over_frames(add_var, jnp.zeros((rows, width), F32)) / count
        inv = lax.rsqrt(var + 1e-05)
        inv_ref[:, lanes] = inv
        gain = jnp.broadcast_to(gain_ref[:, lanes], (rows, width))
        bias = jnp.broadcast_to(bias_ref[:, lanes], (rows, width))

        def finish(carry, g, f, masked):
            normed = (frame(g, f) - mean) * inv
            gelu, slope = gelu_and_slope(normed * gain + bias)
            t = g * GROUP + f
            normed_ref[t, :, lanes] = masked_to(normed, g, f, masked)
            slope_ref[t, :, lanes] = masked_to(slope, g, f, masked)
            act_ref = odd_ref if f % 2 else even_ref
            act_ref[g * (GROUP // 2) + f // 2, :, lanes] = masked_to(gelu, g, f, masked).astype(BF16)
            return carry

        over_frames(finish, 0)
    for ref, used in ((even_ref, (frames0 + 1) // 2), (odd_ref, frames0 // 2)):
        ref[used:] = jnp.zeros((ref.shape[0] - used,) + ref.shape[1:], BF16)

    grad_ref[0] = jnp.zeros(grad_ref.shape[1:], BF16)
    grad_ref[frames1 + 1] = jnp.zeros(grad_ref.shape[1:], BF16)
    padded = grad_t_ref.shape[1]
    used = frames1 * rows
    grad_t_ref[:, (used // 128) * 128 :] = jnp.zeros((chans, padded - (used // 128) * 128), BF16)
    valid = jnp.broadcast_to(valid_ref[:, :1], (rows, chans))
    valid1 = lax.shift_right_arithmetic(valid - 3, 1) + 1
    chunk = 12
    for first in range(0, frames1 - chunk + 1, chunk):
        count = chunk if first + 2 * chunk <= frames1 else frames1 - first
        size = count * rows
        total = dot(even_ref[first : first + count].reshape(size, chans), w_ref[0])
        total += dot(odd_ref[first : first + count].reshape(size, chans), w_ref[1])
        total += dot(even_ref[first + 1 : first + count + 1].reshape(size, chans), w_ref[2])
        pre1[:count] = total.reshape(count, rows, chans)

        def activate(u, carry):
            gelu, slope = gelu_and_slope(pre1[u])
            keep = valid1 > u + first
            feat_ref[u + first] = jnp.where(keep, gelu, 0.0).astype(BF16)
            grad = cot_ref[u + first].astype(F32) * slope
            grad_ref[u + first + 1] = jnp.where(keep, grad, 0.0).astype(BF16)
            return carry

        lax.fori_loop(0, count, activate, 0)
        turned = grad_ref[first + 1 : first + 1 + count].reshape(size, chans).T
        slab = chans // len(reverse)
        for place, source in enumerate(reverse):
            grad_t_ref[place * slab : (place + 1) * slab, first * rows : first * rows + size] = turned[
                source * slab : (source + 1) * slab
            ]


def outer_kernel(even_ref, odd_ref, grad_t_ref, keep_ref, send_ref):
    frames = grad_t_ref.shape[1] // even_ref.shape[1]
    rows, chans = even_ref.shape[1:]
    half = chans // 2
    core = lax.rem(lax.axis_index("grp"), 2)
    turned = grad_t_ref[...]
    for tap, (ref, skip) in enumerate(((even_ref, 0), (odd_ref, 0), (even_ref, 1))):
        for side, out_ref in ((core, keep_ref), (1 - core, send_ref)):
            lanes = pl.ds(pl.multiple_of(side * half, half), half)
            acts = ref[skip : skip + frames, :, lanes].reshape(frames * rows, half)
            out_ref[:, tap * half : (tap + 1) * half] = dot(turned, acts).astype(out_ref.dtype)


def backward_kernel(
    frames0,
    frames1,
    taps,
    valid_ref,
    normed_ref,
    slope_ref,
    inv_ref,
    patch_ref,
    grad_ref,
    gain_ref,
    w_ref,
    out_ref,
    lift,
    dpre0,
    spread,
):
    groups, rows, depth = patch_ref.shape
    chans = gain_ref.shape[1]
    stride = taps // 2
    width = dpre0.shape[2] // GROUP
    full_groups = frames0 // GROUP
    patches = patch_ref[...].reshape(groups * rows, depth)
    evens = (frames0 + 1) // 2
    odds = frames0 // 2
    first = grad_ref[1 : evens + 1].reshape(evens * rows, chans)
    second = grad_ref[1 : odds + 1].reshape(odds * rows, chans)
    third = grad_ref[0:evens].reshape(evens * rows, chans)
    for block in range(chans // width):
        lanes = slice(block * width, (block + 1) * width)
        lift[0, :evens] = (cols_both(first, w_ref[0, lanes]) + cols_both(third, w_ref[2, lanes])).reshape(
            evens, rows, width
        )
        lift[1, :odds] = cols_both(second, w_ref[1, lanes]).reshape(odds, rows, width)

        def slopes(parity, e, carry):
            bias_sum, gain_sum = carry
            t = 2 * e + parity
            dlift = lift[parity, e] * slope_ref[t, :, lanes]
            lift[parity, e] = dlift
            return bias_sum + dlift, gain_sum + dlift * normed_ref[t, :, lanes]

        def both(e, carry):
            return slopes(1, e, slopes(0, e, carry))

        zero = jnp.zeros((rows, width), F32)
        carry = lax.fori_loop(0, odds, both, (zero, zero))
        if evens > odds:
            carry = slopes(0, odds, carry)
        bias_sum, gain_sum = carry
        out_ref[taps : taps + 1, lanes] = jnp.sum(gain_sum, axis=0, keepdims=True)
        out_ref[taps + 1 : taps + 2, lanes] = jnp.sum(bias_sum, axis=0, keepdims=True)
        valid = jnp.broadcast_to(valid_ref[:, :1], (rows, width))
        count = valid.astype(F32)
        scale = inv_ref[:, lanes] * gain_ref[:, lanes]
        bias_sum = bias_sum / count
        gain_sum = gain_sum / count

        def finish(g, f):
            t = g * GROUP + f
            dlift = lift[f % 2, g * (GROUP // 2) + f // 2]
            value = scale * (dlift - bias_sum - normed_ref[t, :, lanes] * gain_sum)
            dpre0[g, :, f * width : (f + 1) * width] = jnp.where(valid > t, value, 0.0).astype(BF16)

        def whole(g, carry):
            for f in range(GROUP):
                finish(g, f)
            return carry

        lax.fori_loop(0, full_groups, whole, 0)
        rest = frames0 - full_groups * GROUP
        for f in range(rest):
            finish(full_groups, f)
        if full_groups < groups:
            dpre0[full_groups, :, rest * width :] = jnp.zeros((rows, (GROUP - rest) * width), BF16)
        spread[...] = rows_first(patches, dpre0[...].reshape(groups * rows, GROUP * width))
        total = jnp.zeros((taps, width), F32)
        for f in range(GROUP):
            total += spread[stride * f : stride * f + taps, f * width : (f + 1) * width]
        out_ref[:taps, lanes] = total


def fold_kernel(axis, bit, keep_ref, got_ref, next_ref, send_ref):
    half = keep_ref.shape[0] // 2
    side = lax.rem(lax.shift_right_logical(lax.axis_index(axis), bit), 2)
    mine = pl.ds(pl.multiple_of(side * half, half), half)
    other = pl.ds(pl.multiple_of((1 - side) * half, half), half)
    next_ref[...] = keep_ref[mine, :] + got_ref[mine, :].astype(F32)
    send_ref[...] = (keep_ref[other, :] + got_ref[other, :].astype(F32)).astype(BF16)


def last_fold_kernel(keep_ref, got_ref, send_ref):
    send_ref[...] = (keep_ref[...] + got_ref[...].astype(F32)).astype(BF16)


def join_kernel(own_ref, other_ref, out_ref):
    half = out_ref.shape[2] // 2
    core = lax.rem(lax.axis_index("grp"), 2)
    for tap in range(out_ref.shape[0]):
        lanes = slice(tap * half, (tap + 1) * half)
        out_ref[tap, :, pl.ds(pl.multiple_of(core * half, half), half)] = own_ref[:, lanes]
        out_ref[tap, :, pl.ds(pl.multiple_of((1 - core) * half, half), half)] = other_ref[:, lanes]


def call(kernel, outs, args, scratch=(), limit=32, flops=0, touched=0):
    vmem = pl.BlockSpec(memory_space=pltpu.VMEM)
    return pl.pallas_call(
        kernel,
        out_shape=[jax.ShapeDtypeStruct(shape, kind) for shape, kind in outs],
        in_specs=[vmem] * len(args),
        out_specs=[vmem] * len(outs),
        scratch_shapes=[pltpu.VMEM(shape, kind) for shape, kind in scratch],
        compiler_params=pltpu.CompilerParams(vmem_limit_bytes=limit * MIB),
        cost_estimate=pl.CostEstimate(flops=flops, bytes_accessed=touched, transcendentals=0),
    )(*args)


def swap(value, axis, bit):
    size = lax.axis_size(axis)
    return lax.ppermute(value, axis, [(i, i ^ (1 << bit)) for i in range(size)])


def shards(wave, lengths, order, w_first, norm_gain, norm_bias, w_second, cot):
    members = lax.axis_size("dev")
    groups_of = lax.axis_size("grp")
    rows, samp = wave.shape
    taps, chans = w_first.shape
    taps_second = w_second.shape[0]
    stride = taps // 2
    frames0 = (samp - taps) // stride + 1
    frames1 = (frames0 - taps_second) // 2 + 1
    groups = -(-frames0 // GROUP)
    depth = 128
    width = 256
    dev_bits = members.bit_length() - 1
    grp_bits = groups_of.bit_length() - 1

    outgoing = call(functools.partial(deal_kernel, members), [((rows, samp), BF16)], [order, wave])[0]
    arrived = lax.all_to_all(outgoing, "dev", split_axis=0, concat_axis=0, tiled=True)
    valid, band = call(
        functools.partial(setup_kernel, members, frames0),
        [((rows, 128), jnp.int32), ((depth, GROUP * chans), BF16)],
        [order, lengths.reshape(members, rows), w_first],
    )
    gain = norm_gain.reshape(1, chans)
    bias = norm_bias.reshape(1, chans)
    cot_t = cot.transpose(1, 0, 2)
    pad_frames = -(-frames1 // 4) * 4
    reverse = [int(format(i, "b").zfill(dev_bits)[::-1], 2) for i in range(members)]
    feat, even, odd, normed, slope, inv, patch, grad, grad_t = call(
        functools.partial(forward_kernel, frames0, frames1, taps, reverse),
        [
            ((frames1, rows, chans), BF16),
            ((pad_frames + 1, rows, chans), BF16),
            ((pad_frames, rows, chans), BF16),
            ((frames0, rows, chans), F32),
            ((frames0, rows, chans), F32),
            ((rows, chans), F32),
            ((groups, rows, depth), BF16),
            ((frames1 + 2, rows, chans), BF16),
            ((chans, pad_frames * rows), BF16),
        ],
        [arrived, valid, band, gain, bias, w_second, cot_t],
        scratch=[((groups, rows, GROUP * width), F32), ((16, rows, chans), F32)],
        limit=48,
    )
    keep, send = call(
        outer_kernel,
        [((chans, taps_second * chans // 2), F32), ((chans, taps_second * chans // 2), BF16)],
        [even, odd, grad_t],
    )
    small = call(
        functools.partial(backward_kernel, frames0, frames1, taps),
        [((16, chans), F32)],
        [valid, normed, slope, inv, patch, grad, gain, w_second],
        scratch=[
            ((2, (frames0 + 1) // 2, rows, width), F32),
            ((groups, rows, GROUP * width), BF16),
            ((depth, GROUP * width), F32),
        ],
        limit=48,
    )[0]

    got = swap(send, "grp", 0)
    for bit in range(dev_bits):
        half = (keep.shape[0] // 2, keep.shape[1])
        keep, send = call(functools.partial(fold_kernel, "dev", bit), [(half, F32), (half, BF16)], [keep, got])
        got = swap(send, "dev", bit)
    total = call(last_fold_kernel, [(keep.shape, BF16)], [keep, got])[0]
    for bit in range(1, grp_bits):
        got = swap(total, "grp", bit)
        total = total.astype(F32) + got.astype(F32)
        if bit < grp_bits - 1:
            total = total.astype(BF16)
    total = total.astype(F32)
    other = swap(total, "grp", 0)
    grad_second = call(join_kernel, [((taps_second, chans // members, chans), F32)], [total, other])[0]

    for axis, bits in (("dev", dev_bits), ("grp", grp_bits)):
        for bit in range(bits):
            small = small + swap(small, axis, bit)
    member = lax.axis_index("dev")
    share = chans // members
    owned = lax.dynamic_slice_in_dim(small, member * share, share, 1)
    return (
        feat.transpose(1, 0, 2),
        grad_second.transpose(0, 2, 1),
        owned[:taps],
        owned[taps],
        owned[taps + 1],
    )


def solution(mesh):
    placed = (
        P(("grp", "dev"), None),
        P("grp"),
        P("grp", None),
        P(),
        P(),
        P(),
        P(),
        P(("grp", "dev"), None, None),
    )
    return jax.shard_map(
        shards,
        mesh=mesh,
        in_specs=placed,
        out_specs=(
            P(("grp", "dev"), None, None),
            P(None, None, "dev"),
            P(None, "dev"),
            P("dev"),
            P("dev"),
        ),
        check_vma=False,
    )
```

time: 267 us -> 92 us (0.34)
  waiting for transfers between devices: 138 us -> 29.6 us
  local copies, waits for them, and re-layouts: 58.9 us -> 10 us
  Pallas kernels: 0 us -> 34.1 us
  other arithmetic: 25 us -> 0.12 us
  matrix products: 22.1 us -> 0 us
  between operations: 14.3 us -> 0.74 us
  starting transfers between devices: 7.29 us -> 16.9 us
    psum x1 -> x0, waiting for transfers between devices: 136 us -> none  [shards(): totals = lax.psum(grads, ('grp', 'dev'))]
    pallas_call x0 -> x10, Pallas kernels: none -> 34.1 us  [call(): pl.pallas_call(kernel, out_shape=[jax.ShapeDtypeStruct(shape, kind) for s...]
    slice x8 -> x0, local copies, waits for them, and re-layouts: 32.6 us -> none  [the longest x1 9.88 us: local_pass(): act0[:, 2:span + 1:2]]
    ppermute x0 -> x11, waiting for transfers between devices: none -> 25.5 us  [swap(): return lax.ppermute(value, axis, [(i, i ^ 1 << bit) for i in range(size)])]
    dot_general x5 -> x0, matrix products: 22.1 us -> none  [the longest x1 11.5 us: local_pass(): jnp.dot(taps, kernel, preferred_element_type=jnp.float32)]
    convert_element_type x4 -> x0, other arithmetic: 14.3 us -> none  [the longest x1 14.2 us: local_pass(): act0 = (jax.nn.gelu(lifted, approximate=False) * mask0).astype(jnp.bfloat16)]
    concatenate x1 -> x0, local copies, waits for them, and re-layouts: 9.9 us -> none  [local_pass(): jnp.concatenate([grad_kernel, grad_filter, grad_gain[None, :], grad_bias[...]
    ppermute x0 -> x11, starting transfers between devices: none -> 9.69 us  [swap(): return lax.ppermute(value, axis, [(i, i ^ 1 << bit) for i in range(size)])]
  transfers between devices with their start and end apart: 2 -> 12, of which waited for: 2 -> 11; matrix products, arithmetic and copies ran while one was open for 2% -> 1% of each run, Pallas kernels for 0% -> 12%
where the time goes in v1:
time: 92 us; the launch traced here: 91.5 us
  Pallas kernels  34.1 us (37%)
  waiting for transfers between devices  29.6 us (32%)
  starting transfers between devices  16.9 us (18%)
  local copies, waits for them, and re-layouts  10 us (11%)
    pallas_call x10, Pallas kernels, call(): pl.pallas_call(kernel, out_shape=[jax.ShapeDtypeStruct(shape, kind) for s...  34.1 us
    ppermute x11, waiting for transfers between devices, swap(): return lax.ppermute(value, axis, [(i, i ^ 1 << bit) for i in range(size)])  25.5 us
    ppermute x11, starting transfers between devices, swap(): return lax.ppermute(value, axis, [(i, i ^ 1 << bit) for i in range(size)])  9.69 us
    unnamed x24, local copies, waits for them, and re-layouts  8.12 us
    all_to_all x1, starting transfers between devices, shards(): lax.all_to_all(outgoing, 'dev', split_axis=0, concat_axis=0, tiled=True)  7.25 us
    all_to_all x1, waiting for transfers between devices, shards(): lax.all_to_all(outgoing, 'dev', split_axis=0, concat_axis=0, tiled=True)  4.04 us
  transfers between devices with their start and end apart: 12, of which 11 were waited for; matrix products, arithmetic and copies ran while one was open for 1% of the time, Pallas kernels for 12%

profile of v1, /device:TPU:0, one launch (start us, length us, event | category | flops | bytes accessed | tf_op | source)
XLA Modules:
  0.0 91.5 jit_solution(6222212822078642959)
XLA Ops:
  0.6 0.0 copy-start.4
  0.6 0.7 copy-done.4
  1.4 0.0 copy-start.6
  1.4 0.7 copy-done.6
  2.1 0.2 shard_map.119
  2.3 0.6 all_to_all.7
  2.9 7.3 %all-to-all-start = ((bf16[8,4,384]{2,1,0:T(4,128)(2,1)}), bf16[8,4,384]{2,1,0:T(4,128)(2,1)S(1)}, u32[]{:S(2)}, u32[]{:S(2)}) async-start(bf16[8,4,384]{2,1,0:T(4,128)(2,1)} %all_to_all.7), calls=%async_computation | async-start | bytes 49152 | tf_op jit(solution)/shard_map/all_to_all | solution.py:367
  10.2 0.8 reshape.21.len_ref
  10.9 0.0 copy-start.5
  10.9 0.7 copy-done.5
  11.7 0.0 copy-start.7
  11.7 0.7 copy-done.7
  12.3 0.4 shard_map.120
  12.8 4.0 %all-to-all-done = bf16[8,4,384]{2,1,0:T(4,128)(2,1)S(1)} async-done(((bf16[8,4,384]{2,1,0:T(4,128)(2,1)}), bf16[8,4,384]{2,1,0:T(4,128)(2,1)S(1)}, u32[]{:S(2)}, u32[]{:S(2)}) %all-to-all-start) | async-done | bytes 24608 | tf_op jit(solution)/shard_map/all_to_all | solution.py:367
  16.8 0.0 copy-start.3
  16.8 1.3 %copy-done.3 = bf16[32,37,512]{2,0,1:T(8,128)(2,1)S(1)} copy-done((bf16[32,37,512]{2,0,1:T(8,128)(2,1)S(1)}, bf16[32,37,512]{2,0,1:T(8,128)(2,1)}, u32[]{:S(2)}) %copy-start.3) | copy-done | bytes 1212440
  18.1 0.0 copy-start.8
  18.1 0.7 copy-done.8
  18.8 0.0 copy-start.10
  18.8 0.7 copy-done.10
  19.5 19.6 %shard_map.121 = (bf16[37,32,512]{2,1,0:T(8,128)(2,1)}, bf16[41,32,512]{2,1,0:T(8,128)(2,1)}, bf16[40,32,512]{2,1,0:T(8,128)(2,1)S(1)}, f32[75,32,512]{2,1,0:T(8...) custom-call(bf16[32,384]{1,0:T(8,128)(2,1)S(1)} %all_to_all.9.wave_r, ...), custom_call_target="tpu_custom_call" | custom-call | tf_op jit(solution)/shard_map/pallas_call | solution.py:335
  39.1 0.0 copy-start.1
  39.1 1.3 %copy-done.1 = bf16[41,32,512]{2,1,0:T(8,128)(2,1)S(1)} copy-done((bf16[41,32,512]{2,1,0:T(8,128)(2,1)S(1)}, bf16[41,32,512]{2,1,0:T(8,128)(2,1)}, u32[]{:S(2)}) %copy-start.1) | copy-done | bytes 1343512
  40.4 0.0 copy-start.2
  40.4 1.3 %copy-done.2 = bf16[512,1280]{1,0:T(8,128)(2,1)S(1)} copy-done((bf16[512,1280]{1,0:T(8,128)(2,1)S(1)}, bf16[512,1280]{1,0:T(8,128)(2,1)}, u32[]{:S(2)}) %copy-start.2) | copy-done | bytes 1310744
  41.8 2.2 %shard_map.122 = (f32[512,768]{1,0:T(8,128)S(1)}, bf16[512,768]{1,0:T(8,128)(2,1)S(1)}) custom-call(bf16[41,32,512]{2,1,0:T(8,128)(2,1)S(1)} %copy-done.1, bf16[40,32,512]{2,1,0:T(8,128)(2,1)S(1)} %get-tuple-element.28.odd_ref, bf16[512,1280]{1,0:T(8,128)(2,1)S(1)} %copy-done.2), custom_call_target="tpu_custom_call" | custom-call | tf_op jit(solution)/shard_map/pallas_call | solution.py:335
  44.0 0.1 collective-permute-start
  44.0 2.3 %collective-permute-done.got_ref = bf16[512,768]{1,0:T(8,128)(2,1)S(1)} collective-permute-done((bf16[512,768]{1,0:T(8,128)(2,1)S(1)}, bf16[512,768]{1,0:T(8,128)(2,1)S(1)}, u32[]{:S(2)}, u32[]{:S(2)}) %collective-permute-start) | collective-permute-done | bytes 786464 | tf_op jit(solution)/shard_map/ppermute | solution.py:348
  46.3 0.0 copy-start
  46.3 0.0 copy-start.9
  46.3 0.1 shard_map.123
  46.4 0.6 collective-permute-start.1
  47.0 10.7 %collective-permute-done.1.got_ref = bf16[256,768]{1,0:T(8,128)(2,1)S(1)} collective-permute-done((bf16[256,768]{1,0:T(8,128)(2,1)S(1)}, bf16[256,768]{1,0:T(8,128)(2,1)S(1)}, u32[]{:S(2)}, u32[]{:S(2)}) %collective-permute-start.1) | collective-permute-done | bytes 393248 | tf_op jit(solution)/shard_map/ppermute | solution.py:348
  57.7 0.1 shard_map.124
  57.7 0.5 collective-permute-start.2
  58.2 0.0 copy-done
  58.2 0.0 copy-done.9
  58.2 10.5 %shard_map.128 = f32[16,512]{1,0:T(8,128)S(1)} custom-call(s32[32,128]{1,0:T(8,128)S(1)} %get-tuple-element.24.valid_ref, f32[75,32,512]{2,1,0:T(8,128)} %get-tuple-element.38.normed_ref, f32[75,32,512]{2,1,0:T(8,128)} %get-tuple-element.39.slope_ref, f32[32,512]{1,0:T(8,128)S(1)} %get-tuple-element.40.inv_ref, ...), custom_call_target="tpu_custom_call" | custom-call | tf_op jit(solution)/shard_map/pallas_call | solution.py:335
  68.8 0.8 collective-permute-start.6
  69.6 3.2 %collective-permute-done.6 = f32[16,512]{1,0:T(8,128)S(1)} collective-permute-done((f32[16,512]{1,0:T(8,128)S(1)}, f32[16,512]{1,0:T(8,128)S(1)}, u32[]{:S(2)}, u32[]{:S(2)}) %collective-permute-start.6) | collective-permute-done | bytes 32800 | tf_op jit(solution)/shard_map/ppermute | solution.py:348
  72.8 1.6 %collective-permute-start.7 = (f32[16,512]{1,0:T(8,128)S(1)}, f32[16,512]{1,0:T(8,128)S(1)}, u32[]{:S(2)}, u32[]{:S(2)}) collective-permute-start(f32[16,512]{1,0:T(8,128)S(1)} %add.22), channel_id=1, source_target_pairs={{0,2},{1,3},{2,0},{3,1},{4,6},{5,7},{6,4},{7,5},{8,10},{9,11},{10,... | collective-permute-start | bytes 98312 | tf_op jit(solution)/shard_map/ppermute | solution.py:348
  74.4 2.3 %collective-permute-done.7 = f32[16,512]{1,0:T(8,128)S(1)} collective-permute-done((f32[16,512]{1,0:T(8,128)S(1)}, f32[16,512]{1,0:T(8,128)S(1)}, u32[]{:S(2)}, u32[]{:S(2)}) %collective-permute-start.7) | collective-permute-done | bytes 32800 | tf_op jit(solution)/shard_map/ppermute | solution.py:348
  76.7 0.7 collective-permute-start.8
  77.4 0.0 collective-permute-done.2.got_ref
  77.4 2.3 %collective-permute-start.3 = (bf16[64,768]{1,0:T(8,128)(2,1)S(1)}, bf16[64,768]{1,0:T(8,128)(2,1)S(1)}, u32[]{:S(2)}, u32[]{:S(2)}) collective-permute-start(bf16[64,768]{1,0:T(8,128)(2,1)S(1)} %get-tuple-element.37), channel_id=1, source_target_pairs={{0,4},{1,5},{2,6},{3,7},{4,0},{5,1},{6,2},{7,3},{8,12},{9,13},{10,... | collective-permute-start | bytes 294920 | tf_op jit(solution)/shard_map/ppermute | solution.py:348
  79.7 1.8 %collective-permute-done.8 = f32[16,512]{1,0:T(8,128)S(1)} collective-permute-done((f32[16,512]{1,0:T(8,128)S(1)}, f32[16,512]{1,0:T(8,128)S(1)}, u32[]{:S(2)}, u32[]{:S(2)}) %collective-permute-start.8) | collective-permute-done | bytes 32800 | tf_op jit(solution)/shard_map/ppermute | solution.py:348
  81.5 0.0 collective-permute-start.9
  81.5 1.2 %collective-permute-done.9 = f32[16,512]{1,0:T(8,128)S(1)} collective-permute-done((f32[16,512]{1,0:T(8,128)S(1)}, f32[16,512]{1,0:T(8,128)S(1)}, u32[]{:S(2)}, u32[]{:S(2)}) %collective-permute-start.9) | collective-permute-done | bytes 32800 | tf_op jit(solution)/shard_map/ppermute | solution.py:348
  82.7 1.5 %collective-permute-start.10 = (f32[16,512]{1,0:T(8,128)S(1)}, f32[16,512]{1,0:T(8,128)S(1)}, u32[]{:S(2)}, u32[]{:S(2)}) collective-permute-start(f32[16,512]{1,0:T(8,128)S(1)} %add.25), channel_id=1, source_target_pairs={{0,16},{8,24},{16,0},{24,8},{1,17},{9,25},{17,1},{25,9},{2,18},{10... | collective-permute-start | bytes 98312 | tf_op jit(solution)/shard_map/ppermute | solution.py:348
  84.3 0.2 collective-permute-done.3.got_ref
  84.5 1.6 %collective-permute-start.4 = (bf16[64,768]{1,0:T(8,128)(2,1)S(1)}, bf16[64,768]{1,0:T(8,128)(2,1)S(1)}, u32[]{:S(2)}, u32[]{:S(2)}) collective-permute-start(bf16[64,768]{1,0:T(8,128)(2,1)S(1)} %shard_map.126), channel_id=1, source_target_pairs={{0,16},{8,24},{16,0},{24,8},{1,17},{9,25},{17,1},{25,9},{2,18},{10... | collective-permute-start | bytes 294920 | tf_op jit(solution)/shard_map/ppermute | solution.py:348
  86.0 0.6 collective-permute-done.10
  86.7 0.1 dynamic-slice_add_fusion
  86.7 0.0 copy-start.11
  86.7 2.4 %collective-permute-done.4 = bf16[64,768]{1,0:T(8,128)(2,1)S(1)} collective-permute-done((bf16[64,768]{1,0:T(8,128)(2,1)S(1)}, bf16[64,768]{1,0:T(8,128)(2,1)S(1)}, u32[]{:S(2)}, u32[]{:S(2)}) %collective-permute-start.4) | collective-permute-done | bytes 98336 | tf_op jit(solution)/shard_map/ppermute | solution.py:348
  89.2 0.1 collective-permute-start.5
  89.2 0.5 slice_bitcast_fusion
  89.8 0.9 collective-permute-done.5.other_ref
  90.7 0.8 shard_map.127
  91.4 0.0 copy-done.11
  (8 shorter events, 0.1 us)
Async XLA Ops:
  0.6 0.7 copy-start.4
  1.4 0.7 copy-start.6
  2.9 13.9 %all-to-all-start = ((bf16[8,4,384]{2,1,0:T(4,128)(2,1)}), bf16[8,4,384]{2,1,0:T(4,128)(2,1)S(1)}, u32[]{:S(2)}, u32[]{:S(2)}) async-start(bf16[8,4,384]{2,1,0:T(4,128)(2,1)} %all_to_all.7), calls=%async_computation | async-start | bytes 49152 | tf_op jit(solution)/shard_map/all_to_all | solution.py:367
  10.9 0.7 copy-start.5
  11.7 0.7 copy-start.7
  16.8 1.3 %copy-start.3 = (bf16[32,37,512]{2,0,1:T(8,128)(2,1)S(1)}, bf16[32,37,512]{2,0,1:T(8,128)(2,1)}, u32[]{:S(2)}) copy-start(bf16[32,37,512]{2,0,1:T(8,128)(2,1)} %param.15) | copy-start | bytes 3637252
  18.1 0.7 copy-start.8
  18.8 0.7 copy-start.10
  39.1 1.3 %copy-start.1 = (bf16[41,32,512]{2,1,0:T(8,128)(2,1)S(1)}, bf16[41,32,512]{2,1,0:T(8,128)(2,1)}, u32[]{:S(2)}) copy-start(bf16[41,32,512]{2,1,0:T(8,128)(2,1)} %get-tuple-element.27.even_ref) | copy-start | bytes 4030468
  40.4 1.3 %copy-start.2 = (bf16[512,1280]{1,0:T(8,128)(2,1)S(1)}, bf16[512,1280]{1,0:T(8,128)(2,1)}, u32[]{:S(2)}) copy-start(bf16[512,1280]{1,0:T(8,128)(2,1)} %get-tuple-element.29.grad_t_ref) | copy-start | bytes 3932164
  44.0 2.4 %collective-permute-start = (bf16[512,768]{1,0:T(8,128)(2,1)S(1)}, bf16[512,768]{1,0:T(8,128)(2,1)S(1)}, u32[]{:S(2)}, u32[]{:S(2)}) collective-permute-start(bf16[512,768]{1,0:T(8,128)(2,1)S(1)} %get-tuple-element.31), channel_id=1, source_target_pairs={{0,8},{8,0},{16,24},{24,16},{1,9},{9,1},{17,25},{25,17},{2,10},{10... | collective-permute-start | bytes 2359304 | tf_op jit(solution)/shard_map/ppermute | solution.py:348
  46.3 11.9 %copy-start = (bf16[3,512,512]{2,1,0:T(8,128)(2,1)S(1)}, bf16[3,512,512]{2,1,0:T(8,128)(2,1)}, u32[]{:S(2)}) copy-start(bf16[3,512,512]{2,1,0:T(8,128)(2,1)} %w_ref.5) | copy-start | bytes 4718596
  46.3 11.9 %copy-start.9 = (f32[512]{0:T(512)S(1)}, f32[512]{0:T(512)}, u32[]{:S(2)}) copy-start(f32[512]{0:T(512)} %param.12) | copy-start | bytes 6148
  46.4 11.2 %collective-permute-start.1 = (bf16[256,768]{1,0:T(8,128)(2,1)S(1)}, bf16[256,768]{1,0:T(8,128)(2,1)S(1)}, u32[]{:S(2)}, u32[]{:S(2)}) collective-permute-start(bf16[256,768]{1,0:T(8,128)(2,1)S(1)} %get-tuple-element.33), channel_id=1, source_target_pairs={{0,1},{1,0},{2,3},{3,2},{4,5},{5,4},{6,7},{7,6},{8,9},{9,8},{10,11... | collective-permute-start | bytes 1179656 | tf_op jit(solution)/shard_map/ppermute | solution.py:348
  57.7 19.7 %collective-permute-start.2 = (bf16[128,768]{1,0:T(8,128)(2,1)S(1)}, bf16[128,768]{1,0:T(8,128)(2,1)S(1)}, u32[]{:S(2)}, u32[]{:S(2)}) collective-permute-start(bf16[128,768]{1,0:T(8,128)(2,1)S(1)} %get-tuple-element.35), channel_id=1, source_target_pairs={{0,2},{1,3},{2,0},{3,1},{4,6},{5,7},{6,4},{7,5},{8,10},{9,11},{10,... | collective-permute-start | bytes 589832 | tf_op jit(solution)/shard_map/ppermute | solution.py:348
  68.8 4.0 %collective-permute-start.6 = (f32[16,512]{1,0:T(8,128)S(1)}, f32[16,512]{1,0:T(8,128)S(1)}, u32[]{:S(2)}, u32[]{:S(2)}) collective-permute-start(f32[16,512]{1,0:T(8,128)S(1)} %shard_map.128), channel_id=1, source_target_pairs={{0,1},{1,0},{2,3},{3,2},{4,5},{5,4},{6,7},{7,6},{8,9},{9,8},{10,11... | collective-permute-start | bytes 98312 | tf_op jit(solution)/shard_map/ppermute | solution.py:348
  72.8 3.9 %collective-permute-start.7 = (f32[16,512]{1,0:T(8,128)S(1)}, f32[16,512]{1,0:T(8,128)S(1)}, u32[]{:S(2)}, u32[]{:S(2)}) collective-permute-start(f32[16,512]{1,0:T(8,128)S(1)} %add.22), channel_id=1, source_target_pairs={{0,2},{1,3},{2,0},{3,1},{4,6},{5,7},{6,4},{7,5},{8,10},{9,11},{10,... | collective-permute-start | bytes 98312 | tf_op jit(solution)/shard_map/ppermute | solution.py:348
  76.7 4.8 %collective-permute-start.8 = (f32[16,512]{1,0:T(8,128)S(1)}, f32[16,512]{1,0:T(8,128)S(1)}, u32[]{:S(2)}, u32[]{:S(2)}) collective-permute-start(f32[16,512]{1,0:T(8,128)S(1)} %add.23), channel_id=1, source_target_pairs={{0,4},{1,5},{2,6},{3,7},{4,0},{5,1},{6,2},{7,3},{8,12},{9,13},{10,... | collective-permute-start | bytes 98312 | tf_op jit(solution)/shard_map/ppermute | solution.py:348
  77.4 7.0 %collective-permute-start.3 = (bf16[64,768]{1,0:T(8,128)(2,1)S(1)}, bf16[64,768]{1,0:T(8,128)(2,1)S(1)}, u32[]{:S(2)}, u32[]{:S(2)}) collective-permute-start(bf16[64,768]{1,0:T(8,128)(2,1)S(1)} %get-tuple-element.37), channel_id=1, source_target_pairs={{0,4},{1,5},{2,6},{3,7},{4,0},{5,1},{6,2},{7,3},{8,12},{9,13},{10,... | collective-permute-start | bytes 294920 | tf_op jit(solution)/shard_map/ppermute | solution.py:348
  81.5 1.2 %collective-permute-start.9 = (f32[16,512]{1,0:T(8,128)S(1)}, f32[16,512]{1,0:T(8,128)S(1)}, u32[]{:S(2)}, u32[]{:S(2)}) collective-permute-start(f32[16,512]{1,0:T(8,128)S(1)} %add.24), channel_id=1, source_target_pairs={{0,8},{8,0},{16,24},{24,16},{1,9},{9,1},{17,25},{25,17},{2,10},{10... | collective-permute-start | bytes 98312 | tf_op jit(solution)/shard_map/ppermute | solution.py:348
  82.7 3.9 %collective-permute-start.10 = (f32[16,512]{1,0:T(8,128)S(1)}, f32[16,512]{1,0:T(8,128)S(1)}, u32[]{:S(2)}, u32[]{:S(2)}) collective-permute-start(f32[16,512]{1,0:T(8,128)S(1)} %add.25), channel_id=1, source_target_pairs={{0,16},{8,24},{16,0},{24,8},{1,17},{9,25},{17,1},{25,9},{2,18},{10... | collective-permute-start | bytes 98312 | tf_op jit(solution)/shard_map/ppermute | solution.py:348
  84.5 4.7 %collective-permute-start.4 = (bf16[64,768]{1,0:T(8,128)(2,1)S(1)}, bf16[64,768]{1,0:T(8,128)(2,1)S(1)}, u32[]{:S(2)}, u32[]{:S(2)}) collective-permute-start(bf16[64,768]{1,0:T(8,128)(2,1)S(1)} %shard_map.126), channel_id=1, source_target_pairs={{0,16},{8,24},{16,0},{24,8},{1,17},{9,25},{17,1},{25,9},{2,18},{10... | collective-permute-start | bytes 294920 | tf_op jit(solution)/shard_map/ppermute | solution.py:348
  86.7 4.7 %copy-start.11 = (f32[16,64]{1,0:T(8,128)}, f32[16,64]{1,0:T(8,128)S(1)}, u32[]{:S(2)}) copy-start(f32[16,64]{1,0:T(8,128)S(1)} %dynamic-slice_add_fusion) | copy-start | bytes 12292
  89.2 1.5 %collective-permute-start.5 = (f32[64,768]{1,0:T(8,128)S(1)}, f32[64,768]{1,0:T(8,128)S(1)}, u32[]{:S(2)}, u32[]{:S(2)}) collective-permute-start(f32[64,768]{1,0:T(8,128)S(1)} %convert_add_fusion.own_ref), channel_id=1, source_target_pairs={{0,8},{8,0},{16,24},{24,16},{1,9},{9,1},{17,25},{25,17},{2,10},{10... | collective-permute-start | bytes 589832 | tf_op jit(solution)/shard_map/ppermute | solution.py:348

commit v2 on v1

--- a/solution.py
+++ b/solution.py
@@ -49,7 +49,16 @@
     return mask.astype(F32).astype(BF16)
 
 
-def deal_kernel(members, order_ref, wave_ref, out_ref):
+def copies(sources, targets, sems):
+    started = [pltpu.make_async_copy(source, target, sems.at[i]) for i, (source, target) in enumerate(zip(sources, targets))]
+    for copy in started:
+        copy.start()
+    return started
+
+
+def deal_kernel(members, order_hbm, wave_hbm, out_ref, order_ref, wave_ref, sems):
+    for copy in copies((order_hbm, wave_hbm), (order_ref, wave_ref), sems):
+        copy.wait()
     rows = wave_ref.shape[0]
     share = rows // members
     own = order_ref[pl.ds(lax.axis_index("dev"), 1), :]
@@ -58,7 +67,7 @@
     column = iota((rows, rows), 1)
     swap = onehot(column == lax.rem(row, share) * members + row // share)
     choose = cols_both(swap, picks).astype(BF16)
-    out_ref[...] = dot(choose, wave_ref[...]).astype(BF16)
+    out_ref[...] = dot(choose, wave_ref[...]).astype(BF16).reshape(out_ref.shape)
 
 
 def setup_kernel(members, frames0, order_ref, len_ref, w_ref, valid_ref, band_ref):
@@ -94,10 +103,10 @@
     wave_ref,
     valid_ref,
     band_ref,
-    gain_ref,
-    bias_ref,
-    w_ref,
-    cot_ref,
+    gain_hbm,
+    bias_hbm,
+    w_hbm,
+    cot_hbm,
     feat_ref,
     even_ref,
     odd_ref,
@@ -109,7 +118,13 @@
     grad_t_ref,
     pre0,
     pre1,
+    gain_ref,
+    bias_ref,
+    w_ref,
+    cot_ref,
+    sems,
 ):
+    waiting = copies((gain_hbm, bias_hbm, w_hbm, cot_hbm), (gain_ref, bias_ref, w_ref, cot_ref), sems)
     rows, samp = wave_ref.shape
     chans = gain_ref.shape[1]
     stride = taps // 2
@@ -163,6 +178,9 @@
         var = over_frames(add_var, jnp.zeros((rows, width), F32)) / count
         inv = lax.rsqrt(var + 1e-05)
         inv_ref[:, lanes] = inv
+        if block == 0:
+            waiting[0].wait()
+            waiting[1].wait()
         gain = jnp.broadcast_to(gain_ref[:, lanes], (rows, width))
         bias = jnp.broadcast_to(bias_ref[:, lanes], (rows, width))
 
@@ -180,6 +198,8 @@
     for ref, used in ((even_ref, (frames0 + 1) // 2), (odd_ref, frames0 // 2)):
         ref[used:] = jnp.zeros((ref.shape[0] - used,) + ref.shape[1:], BF16)
 
+    waiting[2].wait()
+    waiting[3].wait()
     grad_ref[0] = jnp.zeros(grad_ref.shape[1:], BF16)
     grad_ref[frames1 + 1] = jnp.zeros(grad_ref.shape[1:], BF16)
     padded = grad_t_ref.shape[1]
@@ -308,44 +328,133 @@
         out_ref[:taps, lanes] = total
 
 
-def fold_kernel(axis, bit, keep_ref, got_ref, next_ref, send_ref):
-    half = keep_ref.shape[0] // 2
-    side = lax.rem(lax.shift_right_logical(lax.axis_index(axis), bit), 2)
-    mine = pl.ds(pl.multiple_of(side * half, half), half)
-    other = pl.ds(pl.multiple_of((1 - side) * half, half), half)
-    next_ref[...] = keep_ref[mine, :] + got_ref[mine, :].astype(F32)
-    send_ref[...] = (keep_ref[other, :] + got_ref[other, :].astype(F32)).astype(BF16)
-
-
-def last_fold_kernel(keep_ref, got_ref, send_ref):
-    send_ref[...] = (keep_ref[...] + got_ref[...].astype(F32)).astype(BF16)
-
-
-def join_kernel(own_ref, other_ref, out_ref):
-    half = out_ref.shape[2] // 2
+def pack(value):
+    high = value.astype(BF16)
+    return high, (value - high.astype(F32)).astype(BF16)
+
+
+def plane_kernel(keep_ref, got_ref, own_ref, *send_refs):
+    size = own_ref.shape[0]
+    place = lax.rem(lax.axis_index("dev"), 4)
+
+    def quarter(index):
+        lines = pl.ds(pl.multiple_of(index * size, size), size)
+        return keep_ref[lines, :] + got_ref[lines, :].astype(F32)
+
+    own_ref[...] = quarter(place)
+    for offset, send_ref in enumerate(send_refs, 1):
+        send_ref[...] = quarter(jnp.bitwise_xor(place, offset)).astype(BF16)
+
+
+def gather_kernel(
+    bit, own_ref, got1, got2, got3, small_ref, small1, small2, small3, next_ref, send_ref, total_ref
+):
+    half = next_ref.shape[0]
+    side = lax.rem(lax.shift_right_logical(lax.axis_index("dev"), bit), 2)
+
+    def part(index):
+        lines = pl.ds(pl.multiple_of(index * half, half), half)
+        return own_ref[lines, :] + (
+            got1[lines, :].astype(F32) + got2[lines, :].astype(F32) + got3[lines, :].astype(F32)
+        )
+
+    next_ref[...] = part(side)
+    send_ref[:half] = part(1 - side).astype(BF16)
+    total = (small_ref[...] + small1[...]) + (small2[...] + small3[...])
+    total_ref[...] = total
+    write_small(send_ref, half, total)
+
+
+def write_small(send_ref, first, total):
+    lines, chans = total.shape
+    send_ref[first:, chans:] = jnp.zeros((2 * lines, send_ref.shape[1] - chans), BF16)
+    for place, term in enumerate(pack(total)):
+        send_ref[first + place * lines : first + (place + 1) * lines, :chans] = term
+
+
+def read_small(got_ref, first, lines, chans):
+    return (
+        got_ref[first : first + lines, :chans].astype(F32)
+        + got_ref[first + lines : first + 2 * lines, :chans].astype(F32)
+    )
+
+
+def fold_kernel(bit, last, keep_ref, got_ref, small_ref, *out_refs):
+    lines, chans = small_ref.shape
+    half = keep_ref.shape[0]
+    total = small_ref[...] + read_small(got_ref, half, lines, chans)
+    total_ref, send_ref = out_refs[0], out_refs[1]
+    total_ref[...] = total
+    if last:
+        send_ref[:half] = (keep_ref[...] + got_ref[:half].astype(F32)).astype(BF16)
+        write_small(send_ref, half, total)
+        return
+    next_ref = out_refs[2]
+    size = next_ref.shape[0]
+    side = lax.rem(lax.shift_right_logical(lax.axis_index("dev"), bit), 2)
+
+    def part(index):
+        here = pl.ds(pl.multiple_of(index * size, size), size)
+        return keep_ref[here, :] + got_ref[here, :].astype(F32)
+
+    next_ref[...] = part(side)
+    send_ref[:size] = part(1 - side).astype(BF16)
+    write_small(send_ref, size, total)
+
+
+def across_kernel(last, mine_ref, got_ref, small_ref, total_ref, out_ref):
+    lines, chans = small_ref.shape
+    half = mine_ref.shape[0] - 2 * lines
+    total = read_small(mine_ref, half, lines, chans) + read_small(got_ref, half, lines, chans)
+    value = mine_ref[:half].astype(F32) + got_ref[:half].astype(F32)
+    total_ref[...] = total
+    out_ref[:half] = value.astype(out_ref.dtype)
+    if last:
+        out_ref[half:, chans:] = jnp.zeros((lines, out_ref.shape[1] - chans), F32)
+        out_ref[half:, :chans] = total
+    else:
+        write_small(out_ref, half, total)
+
+
+def join_kernel(members, taps, own_ref, other_ref, out_ref, first_ref, gain_ref, bias_ref):
+    second, size, chans = out_ref.shape
+    half = chans // 2
     core = lax.rem(lax.axis_index("grp"), 2)
-    for tap in range(out_ref.shape[0]):
+    for tap in range(second):
         lanes = slice(tap * half, (tap + 1) * half)
-        out_ref[tap, :, pl.ds(pl.multiple_of(core * half, half), half)] = own_ref[:, lanes]
-        out_ref[tap, :, pl.ds(pl.multiple_of((1 - core) * half, half), half)] = other_ref[:, lanes]
-
-
-def call(kernel, outs, args, scratch=(), limit=32, flops=0, touched=0):
+        out_ref[tap, :, pl.ds(pl.multiple_of(core * half, half), half)] = own_ref[:size, lanes]
+        out_ref[tap, :, pl.ds(pl.multiple_of((1 - core) * half, half), half)] = other_ref[:size, lanes]
+    wide = max(size, 128)
+    member = lax.axis_index("dev")
+    block = pl.ds(pl.multiple_of(member // (wide // size) * wide, wide), wide)
+    total = own_ref[size:, block] + other_ref[size:, block]
+    value = total[:, :size]
+    for place in range(1, wide // size):
+        value = jnp.where(lax.rem(member, wide // size) == place, total[:, place * size : (place + 1) * size], value)
+    first_ref[...] = value[:taps]
+    gain_ref[...] = value[taps : taps + 1]
+    bias_ref[...] = value[taps + 1 : taps + 2]
+
+
+def call(kernel, outs, args, scratch=(), limit=24, flops=0, touched=0, outside=()):
     vmem = pl.BlockSpec(memory_space=pltpu.VMEM)
+    args = [pltpu.with_memory_space_constraint(arg, pltpu.HBM) if i in outside else arg for i, arg in enumerate(args)]
     return pl.pallas_call(
         kernel,
-        out_shape=[jax.ShapeDtypeStruct(shape, kind) for shape, kind in outs],
-        in_specs=[vmem] * len(args),
+        out_shape=[
+            jax.ShapeDtypeStruct(out[0], out[1]) if len(out) > 2 else pltpu.VMEM(out[0], out[1]) for out in outs
+        ],
+        in_specs=[pl.BlockSpec(memory_space=pltpu.HBM) if i in outside else vmem for i in range(len(args))],
         out_specs=[vmem] * len(outs),
-        scratch_shapes=[pltpu.VMEM(shape, kind) for shape, kind in scratch],
+        scratch_shapes=[pltpu.VMEM(*entry) if isinstance(entry, tuple) else entry for entry in scratch],
         compiler_params=pltpu.CompilerParams(vmem_limit_bytes=limit * MIB),
         cost_estimate=pl.CostEstimate(flops=flops, bytes_accessed=touched, transcendentals=0),
     )(*args)
 
 
-def swap(value, axis, bit):
+def swap(value, axis, offset):
     size = lax.axis_size(axis)
-    return lax.ppermute(value, axis, [(i, i ^ (1 << bit)) for i in range(size)])
+    return lax.ppermute(value, axis, [(i, i ^ offset) for i in range(size)])
 
 
 def shards(wave, lengths, order, w_first, norm_gain, norm_bias, w_second, cot):
@@ -363,8 +472,14 @@
     dev_bits = members.bit_length() - 1
     grp_bits = groups_of.bit_length() - 1
 
-    outgoing = call(functools.partial(deal_kernel, members), [((rows, samp), BF16)], [order, wave])[0]
-    arrived = lax.all_to_all(outgoing, "dev", split_axis=0, concat_axis=0, tiled=True)
+    outgoing = call(
+        functools.partial(deal_kernel, members),
+        [((members, rows // members, samp), BF16)],
+        [order, wave],
+        scratch=[(order.shape, order.dtype), (wave.shape, wave.dtype), pltpu.SemaphoreType.DMA((2,))],
+        outside=(0, 1),
+    )[0]
+    arrived = lax.all_to_all(outgoing, "dev", split_axis=0, concat_axis=0, tiled=True).reshape(rows, samp)
     valid, band = call(
         functools.partial(setup_kernel, members, frames0),
         [((rows, 128), jnp.int32), ((depth, GROUP * chans), BF16)],
@@ -374,11 +489,13 @@
     bias = norm_bias.reshape(1, chans)
     cot_t = cot.transpose(1, 0, 2)
     pad_frames = -(-frames1 // 4) * 4
-    reverse = [int(format(i, "b").zfill(dev_bits)[::-1], 2) for i in range(members)]
+    places = [0] * members
+    for dev in range(members):
+        places[dev % 4 * (members // 4) + dev // 4] = dev
     feat, even, odd, normed, slope, inv, patch, grad, grad_t = call(
-        functools.partial(forward_kernel, frames0, frames1, taps, reverse),
+        functools.partial(forward_kernel, frames0, frames1, taps, places),
         [
-            ((frames1, rows, chans), BF16),
+            ((frames1, rows, chans), BF16, "out"),
             ((pad_frames + 1, rows, chans), BF16),
             ((pad_frames, rows, chans), BF16),
             ((frames0, rows, chans), F32),
@@ -389,14 +506,23 @@
             ((chans, pad_frames * rows), BF16),
         ],
         [arrived, valid, band, gain, bias, w_second, cot_t],
-        scratch=[((groups, rows, GROUP * width), F32), ((16, rows, chans), F32)],
-        limit=48,
-    )
-    keep, send = call(
-        outer_kernel,
-        [((chans, taps_second * chans // 2), F32), ((chans, taps_second * chans // 2), BF16)],
-        [even, odd, grad_t],
-    )
+        scratch=[
+            ((groups, rows, GROUP * width), F32),
+            ((16, rows, chans), F32),
+            (gain.shape, F32),
+            (bias.shape, F32),
+            (w_second.shape, BF16),
+            (cot_t.shape, BF16),
+            pltpu.SemaphoreType.DMA((4,)),
+        ],
+        outside=(3, 4, 5, 6),
+    )
+    wide = taps_second * chans // 2
+    keep, send = call(outer_kernel, [((chans, wide), F32), ((chans, wide), BF16)], [even, odd, grad_t], flops=1 << 30)
+    got = swap(send, "grp", 1)
+    quarter = chans // 4
+    own, *sends = call(plane_kernel, [((quarter, wide), F32)] + [((quarter, wide), BF16)] * 3, [keep, got])
+    gots = [swap(part, "dev", offset) for offset, part in enumerate(sends, 1)]
     small = call(
         functools.partial(backward_kernel, frames0, frames1, taps),
         [((16, chans), F32)],
@@ -406,36 +532,47 @@
             ((groups, rows, GROUP * width), BF16),
             ((depth, GROUP * width), F32),
         ],
-        limit=48,
+        flops=1 << 32,
     )[0]
-
-    got = swap(send, "grp", 0)
-    for bit in range(dev_bits):
-        half = (keep.shape[0] // 2, keep.shape[1])
-        keep, send = call(functools.partial(fold_kernel, "dev", bit), [(half, F32), (half, BF16)], [keep, got])
-        got = swap(send, "dev", bit)
-    total = call(last_fold_kernel, [(keep.shape, BF16)], [keep, got])[0]
+    smalls = [swap(small, "dev", offset) for offset in (1, 2, 3)]
+    size = quarter // 2
+    extra = 2 * small.shape[0]
+    keep, send, small = call(
+        functools.partial(gather_kernel, dev_bits - 1),
+        [((size, wide), F32), ((size + extra, wide), BF16), (small.shape, F32)],
+        [own, *gots, small, *smalls],
+    )
+    for bit in range(dev_bits - 1, 1, -1):
+        got = swap(send, "dev", 1 << bit)
+        last = bit == 2
+        outs = [(small.shape, F32), ((size + extra, wide), BF16)]
+        if not last:
+            size //= 2
+            outs = [(small.shape, F32), ((size + extra, wide), BF16), ((size, wide), F32)]
+        small, send, *rest = call(functools.partial(fold_kernel, bit - 1, last), outs, [keep, got, small])
+        keep = rest[0] if rest else None
     for bit in range(1, grp_bits):
-        got = swap(total, "grp", bit)
-        total = total.astype(F32) + got.astype(F32)
-        if bit < grp_bits - 1:
-            total = total.astype(BF16)
-    total = total.astype(F32)
-    other = swap(total, "grp", 0)
-    grad_second = call(join_kernel, [((taps_second, chans // members, chans), F32)], [total, other])[0]
-
-    for axis, bits in (("dev", dev_bits), ("grp", grp_bits)):
-        for bit in range(bits):
-            small = small + swap(small, axis, bit)
-    member = lax.axis_index("dev")
-    share = chans // members
-    owned = lax.dynamic_slice_in_dim(small, member * share, share, 1)
+        got = swap(send, "grp", 1 << bit)
+        last = bit == grp_bits - 1
+        shape = ((size + small.shape[0], wide), F32) if last else (send.shape, BF16)
+        small, send = call(functools.partial(across_kernel, last), [(small.shape, F32), shape], [send, got, small])
+    other = swap(send, "grp", 1)
+    grad_second, grad_first, grad_gain, grad_bias = call(
+        functools.partial(join_kernel, members, taps),
+        [
+            ((taps_second, size, chans), F32, "out"),
+            ((taps, size), F32, "out"),
+            ((1, size), F32, "out"),
+            ((1, size), F32, "out"),
+        ],
+        [send, other],
+    )
     return (
         feat.transpose(1, 0, 2),
         grad_second.transpose(0, 2, 1),
-        owned[:taps],
-        owned[taps],
-        owned[taps + 1],
+        grad_first,
+        grad_gain.reshape(size),
+        grad_bias.reshape(size),
     )
 
 

time: 92 us -> 71 us (0.77)
  local copies, waits for them, and re-layouts: 10 us -> 2.18 us
  Pallas kernels: 34.1 us -> 27.4 us
  waiting for transfers between devices: 29.6 us -> 24.7 us
  starting transfers between devices: 16.9 us -> 15.6 us
    unnamed x24 -> x8, local copies, waits for them, and re-layouts: 8.12 us -> 1.42 us
    pallas_call x10, Pallas kernels: 34.1 us -> 27.4 us  [call(): pl.pallas_call(kernel, out_shape=[jax.ShapeDtypeStruct(out[0], out[1]) if...]
    ppermute x11 -> x10, waiting for transfers between devices: 25.5 us -> 20.6 us  [swap(): return lax.ppermute(value, axis, [(i, i ^ offset) for i in range(size)])]
    ppermute x11 -> x10, starting transfers between devices: 9.69 us -> 8.33 us  [swap(): return lax.ppermute(value, axis, [(i, i ^ offset) for i in range(size)])]
  transfers between devices with their start and end apart: 12 -> 11, of which waited for: 11 -> 7; matrix products, arithmetic and copies ran while one was open for 1% -> 1% of each run, Pallas kernels for 12% -> 10%
where the time goes in v2:
time: 71 us; the launch traced here: 70.6 us
  Pallas kernels  27.4 us (39%)
  waiting for transfers between devices  24.7 us (35%)
  starting transfers between devices  15.6 us (22%)
  local copies, waits for them, and re-layouts  2.18 us (3%)
  between operations  0.72 us (1%)
    pallas_call x10, Pallas kernels, call(): pl.pallas_call(kernel, out_shape=[jax.ShapeDtypeStruct(out[0], out[1]) if...  27.4 us
    ppermute x10, waiting for transfers between devices, swap(): return lax.ppermute(value, axis, [(i, i ^ offset) for i in range(size)])  20.6 us
    ppermute x10, starting transfers between devices, swap(): return lax.ppermute(value, axis, [(i, i ^ offset) for i in range(size)])  8.33 us
    all_to_all x1, starting transfers between devices, shards(): lax.all_to_all(outgoing, 'dev', split_axis=0, concat_axis=0, tiled=True)  7.26 us
    all_to_all x1, waiting for transfers between devices, shards(): lax.all_to_all(outgoing, 'dev', split_axis=0, concat_axis=0, tiled=True)  4.05 us
  transfers between devices with their start and end apart: 11, of which 7 were waited for; matrix products, arithmetic and copies ran while one was open for 1% of the time, Pallas kernels for 10%

profile of v2, /device:TPU:0, one launch (start us, length us, event | category | flops | bytes accessed | tf_op | source)
XLA Modules:
  0.0 70.6 jit_solution(8545118637401074608)
XLA Ops:
  0.6 1.6 %shard_map.119 = bf16[8,4,384]{2,1,0:T(4,128)(2,1)} custom-call(s32[8,32]{1,0:T(8,128)} %order_ref.1, bf16[32,384]{1,0:T(8,128)(2,1)} %wave_hbm.1), custom_call_target="tpu_custom_call" | custom-call | tf_op jit(solution)/shard_map/pallas_call | solution.py:442
  2.3 7.3 %all-to-all-start = ((bf16[8,4,384]{2,1,0:T(4,128)(2,1)}), bf16[8,4,384]{2,1,0:T(4,128)(2,1)S(1)}, u32[]{:S(2)}, u32[]{:S(2)}) async-start(bf16[8,4,384]{2,1,0:T(4,128)(2,1)} %shard_map.119), calls=%async_computation | async-start | bytes 49152 | tf_op jit(solution)/shard_map/all_to_all | solution.py:482
  9.5 0.8 %reshape.29.len_ref = s32[8,32]{1,0:T(8,128)S(1)} reshape(s32[256]{0:T(256)} %param.9) | data formatting | bytes 2048 | tf_op jit(solution)/shard_map/reshape | solution.py:486
  10.3 0.0 copy-start.1
  10.3 0.7 %copy-done.1 = bf16[10,512]{1,0:T(8,128)(2,1)S(1)} copy-done((bf16[10,512]{1,0:T(8,128)(2,1)S(1)}, bf16[10,512]{1,0:T(8,128)(2,1)}, u32[]{:S(2)}) %copy-start.1) | copy-done | bytes 10264
  11.0 0.0 copy-start.2
  11.0 0.7 copy-done.2
  11.7 0.4 shard_map.120
  12.1 4.0 %all-to-all-done = bf16[8,4,384]{2,1,0:T(4,128)(2,1)S(1)} async-done(((bf16[8,4,384]{2,1,0:T(4,128)(2,1)}), bf16[8,4,384]{2,1,0:T(4,128)(2,1)S(1)}, u32[]{:S(2)}, u32[]{:S(2)}) %all-to-all-start) | async-done | bytes 24608 | tf_op jit(solution)/shard_map/all_to_all | solution.py:482
  16.2 14.6 %shard_map.121 = (bf16[37,32,512]{2,1,0:T(8,128)(2,1)}, bf16[41,32,512]{2,1,0:T(8,128)(2,1)S(1)}, bf16[40,32,512]{2,1,0:T(8,128)(2,1)S(1)}, f32[75,32,512]{2,1,0...) custom-call(bf16[32,384]{1,0:T(8,128)(2,1)S(1)} %reshape.28.wave_ref, ...), custom_call_target="tpu_custom_call" | custom-call | tf_op jit(solution)/shard_map/pallas_call | solution.py:442
  30.8 2.2 %shard_map.122 = (f32[512,768]{1,0:T(8,128)S(1)}, bf16[512,768]{1,0:T(8,128)(2,1)S(1)}) custom-call(bf16[41,32,512]{2,1,0:T(8,128)(2,1)S(1)} %get-tuple-element.35.even_ref, bf16[40,32,512]{2,1,0:T(8,128)(2,1)S(1)} %get-tuple-element.36.odd_ref, bf16[512,1280]{1,0:T(8,128)(2,1)S(1)} %get-tuple-element.37.grad_t_ref), custom_call_target="tpu_custom_call" | custom-call | flops 1073741824 | tf_op jit(solution)/shard_map/pallas_call | solution.py:442
  33.0 0.0 copy-start
  33.0 0.0 copy-start.3
  33.1 0.1 collective-permute-start
  33.1 2.3 %collective-permute-done.got_ref = bf16[512,768]{1,0:T(8,128)(2,1)S(1)} collective-permute-done((bf16[512,768]{1,0:T(8,128)(2,1)S(1)}, bf16[512,768]{1,0:T(8,128)(2,1)S(1)}, u32[]{:S(2)}, u32[]{:S(2)}) %collective-permute-start) | collective-permute-done | bytes 786464 | tf_op jit(solution)/shard_map/ppermute | solution.py:457
  35.4 0.1 shard_map.123
  35.5 0.6 collective-permute-start.1
  36.1 0.7 collective-permute-start.2
  36.8 2.3 %collective-permute-start.3 = (bf16[128,768]{1,0:T(8,128)(2,1)S(1)}, bf16[128,768]{1,0:T(8,128)(2,1)S(1)}, u32[]{:S(2)}, u32[]{:S(2)}) collective-permute-start(bf16[128,768]{1,0:T(8,128)(2,1)S(1)} %get-tuple-element.43), channel_id=1, source_target_pairs={{0,3},{1,2},{2,1},{3,0},{4,7},{5,6},{6,5},{7,4},{8,11},{9,10},{10,... | collective-permute-start | bytes 589832 | tf_op jit(solution)/shard_map/ppermute | solution.py:457
  39.1 0.0 copy-done
  39.1 0.0 copy-done.3
  39.1 6.8 %shard_map.124.small_ref = f32[16,512]{1,0:T(8,128)S(1)} custom-call(s32[32,128]{1,0:T(8,128)S(1)} %get-tuple-element.32.valid_ref, f32[75,32,512]{2,1,0:T(8,128)S(1)} %get-tuple-element.44.normed_ref, f32[75,32,512]{2,1,0:T(8,128)S(1)} %get-tuple-element.45.slope_ref, f32[32,512]{1,0:T(8,128)S(1)} %get-tuple-element.46.inv_ref, ...), custom_call_target="tpu_custom_call" | custom-call | flops 4294967296 | tf_op jit(solution)/shard_map/pallas_call | solution.py:442
  45.9 0.7 collective-permute-start.6
  46.5 1.4 %collective-permute-start.5 = (f32[16,512]{1,0:T(8,128)S(1)}, f32[16,512]{1,0:T(8,128)S(1)}, u32[]{:S(2)}, u32[]{:S(2)}) collective-permute-start(f32[16,512]{1,0:T(8,128)S(1)} %shard_map.124.small_ref), channel_id=1, source_target_pairs={{0,2},{1,3},{2,0},{3,1},{4,6},{5,7},{6,4},{7,5},{8,10},{9,11},{10,... | collective-permute-start | bytes 98312 | tf_op jit(solution)/shard_map/ppermute | solution.py:457
  47.9 2.9 %collective-permute-done.6.small3 = f32[16,512]{1,0:T(8,128)S(1)} collective-permute-done((f32[16,512]{1,0:T(8,128)S(1)}, f32[16,512]{1,0:T(8,128)S(1)}, u32[]{:S(2)}, u32[]{:S(2)}) %collective-permute-start.6) | collective-permute-done | bytes 32800 | tf_op jit(solution)/shard_map/ppermute | solution.py:457
  50.8 0.5 collective-permute-start.4
  51.2 0.0 collective-permute-done.5.small2
  51.2 3.4 %collective-permute-done.4.small1 = f32[16,512]{1,0:T(8,128)S(1)} collective-permute-done((f32[16,512]{1,0:T(8,128)S(1)}, f32[16,512]{1,0:T(8,128)S(1)}, u32[]{:S(2)}, u32[]{:S(2)}) %collective-permute-start.4) | collective-permute-done | bytes 32800 | tf_op jit(solution)/shard_map/ppermute | solution.py:457
  54.7 0.0 collective-permute-done.1.got1
  54.7 0.0 collective-permute-done.2.got2
  54.7 0.0 collective-permute-done.3.got3
  54.7 0.1 shard_map.125
  54.8 0.6 collective-permute-start.7
  55.4 7.0 %collective-permute-done.7.got_ref = bf16[96,768]{1,0:T(8,128)(2,1)S(1)} collective-permute-done((bf16[96,768]{1,0:T(8,128)(2,1)S(1)}, bf16[96,768]{1,0:T(8,128)(2,1)S(1)}, u32[]{:S(2)}, u32[]{:S(2)}) %collective-permute-start.7) | collective-permute-done | bytes 147488 | tf_op jit(solution)/shard_map/ppermute | solution.py:457
  62.4 1.6 %collective-permute-start.8 = (bf16[96,768]{1,0:T(8,128)(2,1)S(1)}, bf16[96,768]{1,0:T(8,128)(2,1)S(1)}, u32[]{:S(2)}, u32[]{:S(2)}) collective-permute-start(bf16[96,768]{1,0:T(8,128)(2,1)S(1)} %get-tuple-element.52.mine_ref), channel_id=1, source_target_pairs={{0,16},{8,24},{16,0},{24,8},{1,17},{9,25},{17,1},{25,9},{2,18},{10... | collective-permute-start | bytes 442376 | tf_op jit(solution)/shard_map/ppermute | solution.py:457
  64.0 3.6 %collective-permute-done.8.got_ref = bf16[96,768]{1,0:T(8,128)(2,1)S(1)} collective-permute-done((bf16[96,768]{1,0:T(8,128)(2,1)S(1)}, bf16[96,768]{1,0:T(8,128)(2,1)S(1)}, u32[]{:S(2)}, u32[]{:S(2)}) %collective-permute-start.8) | collective-permute-done | bytes 147488 | tf_op jit(solution)/shard_map/ppermute | solution.py:457
  67.6 0.6 shard_map.127
  68.2 0.0 collective-permute-start.9
  68.2 1.5 %collective-permute-done.9.other_ref = f32[80,768]{1,0:T(8,128)S(1)} collective-permute-done((f32[80,768]{1,0:T(8,128)S(1)}, f32[80,768]{1,0:T(8,128)S(1)}, u32[]{:S(2)}, u32[]{:S(2)}) %collective-permute-start.9) | collective-permute-done | bytes 245792 | tf_op jit(solution)/shard_map/ppermute | solution.py:457
  69.7 0.8 %shard_map.128 = (f32[3,64,512]{2,1,0:T(8,128)}, f32[10,64]{1,0:T(8,128)}, f32[1,64]{1,0:T(1,128)}, f32[1,64]{1,0:T(1,128)}) custom-call(f32[80,768]{1,0:T(8,128)S(1)} %get-tuple-element.54.own_ref, f32[80,768]{1,0:T(8,128)S(1)} %collective-permute-done.9.other_ref), custom_call_target="tpu_custom_call" | custom-call | tf_op jit(solution)/shard_map/pallas_call | solution.py:442
  (2 shorter events, 0.0 us)
Async XLA Ops:
  2.3 13.9 %all-to-all-start = ((bf16[8,4,384]{2,1,0:T(4,128)(2,1)}), bf16[8,4,384]{2,1,0:T(4,128)(2,1)S(1)}, u32[]{:S(2)}, u32[]{:S(2)}) async-start(bf16[8,4,384]{2,1,0:T(4,128)(2,1)} %shard_map.119), calls=%async_computation | async-start | bytes 49152 | tf_op jit(solution)/shard_map/all_to_all | solution.py:482
  10.3 0.7 %copy-start.1 = (bf16[10,512]{1,0:T(8,128)(2,1)S(1)}, bf16[10,512]{1,0:T(8,128)(2,1)}, u32[]{:S(2)}) copy-start(bf16[10,512]{1,0:T(8,128)(2,1)} %w_ref.2) | copy-start | bytes 30724
  11.0 0.7 copy-start.2
  33.0 6.1 %copy-start = (bf16[3,512,512]{2,1,0:T(8,128)(2,1)S(1)}, bf16[3,512,512]{2,1,0:T(8,128)(2,1)}, u32[]{:S(2)}) copy-start(bf16[3,512,512]{2,1,0:T(8,128)(2,1)} %w_ref.3) | copy-start | bytes 4718596
  33.0 6.1 %copy-start.3 = (f32[512]{0:T(512)S(1)}, f32[512]{0:T(512)}, u32[]{:S(2)}) copy-start(f32[512]{0:T(512)} %param.12) | copy-start | bytes 6148
  33.1 2.4 %collective-permute-start = (bf16[512,768]{1,0:T(8,128)(2,1)S(1)}, bf16[512,768]{1,0:T(8,128)(2,1)S(1)}, u32[]{:S(2)}, u32[]{:S(2)}) collective-permute-start(bf16[512,768]{1,0:T(8,128)(2,1)S(1)} %get-tuple-element.39), channel_id=1, source_target_pairs={{0,8},{8,0},{16,24},{24,16},{1,9},{9,1},{17,25},{25,17},{2,10},{10... | collective-permute-start | bytes 2359304 | tf_op jit(solution)/shard_map/ppermute | solution.py:457
  35.5 19.1 %collective-permute-start.1 = (bf16[128,768]{1,0:T(8,128)(2,1)S(1)}, bf16[128,768]{1,0:T(8,128)(2,1)S(1)}, u32[]{:S(2)}, u32[]{:S(2)}) collective-permute-start(bf16[128,768]{1,0:T(8,128)(2,1)S(1)} %get-tuple-element.41), channel_id=1, source_target_pairs={{0,1},{1,0},{2,3},{3,2},{4,5},{5,4},{6,7},{7,6},{8,9},{9,8},{10,11... | collective-permute-start | bytes 589832 | tf_op jit(solution)/shard_map/ppermute | solution.py:457
  36.1 18.6 %collective-permute-start.2 = (bf16[128,768]{1,0:T(8,128)(2,1)S(1)}, bf16[128,768]{1,0:T(8,128)(2,1)S(1)}, u32[]{:S(2)}, u32[]{:S(2)}) collective-permute-start(bf16[128,768]{1,0:T(8,128)(2,1)S(1)} %get-tuple-element.42), channel_id=1, source_target_pairs={{0,2},{1,3},{2,0},{3,1},{4,6},{5,7},{6,4},{7,5},{8,10},{9,11},{10,... | collective-permute-start | bytes 589832 | tf_op jit(solution)/shard_map/ppermute | solution.py:457
  36.8 17.9 %collective-permute-start.3 = (bf16[128,768]{1,0:T(8,128)(2,1)S(1)}, bf16[128,768]{1,0:T(8,128)(2,1)S(1)}, u32[]{:S(2)}, u32[]{:S(2)}) collective-permute-start(bf16[128,768]{1,0:T(8,128)(2,1)S(1)} %get-tuple-element.43), channel_id=1, source_target_pairs={{0,3},{1,2},{2,1},{3,0},{4,7},{5,6},{6,5},{7,4},{8,11},{9,10},{10,... | collective-permute-start | bytes 589832 | tf_op jit(solution)/shard_map/ppermute | solution.py:457
  45.9 4.9 %collective-permute-start.6 = (f32[16,512]{1,0:T(8,128)S(1)}, f32[16,512]{1,0:T(8,128)S(1)}, u32[]{:S(2)}, u32[]{:S(2)}) collective-permute-start(f32[16,512]{1,0:T(8,128)S(1)} %shard_map.124.small_ref), channel_id=1, source_target_pairs={{0,3},{1,2},{2,1},{3,0},{4,7},{5,6},{6,5},{7,4},{8,11},{9,10},{10,... | collective-permute-start | bytes 98312 | tf_op jit(solution)/shard_map/ppermute | solution.py:457
  46.5 4.7 %collective-permute-start.5 = (f32[16,512]{1,0:T(8,128)S(1)}, f32[16,512]{1,0:T(8,128)S(1)}, u32[]{:S(2)}, u32[]{:S(2)}) collective-permute-start(f32[16,512]{1,0:T(8,128)S(1)} %shard_map.124.small_ref), channel_id=1, source_target_pairs={{0,2},{1,3},{2,0},{3,1},{4,6},{5,7},{6,4},{7,5},{8,10},{9,11},{10,... | collective-permute-start | bytes 98312 | tf_op jit(solution)/shard_map/ppermute | solution.py:457
  50.8 3.9 %collective-permute-start.4 = (f32[16,512]{1,0:T(8,128)S(1)}, f32[16,512]{1,0:T(8,128)S(1)}, u32[]{:S(2)}, u32[]{:S(2)}) collective-permute-start(f32[16,512]{1,0:T(8,128)S(1)} %shard_map.124.small_ref), channel_id=1, source_target_pairs={{0,1},{1,0},{2,3},{3,2},{4,5},{5,4},{6,7},{7,6},{8,9},{9,8},{10,11... | collective-permute-start | bytes 98312 | tf_op jit(solution)/shard_map/ppermute | solution.py:457
  54.8 7.6 %collective-permute-start.7 = (bf16[96,768]{1,0:T(8,128)(2,1)S(1)}, bf16[96,768]{1,0:T(8,128)(2,1)S(1)}, u32[]{:S(2)}, u32[]{:S(2)}) collective-permute-start(bf16[96,768]{1,0:T(8,128)(2,1)S(1)} %get-tuple-element.50), channel_id=1, source_target_pairs={{0,4},{1,5},{2,6},{3,7},{4,0},{5,1},{6,2},{7,3},{8,12},{9,13},{10,... | collective-permute-start | bytes 442376 | tf_op jit(solution)/shard_map/ppermute | solution.py:457
  62.4 5.2 %collective-permute-start.8 = (bf16[96,768]{1,0:T(8,128)(2,1)S(1)}, bf16[96,768]{1,0:T(8,128)(2,1)S(1)}, u32[]{:S(2)}, u32[]{:S(2)}) collective-permute-start(bf16[96,768]{1,0:T(8,128)(2,1)S(1)} %get-tuple-element.52.mine_ref), channel_id=1, source_target_pairs={{0,16},{8,24},{16,0},{24,8},{1,17},{9,25},{17,1},{25,9},{2,18},{10... | collective-permute-start | bytes 442376 | tf_op jit(solution)/shard_map/ppermute | solution.py:457
  68.2 1.5 %collective-permute-start.9 = (f32[80,768]{1,0:T(8,128)S(1)}, f32[80,768]{1,0:T(8,128)S(1)}, u32[]{:S(2)}, u32[]{:S(2)}) collective-permute-start(f32[80,768]{1,0:T(8,128)S(1)} %get-tuple-element.54.own_ref), channel_id=1, source_target_pairs={{0,8},{8,0},{16,24},{24,16},{1,9},{9,1},{17,25},{25,17},{2,10},{10... | collective-permute-start | bytes 737288 | tf_op jit(solution)/shard_map/ppermute | solution.py:457

commit v3 on v2

--- a/solution.py
+++ b/solution.py
@@ -56,37 +56,40 @@
     return started
 
 
-def deal_kernel(members, order_hbm, wave_hbm, out_ref, order_ref, wave_ref, sems):
-    for copy in copies((order_hbm, wave_hbm), (order_ref, wave_ref), sems):
+def setup_kernel(
+    members,
+    order_hbm,
+    len_hbm,
+    w_hbm,
+    wave_hbm,
+    valid_ref,
+    band_ref,
+    near_ref,
+    far_ref,
+    own_ref,
+    order_ref,
+    len_ref,
+    w_ref,
+    sems,
+):
+    for copy in copies((order_hbm, len_hbm, w_hbm, wave_hbm), (order_ref, len_ref, w_ref, own_ref), sems):
         copy.wait()
-    rows = wave_ref.shape[0]
-    share = rows // members
-    own = order_ref[pl.ds(lax.axis_index("dev"), 1), :]
-    picks = onehot(iota((rows, rows), 0) == own)
-    row = iota((rows, rows), 0)
-    column = iota((rows, rows), 1)
-    swap = onehot(column == lax.rem(row, share) * members + row // share)
-    choose = cols_both(swap, picks).astype(BF16)
-    out_ref[...] = dot(choose, wave_ref[...]).astype(BF16).reshape(out_ref.shape)
-
-
-def setup_kernel(members, frames0, order_ref, len_ref, w_ref, valid_ref, band_ref):
     rows = order_ref.shape[1]
     share = rows // members
     taps, chans = w_ref.shape
     stride = taps // 2
-    dealt = iota((rows, members), 0)
-    owner = onehot(dealt // share == iota((rows, members), 1))
+    owner = onehot(iota((rows, members), 0) // share == iota((rows, members), 1))
     order_of = dot(owner, order_ref[...].astype(F32).astype(BF16))
-    high = len_ref[...] // 16
-    low = len_ref[...] - high * 16
-    lens_of = dot(owner, high.astype(F32).astype(BF16)) * 16.0 + dot(owner, low.astype(F32).astype(BF16))
-    row = iota((rows, rows), 0)
-    column = iota((rows, rows), 1)
-    mine = column == lax.rem(row, share) * members + lax.axis_index("dev")
-    index = jnp.sum(jnp.where(mine, order_of, 0.0), axis=1, keepdims=True)
-    picked = column == index.astype(jnp.int32)
-    lens = jnp.sum(jnp.where(picked, lens_of, 0.0), axis=1, keepdims=True).astype(jnp.int32)
+    slot = iota((rows, rows), 1) - lax.rem(iota((rows, rows), 0), share) * members
+    owner_first = iota((rows, 1), 0) // share * rows
+    column = iota((rows, members * rows), 1)
+    member = lax.axis_index("dev")
+    for target, out_ref in ((member, near_ref), (jnp.bitwise_xor(member, members // 2), far_ref)):
+        local = jnp.sum(jnp.where(slot == target, order_of, 0.0), axis=1, keepdims=True).astype(jnp.int32)
+        picked = column == owner_first + local
+        out_ref[...] = onehot(picked)
+        if out_ref is near_ref:
+            lens = jnp.sum(jnp.where(picked, len_ref[...], 0), axis=1, keepdims=True)
     valid = (lens - taps) // stride + 1
     valid_ref[...] = jnp.broadcast_to(valid, valid_ref.shape)
     depth = band_ref.shape[0]
@@ -95,12 +98,24 @@
         band_ref[:, f * chans : (f + 1) * chans] = dot(spread, w_ref[...]).astype(BF16)
 
 
+def pick_kernel(offsets, near_ref, far_ref, *refs):
+    waves, (mine_ref, send_ref, all_ref) = refs[:-3], refs[-3:]
+    rows = mine_ref.shape[0]
+    all_ref[...] = jnp.zeros(all_ref.shape, BF16)
+    for offset, wave_ref in zip(offsets, waves):
+        first = pl.multiple_of(jnp.bitwise_xor(lax.axis_index("dev"), offset) * rows, rows)
+        all_ref[pl.ds(first, rows), :] = wave_ref[...]
+    mine_ref[...] = dot(near_ref[...], all_ref[...]).astype(BF16)
+    send_ref[...] = dot(far_ref[...], all_ref[...]).astype(BF16)
+
+
 def forward_kernel(
     frames0,
     frames1,
     taps,
     reverse,
-    wave_ref,
+    near_ref,
+    far_ref,
     valid_ref,
     band_ref,
     gain_hbm,
@@ -116,16 +131,16 @@
     patch_ref,
     grad_ref,
     grad_t_ref,
+    gain_ref,
+    w_ref,
     pre0,
     pre1,
-    gain_ref,
     bias_ref,
-    w_ref,
     cot_ref,
     sems,
 ):
     waiting = copies((gain_hbm, bias_hbm, w_hbm, cot_hbm), (gain_ref, bias_ref, w_ref, cot_ref), sems)
-    rows, samp = wave_ref.shape
+    rows, samp = near_ref.shape
     chans = gain_ref.shape[1]
     stride = taps // 2
     depth = band_ref.shape[0]
@@ -134,7 +149,7 @@
     min_valid = (MIN_SAMPLES - taps) // stride + 1
     free_groups = min(min_valid // GROUP, frames0 // GROUP)
     full_groups = frames0 // GROUP
-    wave = wave_ref[...]
+    wave = near_ref[...] + far_ref[...]
     for g in range(groups):
         pick = onehot(iota((samp, depth), 0) == iota((samp, depth), 1) + GROUP * stride * g)
         patch_ref[g] = dot(wave, pick).astype(BF16)
@@ -246,18 +261,27 @@
             out_ref[:, tap * half : (tap + 1) * half] = dot(turned, acts).astype(out_ref.dtype)
 
 
+def input_kernel(grad_ref, w_ref, even_ref, odd_ref):
+    evens, rows, chans = even_ref.shape
+    odds = odd_ref.shape[0]
+    first = grad_ref[1 : evens + 1].reshape(evens * rows, chans)
+    third = grad_ref[0:evens].reshape(evens * rows, chans)
+    even_ref[...] = (cols_both(first, w_ref[0]) + cols_both(third, w_ref[2])).reshape(even_ref.shape)
+    second = grad_ref[1 : odds + 1].reshape(odds * rows, chans)
+    odd_ref[...] = cols_both(second, w_ref[1]).reshape(odd_ref.shape)
+
+
 def backward_kernel(
     frames0,
-    frames1,
     taps,
     valid_ref,
     normed_ref,
     slope_ref,
     inv_ref,
     patch_ref,
-    grad_ref,
+    even_ref,
+    odd_ref,
     gain_ref,
-    w_ref,
     out_ref,
     lift,
     dpre0,
@@ -268,33 +292,28 @@
     stride = taps // 2
     width = dpre0.shape[2] // GROUP
     full_groups = frames0 // GROUP
+    rest = frames0 - full_groups * GROUP
     patches = patch_ref[...].reshape(groups * rows, depth)
-    evens = (frames0 + 1) // 2
-    odds = frames0 // 2
-    first = grad_ref[1 : evens + 1].reshape(evens * rows, chans)
-    second = grad_ref[1 : odds + 1].reshape(odds * rows, chans)
-    third = grad_ref[0:evens].reshape(evens * rows, chans)
     for block in range(chans // width):
         lanes = slice(block * width, (block + 1) * width)
-        lift[0, :evens] = (cols_both(first, w_ref[0, lanes]) + cols_both(third, w_ref[2, lanes])).reshape(
-            evens, rows, width
-        )
-        lift[1, :odds] = cols_both(second, w_ref[1, lanes]).reshape(odds, rows, width)
-
-        def slopes(parity, e, carry):
+
+        def slopes(g, f, carry):
             bias_sum, gain_sum = carry
-            t = 2 * e + parity
-            dlift = lift[parity, e] * slope_ref[t, :, lanes]
-            lift[parity, e] = dlift
+            t = g * GROUP + f
+            dact = (odd_ref if f % 2 else even_ref)[g * (GROUP // 2) + f // 2, :, lanes]
+            dlift = dact * slope_ref[t, :, lanes]
+            lift[t] = dlift
             return bias_sum + dlift, gain_sum + dlift * normed_ref[t, :, lanes]
 
-        def both(e, carry):
-            return slopes(1, e, slopes(0, e, carry))
+        def add(g, carry):
+            for f in range(GROUP):
+                carry = slopes(g, f, carry)
+            return carry
 
         zero = jnp.zeros((rows, width), F32)
-        carry = lax.fori_loop(0, odds, both, (zero, zero))
-        if evens > odds:
-            carry = slopes(0, odds, carry)
+        carry = lax.fori_loop(0, full_groups, add, (zero, zero))
+        for f in range(rest):
+            carry = slopes(full_groups, f, carry)
         bias_sum, gain_sum = carry
         out_ref[taps : taps + 1, lanes] = jnp.sum(gain_sum, axis=0, keepdims=True)
         out_ref[taps + 1 : taps + 2, lanes] = jnp.sum(bias_sum, axis=0, keepdims=True)
@@ -306,8 +325,7 @@
 
         def finish(g, f):
             t = g * GROUP + f
-            dlift = lift[f % 2, g * (GROUP // 2) + f // 2]
-            value = scale * (dlift - bias_sum - normed_ref[t, :, lanes] * gain_sum)
+            value = scale * (lift[t] - bias_sum - normed_ref[t, :, lanes] * gain_sum)
             dpre0[g, :, f * width : (f + 1) * width] = jnp.where(valid > t, value, 0.0).astype(BF16)
 
         def whole(g, carry):
@@ -316,7 +334,6 @@
             return carry
 
         lax.fori_loop(0, full_groups, whole, 0)
-        rest = frames0 - full_groups * GROUP
         for f in range(rest):
             finish(full_groups, f)
         if full_groups < groups:
@@ -328,12 +345,7 @@
         out_ref[:taps, lanes] = total
 
 
-def pack(value):
-    high = value.astype(BF16)
-    return high, (value - high.astype(F32)).astype(BF16)
-
-
-def plane_kernel(keep_ref, got_ref, own_ref, *send_refs):
+def plane_kernel(keep_ref, got_ref, later_ref, own_ref, *send_refs):
     size = own_ref.shape[0]
     place = lax.rem(lax.axis_index("dev"), 4)
 
@@ -346,9 +358,7 @@
         send_ref[...] = quarter(jnp.bitwise_xor(place, offset)).astype(BF16)
 
 
-def gather_kernel(
-    bit, own_ref, got1, got2, got3, small_ref, small1, small2, small3, next_ref, send_ref, total_ref
-):
+def gather_kernel(bit, own_ref, got1, got2, got3, small_ref, small_got, next_ref, send_ref, total_ref):
     half = next_ref.shape[0]
     side = lax.rem(lax.shift_right_logical(lax.axis_index("dev"), bit), 2)
 
@@ -359,37 +369,11 @@
         )
 
     next_ref[...] = part(side)
-    send_ref[:half] = part(1 - side).astype(BF16)
-    total = (small_ref[...] + small1[...]) + (small2[...] + small3[...])
-    total_ref[...] = total
-    write_small(send_ref, half, total)
-
-
-def write_small(send_ref, first, total):
-    lines, chans = total.shape
-    send_ref[first:, chans:] = jnp.zeros((2 * lines, send_ref.shape[1] - chans), BF16)
-    for place, term in enumerate(pack(total)):
-        send_ref[first + place * lines : first + (place + 1) * lines, :chans] = term
-
-
-def read_small(got_ref, first, lines, chans):
-    return (
-        got_ref[first : first + lines, :chans].astype(F32)
-        + got_ref[first + lines : first + 2 * lines, :chans].astype(F32)
-    )
-
-
-def fold_kernel(bit, last, keep_ref, got_ref, small_ref, *out_refs):
-    lines, chans = small_ref.shape
-    half = keep_ref.shape[0]
-    total = small_ref[...] + read_small(got_ref, half, lines, chans)
-    total_ref, send_ref = out_refs[0], out_refs[1]
-    total_ref[...] = total
-    if last:
-        send_ref[:half] = (keep_ref[...] + got_ref[:half].astype(F32)).astype(BF16)
-        write_small(send_ref, half, total)
-        return
-    next_ref = out_refs[2]
+    send_ref[...] = part(1 - side).astype(BF16)
+    total_ref[...] = small_ref[...] + small_got[...]
+
+
+def fold_kernel(bit, keep_ref, got_ref, send_ref, next_ref):
     size = next_ref.shape[0]
     side = lax.rem(lax.shift_right_logical(lax.axis_index("dev"), bit), 2)
 
@@ -398,36 +382,33 @@
         return keep_ref[here, :] + got_ref[here, :].astype(F32)
 
     next_ref[...] = part(side)
-    send_ref[:size] = part(1 - side).astype(BF16)
-    write_small(send_ref, size, total)
-
-
-def across_kernel(last, mine_ref, got_ref, small_ref, total_ref, out_ref):
-    lines, chans = small_ref.shape
-    half = mine_ref.shape[0] - 2 * lines
-    total = read_small(mine_ref, half, lines, chans) + read_small(got_ref, half, lines, chans)
-    value = mine_ref[:half].astype(F32) + got_ref[:half].astype(F32)
-    total_ref[...] = total
-    out_ref[:half] = value.astype(out_ref.dtype)
-    if last:
-        out_ref[half:, chans:] = jnp.zeros((lines, out_ref.shape[1] - chans), F32)
-        out_ref[half:, :chans] = total
-    else:
-        write_small(out_ref, half, total)
-
-
-def join_kernel(members, taps, own_ref, other_ref, out_ref, first_ref, gain_ref, bias_ref):
+    send_ref[...] = part(1 - side).astype(BF16)
+
+
+def round_kernel(keep_ref, got_ref, small0, small1, small2, small3, send_ref, total_ref):
+    send_ref[...] = (keep_ref[...] + got_ref[...].astype(F32)).astype(BF16)
+    total_ref[...] = (small0[...] + small1[...]) + (small2[...] + small3[...])
+
+
+def across_kernel(mine_ref, got_ref, *refs):
+    out_ref = refs[2] if len(refs) > 2 else refs[0]
+    out_ref[...] = (mine_ref[...].astype(F32) + got_ref[...].astype(F32)).astype(out_ref.dtype)
+    if len(refs) > 2:
+        refs[3][...] = refs[0][...] + refs[1][...]
+
+
+def join_kernel(members, taps, own_ref, other_ref, small_ref, out_ref, first_ref, gain_ref, bias_ref):
     second, size, chans = out_ref.shape
     half = chans // 2
     core = lax.rem(lax.axis_index("grp"), 2)
     for tap in range(second):
         lanes = slice(tap * half, (tap + 1) * half)
-        out_ref[tap, :, pl.ds(pl.multiple_of(core * half, half), half)] = own_ref[:size, lanes]
-        out_ref[tap, :, pl.ds(pl.multiple_of((1 - core) * half, half), half)] = other_ref[:size, lanes]
+        out_ref[tap, :, pl.ds(pl.multiple_of(core * half, half), half)] = own_ref[:, lanes]
+        out_ref[tap, :, pl.ds(pl.multiple_of((1 - core) * half, half), half)] = other_ref[:, lanes]
     wide = max(size, 128)
     member = lax.axis_index("dev")
     block = pl.ds(pl.multiple_of(member // (wide // size) * wide, wide), wide)
-    total = own_ref[size:, block] + other_ref[size:, block]
+    total = small_ref[:, block]
     value = total[:, :size]
     for place in range(1, wide // size):
         value = jnp.where(lax.rem(member, wide // size) == place, total[:, place * size : (place + 1) * size], value)
@@ -472,19 +453,38 @@
     dev_bits = members.bit_length() - 1
     grp_bits = groups_of.bit_length() - 1
 
-    outgoing = call(
-        functools.partial(deal_kernel, members),
-        [((members, rows // members, samp), BF16)],
-        [order, wave],
-        scratch=[(order.shape, order.dtype), (wave.shape, wave.dtype), pltpu.SemaphoreType.DMA((2,))],
-        outside=(0, 1),
-    )[0]
-    arrived = lax.all_to_all(outgoing, "dev", split_axis=0, concat_axis=0, tiled=True).reshape(rows, samp)
-    valid, band = call(
-        functools.partial(setup_kernel, members, frames0),
-        [((rows, 128), jnp.int32), ((depth, GROUP * chans), BF16)],
-        [order, lengths.reshape(members, rows), w_first],
-    )
+    offsets = [0, 1, 2, 3]
+    waves = [wave] + [swap(wave, "dev", offset) for offset in offsets[1:]]
+    for bit in range(2, dev_bits - 1):
+        offsets += [offset | (1 << bit) for offset in offsets]
+        waves += [swap(held, "dev", 1 << bit) for held in waves]
+    lens = lengths.reshape(1, members * rows)
+    every = members * rows
+    valid, band, near_sel, far_sel, own_wave = call(
+        functools.partial(setup_kernel, members),
+        [
+            ((rows, 128), jnp.int32),
+            ((depth, GROUP * chans), BF16),
+            ((rows, every), BF16),
+            ((rows, every), BF16),
+            ((rows, samp), BF16),
+        ],
+        [order, lens, w_first, wave],
+        scratch=[
+            (order.shape, order.dtype),
+            (lens.shape, lens.dtype),
+            (w_first.shape, BF16),
+            pltpu.SemaphoreType.DMA((4,)),
+        ],
+        outside=(0, 1, 2, 3),
+    )
+    near, send = call(
+        functools.partial(pick_kernel, offsets),
+        [((rows, samp), BF16), ((rows, samp), BF16)],
+        [near_sel, far_sel, own_wave, *waves[1:]],
+        scratch=[((every, samp), BF16)],
+    )
+    far = swap(send, "dev", members // 2)
     gain = norm_gain.reshape(1, chans)
     bias = norm_bias.reshape(1, chans)
     cot_t = cot.transpose(1, 0, 2)
@@ -492,7 +492,7 @@
     places = [0] * members
     for dev in range(members):
         places[dev % 4 * (members // 4) + dev // 4] = dev
-    feat, even, odd, normed, slope, inv, patch, grad, grad_t = call(
+    feat, even, odd, normed, slope, inv, patch, grad, grad_t, gain_in, w_in = call(
         functools.partial(forward_kernel, frames0, frames1, taps, places),
         [
             ((frames1, rows, chans), BF16, "out"),
@@ -504,58 +504,71 @@
             ((groups, rows, depth), BF16),
             ((frames1 + 2, rows, chans), BF16),
             ((chans, pad_frames * rows), BF16),
+            ((1, chans), F32),
+            (w_second.shape, BF16),
         ],
-        [arrived, valid, band, gain, bias, w_second, cot_t],
+        [near, far, valid, band, gain, bias, w_second, cot_t],
         scratch=[
             ((groups, rows, GROUP * width), F32),
             ((16, rows, chans), F32),
-            (gain.shape, F32),
             (bias.shape, F32),
-            (w_second.shape, BF16),
             (cot_t.shape, BF16),
             pltpu.SemaphoreType.DMA((4,)),
         ],
-        outside=(3, 4, 5, 6),
+        outside=(4, 5, 6, 7),
     )
     wide = taps_second * chans // 2
     keep, send = call(outer_kernel, [((chans, wide), F32), ((chans, wide), BF16)], [even, odd, grad_t], flops=1 << 30)
     got = swap(send, "grp", 1)
+    evens, odds = (frames0 + 1) // 2, frames0 // 2
+    dact_even, dact_odd = call(
+        input_kernel,
+        [((evens, rows, chans), F32), ((odds, rows, chans), F32)],
+        [grad, w_in],
+        flops=1 << 30,
+    )
     quarter = chans // 4
-    own, *sends = call(plane_kernel, [((quarter, wide), F32)] + [((quarter, wide), BF16)] * 3, [keep, got])
+    own, *sends = call(
+        plane_kernel, [((quarter, wide), F32)] + [((quarter, wide), BF16)] * 3, [keep, got, dact_odd]
+    )
     gots = [swap(part, "dev", offset) for offset, part in enumerate(sends, 1)]
     small = call(
-        functools.partial(backward_kernel, frames0, frames1, taps),
+        functools.partial(backward_kernel, frames0, taps),
         [((16, chans), F32)],
-        [valid, normed, slope, inv, patch, grad, gain, w_second],
+        [valid, normed, slope, inv, patch, dact_even, dact_odd, gain_in],
         scratch=[
-            ((2, (frames0 + 1) // 2, rows, width), F32),
+            ((frames0, rows, width), F32),
             ((groups, rows, GROUP * width), BF16),
             ((depth, GROUP * width), F32),
         ],
         flops=1 << 32,
     )[0]
-    smalls = [swap(small, "dev", offset) for offset in (1, 2, 3)]
+    small = small + swap(small, "grp", 1)
+    for bit in range(1, grp_bits - 1):
+        small = small + swap(small, "grp", 1 << bit)
     size = quarter // 2
-    extra = 2 * small.shape[0]
     keep, send, small = call(
         functools.partial(gather_kernel, dev_bits - 1),
-        [((size, wide), F32), ((size + extra, wide), BF16), (small.shape, F32)],
-        [own, *gots, small, *smalls],
-    )
-    for bit in range(dev_bits - 1, 1, -1):
-        got = swap(send, "dev", 1 << bit)
-        last = bit == 2
-        outs = [(small.shape, F32), ((size + extra, wide), BF16)]
-        if not last:
-            size //= 2
-            outs = [(small.shape, F32), ((size + extra, wide), BF16), ((size, wide), F32)]
-        small, send, *rest = call(functools.partial(fold_kernel, bit - 1, last), outs, [keep, got, small])
-        keep = rest[0] if rest else None
-    for bit in range(1, grp_bits):
+        [((size, wide), F32), ((size, wide), BF16), (small.shape, F32)],
+        [own, *gots, small, swap(small, "grp", groups_of // 2)],
+    )
+    got = swap(send, "dev", members // 2)
+    smalls = [small] + [swap(small, "dev", offset) for offset in (1, 2, 3)]
+    for bit in range(dev_bits - 1, 2, -1):
+        size //= 2
+        send, keep = call(
+            functools.partial(fold_kernel, bit - 1), [((size, wide), BF16), ((size, wide), F32)], [keep, got]
+        )
+        got = swap(send, "dev", 1 << (bit - 1))
+    send, small = call(round_kernel, [((size, wide), BF16), (small.shape, F32)], [keep, got, *smalls])
+    for bit in range(3, dev_bits):
+        small = small + swap(small, "dev", 1 << bit)
+    small_got = swap(small, "dev", 4)
+    for bit in range(1, grp_bits - 1):
         got = swap(send, "grp", 1 << bit)
-        last = bit == grp_bits - 1
-        shape = ((size + small.shape[0], wide), F32) if last else (send.shape, BF16)
-        small, send = call(functools.partial(across_kernel, last), [(small.shape, F32), shape], [send, got, small])
+        send = call(across_kernel, [((size, wide), BF16)], [send, got])[0]
+    got = swap(send, "grp", groups_of // 2)
+    send, small = call(across_kernel, [((size, wide), F32), (small.shape, F32)], [send, got, small, small_got])
     other = swap(send, "grp", 1)
     grad_second, grad_first, grad_gain, grad_bias = call(
         functools.partial(join_kernel, members, taps),
@@ -565,7 +578,7 @@
             ((1, size), F32, "out"),
             ((1, size), F32, "out"),
         ],
-        [send, other],
+        [send, other, small],
     )
     return (
         feat.transpose(1, 0, 2),

time: 71 us -> 65.1 us (0.917)
  waiting for transfers between devices: 24.7 us -> 18.7 us
  starting transfers between devices: 15.6 us -> 20.8 us
  Pallas kernels: 27.4 us -> 24.7 us
  local copies, waits for them, and re-layouts: 2.18 us -> 0 us
    ppermute x10 -> x17, starting transfers between devices: 8.33 us -> 20.8 us  [swap(): return lax.ppermute(value, axis, [(i, i ^ offset) for i in range(size)])]
    all_to_all x1 -> x0, starting transfers between devices: 7.26 us -> none  [shards(): lax.all_to_all(outgoing, 'dev', split_axis=0, concat_axis=0, tiled=True)]
    all_to_all x1 -> x0, waiting for transfers between devices: 4.05 us -> none  [shards(): lax.all_to_all(outgoing, 'dev', split_axis=0, concat_axis=0, tiled=True)]
    pallas_call x10 -> x11, Pallas kernels: 27.4 us -> 24.7 us  [call(): pl.pallas_call(kernel, out_shape=[jax.ShapeDtypeStruct(out[0], out[1]) if...]
    ppermute x10 -> x17, waiting for transfers between devices: 20.6 us -> 18.7 us  [swap(): return lax.ppermute(value, axis, [(i, i ^ offset) for i in range(size)])]
    unnamed x8 -> x0, local copies, waits for them, and re-layouts: 1.42 us -> none
    reshape x2 -> x0, local copies, waits for them, and re-layouts: 0.77 us -> none  [the longest x1 0.75 us: shards(): lengths.reshape(members, rows)]
  transfers between devices with their start and end apart: 11 -> 17, of which waited for: 7 -> 11; matrix products, arithmetic and copies ran while one was open for 1% -> 0% of each run, Pallas kernels for 10% -> 10%
where the time goes in v3:
time: 65.1 us; the launch traced here: 64.9 us
  Pallas kernels  24.7 us (38%)
  starting transfers between devices  20.8 us (32%)
  waiting for transfers between devices  18.7 us (29%)
  between operations  0.74 us (1%)
    pallas_call x11, Pallas kernels, call(): pl.pallas_call(kernel, out_shape=[jax.ShapeDtypeStruct(out[0], out[1]) if...  24.7 us
    ppermute x17, starting transfers between devices, swap(): return lax.ppermute(value, axis, [(i, i ^ offset) for i in range(size)])  20.8 us
    ppermute x17, waiting for transfers between devices, swap(): return lax.ppermute(value, axis, [(i, i ^ offset) for i in range(size)])  18.7 us
  transfers between devices with their start and end apart: 17, of which 11 were waited for; matrix products, arithmetic and copies ran while one was open for 0% of the time, Pallas kernels for 10%

profile of v3, /device:TPU:0, one launch (start us, length us, event | category | flops | bytes accessed | tf_op | source)
XLA Modules:
  0.0 64.9 jit_solution(15773829669598968164)
XLA Ops:
  0.6 3.0 %collective-permute-start = (bf16[32,384]{1,0:T(8,128)(2,1)}, bf16[32,384]{1,0:T(8,128)(2,1)S(1)}, u32[]{:S(2)}, u32[]{:S(2)}) collective-permute-start(bf16[32,384]{1,0:T(8,128)(2,1)} %wave_hbm.1), channel_id=1, source_target_pairs={{0,1},{1,0},{2,3},{3,2},{4,5},{5,4},{6,7},{7,6},{8,9},{9,8},{10,11... | collective-permute-start | bytes 73736 | tf_op jit(solution)/shard_map/ppermute | solution.py:438
  3.6 1.5 %collective-permute-start.2 = (bf16[32,384]{1,0:T(8,128)(2,1)}, bf16[32,384]{1,0:T(8,128)(2,1)S(1)}, u32[]{:S(2)}, u32[]{:S(2)}) collective-permute-start(bf16[32,384]{1,0:T(8,128)(2,1)} %wave_hbm.1), channel_id=1, source_target_pairs={{0,3},{1,2},{2,1},{3,0},{4,7},{5,6},{6,5},{7,4},{8,11},{9,10},{10,... | collective-permute-start | bytes 73736 | tf_op jit(solution)/shard_map/ppermute | solution.py:438
  5.2 0.0 collective-permute-start.1
  5.2 1.3 %shard_map.119 = (s32[32,128]{1,0:T(8,128)S(1)}, bf16[128,4096]{1,0:T(8,128)(2,1)S(1)}, bf16[32,256]{1,0:T(8,128)(2,1)S(1)}, bf16[32,256]{1,0:T(8,128)(2,1)S(1)}, bf16[32,384]{1,0:T(8,128)(2,1)S(1)}) custom-call(s32[8,32]{1,0:T(8,128)} %order_hbm.1, s32[1,256]{1,0:T(1,128)} %bitcast.11, bf16[10,512]{1,0:T(8,128)(2,1)} %w_hbm.2, bf16[32,384]{1,0:T(8,128)(2,1)} %wave_hbm.1), custom_call_target="tpu_custom_call" | custom-call | tf_op jit(solution)/shard_map/pallas_call | solution.py:423
  6.5 0.0 collective-permute-done.refs_1_
  6.5 2.2 %collective-permute-done.2.refs_3_ = bf16[32,384]{1,0:T(8,128)(2,1)S(1)} collective-permute-done((bf16[32,384]{1,0:T(8,128)(2,1)}, bf16[32,384]{1,0:T(8,128)(2,1)S(1)}, u32[]{:S(2)}, u32[]{:S(2)}) %collective-permute-start.2) | collective-permute-done | bytes 24608 | tf_op jit(solution)/shard_map/ppermute | solution.py:438
  8.7 0.5 collective-permute-done.1.refs_2_
  9.2 0.2 shard_map.120
  9.4 2.7 %collective-permute-start.3 = (bf16[32,384]{1,0:T(8,128)(2,1)S(1)}, bf16[32,384]{1,0:T(8,128)(2,1)S(1)}, u32[]{:S(2)}, u32[]{:S(2)}) collective-permute-start(bf16[32,384]{1,0:T(8,128)(2,1)S(1)} %get-tuple-element.46), channel_id=1, source_target_pairs={{0,4},{1,5},{2,6},{3,7},{4,0},{5,1},{6,2},{7,3},{8,12},{9,13},{10,... | collective-permute-start | bytes 73736 | tf_op jit(solution)/shard_map/ppermute | solution.py:438
  12.1 2.1 %collective-permute-done.3.far_ref = bf16[32,384]{1,0:T(8,128)(2,1)S(1)} collective-permute-done((bf16[32,384]{1,0:T(8,128)(2,1)S(1)}, bf16[32,384]{1,0:T(8,128)(2,1)S(1)}, u32[]{:S(2)}, u32[]{:S(2)}) %collective-permute-start.3) | collective-permute-done | bytes 24608 | tf_op jit(solution)/shard_map/ppermute | solution.py:438
  14.2 14.6 %shard_map.121 = (bf16[37,32,512]{2,1,0:T(8,128)(2,1)}, bf16[41,32,512]{2,1,0:T(8,128)(2,1)S(1)}, bf16[40,32,512]{2,1,0:T(8,128)(2,1)S(1)}, f32[75,32,512]{2,1,0...) custom-call(bf16[32,384]{1,0:T(8,128)(2,1)S(1)} %get-tuple-element.4, ...), custom_call_target="tpu_custom_call" | custom-call | tf_op jit(solution)/shard_map/pallas_call | solution.py:423
  28.9 2.2 %shard_map.122 = (f32[512,768]{1,0:T(8,128)S(1)}, bf16[512,768]{1,0:T(8,128)(2,1)S(1)}) custom-call(bf16[41,32,512]{2,1,0:T(8,128)(2,1)S(1)} %get-tuple-element.50.even_ref, bf16[40,32,512]{2,1,0:T(8,128)(2,1)S(1)} %get-tuple-element.51.odd_ref, bf16[512,1280]{1,0:T(8,128)(2,1)S(1)} %get-tuple-element.52.grad_t_ref), custom_call_target="tpu_custom_call" | custom-call | flops 1073741824 | tf_op jit(solution)/shard_map/pallas_call | solution.py:423
  31.1 0.1 collective-permute-start.4
  31.2 2.1 %shard_map.123 = (f32[38,32,512]{2,1,0:T(8,128)S(1)}, f32[37,32,512]{2,1,0:T(8,128)S(1)}) custom-call(bf16[39,32,512]{2,1,0:T(8,128)(2,1)S(1)} %get-tuple-element.55.grad_ref, bf16[3,512,512]{2,1,0:T(8,128)(2,1)S(1)} %get-tuple-element.56.w_ref), custom_call_target="tpu_custom_call" | custom-call | flops 1073741824 | tf_op jit(solution)/shard_map/pallas_call | solution.py:423
  33.3 0.2 collective-permute-done.4.got_ref
  33.4 0.1 shard_map.124
  33.6 1.7 %collective-permute-start.5 = (bf16[128,768]{1,0:T(8,128)(2,1)S(1)}, bf16[128,768]{1,0:T(8,128)(2,1)S(1)}, u32[]{:S(2)}, u32[]{:S(2)}) collective-permute-start(bf16[128,768]{1,0:T(8,128)(2,1)S(1)} %get-tuple-element.59), channel_id=1, source_target_pairs={{0,1},{1,0},{2,3},{3,2},{4,5},{5,4},{6,7},{7,6},{8,9},{9,8},{10,11... | collective-permute-start | bytes 589832 | tf_op jit(solution)/shard_map/ppermute | solution.py:438
  35.3 0.3 collective-permute-start.6
  35.6 1.5 %collective-permute-start.7 = (bf16[128,768]{1,0:T(8,128)(2,1)S(1)}, bf16[128,768]{1,0:T(8,128)(2,1)S(1)}, u32[]{:S(2)}, u32[]{:S(2)}) collective-permute-start(bf16[128,768]{1,0:T(8,128)(2,1)S(1)} %get-tuple-element.61), channel_id=1, source_target_pairs={{0,3},{1,2},{2,1},{3,0},{4,7},{5,6},{6,5},{7,4},{8,11},{9,10},{10,... | collective-permute-start | bytes 589832 | tf_op jit(solution)/shard_map/ppermute | solution.py:438
  37.1 3.2 %shard_map.125 = f32[16,512]{1,0:T(8,128)S(1)} custom-call(s32[32,128]{1,0:T(8,128)S(1)} %get-tuple-element.47.valid_ref, f32[75,32,512]{2,1,0:T(8,128)S(1)} %get-tuple-element.62.normed_ref, f32[75,32,512]{2,1,0:T(8,128)S(1)} %get-tuple-element.63.slope_ref, f32[32,512]{1,0:T(8,128)S(1)} %get-tuple-element.64.inv_ref, ...), custom_call_target="tpu_custom_call" | custom-call | flops 4294967296 | tf_op jit(solution)/shard_map/pallas_call | solution.py:423
  40.3 0.1 collective-permute-start.8
  40.4 1.2 %collective-permute-done.8 = f32[16,512]{1,0:T(8,128)S(1)} collective-permute-done((f32[16,512]{1,0:T(8,128)S(1)}, f32[16,512]{1,0:T(8,128)S(1)}, u32[]{:S(2)}, u32[]{:S(2)}) %collective-permute-start.8) | collective-permute-done | bytes 32800 | tf_op jit(solution)/shard_map/ppermute | solution.py:438
  41.6 1.5 %collective-permute-start.9 = (f32[16,512]{1,0:T(8,128)S(1)}, f32[16,512]{1,0:T(8,128)S(1)}, u32[]{:S(2)}, u32[]{:S(2)}) collective-permute-start(f32[16,512]{1,0:T(8,128)S(1)} %add.3.small_ref), channel_id=1, source_target_pairs={{0,16},{8,24},{16,0},{24,8},{1,17},{9,25},{17,1},{25,9},{2,18},{10... | collective-permute-start | bytes 98312 | tf_op jit(solution)/shard_map/ppermute | solution.py:438
  43.1 2.4 %collective-permute-done.9.small_got = f32[16,512]{1,0:T(8,128)S(1)} collective-permute-done((f32[16,512]{1,0:T(8,128)S(1)}, f32[16,512]{1,0:T(8,128)S(1)}, u32[]{:S(2)}, u32[]{:S(2)}) %collective-permute-start.9) | collective-permute-done | bytes 32800 | tf_op jit(solution)/shard_map/ppermute | solution.py:438
  45.5 0.0 collective-permute-done.5.got1
  45.5 0.0 collective-permute-done.6.got2
  45.5 0.7 %collective-permute-done.7.got3 = bf16[128,768]{1,0:T(8,128)(2,1)S(1)} collective-permute-done((bf16[128,768]{1,0:T(8,128)(2,1)S(1)}, bf16[128,768]{1,0:T(8,128)(2,1)S(1)}, u32[]{:S(2)}, u32[]{:S(2)}) %collective-permute-start.7) | collective-permute-done | bytes 196640 | tf_op jit(solution)/shard_map/ppermute | solution.py:438
  46.2 0.1 shard_map.126
  46.3 2.7 %collective-permute-start.10 = (bf16[64,768]{1,0:T(8,128)(2,1)S(1)}, bf16[64,768]{1,0:T(8,128)(2,1)S(1)}, u32[]{:S(2)}, u32[]{:S(2)}) collective-permute-start(bf16[64,768]{1,0:T(8,128)(2,1)S(1)} %get-tuple-element.69), channel_id=1, source_target_pairs={{0,4},{1,5},{2,6},{3,7},{4,0},{5,1},{6,2},{7,3},{8,12},{9,13},{10,... | collective-permute-start | bytes 294920 | tf_op jit(solution)/shard_map/ppermute | solution.py:438
  48.9 1.4 %collective-permute-start.13 = (f32[16,512]{1,0:T(8,128)S(1)}, f32[16,512]{1,0:T(8,128)S(1)}, u32[]{:S(2)}, u32[]{:S(2)}) collective-permute-start(f32[16,512]{1,0:T(8,128)S(1)} %get-tuple-element.70.small0), channel_id=1, source_target_pairs={{0,3},{1,2},{2,1},{3,0},{4,7},{5,6},{6,5},{7,4},{8,11},{9,10},{10,... | collective-permute-start | bytes 98312 | tf_op jit(solution)/shard_map/ppermute | solution.py:438
  50.3 1.6 %collective-permute-start.12 = (f32[16,512]{1,0:T(8,128)S(1)}, f32[16,512]{1,0:T(8,128)S(1)}, u32[]{:S(2)}, u32[]{:S(2)}) collective-permute-start(f32[16,512]{1,0:T(8,128)S(1)} %get-tuple-element.70.small0), channel_id=1, source_target_pairs={{0,2},{1,3},{2,0},{3,1},{4,6},{5,7},{6,4},{7,5},{8,10},{9,11},{10,... | collective-permute-start | bytes 98312 | tf_op jit(solution)/shard_map/ppermute | solution.py:438
  51.9 0.5 collective-permute-start.11
  52.4 2.0 %collective-permute-done.13.small3 = f32[16,512]{1,0:T(8,128)S(1)} collective-permute-done((f32[16,512]{1,0:T(8,128)S(1)}, f32[16,512]{1,0:T(8,128)S(1)}, u32[]{:S(2)}, u32[]{:S(2)}) %collective-permute-start.13) | collective-permute-done | bytes 32800 | tf_op jit(solution)/shard_map/ppermute | solution.py:438
  54.5 0.0 collective-permute-done.12.small2
  54.5 1.3 %collective-permute-done.11.small1 = f32[16,512]{1,0:T(8,128)S(1)} collective-permute-done((f32[16,512]{1,0:T(8,128)S(1)}, f32[16,512]{1,0:T(8,128)S(1)}, u32[]{:S(2)}, u32[]{:S(2)}) %collective-permute-start.11) | collective-permute-done | bytes 32800 | tf_op jit(solution)/shard_map/ppermute | solution.py:438
  55.8 0.0 collective-permute-done.10.got_ref
  55.8 1.6 %collective-permute-start.14 = (bf16[64,768]{1,0:T(8,128)(2,1)S(1)}, bf16[64,768]{1,0:T(8,128)(2,1)S(1)}, u32[]{:S(2)}, u32[]{:S(2)}) collective-permute-start(bf16[64,768]{1,0:T(8,128)(2,1)S(1)} %get-tuple-element.71.mine_ref), channel_id=1, source_target_pairs={{0,16},{8,24},{16,0},{24,8},{1,17},{9,25},{17,1},{25,9},{2,18},{10... | collective-permute-start | bytes 294920 | tf_op jit(solution)/shard_map/ppermute | solution.py:438
  57.4 0.5 collective-permute-start.15
  57.9 4.6 %collective-permute-done.15.refs_1_ = f32[16,512]{1,0:T(8,128)S(1)} collective-permute-done((f32[16,512]{1,0:T(8,128)S(1)}, f32[16,512]{1,0:T(8,128)S(1)}, u32[]{:S(2)}, u32[]{:S(2)}) %collective-permute-start.15) | collective-permute-done | bytes 32800 | tf_op jit(solution)/shard_map/ppermute | solution.py:438
  62.5 0.0 collective-permute-done.14.got_ref
  62.5 0.1 collective-permute-start.16
  62.6 1.4 %collective-permute-done.16.other_ref = f32[64,768]{1,0:T(8,128)S(1)} collective-permute-done((f32[64,768]{1,0:T(8,128)S(1)}, f32[64,768]{1,0:T(8,128)S(1)}, u32[]{:S(2)}, u32[]{:S(2)}) %collective-permute-start.16) | collective-permute-done | bytes 196640 | tf_op jit(solution)/shard_map/ppermute | solution.py:438
  64.0 0.8 %shard_map.129 = (f32[3,64,512]{2,1,0:T(8,128)}, f32[10,64]{1,0:T(8,128)}, f32[1,64]{1,0:T(1,128)}, f32[1,64]{1,0:T(1,128)}) custom-call(f32[64,768]{1,0:T(8,128)S(1)} %get-tuple-element.73.own_ref, f32[64,768]{1,0:T(8,128)S(1)} %collective-permute-done.16.other_ref, f32[16,512]{1,0:T(8,128)S(1)} %get-tuple-element.74.small_ref), custom_call_target="tpu_custom_call" | custom-call | tf_op jit(solution)/shard_map/pallas_call | solution.py:423
  (3 shorter events, 0.1 us)
Async XLA Ops:
  0.6 5.9 %collective-permute-start = (bf16[32,384]{1,0:T(8,128)(2,1)}, bf16[32,384]{1,0:T(8,128)(2,1)S(1)}, u32[]{:S(2)}, u32[]{:S(2)}) collective-permute-start(bf16[32,384]{1,0:T(8,128)(2,1)} %wave_hbm.1), channel_id=1, source_target_pairs={{0,1},{1,0},{2,3},{3,2},{4,5},{5,4},{6,7},{7,6},{8,9},{9,8},{10,11... | collective-permute-start | bytes 73736 | tf_op jit(solution)/shard_map/ppermute | solution.py:438
  3.6 5.1 %collective-permute-start.2 = (bf16[32,384]{1,0:T(8,128)(2,1)}, bf16[32,384]{1,0:T(8,128)(2,1)S(1)}, u32[]{:S(2)}, u32[]{:S(2)}) collective-permute-start(bf16[32,384]{1,0:T(8,128)(2,1)} %wave_hbm.1), channel_id=1, source_target_pairs={{0,3},{1,2},{2,1},{3,0},{4,7},{5,6},{6,5},{7,4},{8,11},{9,10},{10,... | collective-permute-start | bytes 73736 | tf_op jit(solution)/shard_map/ppermute | solution.py:438
  5.2 4.0 %collective-permute-start.1 = (bf16[32,384]{1,0:T(8,128)(2,1)}, bf16[32,384]{1,0:T(8,128)(2,1)S(1)}, u32[]{:S(2)}, u32[]{:S(2)}) collective-permute-start(bf16[32,384]{1,0:T(8,128)(2,1)} %wave_hbm.1), channel_id=1, source_target_pairs={{0,2},{1,3},{2,0},{3,1},{4,6},{5,7},{6,4},{7,5},{8,10},{9,11},{10,... | collective-permute-start | bytes 73736 | tf_op jit(solution)/shard_map/ppermute | solution.py:438
  9.4 4.8 %collective-permute-start.3 = (bf16[32,384]{1,0:T(8,128)(2,1)S(1)}, bf16[32,384]{1,0:T(8,128)(2,1)S(1)}, u32[]{:S(2)}, u32[]{:S(2)}) collective-permute-start(bf16[32,384]{1,0:T(8,128)(2,1)S(1)} %get-tuple-element.46), channel_id=1, source_target_pairs={{0,4},{1,5},{2,6},{3,7},{4,0},{5,1},{6,2},{7,3},{8,12},{9,13},{10,... | collective-permute-start | bytes 73736 | tf_op jit(solution)/shard_map/ppermute | solution.py:438
  31.1 2.4 %collective-permute-start.4 = (bf16[512,768]{1,0:T(8,128)(2,1)S(1)}, bf16[512,768]{1,0:T(8,128)(2,1)S(1)}, u32[]{:S(2)}, u32[]{:S(2)}) collective-permute-start(bf16[512,768]{1,0:T(8,128)(2,1)S(1)} %get-tuple-element.54), channel_id=1, source_target_pairs={{0,8},{8,0},{16,24},{24,16},{1,9},{9,1},{17,25},{25,17},{2,10},{10... | collective-permute-start | bytes 2359304 | tf_op jit(solution)/shard_map/ppermute | solution.py:438
  33.6 12.0 %collective-permute-start.5 = (bf16[128,768]{1,0:T(8,128)(2,1)S(1)}, bf16[128,768]{1,0:T(8,128)(2,1)S(1)}, u32[]{:S(2)}, u32[]{:S(2)}) collective-permute-start(bf16[128,768]{1,0:T(8,128)(2,1)S(1)} %get-tuple-element.59), channel_id=1, source_target_pairs={{0,1},{1,0},{2,3},{3,2},{4,5},{5,4},{6,7},{7,6},{8,9},{9,8},{10,11... | collective-permute-start | bytes 589832 | tf_op jit(solution)/shard_map/ppermute | solution.py:438
  35.3 10.2 %collective-permute-start.6 = (bf16[128,768]{1,0:T(8,128)(2,1)S(1)}, bf16[128,768]{1,0:T(8,128)(2,1)S(1)}, u32[]{:S(2)}, u32[]{:S(2)}) collective-permute-start(bf16[128,768]{1,0:T(8,128)(2,1)S(1)} %get-tuple-element.60), channel_id=1, source_target_pairs={{0,2},{1,3},{2,0},{3,1},{4,6},{5,7},{6,4},{7,5},{8,10},{9,11},{10,... | collective-permute-start | bytes 589832 | tf_op jit(solution)/shard_map/ppermute | solution.py:438
  35.6 10.6 %collective-permute-start.7 = (bf16[128,768]{1,0:T(8,128)(2,1)S(1)}, bf16[128,768]{1,0:T(8,128)(2,1)S(1)}, u32[]{:S(2)}, u32[]{:S(2)}) collective-permute-start(bf16[128,768]{1,0:T(8,128)(2,1)S(1)} %get-tuple-element.61), channel_id=1, source_target_pairs={{0,3},{1,2},{2,1},{3,0},{4,7},{5,6},{6,5},{7,4},{8,11},{9,10},{10,... | collective-permute-start | bytes 589832 | tf_op jit(solution)/shard_map/ppermute | solution.py:438
  40.3 1.3 %collective-permute-start.8 = (f32[16,512]{1,0:T(8,128)S(1)}, f32[16,512]{1,0:T(8,128)S(1)}, u32[]{:S(2)}, u32[]{:S(2)}) collective-permute-start(f32[16,512]{1,0:T(8,128)S(1)} %shard_map.125), channel_id=1, source_target_pairs={{0,8},{8,0},{16,24},{24,16},{1,9},{9,1},{17,25},{25,17},{2,10},{10... | collective-permute-start | bytes 98312 | tf_op jit(solution)/shard_map/ppermute | solution.py:438
  41.6 3.9 %collective-permute-start.9 = (f32[16,512]{1,0:T(8,128)S(1)}, f32[16,512]{1,0:T(8,128)S(1)}, u32[]{:S(2)}, u32[]{:S(2)}) collective-permute-start(f32[16,512]{1,0:T(8,128)S(1)} %add.3.small_ref), channel_id=1, source_target_pairs={{0,16},{8,24},{16,0},{24,8},{1,17},{9,25},{17,1},{25,9},{2,18},{10... | collective-permute-start | bytes 98312 | tf_op jit(solution)/shard_map/ppermute | solution.py:438
  46.3 9.5 %collective-permute-start.10 = (bf16[64,768]{1,0:T(8,128)(2,1)S(1)}, bf16[64,768]{1,0:T(8,128)(2,1)S(1)}, u32[]{:S(2)}, u32[]{:S(2)}) collective-permute-start(bf16[64,768]{1,0:T(8,128)(2,1)S(1)} %get-tuple-element.69), channel_id=1, source_target_pairs={{0,4},{1,5},{2,6},{3,7},{4,0},{5,1},{6,2},{7,3},{8,12},{9,13},{10,... | collective-permute-start | bytes 294920 | tf_op jit(solution)/shard_map/ppermute | solution.py:438
  48.9 5.5 %collective-permute-start.13 = (f32[16,512]{1,0:T(8,128)S(1)}, f32[16,512]{1,0:T(8,128)S(1)}, u32[]{:S(2)}, u32[]{:S(2)}) collective-permute-start(f32[16,512]{1,0:T(8,128)S(1)} %get-tuple-element.70.small0), channel_id=1, source_target_pairs={{0,3},{1,2},{2,1},{3,0},{4,7},{5,6},{6,5},{7,4},{8,11},{9,10},{10,... | collective-permute-start | bytes 98312 | tf_op jit(solution)/shard_map/ppermute | solution.py:438
  50.3 4.1 %collective-permute-start.12 = (f32[16,512]{1,0:T(8,128)S(1)}, f32[16,512]{1,0:T(8,128)S(1)}, u32[]{:S(2)}, u32[]{:S(2)}) collective-permute-start(f32[16,512]{1,0:T(8,128)S(1)} %get-tuple-element.70.small0), channel_id=1, source_target_pairs={{0,2},{1,3},{2,0},{3,1},{4,6},{5,7},{6,4},{7,5},{8,10},{9,11},{10,... | collective-permute-start | bytes 98312 | tf_op jit(solution)/shard_map/ppermute | solution.py:438
  51.9 3.9 %collective-permute-start.11 = (f32[16,512]{1,0:T(8,128)S(1)}, f32[16,512]{1,0:T(8,128)S(1)}, u32[]{:S(2)}, u32[]{:S(2)}) collective-permute-start(f32[16,512]{1,0:T(8,128)S(1)} %get-tuple-element.70.small0), channel_id=1, source_target_pairs={{0,1},{1,0},{2,3},{3,2},{4,5},{5,4},{6,7},{7,6},{8,9},{9,8},{10,11... | collective-permute-start | bytes 98312 | tf_op jit(solution)/shard_map/ppermute | solution.py:438
  55.8 6.6 %collective-permute-start.14 = (bf16[64,768]{1,0:T(8,128)(2,1)S(1)}, bf16[64,768]{1,0:T(8,128)(2,1)S(1)}, u32[]{:S(2)}, u32[]{:S(2)}) collective-permute-start(bf16[64,768]{1,0:T(8,128)(2,1)S(1)} %get-tuple-element.71.mine_ref), channel_id=1, source_target_pairs={{0,16},{8,24},{16,0},{24,8},{1,17},{9,25},{17,1},{25,9},{2,18},{10... | collective-permute-start | bytes 294920 | tf_op jit(solution)/shard_map/ppermute | solution.py:438
  57.4 5.1 %collective-permute-start.15 = (f32[16,512]{1,0:T(8,128)S(1)}, f32[16,512]{1,0:T(8,128)S(1)}, u32[]{:S(2)}, u32[]{:S(2)}) collective-permute-start(f32[16,512]{1,0:T(8,128)S(1)} %get-tuple-element.72.refs_0_), channel_id=1, source_target_pairs={{0,4},{1,5},{2,6},{3,7},{4,0},{5,1},{6,2},{7,3},{8,12},{9,13},{10,... | collective-permute-start | bytes 98312 | tf_op jit(solution)/shard_map/ppermute | solution.py:438
  62.5 1.5 %collective-permute-start.16 = (f32[64,768]{1,0:T(8,128)S(1)}, f32[64,768]{1,0:T(8,128)S(1)}, u32[]{:S(2)}, u32[]{:S(2)}) collective-permute-start(f32[64,768]{1,0:T(8,128)S(1)} %get-tuple-element.73.own_ref), channel_id=1, source_target_pairs={{0,8},{8,0},{16,24},{24,16},{1,9},{9,1},{17,25},{25,17},{2,10},{10... | collective-permute-start | bytes 589832 | tf_op jit(solution)/shard_map/ppermute | solution.py:438

commit v4 on v3

--- a/solution.py
+++ b/solution.py
@@ -10,23 +10,21 @@
 F32 = jnp.float32
 BF16 = jnp.bfloat16
 GROUP = 8
+LANES = 256
 MIN_SAMPLES = 288
 MIB = 1 << 20
 
 
 def gelu_and_slope(value):
-    size = jnp.abs(value)
-    bell = jnp.exp(value * value * -0.5)
-    base = 1.0 + size * (0.3275911 * 0.7071067811865476)
-    frac = pl.reciprocal(base, approx=True)
-    frac = frac * (2.0 - base * frac)
+    bell = jnp.exp2(value * value * (-0.5 * 1.4426950408889634))
+    base = 1.0 + jnp.abs(value) * (0.3275911 * 0.7071067811865476)
+    frac = pltpu.reciprocal(base, approx=True)
     poly = 0.5 * 1.061405429
     for coef in (-1.453152027, 1.421413741, -0.284496736, 0.254829592):
         poly = poly * frac + 0.5 * coef
     tail = poly * frac * bell
-    gelu = jnp.maximum(value, 0.0) - size * tail
     phi = jnp.where(value < 0.0, tail, 1.0 - tail)
-    return gelu, phi + value * bell * 0.3989422804014327
+    return value * phi, phi + value * bell * 0.3989422804014327
 
 
 def rows_first(a, b):
@@ -113,7 +111,7 @@
     frames0,
     frames1,
     taps,
-    reverse,
+    places,
     near_ref,
     far_ref,
     valid_ref,
@@ -122,22 +120,28 @@
     bias_hbm,
     w_hbm,
     cot_hbm,
-    feat_ref,
+    feat_out,
     even_ref,
     odd_ref,
-    normed_ref,
+    pre0,
     slope_ref,
+    mean_ref,
     inv_ref,
     patch_ref,
     grad_ref,
     grad_t_ref,
     gain_ref,
     w_ref,
-    pre0,
+    stage,
+    fresh,
     pre1,
+    scale_ref,
+    shift_ref,
     bias_ref,
     cot_ref,
+    feat_ref,
     sems,
+    out_sem,
 ):
     waiting = copies((gain_hbm, bias_hbm, w_hbm, cot_hbm), (gain_ref, bias_ref, w_ref, cot_ref), sems)
     rows, samp = near_ref.shape
@@ -145,107 +149,149 @@
     stride = taps // 2
     depth = band_ref.shape[0]
     groups = pre0.shape[0]
-    width = pre0.shape[2] // GROUP
+    width = LANES
+    parts = [slice(first, first + width) for first in range(0, chans, width)]
     min_valid = (MIN_SAMPLES - taps) // stride + 1
-    free_groups = min(min_valid // GROUP, frames0 // GROUP)
     full_groups = frames0 // GROUP
+    free_groups = min(min_valid // GROUP, full_groups)
     wave = near_ref[...] + far_ref[...]
     for g in range(groups):
         pick = onehot(iota((samp, depth), 0) == iota((samp, depth), 1) + GROUP * stride * g)
         patch_ref[g] = dot(wave, pick).astype(BF16)
     patches = patch_ref[...].reshape(groups * rows, depth)
-
-    for block in range(chans // width):
-        lanes = slice(block * width, (block + 1) * width)
-        for f in range(GROUP):
-            cols = slice(f * chans + block * width, f * chans + (block + 1) * width)
-            pre0[:, :, f * width : (f + 1) * width] = dot(patches, band_ref[:, cols]).reshape(groups, rows, width)
-        valid = jnp.broadcast_to(valid_ref[:, :1], (rows, width))
-        count = valid.astype(F32)
-
-        def frame(g, f):
-            return pre0[g, :, f * width : (f + 1) * width]
-
-        def over_frames(body, init):
-            def step(masked, g, carry):
+    for f in range(GROUP):
+        cols = slice(f * chans, (f + 1) * chans)
+        pre0[:, :, cols] = dot(patches, band_ref[:, cols]).reshape(groups, rows, chans)
+
+    valid = jnp.broadcast_to(valid_ref[:, :1], (rows, width))
+    count = valid.astype(F32)
+
+    def frame(g, f, lanes):
+        return pre0[g, :, f * chans + lanes.start : f * chans + lanes.stop]
+
+    def masked_to(value, t, masked):
+        return jnp.where(valid > t, value, 0.0) if masked else value
+
+    for lanes in parts:
+
+        def over_frames(body):
+            def step(masked, g, total):
                 for f in range(GROUP):
-                    carry = body(carry, g, f, masked)
-                return carry
-
-            carry = lax.fori_loop(0, free_groups, functools.partial(step, False), init)
-            carry = lax.fori_loop(free_groups, full_groups, functools.partial(step, True), carry)
+                    total = total + body(g, f, masked)
+                return total
+
+            total = lax.fori_loop(0, free_groups, functools.partial(step, False), jnp.zeros((rows, width), F32))
+            total = lax.fori_loop(free_groups, full_groups, functools.partial(step, True), total)
             for f in range(frames0 - full_groups * GROUP):
-                carry = body(carry, full_groups, f, True)
-            return carry
-
-        def masked_to(value, g, f, masked):
-            return jnp.where(valid > g * GROUP + f, value, 0.0) if masked else value
-
-        def add_mean(total, g, f, masked):
-            return total + masked_to(frame(g, f), g, f, masked)
-
-        mean = over_frames(add_mean, jnp.zeros((rows, width), F32)) / count
-
-        def add_var(total, g, f, masked):
-            centred = masked_to(frame(g, f) - mean, g, f, masked)
-            return total + centred * centred
-
-        var = over_frames(add_var, jnp.zeros((rows, width), F32)) / count
-        inv = lax.rsqrt(var + 1e-05)
+                total = total + body(full_groups, f, True)
+            return total
+
+        mean = over_frames(lambda g, f, masked: masked_to(frame(g, f, lanes), g * GROUP + f, masked)) / count
+
+        def square(g, f, masked):
+            centred = masked_to(frame(g, f, lanes) - mean, g * GROUP + f, masked)
+            return centred * centred
+
+        inv = lax.rsqrt(over_frames(square) / count + 1e-05)
+        mean_ref[:, lanes] = mean
         inv_ref[:, lanes] = inv
-        if block == 0:
+        if lanes.start == 0:
             waiting[0].wait()
             waiting[1].wait()
-        gain = jnp.broadcast_to(gain_ref[:, lanes], (rows, width))
-        bias = jnp.broadcast_to(bias_ref[:, lanes], (rows, width))
-
-        def finish(carry, g, f, masked):
-            normed = (frame(g, f) - mean) * inv
-            gelu, slope = gelu_and_slope(normed * gain + bias)
-            t = g * GROUP + f
-            normed_ref[t, :, lanes] = masked_to(normed, g, f, masked)
-            slope_ref[t, :, lanes] = masked_to(slope, g, f, masked)
-            act_ref = odd_ref if f % 2 else even_ref
-            act_ref[g * (GROUP // 2) + f // 2, :, lanes] = masked_to(gelu, g, f, masked).astype(BF16)
-            return carry
-
-        over_frames(finish, 0)
-    for ref, used in ((even_ref, (frames0 + 1) // 2), (odd_ref, frames0 // 2)):
-        ref[used:] = jnp.zeros((ref.shape[0] - used,) + ref.shape[1:], BF16)
-
+        scale = inv * gain_ref[:, lanes]
+        scale_ref[:, lanes] = scale
+        shift_ref[:, lanes] = bias_ref[:, lanes] - mean * scale
+
+    half = GROUP // 2
+    span = half * rows
+    frames_of = even_ref.shape[0] - 1
+    even_ref[frames_of:] = jnp.zeros((1,) + even_ref.shape[1:], BF16)
+    grad_ref[0] = jnp.zeros(grad_ref.shape[1:], BF16)
+    grad_ref[frames1 + 1] = jnp.zeros(grad_ref.shape[1:], BF16)
+    grad_t_ref[:, frames1 // half * span :] = jnp.zeros((chans, grad_t_ref.shape[1] - frames1 // half * span), BF16)
+    min_valid1 = (min_valid - 3) // 2 + 1
+    valid1 = lax.shift_right_arithmetic(valid - 3, 1) + 1
+    slab = chans // len(places)
+
+    def unstage(g):
+        for f in range(GROUP):
+            (odd_ref if f % 2 else even_ref)[g * half + f // 2] = stage[f]
+
+    def activate0(g, masked, used=GROUP):
+        for f in range(used):
+            for lanes in parts:
+                gelu, slope = gelu_and_slope(frame(g, f, lanes) * scale_ref[:, lanes] + shift_ref[:, lanes])
+                t = g * GROUP + f
+                slope_ref[t, :, lanes] = masked_to(slope, t, masked)
+                stage[f, :, lanes] = masked_to(gelu, t, masked).astype(BF16)
+
+    def convolve(h, used):
+        first = h * half
+        for lanes in parts:
+            total = dot(even_ref[pl.ds(first, used)].reshape(used * rows, chans), w_ref[0, :, lanes])
+            total += dot(odd_ref[pl.ds(first, used)].reshape(used * rows, chans), w_ref[1, :, lanes])
+            total += dot(even_ref[pl.ds(first + 1, used)].reshape(used * rows, chans), w_ref[2, :, lanes])
+            fresh[:used, :, lanes] = total.reshape(used, rows, width)
+
+    def activate1(h, used, masked):
+        for j in range(used):
+            u = h * half + j
+            for lanes in parts:
+                gelu, slope = gelu_and_slope(pre1[j, :, lanes])
+                grad = cot_ref[u, :, lanes].astype(F32) * slope
+                if masked:
+                    gelu, grad = jnp.where(valid1 > u, gelu, 0.0), jnp.where(valid1 > u, grad, 0.0)
+                feat_ref[u, :, lanes] = gelu.astype(BF16)
+                grad_ref[u + 1, :, lanes] = grad.astype(BF16)
+
+    def leave(h, used):
+        frames = pl.ds(h * half, used)
+        pltpu.make_async_copy(feat_ref.at[frames], feat_out.at[frames], out_sem).start()
+
+    def turn(h, used):
+        leave(h, used)
+        turned = grad_ref[pl.ds(h * half + 1, used)].reshape(used * rows, chans).T
+        start = h * span
+        cols = pl.ds(start if isinstance(start, int) else pl.multiple_of(start, span), used * rows)
+        for place, source in enumerate(places):
+            grad_t_ref[place * slab : (place + 1) * slab, cols] = turned[source * slab : (source + 1) * slab]
+
+    def fill(g, carry):
+        unstage(jnp.maximum(g - 1, 0))
+        activate0(g, False)
+        return carry
+
+    def steady(masked, g, carry, used=GROUP):
+        unstage(g - 1)
+        pre1[...] = fresh[...]
+        convolve(g - 2, half)
+        activate1(g - 3, half, masked)
+        activate0(g, masked, used)
+        turn(g - 3, half)
+        return carry
+
+    stage[...] = jnp.zeros(stage.shape, BF16)
+    lax.fori_loop(0, 3, fill, 0)
     waiting[2].wait()
     waiting[3].wait()
-    grad_ref[0] = jnp.zeros(grad_ref.shape[1:], BF16)
-    grad_ref[frames1 + 1] = jnp.zeros(grad_ref.shape[1:], BF16)
-    padded = grad_t_ref.shape[1]
-    used = frames1 * rows
-    grad_t_ref[:, (used // 128) * 128 :] = jnp.zeros((chans, padded - (used // 128) * 128), BF16)
-    valid = jnp.broadcast_to(valid_ref[:, :1], (rows, chans))
-    valid1 = lax.shift_right_arithmetic(valid - 3, 1) + 1
-    chunk = 12
-    for first in range(0, frames1 - chunk + 1, chunk):
-        count = chunk if first + 2 * chunk <= frames1 else frames1 - first
-        size = count * rows
-        total = dot(even_ref[first : first + count].reshape(size, chans), w_ref[0])
-        total += dot(odd_ref[first : first + count].reshape(size, chans), w_ref[1])
-        total += dot(even_ref[first + 1 : first + count + 1].reshape(size, chans), w_ref[2])
-        pre1[:count] = total.reshape(count, rows, chans)
-
-        def activate(u, carry):
-            gelu, slope = gelu_and_slope(pre1[u])
-            keep = valid1 > u + first
-            feat_ref[u + first] = jnp.where(keep, gelu, 0.0).astype(BF16)
-            grad = cot_ref[u + first].astype(F32) * slope
-            grad_ref[u + first + 1] = jnp.where(keep, grad, 0.0).astype(BF16)
-            return carry
-
-        lax.fori_loop(0, count, activate, 0)
-        turned = grad_ref[first + 1 : first + 1 + count].reshape(size, chans).T
-        slab = chans // len(reverse)
-        for place, source in enumerate(reverse):
-            grad_t_ref[place * slab : (place + 1) * slab, first * rows : first * rows + size] = turned[
-                source * slab : (source + 1) * slab
-            ]
+    convolve(0, half)
+    lax.fori_loop(3, free_groups, functools.partial(steady, False), 0)
+    lax.fori_loop(free_groups, full_groups, functools.partial(steady, True), 0)
+    rest = frames0 - full_groups * GROUP
+    if rest:
+        steady(True, full_groups, 0, rest)
+        stage[rest:] = jnp.zeros((GROUP - rest,) + stage.shape[1:], BF16)
+    unstage(groups - 1)
+    last = frames1 // half
+    for h in range(groups - 2, last + 1):
+        pre1[...] = fresh[...]
+        convolve(h, min(half, frames1 - h * half))
+        activate1(h - 1, half, True)
+        turn(h - 1, half)
+    pre1[...] = fresh[...]
+    activate1(last, frames1 - last * half, True)
+    turn(last, frames1 - last * half)
+    pltpu.make_async_copy(feat_ref, feat_out, out_sem).wait()
 
 
 def outer_kernel(even_ref, odd_ref, grad_t_ref, keep_ref, send_ref):
@@ -275,8 +321,9 @@
     frames0,
     taps,
     valid_ref,
-    normed_ref,
+    pre0,
     slope_ref,
+    mean_ref,
     inv_ref,
     patch_ref,
     even_ref,
@@ -297,13 +344,16 @@
     for block in range(chans // width):
         lanes = slice(block * width, (block + 1) * width)
 
+        def frame(g, f):
+            return pre0[g, :, f * chans + block * width : f * chans + (block + 1) * width]
+
         def slopes(g, f, carry):
             bias_sum, gain_sum = carry
             t = g * GROUP + f
             dact = (odd_ref if f % 2 else even_ref)[g * (GROUP // 2) + f // 2, :, lanes]
             dlift = dact * slope_ref[t, :, lanes]
             lift[t] = dlift
-            return bias_sum + dlift, gain_sum + dlift * normed_ref[t, :, lanes]
+            return bias_sum + dlift, gain_sum + dlift * frame(g, f)
 
         def add(g, carry):
             for f in range(GROUP):
@@ -315,17 +365,19 @@
         for f in range(rest):
             carry = slopes(full_groups, f, carry)
         bias_sum, gain_sum = carry
+        mean, inv = mean_ref[:, lanes], inv_ref[:, lanes]
+        gain_sum = (gain_sum - mean * bias_sum) * inv
         out_ref[taps : taps + 1, lanes] = jnp.sum(gain_sum, axis=0, keepdims=True)
         out_ref[taps + 1 : taps + 2, lanes] = jnp.sum(bias_sum, axis=0, keepdims=True)
         valid = jnp.broadcast_to(valid_ref[:, :1], (rows, width))
         count = valid.astype(F32)
-        scale = inv_ref[:, lanes] * gain_ref[:, lanes]
-        bias_sum = bias_sum / count
-        gain_sum = gain_sum / count
+        scale = inv * gain_ref[:, lanes]
+        slant = scale * inv * gain_sum / count
+        level = scale * bias_sum / count - mean * slant
 
         def finish(g, f):
             t = g * GROUP + f
-            value = scale * (lift[t] - bias_sum - normed_ref[t, :, lanes] * gain_sum)
+            value = scale * lift[t] - frame(g, f) * slant - level
             dpre0[g, :, f * width : (f + 1) * width] = jnp.where(valid > t, value, 0.0).astype(BF16)
 
         def whole(g, carry):
@@ -358,22 +410,45 @@
         send_ref[...] = quarter(jnp.bitwise_xor(place, offset)).astype(BF16)
 
 
-def gather_kernel(bit, own_ref, got1, got2, got3, small_ref, small_got, next_ref, send_ref, total_ref):
+def part_kernel(own_ref, got1, got2, small_ref, sum_ref, total_ref):
+    sum_ref[...] = own_ref[...] + (got1[...].astype(F32) + got2[...].astype(F32))
+    total_ref[...] = small_ref[...]
+
+
+def write_small(send_ref, first, total):
+    lines, chans = total.shape
+    send_ref[first:, :chans] = total.astype(send_ref.dtype)
+    send_ref[first:, chans:] = jnp.zeros((lines, send_ref.shape[1] - chans), send_ref.dtype)
+
+
+def read_small(got_ref, first, chans):
+    return got_ref[first:, :chans].astype(F32)
+
+
+def gather_kernel(bit, own_ref, got3, small0, small1, small2, small3, next_ref, send_ref, total_ref):
     half = next_ref.shape[0]
     side = lax.rem(lax.shift_right_logical(lax.axis_index("dev"), bit), 2)
 
     def part(index):
         lines = pl.ds(pl.multiple_of(index * half, half), half)
-        return own_ref[lines, :] + (
-            got1[lines, :].astype(F32) + got2[lines, :].astype(F32) + got3[lines, :].astype(F32)
-        )
+        return own_ref[lines, :] + got3[lines, :].astype(F32)
 
     next_ref[...] = part(side)
-    send_ref[...] = part(1 - side).astype(BF16)
-    total_ref[...] = small_ref[...] + small_got[...]
-
-
-def fold_kernel(bit, keep_ref, got_ref, send_ref, next_ref):
+    send_ref[:half] = part(1 - side).astype(BF16)
+    total = (small0[...] + small1[...]) + (small2[...] + small3[...])
+    total_ref[...] = total
+    write_small(send_ref, half, total)
+
+
+def fold_kernel(bit, keep_ref, got_ref, small_ref, total_ref, send_ref, *rest):
+    half = keep_ref.shape[0]
+    total = small_ref[...] + read_small(got_ref, half, small_ref.shape[1])
+    total_ref[...] = total
+    if not rest:
+        send_ref[:half] = (keep_ref[...] + got_ref[:half].astype(F32)).astype(BF16)
+        write_small(send_ref, half, total)
+        return
+    next_ref = rest[0]
     size = next_ref.shape[0]
     side = lax.rem(lax.shift_right_logical(lax.axis_index("dev"), bit), 2)
 
@@ -382,33 +457,26 @@
         return keep_ref[here, :] + got_ref[here, :].astype(F32)
 
     next_ref[...] = part(side)
-    send_ref[...] = part(1 - side).astype(BF16)
-
-
-def round_kernel(keep_ref, got_ref, small0, small1, small2, small3, send_ref, total_ref):
-    send_ref[...] = (keep_ref[...] + got_ref[...].astype(F32)).astype(BF16)
-    total_ref[...] = (small0[...] + small1[...]) + (small2[...] + small3[...])
-
-
-def across_kernel(mine_ref, got_ref, *refs):
-    out_ref = refs[2] if len(refs) > 2 else refs[0]
+    send_ref[:size] = part(1 - side).astype(BF16)
+    write_small(send_ref, size, total)
+
+
+def across_kernel(mine_ref, got_ref, out_ref):
     out_ref[...] = (mine_ref[...].astype(F32) + got_ref[...].astype(F32)).astype(out_ref.dtype)
-    if len(refs) > 2:
-        refs[3][...] = refs[0][...] + refs[1][...]
-
-
-def join_kernel(members, taps, own_ref, other_ref, small_ref, out_ref, first_ref, gain_ref, bias_ref):
+
+
+def join_kernel(members, taps, own_ref, other_ref, out_ref, first_ref, gain_ref, bias_ref):
     second, size, chans = out_ref.shape
     half = chans // 2
     core = lax.rem(lax.axis_index("grp"), 2)
     for tap in range(second):
         lanes = slice(tap * half, (tap + 1) * half)
-        out_ref[tap, :, pl.ds(pl.multiple_of(core * half, half), half)] = own_ref[:, lanes]
-        out_ref[tap, :, pl.ds(pl.multiple_of((1 - core) * half, half), half)] = other_ref[:, lanes]
+        out_ref[tap, :, pl.ds(pl.multiple_of(core * half, half), half)] = own_ref[:size, lanes]
+        out_ref[tap, :, pl.ds(pl.multiple_of((1 - core) * half, half), half)] = other_ref[:size, lanes]
     wide = max(size, 128)
     member = lax.axis_index("dev")
     block = pl.ds(pl.multiple_of(member // (wide // size) * wide, wide), wide)
-    total = small_ref[:, block]
+    total = own_ref[size:, block] + other_ref[size:, block]
     value = total[:, :size]
     for place in range(1, wide // size):
         value = jnp.where(lax.rem(member, wide // size) == place, total[:, place * size : (place + 1) * size], value)
@@ -426,7 +494,7 @@
             jax.ShapeDtypeStruct(out[0], out[1]) if len(out) > 2 else pltpu.VMEM(out[0], out[1]) for out in outs
         ],
         in_specs=[pl.BlockSpec(memory_space=pltpu.HBM) if i in outside else vmem for i in range(len(args))],
-        out_specs=[vmem] * len(outs),
+        out_specs=[pl.BlockSpec(memory_space=pl.ANY) if out[-1] == "hbm" else vmem for out in outs],
         scratch_shapes=[pltpu.VMEM(*entry) if isinstance(entry, tuple) else entry for entry in scratch],
         compiler_params=pltpu.CompilerParams(vmem_limit_bytes=limit * MIB),
         cost_estimate=pl.CostEstimate(flops=flops, bytes_accessed=touched, transcendentals=0),
@@ -449,7 +517,7 @@
     frames1 = (frames0 - taps_second) // 2 + 1
     groups = -(-frames0 // GROUP)
     depth = 128
-    width = 256
+    width = LANES
     dev_bits = members.bit_length() - 1
     grp_bits = groups_of.bit_length() - 1
 
@@ -492,14 +560,15 @@
     places = [0] * members
     for dev in range(members):
         places[dev % 4 * (members // 4) + dev // 4] = dev
-    feat, even, odd, normed, slope, inv, patch, grad, grad_t, gain_in, w_in = call(
+    feat, even, odd, pre0, slope, mean, inv, patch, grad, grad_t, gain_in, w_in = call(
         functools.partial(forward_kernel, frames0, frames1, taps, places),
         [
-            ((frames1, rows, chans), BF16, "out"),
+            ((frames1, rows, chans), BF16, "hbm"),
             ((pad_frames + 1, rows, chans), BF16),
             ((pad_frames, rows, chans), BF16),
-            ((frames0, rows, chans), F32),
-            ((frames0, rows, chans), F32),
+            ((groups, rows, GROUP * chans), F32),
+            ((groups * GROUP, rows, chans), F32),
+            ((rows, chans), F32),
             ((rows, chans), F32),
             ((groups, rows, depth), BF16),
             ((frames1 + 2, rows, chans), BF16),
@@ -509,11 +578,16 @@
         ],
         [near, far, valid, band, gain, bias, w_second, cot_t],
         scratch=[
-            ((groups, rows, GROUP * width), F32),
-            ((16, rows, chans), F32),
+            ((GROUP, rows, chans), BF16),
+            ((GROUP // 2, rows, chans), F32),
+            ((GROUP // 2, rows, chans), F32),
+            ((rows, chans), F32),
+            ((rows, chans), F32),
             (bias.shape, F32),
             (cot_t.shape, BF16),
+            (cot_t.shape, BF16),
             pltpu.SemaphoreType.DMA((4,)),
+            pltpu.SemaphoreType.DMA,
         ],
         outside=(4, 5, 6, 7),
     )
@@ -535,7 +609,7 @@
     small = call(
         functools.partial(backward_kernel, frames0, taps),
         [((16, chans), F32)],
-        [valid, normed, slope, inv, patch, dact_even, dact_odd, gain_in],
+        [valid, pre0, slope, mean, inv, patch, dact_even, dact_odd, gain_in],
         scratch=[
             ((frames0, rows, width), F32),
             ((groups, rows, GROUP * width), BF16),
@@ -543,32 +617,28 @@
         ],
         flops=1 << 32,
     )[0]
-    small = small + swap(small, "grp", 1)
-    for bit in range(1, grp_bits - 1):
-        small = small + swap(small, "grp", 1 << bit)
     size = quarter // 2
+    lines = small.shape[0]
+    near_smalls = [swap(small, "dev", 1), swap(small, "dev", 2)]
+    own, small_again = call(
+        part_kernel, [((quarter, wide), F32), (small.shape, F32)], [own, gots[0], gots[1], small]
+    )
     keep, send, small = call(
         functools.partial(gather_kernel, dev_bits - 1),
-        [((size, wide), F32), ((size, wide), BF16), (small.shape, F32)],
-        [own, *gots, small, swap(small, "grp", groups_of // 2)],
-    )
-    got = swap(send, "dev", members // 2)
-    smalls = [small] + [swap(small, "dev", offset) for offset in (1, 2, 3)]
-    for bit in range(dev_bits - 1, 2, -1):
-        size //= 2
-        send, keep = call(
-            functools.partial(fold_kernel, bit - 1), [((size, wide), BF16), ((size, wide), F32)], [keep, got]
-        )
-        got = swap(send, "dev", 1 << (bit - 1))
-    send, small = call(round_kernel, [((size, wide), BF16), (small.shape, F32)], [keep, got, *smalls])
-    for bit in range(3, dev_bits):
-        small = small + swap(small, "dev", 1 << bit)
-    small_got = swap(small, "dev", 4)
-    for bit in range(1, grp_bits - 1):
+        [((size, wide), F32), ((size + lines, wide), BF16), (small.shape, F32)],
+        [own, gots[2], small, *near_smalls, swap(small_again, "dev", 3)],
+    )
+    for bit in range(dev_bits - 1, 1, -1):
+        got = swap(send, "dev", 1 << bit)
+        outs = [(small.shape, F32), ((size + lines, wide), BF16)]
+        if bit > 2:
+            size //= 2
+            outs = [(small.shape, F32), ((size + lines, wide), BF16), ((size, wide), F32)]
+        small, send, *rest = call(functools.partial(fold_kernel, bit - 1), outs, [keep, got, small])
+        keep = rest[0] if rest else None
+    for bit in range(1, grp_bits):
         got = swap(send, "grp", 1 << bit)
-        send = call(across_kernel, [((size, wide), BF16)], [send, got])[0]
-    got = swap(send, "grp", groups_of // 2)
-    send, small = call(across_kernel, [((size, wide), F32), (small.shape, F32)], [send, got, small, small_got])
+        send = call(across_kernel, [((size + lines, wide), F32 if bit == grp_bits - 1 else BF16)], [send, got])[0]
     other = swap(send, "grp", 1)
     grad_second, grad_first, grad_gain, grad_bias = call(
         functools.partial(join_kernel, members, taps),
@@ -578,7 +648,7 @@
             ((1, size), F32, "out"),
             ((1, size), F32, "out"),
         ],
-        [send, other, small],
+        [send, other],
     )
     return (
         feat.transpose(1, 0, 2),

time: 65.1 us -> 61.2 us (0.940)
  starting transfers between devices: 20.8 us -> 17.9 us
  Pallas kernels: 24.7 us -> 22.3 us
  waiting for transfers between devices: 18.7 us -> 20.1 us
    ppermute x17 -> x14, starting transfers between devices: 20.8 us -> 17.9 us  [swap(): return lax.ppermute(value, axis, [(i, i ^ offset) for i in range(size)])]
    pallas_call x11 -> x12, Pallas kernels: 24.7 us -> 22.3 us  [call(): pl.pallas_call(kernel, out_shape=[jax.ShapeDtypeStruct(out[0], out[1]) if...]
    ppermute x17 -> x14, waiting for transfers between devices: 18.7 us -> 20.1 us  [swap(): return lax.ppermute(value, axis, [(i, i ^ offset) for i in range(size)])]
  transfers between devices with their start and end apart: 17 -> 14, of which waited for: 11 -> 10; matrix products, arithmetic and copies ran while one was open for 0% -> 0% of each run, Pallas kernels for 10% -> 11%
where the time goes in v4:
time: 61.2 us; the launch traced here: 61 us
  Pallas kernels  22.3 us (36%)
  waiting for transfers between devices  20.1 us (33%)
  starting transfers between devices  17.9 us (29%)
  between operations  0.73 us (1%)
    pallas_call x12, Pallas kernels, call(): pl.pallas_call(kernel, out_shape=[jax.ShapeDtypeStruct(out[0], out[1]) if...  22.3 us
    ppermute x14, waiting for transfers between devices, swap(): return lax.ppermute(value, axis, [(i, i ^ offset) for i in range(size)])  20.1 us
    ppermute x14, starting transfers between devices, swap(): return lax.ppermute(value, axis, [(i, i ^ offset) for i in range(size)])  17.9 us
  transfers between devices with their start and end apart: 14, of which 10 were waited for; matrix products, arithmetic and copies ran while one was open for 0% of the time, Pallas kernels for 11%

profile of v4, /device:TPU:0, one launch (start us, length us, event | category | flops | bytes accessed | tf_op | source)
XLA Modules:
  0.0 61.0 jit_solution(18283525545611433149)
XLA Ops:
  0.6 3.0 %collective-permute-start = (bf16[32,384]{1,0:T(8,128)(2,1)}, bf16[32,384]{1,0:T(8,128)(2,1)S(1)}, u32[]{:S(2)}, u32[]{:S(2)}) collective-permute-start(bf16[32,384]{1,0:T(8,128)(2,1)} %wave_hbm.1), channel_id=1, source_target_pairs={{0,1},{1,0},{2,3},{3,2},{4,5},{5,4},{6,7},{7,6},{8,9},{9,8},{10,11... | collective-permute-start | bytes 73736 | tf_op jit(solution)/shard_map/ppermute | solution.py:506
  3.6 1.5 %collective-permute-start.2 = (bf16[32,384]{1,0:T(8,128)(2,1)}, bf16[32,384]{1,0:T(8,128)(2,1)S(1)}, u32[]{:S(2)}, u32[]{:S(2)}) collective-permute-start(bf16[32,384]{1,0:T(8,128)(2,1)} %wave_hbm.1), channel_id=1, source_target_pairs={{0,3},{1,2},{2,1},{3,0},{4,7},{5,6},{6,5},{7,4},{8,11},{9,10},{10,... | collective-permute-start | bytes 73736 | tf_op jit(solution)/shard_map/ppermute | solution.py:506
  5.2 0.0 collective-permute-start.1
  5.2 1.3 %shard_map.119 = (s32[32,128]{1,0:T(8,128)S(1)}, bf16[128,4096]{1,0:T(8,128)(2,1)S(1)}, bf16[32,256]{1,0:T(8,128)(2,1)S(1)}, bf16[32,256]{1,0:T(8,128)(2,1)S(1)}, bf16[32,384]{1,0:T(8,128)(2,1)S(1)}) custom-call(s32[8,32]{1,0:T(8,128)} %order_hbm.1, s32[1,256]{1,0:T(1,128)} %bitcast.11, bf16[10,512]{1,0:T(8,128)(2,1)} %w_hbm.2, bf16[32,384]{1,0:T(8,128)(2,1)} %wave_hbm.1), custom_call_target="tpu_custom_call" | custom-call | tf_op jit(solution)/shard_map/pallas_call | solution.py:491
  6.5 0.0 collective-permute-done.refs_1_
  6.5 2.2 %collective-permute-done.2.refs_3_ = bf16[32,384]{1,0:T(8,128)(2,1)S(1)} collective-permute-done((bf16[32,384]{1,0:T(8,128)(2,1)}, bf16[32,384]{1,0:T(8,128)(2,1)S(1)}, u32[]{:S(2)}, u32[]{:S(2)}) %collective-permute-start.2) | collective-permute-done | bytes 24608 | tf_op jit(solution)/shard_map/ppermute | solution.py:506
  8.7 0.5 collective-permute-done.1.refs_2_
  9.2 0.2 shard_map.120
  9.4 2.7 %collective-permute-start.3 = (bf16[32,384]{1,0:T(8,128)(2,1)S(1)}, bf16[32,384]{1,0:T(8,128)(2,1)S(1)}, u32[]{:S(2)}, u32[]{:S(2)}) collective-permute-start(bf16[32,384]{1,0:T(8,128)(2,1)S(1)} %get-tuple-element.46), channel_id=1, source_target_pairs={{0,4},{1,5},{2,6},{3,7},{4,0},{5,1},{6,2},{7,3},{8,12},{9,13},{10,... | collective-permute-start | bytes 73736 | tf_op jit(solution)/shard_map/ppermute | solution.py:506
  12.1 2.1 %collective-permute-done.3.far_ref = bf16[32,384]{1,0:T(8,128)(2,1)S(1)} collective-permute-done((bf16[32,384]{1,0:T(8,128)(2,1)S(1)}, bf16[32,384]{1,0:T(8,128)(2,1)S(1)}, u32[]{:S(2)}, u32[]{:S(2)}) %collective-permute-start.3) | collective-permute-done | bytes 24608 | tf_op jit(solution)/shard_map/ppermute | solution.py:506
  14.2 11.5 %shard_map.121 = (bf16[37,32,512]{2,1,0:T(8,128)(2,1)}, bf16[41,32,512]{2,1,0:T(8,128)(2,1)S(1)}, bf16[40,32,512]{2,1,0:T(8,128)(2,1)S(1)}, f32[10,32,4096]{2,1,...) custom-call(bf16[32,384]{1,0:T(8,128)(2,1)S(1)} %get-tuple-element.4, ...), custom_call_target="tpu_custom_call" | custom-call | tf_op jit(solution)/shard_map/pallas_call | solution.py:491
  25.7 2.2 %shard_map.122 = (f32[512,768]{1,0:T(8,128)S(1)}, bf16[512,768]{1,0:T(8,128)(2,1)S(1)}) custom-call(bf16[41,32,512]{2,1,0:T(8,128)(2,1)S(1)} %get-tuple-element.50.even_ref, bf16[40,32,512]{2,1,0:T(8,128)(2,1)S(1)} %get-tuple-element.51.odd_ref, bf16[512,1280]{1,0:T(8,128)(2,1)S(1)} %get-tuple-element.52.grad_t_ref), custom_call_target="tpu_custom_call" | custom-call | flops 1073741824 | tf_op jit(solution)/shard_map/pallas_call | solution.py:491
  27.9 0.1 collective-permute-start.4
  28.0 2.1 %shard_map.123 = (f32[38,32,512]{2,1,0:T(8,128)S(1)}, f32[37,32,512]{2,1,0:T(8,128)S(1)}) custom-call(bf16[39,32,512]{2,1,0:T(8,128)(2,1)S(1)} %get-tuple-element.55.grad_ref, bf16[3,512,512]{2,1,0:T(8,128)(2,1)S(1)} %get-tuple-element.56.w_ref), custom_call_target="tpu_custom_call" | custom-call | flops 1073741824 | tf_op jit(solution)/shard_map/pallas_call | solution.py:491
  30.1 0.2 collective-permute-done.4.got_ref
  30.3 0.1 shard_map.124
  30.4 1.7 %collective-permute-start.5 = (bf16[128,768]{1,0:T(8,128)(2,1)S(1)}, bf16[128,768]{1,0:T(8,128)(2,1)S(1)}, u32[]{:S(2)}, u32[]{:S(2)}) collective-permute-start(bf16[128,768]{1,0:T(8,128)(2,1)S(1)} %get-tuple-element.59), channel_id=1, source_target_pairs={{0,1},{1,0},{2,3},{3,2},{4,5},{5,4},{6,7},{7,6},{8,9},{9,8},{10,11... | collective-permute-start | bytes 589832 | tf_op jit(solution)/shard_map/ppermute | solution.py:506
  32.2 0.3 collective-permute-start.6
  32.5 1.5 %collective-permute-start.7 = (bf16[128,768]{1,0:T(8,128)(2,1)S(1)}, bf16[128,768]{1,0:T(8,128)(2,1)S(1)}, u32[]{:S(2)}, u32[]{:S(2)}) collective-permute-start(bf16[128,768]{1,0:T(8,128)(2,1)S(1)} %get-tuple-element.69), channel_id=1, source_target_pairs={{0,3},{1,2},{2,1},{3,0},{4,7},{5,6},{6,5},{7,4},{8,11},{9,10},{10,... | collective-permute-start | bytes 589832 | tf_op jit(solution)/shard_map/ppermute | solution.py:506
  34.0 3.2 %shard_map.125.small_ref.small0 = f32[16,512]{1,0:T(8,128)S(1)} custom-call(s32[32,128]{1,0:T(8,128)S(1)} %get-tuple-element.47.valid_ref, f32[10,32,4096]{2,1,0:T(8,128)S(1)} %get-tuple-element.61.pre0, f32[80,32,512]{2,1,0:T(8,128)S(1)} %get-tuple-element.62.slope_ref, f32[32,512]{1,0:T(8,128)S(1)} %get-tuple-element.63.mean_ref, ...), custom_call_target="tpu_custom_call" | custom-call | flops 4294967296 | tf_op jit(solution)/shard_map/pallas_call | solution.py:491
  37.3 1.0 %collective-permute-start.9 = (f32[16,512]{1,0:T(8,128)S(1)}, f32[16,512]{1,0:T(8,128)S(1)}, u32[]{:S(2)}, u32[]{:S(2)}) collective-permute-start(f32[16,512]{1,0:T(8,128)S(1)} %shard_map.125.small_ref.small0), channel_id=1, source_target_pairs={{0,2},{1,3},{2,0},{3,1},{4,6},{5,7},{6,4},{7,5},{8,10},{9,11},{10,... | collective-permute-start | bytes 98312 | tf_op jit(solution)/shard_map/ppermute | solution.py:506
  38.3 1.0 %collective-permute-start.8 = (f32[16,512]{1,0:T(8,128)S(1)}, f32[16,512]{1,0:T(8,128)S(1)}, u32[]{:S(2)}, u32[]{:S(2)}) collective-permute-start(f32[16,512]{1,0:T(8,128)S(1)} %shard_map.125.small_ref.small0), channel_id=1, source_target_pairs={{0,1},{1,0},{2,3},{3,2},{4,5},{5,4},{6,7},{7,6},{8,9},{9,8},{10,11... | collective-permute-start | bytes 98312 | tf_op jit(solution)/shard_map/ppermute | solution.py:506
  39.3 0.0 collective-permute-done.5.got1
  39.3 0.6 %collective-permute-done.6.got2 = bf16[128,768]{1,0:T(8,128)(2,1)S(1)} collective-permute-done((bf16[128,768]{1,0:T(8,128)(2,1)S(1)}, bf16[128,768]{1,0:T(8,128)(2,1)S(1)}, u32[]{:S(2)}, u32[]{:S(2)}) %collective-permute-start.6) | collective-permute-done | bytes 196640 | tf_op jit(solution)/shard_map/ppermute | solution.py:506
  39.9 0.1 shard_map.126
  40.0 1.0 %collective-permute-start.10 = (f32[16,512]{1,0:T(8,128)S(1)}, f32[16,512]{1,0:T(8,128)S(1)}, u32[]{:S(2)}, u32[]{:S(2)}) collective-permute-start(f32[16,512]{1,0:T(8,128)S(1)} %get-tuple-element.70), channel_id=1, source_target_pairs={{0,3},{1,2},{2,1},{3,0},{4,7},{5,6},{6,5},{7,4},{8,11},{9,10},{10,... | collective-permute-start | bytes 98312 | tf_op jit(solution)/shard_map/ppermute | solution.py:506
  40.9 3.4 %collective-permute-done.9.small2 = f32[16,512]{1,0:T(8,128)S(1)} collective-permute-done((f32[16,512]{1,0:T(8,128)S(1)}, f32[16,512]{1,0:T(8,128)S(1)}, u32[]{:S(2)}, u32[]{:S(2)}) %collective-permute-start.9) | collective-permute-done | bytes 32800 | tf_op jit(solution)/shard_map/ppermute | solution.py:506
  44.4 0.0 collective-permute-done.8.small1
  44.4 0.0 collective-permute-done.7.got3
  44.4 0.5 collective-permute-done.10.small3
  44.9 0.1 shard_map.127
  44.9 2.5 %collective-permute-start.11 = (bf16[80,768]{1,0:T(8,128)(2,1)S(1)}, bf16[80,768]{1,0:T(8,128)(2,1)S(1)}, u32[]{:S(2)}, u32[]{:S(2)}) collective-permute-start(bf16[80,768]{1,0:T(8,128)(2,1)S(1)} %get-tuple-element.72), channel_id=1, source_target_pairs={{0,4},{1,5},{2,6},{3,7},{4,0},{5,1},{6,2},{7,3},{8,12},{9,13},{10,... | collective-permute-start | bytes 368648 | tf_op jit(solution)/shard_map/ppermute | solution.py:506
  47.4 5.6 %collective-permute-done.11.got_ref = bf16[80,768]{1,0:T(8,128)(2,1)S(1)} collective-permute-done((bf16[80,768]{1,0:T(8,128)(2,1)S(1)}, bf16[80,768]{1,0:T(8,128)(2,1)S(1)}, u32[]{:S(2)}, u32[]{:S(2)}) %collective-permute-start.11) | collective-permute-done | bytes 122912 | tf_op jit(solution)/shard_map/ppermute | solution.py:506
  53.0 0.6 %shard_map.128 = (f32[16,512]{1,0:T(8,128)}, bf16[80,768]{1,0:T(8,128)(2,1)S(1)}) custom-call(f32[64,768]{1,0:T(8,128)S(1)} %get-tuple-element.71.keep_ref, bf16[80,768]{1,0:T(8,128)(2,1)S(1)} %collective-permute-done.11.got_ref, f32[16,512]{1,0:T(8,128)S(1)} %get-tuple-element.73.small_ref), custom_call_target="tpu_custom_call" | custom-call | tf_op jit(solution)/shard_map/pallas_call | solution.py:491
  53.7 1.5 %collective-permute-start.12 = (bf16[80,768]{1,0:T(8,128)(2,1)S(1)}, bf16[80,768]{1,0:T(8,128)(2,1)S(1)}, u32[]{:S(2)}, u32[]{:S(2)}) collective-permute-start(bf16[80,768]{1,0:T(8,128)(2,1)S(1)} %get-tuple-element.74.mine_ref), channel_id=1, source_target_pairs={{0,16},{8,24},{16,0},{24,8},{1,17},{9,25},{17,1},{25,9},{2,18},{10... | collective-permute-start | bytes 368648 | tf_op jit(solution)/shard_map/ppermute | solution.py:506
  55.2 3.4 %collective-permute-done.12.got_ref = bf16[80,768]{1,0:T(8,128)(2,1)S(1)} collective-permute-done((bf16[80,768]{1,0:T(8,128)(2,1)S(1)}, bf16[80,768]{1,0:T(8,128)(2,1)S(1)}, u32[]{:S(2)}, u32[]{:S(2)}) %collective-permute-start.12) | collective-permute-done | bytes 122912 | tf_op jit(solution)/shard_map/ppermute | solution.py:506
  58.6 0.1 collective-permute-start.13
  58.7 1.5 %collective-permute-done.13.other_ref = f32[80,768]{1,0:T(8,128)S(1)} collective-permute-done((f32[80,768]{1,0:T(8,128)S(1)}, f32[80,768]{1,0:T(8,128)S(1)}, u32[]{:S(2)}, u32[]{:S(2)}) %collective-permute-start.13) | collective-permute-done | bytes 245792 | tf_op jit(solution)/shard_map/ppermute | solution.py:506
  60.2 0.8 %shard_map.130 = (f32[3,64,512]{2,1,0:T(8,128)}, f32[10,64]{1,0:T(8,128)}, f32[1,64]{1,0:T(1,128)}, f32[1,64]{1,0:T(1,128)}) custom-call(f32[80,768]{1,0:T(8,128)S(1)} %shard_map.129.own_ref, f32[80,768]{1,0:T(8,128)S(1)} %collective-permute-done.13.other_ref), custom_call_target="tpu_custom_call" | custom-call | tf_op jit(solution)/shard_map/pallas_call | solution.py:491
  (1 shorter events, 0.0 us)
Async XLA Ops:
  0.6 5.9 %collective-permute-start = (bf16[32,384]{1,0:T(8,128)(2,1)}, bf16[32,384]{1,0:T(8,128)(2,1)S(1)}, u32[]{:S(2)}, u32[]{:S(2)}) collective-permute-start(bf16[32,384]{1,0:T(8,128)(2,1)} %wave_hbm.1), channel_id=1, source_target_pairs={{0,1},{1,0},{2,3},{3,2},{4,5},{5,4},{6,7},{7,6},{8,9},{9,8},{10,11... | collective-permute-start | bytes 73736 | tf_op jit(solution)/shard_map/ppermute | solution.py:506
  3.6 5.1 %collective-permute-start.2 = (bf16[32,384]{1,0:T(8,128)(2,1)}, bf16[32,384]{1,0:T(8,128)(2,1)S(1)}, u32[]{:S(2)}, u32[]{:S(2)}) collective-permute-start(bf16[32,384]{1,0:T(8,128)(2,1)} %wave_hbm.1), channel_id=1, source_target_pairs={{0,3},{1,2},{2,1},{3,0},{4,7},{5,6},{6,5},{7,4},{8,11},{9,10},{10,... | collective-permute-start | bytes 73736 | tf_op jit(solution)/shard_map/ppermute | solution.py:506
  5.2 4.0 %collective-permute-start.1 = (bf16[32,384]{1,0:T(8,128)(2,1)}, bf16[32,384]{1,0:T(8,128)(2,1)S(1)}, u32[]{:S(2)}, u32[]{:S(2)}) collective-permute-start(bf16[32,384]{1,0:T(8,128)(2,1)} %wave_hbm.1), channel_id=1, source_target_pairs={{0,2},{1,3},{2,0},{3,1},{4,6},{5,7},{6,4},{7,5},{8,10},{9,11},{10,... | collective-permute-start | bytes 73736 | tf_op jit(solution)/shard_map/ppermute | solution.py:506
  9.4 4.8 %collective-permute-start.3 = (bf16[32,384]{1,0:T(8,128)(2,1)S(1)}, bf16[32,384]{1,0:T(8,128)(2,1)S(1)}, u32[]{:S(2)}, u32[]{:S(2)}) collective-permute-start(bf16[32,384]{1,0:T(8,128)(2,1)S(1)} %get-tuple-element.46), channel_id=1, source_target_pairs={{0,4},{1,5},{2,6},{3,7},{4,0},{5,1},{6,2},{7,3},{8,12},{9,13},{10,... | collective-permute-start | bytes 73736 | tf_op jit(solution)/shard_map/ppermute | solution.py:506
  27.9 2.4 %collective-permute-start.4 = (bf16[512,768]{1,0:T(8,128)(2,1)S(1)}, bf16[512,768]{1,0:T(8,128)(2,1)S(1)}, u32[]{:S(2)}, u32[]{:S(2)}) collective-permute-start(bf16[512,768]{1,0:T(8,128)(2,1)S(1)} %get-tuple-element.54), channel_id=1, source_target_pairs={{0,8},{8,0},{16,24},{24,16},{1,9},{9,1},{17,25},{25,17},{2,10},{10... | collective-permute-start | bytes 2359304 | tf_op jit(solution)/shard_map/ppermute | solution.py:506
  30.4 8.8 %collective-permute-start.5 = (bf16[128,768]{1,0:T(8,128)(2,1)S(1)}, bf16[128,768]{1,0:T(8,128)(2,1)S(1)}, u32[]{:S(2)}, u32[]{:S(2)}) collective-permute-start(bf16[128,768]{1,0:T(8,128)(2,1)S(1)} %get-tuple-element.59), channel_id=1, source_target_pairs={{0,1},{1,0},{2,3},{3,2},{4,5},{5,4},{6,7},{7,6},{8,9},{9,8},{10,11... | collective-permute-start | bytes 589832 | tf_op jit(solution)/shard_map/ppermute | solution.py:506
  32.2 7.8 %collective-permute-start.6 = (bf16[128,768]{1,0:T(8,128)(2,1)S(1)}, bf16[128,768]{1,0:T(8,128)(2,1)S(1)}, u32[]{:S(2)}, u32[]{:S(2)}) collective-permute-start(bf16[128,768]{1,0:T(8,128)(2,1)S(1)} %get-tuple-element.60), channel_id=1, source_target_pairs={{0,2},{1,3},{2,0},{3,1},{4,6},{5,7},{6,4},{7,5},{8,10},{9,11},{10,... | collective-permute-start | bytes 589832 | tf_op jit(solution)/shard_map/ppermute | solution.py:506
  32.5 11.9 %collective-permute-start.7 = (bf16[128,768]{1,0:T(8,128)(2,1)S(1)}, bf16[128,768]{1,0:T(8,128)(2,1)S(1)}, u32[]{:S(2)}, u32[]{:S(2)}) collective-permute-start(bf16[128,768]{1,0:T(8,128)(2,1)S(1)} %get-tuple-element.69), channel_id=1, source_target_pairs={{0,3},{1,2},{2,1},{3,0},{4,7},{5,6},{6,5},{7,4},{8,11},{9,10},{10,... | collective-permute-start | bytes 589832 | tf_op jit(solution)/shard_map/ppermute | solution.py:506
  37.3 7.1 %collective-permute-start.9 = (f32[16,512]{1,0:T(8,128)S(1)}, f32[16,512]{1,0:T(8,128)S(1)}, u32[]{:S(2)}, u32[]{:S(2)}) collective-permute-start(f32[16,512]{1,0:T(8,128)S(1)} %shard_map.125.small_ref.small0), channel_id=1, source_target_pairs={{0,2},{1,3},{2,0},{3,1},{4,6},{5,7},{6,4},{7,5},{8,10},{9,11},{10,... | collective-permute-start | bytes 98312 | tf_op jit(solution)/shard_map/ppermute | solution.py:506
  38.3 6.1 %collective-permute-start.8 = (f32[16,512]{1,0:T(8,128)S(1)}, f32[16,512]{1,0:T(8,128)S(1)}, u32[]{:S(2)}, u32[]{:S(2)}) collective-permute-start(f32[16,512]{1,0:T(8,128)S(1)} %shard_map.125.small_ref.small0), channel_id=1, source_target_pairs={{0,1},{1,0},{2,3},{3,2},{4,5},{5,4},{6,7},{7,6},{8,9},{9,8},{10,11... | collective-permute-start | bytes 98312 | tf_op jit(solution)/shard_map/ppermute | solution.py:506
  40.0 4.9 %collective-permute-start.10 = (f32[16,512]{1,0:T(8,128)S(1)}, f32[16,512]{1,0:T(8,128)S(1)}, u32[]{:S(2)}, u32[]{:S(2)}) collective-permute-start(f32[16,512]{1,0:T(8,128)S(1)} %get-tuple-element.70), channel_id=1, source_target_pairs={{0,3},{1,2},{2,1},{3,0},{4,7},{5,6},{6,5},{7,4},{8,11},{9,10},{10,... | collective-permute-start | bytes 98312 | tf_op jit(solution)/shard_map/ppermute | solution.py:506
  44.9 8.1 %collective-permute-start.11 = (bf16[80,768]{1,0:T(8,128)(2,1)S(1)}, bf16[80,768]{1,0:T(8,128)(2,1)S(1)}, u32[]{:S(2)}, u32[]{:S(2)}) collective-permute-start(bf16[80,768]{1,0:T(8,128)(2,1)S(1)} %get-tuple-element.72), channel_id=1, source_target_pairs={{0,4},{1,5},{2,6},{3,7},{4,0},{5,1},{6,2},{7,3},{8,12},{9,13},{10,... | collective-permute-start | bytes 368648 | tf_op jit(solution)/shard_map/ppermute | solution.py:506
  53.7 4.9 %collective-permute-start.12 = (bf16[80,768]{1,0:T(8,128)(2,1)S(1)}, bf16[80,768]{1,0:T(8,128)(2,1)S(1)}, u32[]{:S(2)}, u32[]{:S(2)}) collective-permute-start(bf16[80,768]{1,0:T(8,128)(2,1)S(1)} %get-tuple-element.74.mine_ref), channel_id=1, source_target_pairs={{0,16},{8,24},{16,0},{24,8},{1,17},{9,25},{17,1},{25,9},{2,18},{10... | collective-permute-start | bytes 368648 | tf_op jit(solution)/shard_map/ppermute | solution.py:506
  58.6 1.6 %collective-permute-start.13 = (f32[80,768]{1,0:T(8,128)S(1)}, f32[80,768]{1,0:T(8,128)S(1)}, u32[]{:S(2)}, u32[]{:S(2)}) collective-permute-start(f32[80,768]{1,0:T(8,128)S(1)} %shard_map.129.own_ref), channel_id=1, source_target_pairs={{0,8},{8,0},{16,24},{24,16},{1,9},{9,1},{17,25},{25,17},{2,10},{10... | collective-permute-start | bytes 737288 | tf_op jit(solution)/shard_map/ppermute | solution.py:506

commit v5 on v4

--- a/solution.py
+++ b/solution.py
@@ -17,13 +17,7 @@
 
 def gelu_and_slope(value):
     bell = jnp.exp2(value * value * (-0.5 * 1.4426950408889634))
-    base = 1.0 + jnp.abs(value) * (0.3275911 * 0.7071067811865476)
-    frac = pltpu.reciprocal(base, approx=True)
-    poly = 0.5 * 1.061405429
-    for coef in (-1.453152027, 1.421413741, -0.284496736, 0.254829592):
-        poly = poly * frac + 0.5 * coef
-    tail = poly * frac * bell
-    phi = jnp.where(value < 0.0, tail, 1.0 - tail)
+    phi = 0.5 + 0.5 * lax.erf(value * 0.7071067811865476)
     return value * phi, phi + value * bell * 0.3989422804014327
 
 
@@ -294,17 +288,18 @@
     pltpu.make_async_copy(feat_ref, feat_out, out_sem).wait()
 
 
-def outer_kernel(even_ref, odd_ref, grad_t_ref, keep_ref, send_ref):
-    frames = grad_t_ref.shape[1] // even_ref.shape[1]
-    rows, chans = even_ref.shape[1:]
+def outer_kernel(skips, *refs):
+    acts, (grad_t_ref, keep_ref, send_ref) = refs[:-3], refs[-3:]
+    frames = grad_t_ref.shape[1] // acts[0].shape[1]
+    rows, chans = acts[0].shape[1:]
     half = chans // 2
     core = lax.rem(lax.axis_index("grp"), 2)
     turned = grad_t_ref[...]
-    for tap, (ref, skip) in enumerate(((even_ref, 0), (odd_ref, 0), (even_ref, 1))):
-        for side, out_ref in ((core, keep_ref), (1 - core, send_ref)):
+    for tap, (ref, skip) in enumerate(zip(acts, skips)):
+        for side, out_ref in ((1 - core, send_ref), (core, keep_ref)):
             lanes = pl.ds(pl.multiple_of(side * half, half), half)
-            acts = ref[skip : skip + frames, :, lanes].reshape(frames * rows, half)
-            out_ref[:, tap * half : (tap + 1) * half] = dot(turned, acts).astype(out_ref.dtype)
+            value = dot(turned, ref[skip : skip + frames, :, lanes].reshape(frames * rows, half))
+            out_ref[:, tap * half : (tap + 1) * half] = value.astype(out_ref.dtype)
 
 
 def input_kernel(grad_ref, w_ref, even_ref, odd_ref):
@@ -329,10 +324,15 @@
     even_ref,
     odd_ref,
     gain_ref,
-    out_ref,
+    mine_ref,
+    send1,
+    send2,
+    send3,
     lift,
     dpre0,
     spread,
+    out_ref,
+    quarters,
 ):
     groups, rows, depth = patch_ref.shape
     chans = gain_ref.shape[1]
@@ -395,19 +395,23 @@
         for f in range(GROUP):
             total += spread[stride * f : stride * f + taps, f * width : (f + 1) * width]
         out_ref[:taps, lanes] = total
-
-
-def plane_kernel(keep_ref, got_ref, later_ref, own_ref, *send_refs):
+    size = chans // lax.axis_size("dev")
+    for place in range(4):
+        columns = [slice(first, first + size) for first in range(place * size, chans, 4 * size)]
+        quarters[place] = jnp.concatenate([out_ref[:, part] for part in columns], axis=1)
+    place = lax.rem(lax.axis_index("dev"), 4)
+    for offset, ref in enumerate((mine_ref, send1, send2, send3)):
+        ref[...] = quarters[jnp.bitwise_xor(place, offset)]
+
+
+def plane_kernel(keep0, got0, keep1, got1, later_ref, own_ref, *send_refs):
     size = own_ref.shape[0]
+    edge = keep0.shape[1]
     place = lax.rem(lax.axis_index("dev"), 4)
-
-    def quarter(index):
-        lines = pl.ds(pl.multiple_of(index * size, size), size)
-        return keep_ref[lines, :] + got_ref[lines, :].astype(F32)
-
-    own_ref[...] = quarter(place)
-    for offset, send_ref in enumerate(send_refs, 1):
-        send_ref[...] = quarter(jnp.bitwise_xor(place, offset)).astype(BF16)
+    for offset, out_ref in enumerate((own_ref, *send_refs)):
+        lines = pl.ds(pl.multiple_of(jnp.bitwise_xor(place, offset) * size, size), size)
+        out_ref[:, :edge] = (keep0[lines, :] + got0[lines, :].astype(F32)).astype(out_ref.dtype)
+        out_ref[:, edge:] = (keep1[lines, :] + got1[lines, :].astype(F32)).astype(out_ref.dtype)
 
 
 def part_kernel(own_ref, got1, got2, small_ref, sum_ref, total_ref):
@@ -415,71 +419,67 @@
     total_ref[...] = small_ref[...]
 
 
-def write_small(send_ref, first, total):
-    lines, chans = total.shape
-    send_ref[first:, :chans] = total.astype(send_ref.dtype)
-    send_ref[first:, chans:] = jnp.zeros((lines, send_ref.shape[1] - chans), send_ref.dtype)
-
-
-def read_small(got_ref, first, chans):
-    return got_ref[first:, :chans].astype(F32)
-
-
-def gather_kernel(bit, own_ref, got3, small0, small1, small2, small3, next_ref, send_ref, total_ref):
-    half = next_ref.shape[0]
+def packed(size, wide):
+    return size + 16, wide - 128
+
+
+def write_packed(ref, value, small):
+    size, lanes = ref.shape[0] - 16, ref.shape[1]
+    ref[:size] = value[:, :lanes].astype(ref.dtype)
+    used = size // 16
+    for block in range(used):
+        piece = value[block * 16 : (block + 1) * 16, lanes:]
+        ref[size:, block * 128 : (block + 1) * 128] = piece.astype(ref.dtype)
+    for first in range(used * 128, lanes - 128, 128):
+        ref[size:, first : first + 128] = jnp.zeros((16, 128), ref.dtype)
+    ref[size:, lanes - 128 :] = small.astype(ref.dtype)
+
+
+def read_packed(ref, first, count):
+    size = ref.shape[0] - 16
+    whole = ref[pl.ds(pl.multiple_of(first, 16), count), :].astype(F32)
+    pieces = [
+        ref[size:, pl.ds(pl.multiple_of(first * 8 + block * 128, 128), 128)].astype(F32) for block in range(count // 16)
+    ]
+    return jnp.concatenate([whole, jnp.concatenate(pieces, axis=0)], axis=1)
+
+
+def gather_kernel(bit, own_ref, got3, small0, small1, small2, small3, keep_ref, send_ref):
+    half = own_ref.shape[0] // 2
     side = lax.rem(lax.shift_right_logical(lax.axis_index("dev"), bit), 2)
-
-    def part(index):
+    total = (small0[...] + small1[...]) + (small2[...] + small3[...])
+    for index, ref in ((1 - side, send_ref), (side, keep_ref)):
         lines = pl.ds(pl.multiple_of(index * half, half), half)
-        return own_ref[lines, :] + got3[lines, :].astype(F32)
-
-    next_ref[...] = part(side)
-    send_ref[:half] = part(1 - side).astype(BF16)
-    total = (small0[...] + small1[...]) + (small2[...] + small3[...])
-    total_ref[...] = total
-    write_small(send_ref, half, total)
-
-
-def fold_kernel(bit, keep_ref, got_ref, small_ref, total_ref, send_ref, *rest):
-    half = keep_ref.shape[0]
-    total = small_ref[...] + read_small(got_ref, half, small_ref.shape[1])
-    total_ref[...] = total
-    if not rest:
-        send_ref[:half] = (keep_ref[...] + got_ref[:half].astype(F32)).astype(BF16)
-        write_small(send_ref, half, total)
-        return
-    next_ref = rest[0]
-    size = next_ref.shape[0]
+        write_packed(ref, own_ref[lines, :] + got3[lines, :].astype(F32), total)
+
+
+def halve_kernel(bit, keep_ref, got_ref, next_ref, send_ref):
+    half = (keep_ref.shape[0] - 16) // 2
     side = lax.rem(lax.shift_right_logical(lax.axis_index("dev"), bit), 2)
-
-    def part(index):
-        here = pl.ds(pl.multiple_of(index * size, size), size)
-        return keep_ref[here, :] + got_ref[here, :].astype(F32)
-
-    next_ref[...] = part(side)
-    send_ref[:size] = part(1 - side).astype(BF16)
-    write_small(send_ref, size, total)
-
-
-def across_kernel(mine_ref, got_ref, out_ref):
+    small = keep_ref[2 * half :, -128:] + got_ref[2 * half :, -128:].astype(F32)
+    for index, ref in ((1 - side, send_ref), (side, next_ref)):
+        first = index * half
+        write_packed(ref, read_packed(keep_ref, first, half) + read_packed(got_ref, first, half), small)
+
+
+def add_kernel(mine_ref, got_ref, out_ref):
     out_ref[...] = (mine_ref[...].astype(F32) + got_ref[...].astype(F32)).astype(out_ref.dtype)
 
 
-def join_kernel(members, taps, own_ref, other_ref, out_ref, first_ref, gain_ref, bias_ref):
+def join_kernel(taps, own_ref, other_ref, out_ref, first_ref, gain_ref, bias_ref):
     second, size, chans = out_ref.shape
     half = chans // 2
     core = lax.rem(lax.axis_index("grp"), 2)
-    for tap in range(second):
-        lanes = slice(tap * half, (tap + 1) * half)
-        out_ref[tap, :, pl.ds(pl.multiple_of(core * half, half), half)] = own_ref[:size, lanes]
-        out_ref[tap, :, pl.ds(pl.multiple_of((1 - core) * half, half), half)] = other_ref[:size, lanes]
-    wide = max(size, 128)
-    member = lax.axis_index("dev")
-    block = pl.ds(pl.multiple_of(member // (wide // size) * wide, wide), wide)
-    total = own_ref[size:, block] + other_ref[size:, block]
+    for ref, side in ((own_ref, core), (other_ref, 1 - core)):
+        value = read_packed(ref, 0, size)
+        for tap in range(second):
+            lanes = pl.ds(pl.multiple_of(side * half, half), half)
+            out_ref[tap, :, lanes] = value[:, tap * half : (tap + 1) * half]
+    total = own_ref[size:, -128:] + other_ref[size:, -128:]
     value = total[:, :size]
-    for place in range(1, wide // size):
-        value = jnp.where(lax.rem(member, wide // size) == place, total[:, place * size : (place + 1) * size], value)
+    for place in range(1, 128 // size):
+        mine = lax.axis_index("dev") // 4 == place
+        value = jnp.where(mine, total[:, place * size : (place + 1) * size], value)
     first_ref[...] = value[:taps]
     gain_ref[...] = value[taps : taps + 1]
     bias_ref[...] = value[taps + 1 : taps + 2]
@@ -591,9 +591,22 @@
         ],
         outside=(4, 5, 6, 7),
     )
-    wide = taps_second * chans // 2
-    keep, send = call(outer_kernel, [((chans, wide), F32), ((chans, wide), BF16)], [even, odd, grad_t], flops=1 << 30)
-    got = swap(send, "grp", 1)
+    half = chans // 2
+    wide = taps_second * half
+    keep0, send0 = call(
+        functools.partial(outer_kernel, (0, 0)),
+        [((chans, 2 * half), F32), ((chans, 2 * half), BF16)],
+        [even, odd, grad_t],
+        flops=1 << 30,
+    )
+    got0 = swap(send0, "grp", 1)
+    keep1, send1 = call(
+        functools.partial(outer_kernel, (1,)),
+        [((chans, half), F32), ((chans, half), BF16)],
+        [even, grad_t],
+        flops=1 << 29,
+    )
+    got1 = swap(send1, "grp", 1)
     evens, odds = (frames0 + 1) // 2, frames0 // 2
     dact_even, dact_odd = call(
         input_kernel,
@@ -603,52 +616,55 @@
     )
     quarter = chans // 4
     own, *sends = call(
-        plane_kernel, [((quarter, wide), F32)] + [((quarter, wide), BF16)] * 3, [keep, got, dact_odd]
+        plane_kernel,
+        [((quarter, wide), F32)] + [((quarter, wide), BF16)] * 3,
+        [keep0, got0, keep1, got1, dact_odd],
     )
     gots = [swap(part, "dev", offset) for offset, part in enumerate(sends, 1)]
-    small = call(
+    small, *smalls = call(
         functools.partial(backward_kernel, frames0, taps),
-        [((16, chans), F32)],
+        [((16, quarter), F32)] * 4,
         [valid, pre0, slope, mean, inv, patch, dact_even, dact_odd, gain_in],
         scratch=[
             ((frames0, rows, width), F32),
             ((groups, rows, GROUP * width), BF16),
             ((depth, GROUP * width), F32),
+            ((16, chans), F32),
+            ((4, 16, quarter), F32),
         ],
         flops=1 << 32,
-    )[0]
+    )
+    small1, small2 = swap(smalls[0], "dev", 1), swap(smalls[1], "dev", 2)
+    own, third = call(
+        part_kernel, [((quarter, wide), F32), (small.shape, F32)], [own, gots[0], gots[1], smalls[2]]
+    )
+    small3 = swap(third, "dev", 3)
     size = quarter // 2
-    lines = small.shape[0]
-    near_smalls = [swap(small, "dev", 1), swap(small, "dev", 2)]
-    own, small_again = call(
-        part_kernel, [((quarter, wide), F32), (small.shape, F32)], [own, gots[0], gots[1], small]
-    )
-    keep, send, small = call(
+    keep, send = call(
         functools.partial(gather_kernel, dev_bits - 1),
-        [((size, wide), F32), ((size + lines, wide), BF16), (small.shape, F32)],
-        [own, gots[2], small, *near_smalls, swap(small_again, "dev", 3)],
-    )
-    for bit in range(dev_bits - 1, 1, -1):
-        got = swap(send, "dev", 1 << bit)
-        outs = [(small.shape, F32), ((size + lines, wide), BF16)]
-        if bit > 2:
-            size //= 2
-            outs = [(small.shape, F32), ((size + lines, wide), BF16), ((size, wide), F32)]
-        small, send, *rest = call(functools.partial(fold_kernel, bit - 1), outs, [keep, got, small])
-        keep = rest[0] if rest else None
+        [(packed(size, wide), F32), (packed(size, wide), BF16)],
+        [own, gots[2], small, small1, small2, small3],
+    )
+    for bit in range(dev_bits - 1, 2, -1):
+        size //= 2
+        keep, send = call(
+            functools.partial(halve_kernel, bit - 1),
+            [(packed(size, wide), F32), (packed(size, wide), BF16)],
+            [keep, swap(send, "dev", 1 << bit)],
+        )
+    send = call(add_kernel, [(packed(size, wide), BF16)], [keep, swap(send, "dev", 4)])[0]
     for bit in range(1, grp_bits):
-        got = swap(send, "grp", 1 << bit)
-        send = call(across_kernel, [((size + lines, wide), F32 if bit == grp_bits - 1 else BF16)], [send, got])[0]
-    other = swap(send, "grp", 1)
+        kind = F32 if bit == grp_bits - 1 else BF16
+        send = call(add_kernel, [(packed(size, wide), kind)], [send, swap(send, "grp", 1 << bit)])[0]
     grad_second, grad_first, grad_gain, grad_bias = call(
-        functools.partial(join_kernel, members, taps),
+        functools.partial(join_kernel, taps),
         [
             ((taps_second, size, chans), F32, "out"),
             ((taps, size), F32, "out"),
             ((1, size), F32, "out"),
             ((1, size), F32, "out"),
         ],
-        [send, other],
+        [send, swap(send, "grp", 1)],
     )
     return (
         feat.transpose(1, 0, 2),

time: 61.2 us -> 56.2 us (0.918)
  Pallas kernels: 22.3 us -> 18.8 us
  waiting for transfers between devices: 20.1 us -> 17.9 us
  starting transfers between devices: 17.9 us -> 18.6 us
    pallas_call x12 -> x13, Pallas kernels: 22.3 us -> 18.8 us  [call(): pl.pallas_call(kernel, out_shape=[jax.ShapeDtypeStruct(out[0], out[1]) if...]
    ppermute x14 -> x15, waiting for transfers between devices: 20.1 us -> 17.9 us  [swap(): return lax.ppermute(value, axis, [(i, i ^ offset) for i in range(size)])]
    ppermute x14 -> x15, starting transfers between devices: 17.9 us -> 18.6 us  [swap(): return lax.ppermute(value, axis, [(i, i ^ offset) for i in range(size)])]
  transfers between devices with their start and end apart: 14 -> 15, of which waited for: 10 -> 10; matrix products, arithmetic and copies ran while one was open for 0% -> 0% of each run, Pallas kernels for 11% -> 14%
where the time goes in v5:
time: 56.2 us; the launch traced here: 56 us
  Pallas kernels  18.8 us (33%)
  starting transfers between devices  18.6 us (33%)
  waiting for transfers between devices  17.9 us (32%)
  between operations  0.75 us (1%)
    pallas_call x13, Pallas kernels, call(): pl.pallas_call(kernel, out_shape=[jax.ShapeDtypeStruct(out[0], out[1]) if...  18.8 us
    ppermute x15, starting transfers between devices, swap(): return lax.ppermute(value, axis, [(i, i ^ offset) for i in range(size)])  18.6 us
    ppermute x15, waiting for transfers between devices, swap(): return lax.ppermute(value, axis, [(i, i ^ offset) for i in range(size)])  17.9 us
  transfers between devices with their start and end apart: 15, of which 10 were waited for; matrix products, arithmetic and copies ran while one was open for 0% of the time, Pallas kernels for 14%

profile of v5, /device:TPU:0, one launch (start us, length us, event | category | flops | bytes accessed | tf_op | source)
XLA Modules:
  0.0 56.0 jit_solution(13871599604128459898)
XLA Ops:
  0.6 3.0 %collective-permute-start = (bf16[32,384]{1,0:T(8,128)(2,1)}, bf16[32,384]{1,0:T(8,128)(2,1)S(1)}, u32[]{:S(2)}, u32[]{:S(2)}) collective-permute-start(bf16[32,384]{1,0:T(8,128)(2,1)} %wave_hbm.1), channel_id=1, source_target_pairs={{0,1},{1,0},{2,3},{3,2},{4,5},{5,4},{6,7},{7,6},{8,9},{9,8},{10,11... | collective-permute-start | bytes 73736 | tf_op jit(solution)/shard_map/ppermute | solution.py:506
  3.6 1.5 %collective-permute-start.2 = (bf16[32,384]{1,0:T(8,128)(2,1)}, bf16[32,384]{1,0:T(8,128)(2,1)S(1)}, u32[]{:S(2)}, u32[]{:S(2)}) collective-permute-start(bf16[32,384]{1,0:T(8,128)(2,1)} %wave_hbm.1), channel_id=1, source_target_pairs={{0,3},{1,2},{2,1},{3,0},{4,7},{5,6},{6,5},{7,4},{8,11},{9,10},{10,... | collective-permute-start | bytes 73736 | tf_op jit(solution)/shard_map/ppermute | solution.py:506
  5.2 0.0 collective-permute-start.1
  5.2 1.3 %shard_map.119 = (s32[32,128]{1,0:T(8,128)S(1)}, bf16[128,4096]{1,0:T(8,128)(2,1)S(1)}, bf16[32,256]{1,0:T(8,128)(2,1)S(1)}, bf16[32,256]{1,0:T(8,128)(2,1)S(1)}, bf16[32,384]{1,0:T(8,128)(2,1)S(1)}) custom-call(s32[8,32]{1,0:T(8,128)} %order_hbm.1, s32[1,256]{1,0:T(1,128)} %bitcast.11, bf16[10,512]{1,0:T(8,128)(2,1)} %w_hbm.2, bf16[32,384]{1,0:T(8,128)(2,1)} %wave_hbm.1), custom_call_target="tpu_custom_call" | custom-call | tf_op jit(solution)/shard_map/pallas_call | solution.py:491
  6.5 0.0 collective-permute-done.refs_1_
  6.5 2.2 %collective-permute-done.2.refs_3_ = bf16[32,384]{1,0:T(8,128)(2,1)S(1)} collective-permute-done((bf16[32,384]{1,0:T(8,128)(2,1)}, bf16[32,384]{1,0:T(8,128)(2,1)S(1)}, u32[]{:S(2)}, u32[]{:S(2)}) %collective-permute-start.2) | collective-permute-done | bytes 24608 | tf_op jit(solution)/shard_map/ppermute | solution.py:506
  8.7 0.5 collective-permute-done.1.refs_2_
  9.2 0.2 shard_map.120
  9.4 2.7 %collective-permute-start.3 = (bf16[32,384]{1,0:T(8,128)(2,1)S(1)}, bf16[32,384]{1,0:T(8,128)(2,1)S(1)}, u32[]{:S(2)}, u32[]{:S(2)}) collective-permute-start(bf16[32,384]{1,0:T(8,128)(2,1)S(1)} %get-tuple-element.50), channel_id=1, source_target_pairs={{0,4},{1,5},{2,6},{3,7},{4,0},{5,1},{6,2},{7,3},{8,12},{9,13},{10,... | collective-permute-start | bytes 73736 | tf_op jit(solution)/shard_map/ppermute | solution.py:506
  12.1 2.1 %collective-permute-done.3.far_ref = bf16[32,384]{1,0:T(8,128)(2,1)S(1)} collective-permute-done((bf16[32,384]{1,0:T(8,128)(2,1)S(1)}, bf16[32,384]{1,0:T(8,128)(2,1)S(1)}, u32[]{:S(2)}, u32[]{:S(2)}) %collective-permute-start.3) | collective-permute-done | bytes 24608 | tf_op jit(solution)/shard_map/ppermute | solution.py:506
  14.2 8.3 %shard_map.121 = (bf16[37,32,512]{2,1,0:T(8,128)(2,1)}, bf16[41,32,512]{2,1,0:T(8,128)(2,1)S(1)}, bf16[40,32,512]{2,1,0:T(8,128)(2,1)S(1)}, f32[10,32,4096]{2,1,...) custom-call(bf16[32,384]{1,0:T(8,128)(2,1)S(1)} %get-tuple-element.4, ...), custom_call_target="tpu_custom_call" | custom-call | tf_op jit(solution)/shard_map/pallas_call | solution.py:491
  22.5 1.5 %shard_map.122 = (f32[512,512]{1,0:T(8,128)S(1)}, bf16[512,512]{1,0:T(8,128)(2,1)S(1)}) custom-call(bf16[41,32,512]{2,1,0:T(8,128)(2,1)S(1)} %get-tuple-element.54.refs_0_, bf16[40,32,512]{2,1,0:T(8,128)(2,1)S(1)} %get-tuple-element.55.refs_1_, bf16[512,1280]{1,0:T(8,128)(2,1)S(1)} %get-tuple-element.56.refs_2_.refs_1_), custom_call_target="tpu_custom_call" | custom-call | flops 1073741824 | tf_op jit(solution)/shard_map/pallas_call | solution.py:491
  24.1 0.1 collective-permute-start.4
  24.2 0.9 %shard_map.123 = (f32[512,256]{1,0:T(8,128)S(1)}, bf16[512,256]{1,0:T(8,128)(2,1)S(1)}) custom-call(bf16[41,32,512]{2,1,0:T(8,128)(2,1)S(1)} %get-tuple-element.54.refs_0_, bf16[512,1280]{1,0:T(8,128)(2,1)S(1)} %get-tuple-element.56.refs_2_.refs_1_), custom_call_target="tpu_custom_call" | custom-call | flops 536870912 | tf_op jit(solution)/shard_map/pallas_call | solution.py:491
  25.0 0.5 collective-permute-start.5
  25.6 2.1 %shard_map.124 = (f32[38,32,512]{2,1,0:T(8,128)S(1)}, f32[37,32,512]{2,1,0:T(8,128)S(1)}) custom-call(bf16[39,32,512]{2,1,0:T(8,128)(2,1)S(1)} %get-tuple-element.61.grad_ref, bf16[3,512,512]{2,1,0:T(8,128)(2,1)S(1)} %get-tuple-element.62.w_ref), custom_call_target="tpu_custom_call" | custom-call | flops 1073741824 | tf_op jit(solution)/shard_map/pallas_call | solution.py:491
  27.7 0.0 collective-permute-done.5.got1
  27.7 0.0 collective-permute-done.4.got0
  27.7 0.2 shard_map.125
  27.9 1.7 %collective-permute-start.6 = (bf16[128,768]{1,0:T(8,128)(2,1)S(1)}, bf16[128,768]{1,0:T(8,128)(2,1)S(1)}, u32[]{:S(2)}, u32[]{:S(2)}) collective-permute-start(bf16[128,768]{1,0:T(8,128)(2,1)S(1)} %get-tuple-element.65), channel_id=1, source_target_pairs={{0,1},{1,0},{2,3},{3,2},{4,5},{5,4},{6,7},{7,6},{8,9},{9,8},{10,11... | collective-permute-start | bytes 589832 | tf_op jit(solution)/shard_map/ppermute | solution.py:506
  29.6 0.3 collective-permute-start.7
  29.9 1.5 %collective-permute-start.8 = (bf16[128,768]{1,0:T(8,128)(2,1)S(1)}, bf16[128,768]{1,0:T(8,128)(2,1)S(1)}, u32[]{:S(2)}, u32[]{:S(2)}) collective-permute-start(bf16[128,768]{1,0:T(8,128)(2,1)S(1)} %get-tuple-element.76), channel_id=1, source_target_pairs={{0,3},{1,2},{2,1},{3,0},{4,7},{5,6},{6,5},{7,4},{8,11},{9,10},{10,... | collective-permute-start | bytes 589832 | tf_op jit(solution)/shard_map/ppermute | solution.py:506
  31.4 3.3 %shard_map.126 = (f32[16,128]{1,0:T(8,128)S(1)}, f32[16,128]{1,0:T(8,128)S(1)}, f32[16,128]{1,0:T(8,128)S(1)}, f32[16,128]{1,0:T(8,128)S(1)}) custom-call(s32[32,128]{1,0:T(8,128)S(1)} %get-tuple-element.51.valid_ref, f32[10,32,4096]{2,1,0:T(8,128)S(1)} %get-tuple-element.67.pre0, f32[80,32,512]{2,1,0:T(8,128)S(1)} %get-tuple-element.68.slope_ref, ...), custom_call_target="tpu_custom_call" | custom-call | flops 4294967296 | tf_op jit(solution)/shard_map/pallas_call | solution.py:491
  34.8 1.7 %collective-permute-start.9 = (f32[16,128]{1,0:T(8,128)S(1)}, f32[16,128]{1,0:T(8,128)S(1)}, u32[]{:S(2)}, u32[]{:S(2)}) collective-permute-start(f32[16,128]{1,0:T(8,128)S(1)} %get-tuple-element.78), channel_id=1, source_target_pairs={{0,1},{1,0},{2,3},{3,2},{4,5},{5,4},{6,7},{7,6},{8,9},{9,8},{10,11... | collective-permute-start | bytes 24584 | tf_op jit(solution)/shard_map/ppermute | solution.py:506
  36.5 0.3 collective-permute-start.10
  36.8 0.0 collective-permute-done.6.got1
  36.8 0.6 %collective-permute-done.7.got2 = bf16[128,768]{1,0:T(8,128)(2,1)S(1)} collective-permute-done((bf16[128,768]{1,0:T(8,128)(2,1)S(1)}, bf16[128,768]{1,0:T(8,128)(2,1)S(1)}, u32[]{:S(2)}, u32[]{:S(2)}) %collective-permute-start.7) | collective-permute-done | bytes 196640 | tf_op jit(solution)/shard_map/ppermute | solution.py:506
  37.4 0.1 shard_map.127
  37.5 1.0 %collective-permute-start.11 = (f32[16,128]{1,0:T(8,128)S(1)}, f32[16,128]{1,0:T(8,128)S(1)}, u32[]{:S(2)}, u32[]{:S(2)}) collective-permute-start(f32[16,128]{1,0:T(8,128)S(1)} %get-tuple-element.80), channel_id=1, source_target_pairs={{0,3},{1,2},{2,1},{3,0},{4,7},{5,6},{6,5},{7,4},{8,11},{9,10},{10,... | collective-permute-start | bytes 24584 | tf_op jit(solution)/shard_map/ppermute | solution.py:506
  38.5 0.7 %collective-permute-done.9.small1 = f32[16,128]{1,0:T(8,128)S(1)} collective-permute-done((f32[16,128]{1,0:T(8,128)S(1)}, f32[16,128]{1,0:T(8,128)S(1)}, u32[]{:S(2)}, u32[]{:S(2)}) %collective-permute-start.9) | collective-permute-done | bytes 8224 | tf_op jit(solution)/shard_map/ppermute | solution.py:506
  39.1 1.5 %collective-permute-done.10.small2 = f32[16,128]{1,0:T(8,128)S(1)} collective-permute-done((f32[16,128]{1,0:T(8,128)S(1)}, f32[16,128]{1,0:T(8,128)S(1)}, u32[]{:S(2)}, u32[]{:S(2)}) %collective-permute-start.10) | collective-permute-done | bytes 8224 | tf_op jit(solution)/shard_map/ppermute | solution.py:506
  40.6 0.0 collective-permute-done.8.got3
  40.6 1.4 %collective-permute-done.11.small3 = f32[16,128]{1,0:T(8,128)S(1)} collective-permute-done((f32[16,128]{1,0:T(8,128)S(1)}, f32[16,128]{1,0:T(8,128)S(1)}, u32[]{:S(2)}, u32[]{:S(2)}) %collective-permute-start.11) | collective-permute-done | bytes 8224 | tf_op jit(solution)/shard_map/ppermute | solution.py:506
  42.1 0.1 shard_map.128
  42.1 2.5 %collective-permute-start.12 = (bf16[80,640]{1,0:T(8,128)(2,1)S(1)}, bf16[80,640]{1,0:T(8,128)(2,1)S(1)}, u32[]{:S(2)}, u32[]{:S(2)}) collective-permute-start(bf16[80,640]{1,0:T(8,128)(2,1)S(1)} %get-tuple-element.82), channel_id=1, source_target_pairs={{0,4},{1,5},{2,6},{3,7},{4,0},{5,1},{6,2},{7,3},{8,12},{9,13},{10,... | collective-permute-start | bytes 307208 | tf_op jit(solution)/shard_map/ppermute | solution.py:506
  44.6 4.2 %collective-permute-done.12.got_ref = bf16[80,640]{1,0:T(8,128)(2,1)S(1)} collective-permute-done((bf16[80,640]{1,0:T(8,128)(2,1)S(1)}, bf16[80,640]{1,0:T(8,128)(2,1)S(1)}, u32[]{:S(2)}, u32[]{:S(2)}) %collective-permute-start.12) | collective-permute-done | bytes 102432 | tf_op jit(solution)/shard_map/ppermute | solution.py:506
  48.9 1.6 %collective-permute-start.13 = (bf16[80,640]{1,0:T(8,128)(2,1)S(1)}, bf16[80,640]{1,0:T(8,128)(2,1)S(1)}, u32[]{:S(2)}, u32[]{:S(2)}) collective-permute-start(bf16[80,640]{1,0:T(8,128)(2,1)S(1)} %shard_map.129.mine_ref), channel_id=1, source_target_pairs={{0,16},{8,24},{16,0},{24,8},{1,17},{9,25},{17,1},{25,9},{2,18},{10... | collective-permute-start | bytes 307208 | tf_op jit(solution)/shard_map/ppermute | solution.py:506
  50.5 3.1 %collective-permute-done.13.got_ref = bf16[80,640]{1,0:T(8,128)(2,1)S(1)} collective-permute-done((bf16[80,640]{1,0:T(8,128)(2,1)S(1)}, bf16[80,640]{1,0:T(8,128)(2,1)S(1)}, u32[]{:S(2)}, u32[]{:S(2)}) %collective-permute-start.13) | collective-permute-done | bytes 102432 | tf_op jit(solution)/shard_map/ppermute | solution.py:506
  53.6 0.1 collective-permute-start.14
  53.7 1.4 %collective-permute-done.14.other_ref = f32[80,640]{1,0:T(8,128)S(1)} collective-permute-done((f32[80,640]{1,0:T(8,128)S(1)}, f32[80,640]{1,0:T(8,128)S(1)}, u32[]{:S(2)}, u32[]{:S(2)}) %collective-permute-start.14) | collective-permute-done | bytes 204832 | tf_op jit(solution)/shard_map/ppermute | solution.py:506
  55.2 0.8 %shard_map.131 = (f32[3,64,512]{2,1,0:T(8,128)}, f32[10,64]{1,0:T(8,128)}, f32[1,64]{1,0:T(1,128)}, f32[1,64]{1,0:T(1,128)}) custom-call(f32[80,640]{1,0:T(8,128)S(1)} %shard_map.130.own_ref, f32[80,640]{1,0:T(8,128)S(1)} %collective-permute-done.14.other_ref), custom_call_target="tpu_custom_call" | custom-call | tf_op jit(solution)/shard_map/pallas_call | solution.py:491
  (2 shorter events, 0.0 us)
Async XLA Ops:
  0.6 5.9 %collective-permute-start = (bf16[32,384]{1,0:T(8,128)(2,1)}, bf16[32,384]{1,0:T(8,128)(2,1)S(1)}, u32[]{:S(2)}, u32[]{:S(2)}) collective-permute-start(bf16[32,384]{1,0:T(8,128)(2,1)} %wave_hbm.1), channel_id=1, source_target_pairs={{0,1},{1,0},{2,3},{3,2},{4,5},{5,4},{6,7},{7,6},{8,9},{9,8},{10,11... | collective-permute-start | bytes 73736 | tf_op jit(solution)/shard_map/ppermute | solution.py:506
  3.6 5.1 %collective-permute-start.2 = (bf16[32,384]{1,0:T(8,128)(2,1)}, bf16[32,384]{1,0:T(8,128)(2,1)S(1)}, u32[]{:S(2)}, u32[]{:S(2)}) collective-permute-start(bf16[32,384]{1,0:T(8,128)(2,1)} %wave_hbm.1), channel_id=1, source_target_pairs={{0,3},{1,2},{2,1},{3,0},{4,7},{5,6},{6,5},{7,4},{8,11},{9,10},{10,... | collective-permute-start | bytes 73736 | tf_op jit(solution)/shard_map/ppermute | solution.py:506
  5.2 4.0 %collective-permute-start.1 = (bf16[32,384]{1,0:T(8,128)(2,1)}, bf16[32,384]{1,0:T(8,128)(2,1)S(1)}, u32[]{:S(2)}, u32[]{:S(2)}) collective-permute-start(bf16[32,384]{1,0:T(8,128)(2,1)} %wave_hbm.1), channel_id=1, source_target_pairs={{0,2},{1,3},{2,0},{3,1},{4,6},{5,7},{6,4},{7,5},{8,10},{9,11},{10,... | collective-permute-start | bytes 73736 | tf_op jit(solution)/shard_map/ppermute | solution.py:506
  9.4 4.8 %collective-permute-start.3 = (bf16[32,384]{1,0:T(8,128)(2,1)S(1)}, bf16[32,384]{1,0:T(8,128)(2,1)S(1)}, u32[]{:S(2)}, u32[]{:S(2)}) collective-permute-start(bf16[32,384]{1,0:T(8,128)(2,1)S(1)} %get-tuple-element.50), channel_id=1, source_target_pairs={{0,4},{1,5},{2,6},{3,7},{4,0},{5,1},{6,2},{7,3},{8,12},{9,13},{10,... | collective-permute-start | bytes 73736 | tf_op jit(solution)/shard_map/ppermute | solution.py:506
  24.1 3.6 %collective-permute-start.4 = (bf16[512,512]{1,0:T(8,128)(2,1)S(1)}, bf16[512,512]{1,0:T(8,128)(2,1)S(1)}, u32[]{:S(2)}, u32[]{:S(2)}) collective-permute-start(bf16[512,512]{1,0:T(8,128)(2,1)S(1)} %get-tuple-element.58), channel_id=1, source_target_pairs={{0,8},{8,0},{16,24},{24,16},{1,9},{9,1},{17,25},{25,17},{2,10},{10... | collective-permute-start | bytes 1572872 | tf_op jit(solution)/shard_map/ppermute | solution.py:506
  25.0 2.7 %collective-permute-start.5 = (bf16[512,256]{1,0:T(8,128)(2,1)S(1)}, bf16[512,256]{1,0:T(8,128)(2,1)S(1)}, u32[]{:S(2)}, u32[]{:S(2)}) collective-permute-start(bf16[512,256]{1,0:T(8,128)(2,1)S(1)} %get-tuple-element.60), channel_id=1, source_target_pairs={{0,8},{8,0},{16,24},{24,16},{1,9},{9,1},{17,25},{25,17},{2,10},{10... | collective-permute-start | bytes 786440 | tf_op jit(solution)/shard_map/ppermute | solution.py:506
  27.9 8.9 %collective-permute-start.6 = (bf16[128,768]{1,0:T(8,128)(2,1)S(1)}, bf16[128,768]{1,0:T(8,128)(2,1)S(1)}, u32[]{:S(2)}, u32[]{:S(2)}) collective-permute-start(bf16[128,768]{1,0:T(8,128)(2,1)S(1)} %get-tuple-element.65), channel_id=1, source_target_pairs={{0,1},{1,0},{2,3},{3,2},{4,5},{5,4},{6,7},{7,6},{8,9},{9,8},{10,11... | collective-permute-start | bytes 589832 | tf_op jit(solution)/shard_map/ppermute | solution.py:506
  29.6 7.8 %collective-permute-start.7 = (bf16[128,768]{1,0:T(8,128)(2,1)S(1)}, bf16[128,768]{1,0:T(8,128)(2,1)S(1)}, u32[]{:S(2)}, u32[]{:S(2)}) collective-permute-start(bf16[128,768]{1,0:T(8,128)(2,1)S(1)} %get-tuple-element.66), channel_id=1, source_target_pairs={{0,2},{1,3},{2,0},{3,1},{4,6},{5,7},{6,4},{7,5},{8,10},{9,11},{10,... | collective-permute-start | bytes 589832 | tf_op jit(solution)/shard_map/ppermute | solution.py:506
  29.9 10.7 %collective-permute-start.8 = (bf16[128,768]{1,0:T(8,128)(2,1)S(1)}, bf16[128,768]{1,0:T(8,128)(2,1)S(1)}, u32[]{:S(2)}, u32[]{:S(2)}) collective-permute-start(bf16[128,768]{1,0:T(8,128)(2,1)S(1)} %get-tuple-element.76), channel_id=1, source_target_pairs={{0,3},{1,2},{2,1},{3,0},{4,7},{5,6},{6,5},{7,4},{8,11},{9,10},{10,... | collective-permute-start | bytes 589832 | tf_op jit(solution)/shard_map/ppermute | solution.py:506
  34.8 4.3 %collective-permute-start.9 = (f32[16,128]{1,0:T(8,128)S(1)}, f32[16,128]{1,0:T(8,128)S(1)}, u32[]{:S(2)}, u32[]{:S(2)}) collective-permute-start(f32[16,128]{1,0:T(8,128)S(1)} %get-tuple-element.78), channel_id=1, source_target_pairs={{0,1},{1,0},{2,3},{3,2},{4,5},{5,4},{6,7},{7,6},{8,9},{9,8},{10,11... | collective-permute-start | bytes 24584 | tf_op jit(solution)/shard_map/ppermute | solution.py:506
  36.5 4.2 %collective-permute-start.10 = (f32[16,128]{1,0:T(8,128)S(1)}, f32[16,128]{1,0:T(8,128)S(1)}, u32[]{:S(2)}, u32[]{:S(2)}) collective-permute-start(f32[16,128]{1,0:T(8,128)S(1)} %get-tuple-element.79), channel_id=1, source_target_pairs={{0,2},{1,3},{2,0},{3,1},{4,6},{5,7},{6,4},{7,5},{8,10},{9,11},{10,... | collective-permute-start | bytes 24584 | tf_op jit(solution)/shard_map/ppermute | solution.py:506
  37.5 4.6 %collective-permute-start.11 = (f32[16,128]{1,0:T(8,128)S(1)}, f32[16,128]{1,0:T(8,128)S(1)}, u32[]{:S(2)}, u32[]{:S(2)}) collective-permute-start(f32[16,128]{1,0:T(8,128)S(1)} %get-tuple-element.80), channel_id=1, source_target_pairs={{0,3},{1,2},{2,1},{3,0},{4,7},{5,6},{6,5},{7,4},{8,11},{9,10},{10,... | collective-permute-start | bytes 24584 | tf_op jit(solution)/shard_map/ppermute | solution.py:506
  42.1 6.7 %collective-permute-start.12 = (bf16[80,640]{1,0:T(8,128)(2,1)S(1)}, bf16[80,640]{1,0:T(8,128)(2,1)S(1)}, u32[]{:S(2)}, u32[]{:S(2)}) collective-permute-start(bf16[80,640]{1,0:T(8,128)(2,1)S(1)} %get-tuple-element.82), channel_id=1, source_target_pairs={{0,4},{1,5},{2,6},{3,7},{4,0},{5,1},{6,2},{7,3},{8,12},{9,13},{10,... | collective-permute-start | bytes 307208 | tf_op jit(solution)/shard_map/ppermute | solution.py:506
  48.9 4.7 %collective-permute-start.13 = (bf16[80,640]{1,0:T(8,128)(2,1)S(1)}, bf16[80,640]{1,0:T(8,128)(2,1)S(1)}, u32[]{:S(2)}, u32[]{:S(2)}) collective-permute-start(bf16[80,640]{1,0:T(8,128)(2,1)S(1)} %shard_map.129.mine_ref), channel_id=1, source_target_pairs={{0,16},{8,24},{16,0},{24,8},{1,17},{9,25},{17,1},{25,9},{2,18},{10... | collective-permute-start | bytes 307208 | tf_op jit(solution)/shard_map/ppermute | solution.py:506
  53.6 1.5 %collective-permute-start.14 = (f32[80,640]{1,0:T(8,128)S(1)}, f32[80,640]{1,0:T(8,128)S(1)}, u32[]{:S(2)}, u32[]{:S(2)}) collective-permute-start(f32[80,640]{1,0:T(8,128)S(1)} %shard_map.130.own_ref), channel_id=1, source_target_pairs={{0,8},{8,0},{16,24},{24,16},{1,9},{9,1},{17,25},{25,17},{2,10},{10... | collective-permute-start | bytes 614408 | tf_op jit(solution)/shard_map/ppermute | solution.py:506

commit v6 on v5

--- a/solution.py
+++ b/solution.py
@@ -76,10 +76,12 @@
     owner_first = iota((rows, 1), 0) // share * rows
     column = iota((rows, members * rows), 1)
     member = lax.axis_index("dev")
+    low_half = member < members // 2
     for target, out_ref in ((member, near_ref), (jnp.bitwise_xor(member, members // 2), far_ref)):
         local = jnp.sum(jnp.where(slot == target, order_of, 0.0), axis=1, keepdims=True).astype(jnp.int32)
         picked = column == owner_first + local
-        out_ref[...] = onehot(picked)
+        picks = picked.astype(F32)
+        out_ref[...] = jnp.where(low_half, picks[: rows // 2], picks[rows // 2 :]).astype(BF16)
         if out_ref is near_ref:
             lens = jnp.sum(jnp.where(picked, len_ref[...], 0), axis=1, keepdims=True)
     valid = (lens - taps) // stride + 1
@@ -92,7 +94,7 @@
 
 def pick_kernel(offsets, near_ref, far_ref, *refs):
     waves, (mine_ref, send_ref, all_ref) = refs[:-3], refs[-3:]
-    rows = mine_ref.shape[0]
+    rows = waves[0].shape[0]
     all_ref[...] = jnp.zeros(all_ref.shape, BF16)
     for offset, wave_ref in zip(offsets, waves):
         first = pl.multiple_of(jnp.bitwise_xor(lax.axis_index("dev"), offset) * rows, rows)
@@ -118,7 +120,8 @@
     even_ref,
     odd_ref,
     pre0,
-    slope_ref,
+    even_slope,
+    odd_slope,
     mean_ref,
     inv_ref,
     patch_ref,
@@ -138,7 +141,7 @@
     out_sem,
 ):
     waiting = copies((gain_hbm, bias_hbm, w_hbm, cot_hbm), (gain_ref, bias_ref, w_ref, cot_ref), sems)
-    rows, samp = near_ref.shape
+    rows, samp = valid_ref.shape[0], near_ref.shape[1]
     chans = gain_ref.shape[1]
     stride = taps // 2
     depth = band_ref.shape[0]
@@ -148,7 +151,9 @@
     min_valid = (MIN_SAMPLES - taps) // stride + 1
     full_groups = frames0 // GROUP
     free_groups = min(min_valid // GROUP, full_groups)
-    wave = near_ref[...] + far_ref[...]
+    low_half = lax.axis_index("dev") < lax.axis_size("dev") // 2
+    near, far = near_ref[...].astype(F32), far_ref[...].astype(F32)
+    wave = jnp.concatenate([jnp.where(low_half, near, far), jnp.where(low_half, far, near)], axis=0).astype(BF16)
     for g in range(groups):
         pick = onehot(iota((samp, depth), 0) == iota((samp, depth), 1) + GROUP * stride * g)
         patch_ref[g] = dot(wave, pick).astype(BF16)
@@ -216,7 +221,8 @@
             for lanes in parts:
                 gelu, slope = gelu_and_slope(frame(g, f, lanes) * scale_ref[:, lanes] + shift_ref[:, lanes])
                 t = g * GROUP + f
-                slope_ref[t, :, lanes] = masked_to(slope, t, masked)
+                slope_ref = odd_slope if f % 2 else even_slope
+                slope_ref[g * half + f // 2, :, lanes] = masked_to(slope, t, masked)
                 stage[f, :, lanes] = masked_to(gelu, t, masked).astype(BF16)
 
     def convolve(h, used):
@@ -302,14 +308,15 @@
             out_ref[:, tap * half : (tap + 1) * half] = value.astype(out_ref.dtype)
 
 
-def input_kernel(grad_ref, w_ref, even_ref, odd_ref):
+def input_kernel(grad_ref, w_ref, even_slope, odd_slope, after_ref, even_ref, odd_ref):
     evens, rows, chans = even_ref.shape
     odds = odd_ref.shape[0]
     first = grad_ref[1 : evens + 1].reshape(evens * rows, chans)
     third = grad_ref[0:evens].reshape(evens * rows, chans)
-    even_ref[...] = (cols_both(first, w_ref[0]) + cols_both(third, w_ref[2])).reshape(even_ref.shape)
+    total = cols_both(first, w_ref[0]) + cols_both(third, w_ref[2])
+    even_ref[...] = total.reshape(even_ref.shape) * even_slope[:evens]
     second = grad_ref[1 : odds + 1].reshape(odds * rows, chans)
-    odd_ref[...] = cols_both(second, w_ref[1]).reshape(odd_ref.shape)
+    odd_ref[...] = cols_both(second, w_ref[1]).reshape(odd_ref.shape) * odd_slope[:odds]
 
 
 def backward_kernel(
@@ -317,7 +324,6 @@
     taps,
     valid_ref,
     pre0,
-    slope_ref,
     mean_ref,
     inv_ref,
     patch_ref,
@@ -328,7 +334,6 @@
     send1,
     send2,
     send3,
-    lift,
     dpre0,
     spread,
     out_ref,
@@ -339,6 +344,7 @@
     stride = taps // 2
     width = dpre0.shape[2] // GROUP
     full_groups = frames0 // GROUP
+    free_groups = min(((MIN_SAMPLES - taps) // stride + 1) // GROUP, full_groups)
     rest = frames0 - full_groups * GROUP
     patches = patch_ref[...].reshape(groups * rows, depth)
     for block in range(chans // width):
@@ -347,23 +353,22 @@
         def frame(g, f):
             return pre0[g, :, f * chans + block * width : f * chans + (block + 1) * width]
 
-        def slopes(g, f, carry):
+        def lift(g, f):
+            return (odd_ref if f % 2 else even_ref)[g * (GROUP // 2) + f // 2, :, lanes]
+
+        def sums(g, f, carry):
             bias_sum, gain_sum = carry
-            t = g * GROUP + f
-            dact = (odd_ref if f % 2 else even_ref)[g * (GROUP // 2) + f // 2, :, lanes]
-            dlift = dact * slope_ref[t, :, lanes]
-            lift[t] = dlift
-            return bias_sum + dlift, gain_sum + dlift * frame(g, f)
+            return bias_sum + lift(g, f), gain_sum + lift(g, f) * frame(g, f)
 
         def add(g, carry):
             for f in range(GROUP):
-                carry = slopes(g, f, carry)
+                carry = sums(g, f, carry)
             return carry
 
         zero = jnp.zeros((rows, width), F32)
         carry = lax.fori_loop(0, full_groups, add, (zero, zero))
         for f in range(rest):
-            carry = slopes(full_groups, f, carry)
+            carry = sums(full_groups, f, carry)
         bias_sum, gain_sum = carry
         mean, inv = mean_ref[:, lanes], inv_ref[:, lanes]
         gain_sum = (gain_sum - mean * bias_sum) * inv
@@ -375,19 +380,21 @@
         slant = scale * inv * gain_sum / count
         level = scale * bias_sum / count - mean * slant
 
-        def finish(g, f):
-            t = g * GROUP + f
-            value = scale * lift[t] - frame(g, f) * slant - level
-            dpre0[g, :, f * width : (f + 1) * width] = jnp.where(valid > t, value, 0.0).astype(BF16)
-
-        def whole(g, carry):
+        def finish(g, f, masked):
+            value = scale * lift(g, f) - frame(g, f) * slant - level
+            if masked:
+                value = jnp.where(valid > g * GROUP + f, value, 0.0)
+            dpre0[g, :, f * width : (f + 1) * width] = value.astype(BF16)
+
+        def whole(masked, g, carry):
             for f in range(GROUP):
-                finish(g, f)
+                finish(g, f, masked)
             return carry
 
-        lax.fori_loop(0, full_groups, whole, 0)
+        lax.fori_loop(0, free_groups, functools.partial(whole, False), 0)
+        lax.fori_loop(free_groups, full_groups, functools.partial(whole, True), 0)
         for f in range(rest):
-            finish(full_groups, f)
+            finish(full_groups, f, True)
         if full_groups < groups:
             dpre0[full_groups, :, rest * width :] = jnp.zeros((rows, (GROUP - rest) * width), BF16)
         spread[...] = rows_first(patches, dpre0[...].reshape(groups * rows, GROUP * width))
@@ -404,7 +411,7 @@
         ref[...] = quarters[jnp.bitwise_xor(place, offset)]
 
 
-def plane_kernel(keep0, got0, keep1, got1, later_ref, own_ref, *send_refs):
+def plane_kernel(keep0, got0, keep1, got1, own_ref, *send_refs):
     size = own_ref.shape[0]
     edge = keep0.shape[1]
     place = lax.rem(lax.axis_index("dev"), 4)
@@ -521,9 +528,8 @@
     dev_bits = members.bit_length() - 1
     grp_bits = groups_of.bit_length() - 1
 
-    offsets = [0, 1, 2, 3]
-    waves = [wave] + [swap(wave, "dev", offset) for offset in offsets[1:]]
-    for bit in range(2, dev_bits - 1):
+    offsets, waves = [0], [wave]
+    for bit in range(dev_bits - 1):
         offsets += [offset | (1 << bit) for offset in offsets]
         waves += [swap(held, "dev", 1 << bit) for held in waves]
     lens = lengths.reshape(1, members * rows)
@@ -533,8 +539,8 @@
         [
             ((rows, 128), jnp.int32),
             ((depth, GROUP * chans), BF16),
-            ((rows, every), BF16),
-            ((rows, every), BF16),
+            ((rows // 2, every), BF16),
+            ((rows // 2, every), BF16),
             ((rows, samp), BF16),
         ],
         [order, lens, w_first, wave],
@@ -548,7 +554,7 @@
     )
     near, send = call(
         functools.partial(pick_kernel, offsets),
-        [((rows, samp), BF16), ((rows, samp), BF16)],
+        [((rows // 2, samp), BF16), ((rows // 2, samp), BF16)],
         [near_sel, far_sel, own_wave, *waves[1:]],
         scratch=[((every, samp), BF16)],
     )
@@ -560,14 +566,15 @@
     places = [0] * members
     for dev in range(members):
         places[dev % 4 * (members // 4) + dev // 4] = dev
-    feat, even, odd, pre0, slope, mean, inv, patch, grad, grad_t, gain_in, w_in = call(
+    feat, even, odd, pre0, even_slope, odd_slope, mean, inv, patch, grad, grad_t, gain_in, w_in = call(
         functools.partial(forward_kernel, frames0, frames1, taps, places),
         [
             ((frames1, rows, chans), BF16, "hbm"),
             ((pad_frames + 1, rows, chans), BF16),
             ((pad_frames, rows, chans), BF16),
             ((groups, rows, GROUP * chans), F32),
-            ((groups * GROUP, rows, chans), F32),
+            ((pad_frames, rows, chans), F32),
+            ((pad_frames, rows, chans), F32),
             ((rows, chans), F32),
             ((rows, chans), F32),
             ((groups, rows, depth), BF16),
@@ -607,26 +614,25 @@
         flops=1 << 29,
     )
     got1 = swap(send1, "grp", 1)
-    evens, odds = (frames0 + 1) // 2, frames0 // 2
-    dact_even, dact_odd = call(
-        input_kernel,
-        [((evens, rows, chans), F32), ((odds, rows, chans), F32)],
-        [grad, w_in],
-        flops=1 << 30,
-    )
     quarter = chans // 4
     own, *sends = call(
         plane_kernel,
         [((quarter, wide), F32)] + [((quarter, wide), BF16)] * 3,
-        [keep0, got0, keep1, got1, dact_odd],
+        [keep0, got0, keep1, got1],
     )
     gots = [swap(part, "dev", offset) for offset, part in enumerate(sends, 1)]
+    evens, odds = (frames0 + 1) // 2, frames0 // 2
+    lift_even, lift_odd = call(
+        input_kernel,
+        [((evens, rows, chans), F32), ((odds, rows, chans), F32)],
+        [grad, w_in, even_slope, odd_slope, own],
+        flops=1 << 30,
+    )
     small, *smalls = call(
         functools.partial(backward_kernel, frames0, taps),
         [((16, quarter), F32)] * 4,
-        [valid, pre0, slope, mean, inv, patch, dact_even, dact_odd, gain_in],
+        [valid, pre0, mean, inv, patch, lift_even, lift_odd, gain_in],
         scratch=[
-            ((frames0, rows, width), F32),
             ((groups, rows, GROUP * width), BF16),
             ((depth, GROUP * width), F32),
             ((16, chans), F32),
@@ -634,11 +640,11 @@
         ],
         flops=1 << 32,
     )
-    small1, small2 = swap(smalls[0], "dev", 1), swap(smalls[1], "dev", 2)
-    own, third = call(
-        part_kernel, [((quarter, wide), F32), (small.shape, F32)], [own, gots[0], gots[1], smalls[2]]
-    )
-    small3 = swap(third, "dev", 3)
+    small3, small2 = swap(smalls[2], "dev", 3), swap(smalls[1], "dev", 2)
+    own, first = call(
+        part_kernel, [((quarter, wide), F32), (small.shape, F32)], [own, gots[0], gots[1], smalls[0]]
+    )
+    small1 = swap(first, "dev", 1)
     size = quarter // 2
     keep, send = call(
         functools.partial(gather_kernel, dev_bits - 1),

time: 56.2 us -> 56.1 us (level)
  starting transfers between devices: 18.6 us -> 21.9 us
  waiting for transfers between devices: 17.9 us -> 14.8 us
    ppermute x15, starting transfers between devices: 18.6 us -> 21.9 us  [swap(): return lax.ppermute(value, axis, [(i, i ^ offset) for i in range(size)])]
    ppermute x15, waiting for transfers between devices: 17.9 us -> 14.8 us  [swap(): return lax.ppermute(value, axis, [(i, i ^ offset) for i in range(size)])]
  transfers between devices with their start and end apart: 15 -> 15, of which waited for: 10 -> 10; matrix products, arithmetic and copies ran while one was open for 0% -> 0% of each run, Pallas kernels for 14% -> 13%
where the time goes in v6:
time: 56.1 us; the launch traced here: 55.9 us
  starting transfers between devices  21.9 us (39%)
  Pallas kernels  18.4 us (33%)
  waiting for transfers between devices  14.8 us (26%)
  between operations  0.73 us (1%)
    ppermute x15, starting transfers between devices, swap(): return lax.ppermute(value, axis, [(i, i ^ offset) for i in range(size)])  21.9 us
    pallas_call x13, Pallas kernels, call(): pl.pallas_call(kernel, out_shape=[jax.ShapeDtypeStruct(out[0], out[1]) if...  18.4 us
    ppermute x15, waiting for transfers between devices, swap(): return lax.ppermute(value, axis, [(i, i ^ offset) for i in range(size)])  14.8 us
  transfers between devices with their start and end apart: 15, of which 10 were waited for; matrix products, arithmetic and copies ran while one was open for 0% of the time, Pallas kernels for 13%

profile of v6, /device:TPU:0, one launch (start us, length us, event | category | flops | bytes accessed | tf_op | source)
XLA Modules:
  0.0 55.9 jit_solution(12844967878163115079)
XLA Ops:
  0.6 3.0 %collective-permute-start = (bf16[32,384]{1,0:T(8,128)(2,1)}, bf16[32,384]{1,0:T(8,128)(2,1)S(1)}, u32[]{:S(2)}, u32[]{:S(2)}) collective-permute-start(bf16[32,384]{1,0:T(8,128)(2,1)} %wave_hbm.1), channel_id=1, source_target_pairs={{0,1},{1,0},{2,3},{3,2},{4,5},{5,4},{6,7},{7,6},{8,9},{9,8},{10,11... | collective-permute-start | bytes 73736 | tf_op jit(solution)/shard_map/ppermute | solution.py:513
  3.6 1.6 %collective-permute-start.1 = (bf16[32,384]{1,0:T(8,128)(2,1)}, bf16[32,384]{1,0:T(8,128)(2,1)S(1)}, u32[]{:S(2)}, u32[]{:S(2)}) collective-permute-start(bf16[32,384]{1,0:T(8,128)(2,1)} %wave_hbm.1), channel_id=1, source_target_pairs={{0,2},{1,3},{2,0},{3,1},{4,6},{5,7},{6,4},{7,5},{8,10},{9,11},{10,... | collective-permute-start | bytes 73736 | tf_op jit(solution)/shard_map/ppermute | solution.py:513
  5.2 0.4 collective-permute-done.refs_1_
  5.7 2.1 %collective-permute-start.2 = (bf16[32,384]{1,0:T(8,128)(2,1)S(1)}, bf16[32,384]{1,0:T(8,128)(2,1)S(1)}, u32[]{:S(2)}, u32[]{:S(2)}) collective-permute-start(bf16[32,384]{1,0:T(8,128)(2,1)S(1)} %collective-permute-done.refs_1_), channel_id=1, source_target_pairs={{0,2},{1,3},{2,0},{3,1},{4,6},{5,7},{6,4},{7,5},{8,10},{9,11},{10,... | collective-permute-start | bytes 73736 | tf_op jit(solution)/shard_map/ppermute | solution.py:513
  7.8 1.2 %shard_map.119 = (s32[32,128]{1,0:T(8,128)S(1)}, bf16[128,4096]{1,0:T(8,128)(2,1)S(1)}, bf16[16,256]{1,0:T(8,128)(2,1)S(1)}, bf16[16,256]{1,0:T(8,128)(2,1)S(1)}, bf16[32,384]{1,0:T(8,128)(2,1)S(1)}) custom-call(s32[8,32]{1,0:T(8,128)} %order_hbm.1, s32[1,256]{1,0:T(1,128)} %bitcast.11, bf16[10,512]{1,0:T(8,128)(2,1)} %w_hbm.2, bf16[32,384]{1,0:T(8,128)(2,1)} %wave_hbm.1), custom_call_target="tpu_custom_call" | custom-call | tf_op jit(solution)/shard_map/pallas_call | solution.py:498
  9.0 0.0 collective-permute-done.1.refs_2_
  9.0 0.6 collective-permute-done.2.refs_3_
  9.6 0.2 shard_map.120
  9.7 3.1 %collective-permute-start.3 = (bf16[16,384]{1,0:T(8,128)(2,1)S(1)}, bf16[16,384]{1,0:T(8,128)(2,1)S(1)}, u32[]{:S(2)}, u32[]{:S(2)}) collective-permute-start(bf16[16,384]{1,0:T(8,128)(2,1)S(1)} %get-tuple-element.51), channel_id=1, source_target_pairs={{0,4},{1,5},{2,6},{3,7},{4,0},{5,1},{6,2},{7,3},{8,12},{9,13},{10,... | collective-permute-start | bytes 36872 | tf_op jit(solution)/shard_map/ppermute | solution.py:513
  12.8 1.7 %collective-permute-done.3.far_ref = bf16[16,384]{1,0:T(8,128)(2,1)S(1)} collective-permute-done((bf16[16,384]{1,0:T(8,128)(2,1)S(1)}, bf16[16,384]{1,0:T(8,128)(2,1)S(1)}, u32[]{:S(2)}, u32[]{:S(2)}) %collective-permute-start.3) | collective-permute-done | bytes 12320 | tf_op jit(solution)/shard_map/ppermute | solution.py:513
  14.5 8.6 %shard_map.121 = (bf16[37,32,512]{2,1,0:T(8,128)(2,1)}, bf16[41,32,512]{2,1,0:T(8,128)(2,1)S(1)}, bf16[40,32,512]{2,1,0:T(8,128)(2,1)S(1)}, f32[10,32,4096]{2,1,...) custom-call(bf16[16,384]{1,0:T(8,128)(2,1)S(1)} %get-tuple-element.5, ...), custom_call_target="tpu_custom_call" | custom-call | tf_op jit(solution)/shard_map/pallas_call | solution.py:498
  23.1 1.5 %shard_map.122 = (f32[512,512]{1,0:T(8,128)S(1)}, bf16[512,512]{1,0:T(8,128)(2,1)S(1)}) custom-call(bf16[41,32,512]{2,1,0:T(8,128)(2,1)S(1)} %get-tuple-element.55.refs_0_, bf16[40,32,512]{2,1,0:T(8,128)(2,1)S(1)} %get-tuple-element.56.refs_1_, bf16[512,1280]{1,0:T(8,128)(2,1)S(1)} %get-tuple-element.57.refs_2_.refs_1_), custom_call_target="tpu_custom_call" | custom-call | flops 1073741824 | tf_op jit(solution)/shard_map/pallas_call | solution.py:498
  24.6 0.1 collective-permute-start.4
  24.7 0.9 %shard_map.123 = (f32[512,256]{1,0:T(8,128)S(1)}, bf16[512,256]{1,0:T(8,128)(2,1)S(1)}) custom-call(bf16[41,32,512]{2,1,0:T(8,128)(2,1)S(1)} %get-tuple-element.55.refs_0_, bf16[512,1280]{1,0:T(8,128)(2,1)S(1)} %get-tuple-element.57.refs_2_.refs_1_), custom_call_target="tpu_custom_call" | custom-call | flops 536870912 | tf_op jit(solution)/shard_map/pallas_call | solution.py:498
  25.6 0.5 collective-permute-start.5
  26.1 1.2 %collective-permute-done.5.got1 = bf16[512,256]{1,0:T(8,128)(2,1)S(1)} collective-permute-done((bf16[512,256]{1,0:T(8,128)(2,1)S(1)}, bf16[512,256]{1,0:T(8,128)(2,1)S(1)}, u32[]{:S(2)}, u32[]{:S(2)}) %collective-permute-start.5) | collective-permute-done | bytes 262176 | tf_op jit(solution)/shard_map/ppermute | solution.py:513
  27.3 0.0 collective-permute-done.4.got0
  27.3 0.1 shard_map.124
  27.4 1.9 %collective-permute-start.6 = (bf16[128,768]{1,0:T(8,128)(2,1)S(1)}, bf16[128,768]{1,0:T(8,128)(2,1)S(1)}, u32[]{:S(2)}, u32[]{:S(2)}) collective-permute-start(bf16[128,768]{1,0:T(8,128)(2,1)S(1)} %get-tuple-element.63), channel_id=1, source_target_pairs={{0,1},{1,0},{2,3},{3,2},{4,5},{5,4},{6,7},{7,6},{8,9},{9,8},{10,11... | collective-permute-start | bytes 589832 | tf_op jit(solution)/shard_map/ppermute | solution.py:513
  29.3 1.6 %collective-permute-start.7 = (bf16[128,768]{1,0:T(8,128)(2,1)S(1)}, bf16[128,768]{1,0:T(8,128)(2,1)S(1)}, u32[]{:S(2)}, u32[]{:S(2)}) collective-permute-start(bf16[128,768]{1,0:T(8,128)(2,1)S(1)} %get-tuple-element.64), channel_id=1, source_target_pairs={{0,2},{1,3},{2,0},{3,1},{4,6},{5,7},{6,4},{7,5},{8,10},{9,11},{10,... | collective-permute-start | bytes 589832 | tf_op jit(solution)/shard_map/ppermute | solution.py:513
  30.9 0.1 collective-permute-start.8
  31.0 2.2 %shard_map.125 = (f32[38,32,512]{2,1,0:T(8,128)S(1)}, f32[37,32,512]{2,1,0:T(8,128)S(1)}) custom-call(bf16[39,32,512]{2,1,0:T(8,128)(2,1)S(1)} %get-tuple-element.69.grad_ref, bf16[3,512,512]{2,1,0:T(8,128)(2,1)S(1)} %get-tuple-element.70.w_ref, f32[40,32,512]{2,1,0:T(8,128)S(1)} %get-tuple-element.71.even_slope, ...), custom_call_target="tpu_custom_call" | custom-call | flops 1073741824 | tf_op jit(solution)/shard_map/pallas_call | solution.py:498
  33.2 2.7 %shard_map.126 = (f32[16,128]{1,0:T(8,128)S(1)}, f32[16,128]{1,0:T(8,128)S(1)}, f32[16,128]{1,0:T(8,128)S(1)}, f32[16,128]{1,0:T(8,128)S(1)}) custom-call(s32[32,128]{1,0:T(8,128)S(1)} %get-tuple-element.52.valid_ref, f32[10,32,4096]{2,1,0:T(8,128)S(1)} %get-tuple-element.65.pre0, f32[32,512]{1,0:T(8,128)S(1)} %get-tuple-element.66.mean_ref, ...), custom_call_target="tpu_custom_call" | custom-call | flops 4294967296 | tf_op jit(solution)/shard_map/pallas_call | solution.py:498
  35.9 2.0 %collective-permute-start.10 = (f32[16,128]{1,0:T(8,128)S(1)}, f32[16,128]{1,0:T(8,128)S(1)}, u32[]{:S(2)}, u32[]{:S(2)}) collective-permute-start(f32[16,128]{1,0:T(8,128)S(1)} %get-tuple-element.81), channel_id=1, source_target_pairs={{0,2},{1,3},{2,0},{3,1},{4,6},{5,7},{6,4},{7,5},{8,10},{9,11},{10,... | collective-permute-start | bytes 24584 | tf_op jit(solution)/shard_map/ppermute | solution.py:513
  37.9 1.4 %collective-permute-start.11 = (f32[16,128]{1,0:T(8,128)S(1)}, f32[16,128]{1,0:T(8,128)S(1)}, u32[]{:S(2)}, u32[]{:S(2)}) collective-permute-start(f32[16,128]{1,0:T(8,128)S(1)} %get-tuple-element.82), channel_id=1, source_target_pairs={{0,3},{1,2},{2,1},{3,0},{4,7},{5,6},{6,5},{7,4},{8,11},{9,10},{10,... | collective-permute-start | bytes 24584 | tf_op jit(solution)/shard_map/ppermute | solution.py:513
  39.3 0.0 collective-permute-done.6.got1
  39.3 0.0 collective-permute-done.7.got2
  39.3 0.1 shard_map.127
  39.3 0.3 collective-permute-start.9
  39.6 1.0 %collective-permute-done.10.small2 = f32[16,128]{1,0:T(8,128)S(1)} collective-permute-done((f32[16,128]{1,0:T(8,128)S(1)}, f32[16,128]{1,0:T(8,128)S(1)}, u32[]{:S(2)}, u32[]{:S(2)}) %collective-permute-start.10) | collective-permute-done | bytes 8224 | tf_op jit(solution)/shard_map/ppermute | solution.py:513
  40.6 1.8 %collective-permute-done.11.small3 = f32[16,128]{1,0:T(8,128)S(1)} collective-permute-done((f32[16,128]{1,0:T(8,128)S(1)}, f32[16,128]{1,0:T(8,128)S(1)}, u32[]{:S(2)}, u32[]{:S(2)}) %collective-permute-start.11) | collective-permute-done | bytes 8224 | tf_op jit(solution)/shard_map/ppermute | solution.py:513
  42.5 0.0 collective-permute-done.8.got3
  42.5 0.6 %collective-permute-done.9.small1 = f32[16,128]{1,0:T(8,128)S(1)} collective-permute-done((f32[16,128]{1,0:T(8,128)S(1)}, f32[16,128]{1,0:T(8,128)S(1)}, u32[]{:S(2)}, u32[]{:S(2)}) %collective-permute-start.9) | collective-permute-done | bytes 8224 | tf_op jit(solution)/shard_map/ppermute | solution.py:513
  43.1 2.7 %collective-permute-start.12 = (bf16[80,640]{1,0:T(8,128)(2,1)S(1)}, bf16[80,640]{1,0:T(8,128)(2,1)S(1)}, u32[]{:S(2)}, u32[]{:S(2)}) collective-permute-start(bf16[80,640]{1,0:T(8,128)(2,1)S(1)} %get-tuple-element.84), channel_id=1, source_target_pairs={{0,4},{1,5},{2,6},{3,7},{4,0},{5,1},{6,2},{7,3},{8,12},{9,13},{10,... | collective-permute-start | bytes 307208 | tf_op jit(solution)/shard_map/ppermute | solution.py:513
  45.8 3.0 %collective-permute-done.12.got_ref = bf16[80,640]{1,0:T(8,128)(2,1)S(1)} collective-permute-done((bf16[80,640]{1,0:T(8,128)(2,1)S(1)}, bf16[80,640]{1,0:T(8,128)(2,1)S(1)}, u32[]{:S(2)}, u32[]{:S(2)}) %collective-permute-start.12) | collective-permute-done | bytes 102432 | tf_op jit(solution)/shard_map/ppermute | solution.py:513
  48.8 1.6 %collective-permute-start.13 = (bf16[80,640]{1,0:T(8,128)(2,1)S(1)}, bf16[80,640]{1,0:T(8,128)(2,1)S(1)}, u32[]{:S(2)}, u32[]{:S(2)}) collective-permute-start(bf16[80,640]{1,0:T(8,128)(2,1)S(1)} %shard_map.129.mine_ref), channel_id=1, source_target_pairs={{0,16},{8,24},{16,0},{24,8},{1,17},{9,25},{17,1},{25,9},{2,18},{10... | collective-permute-start | bytes 307208 | tf_op jit(solution)/shard_map/ppermute | solution.py:513
  50.3 3.1 %collective-permute-done.13.got_ref = bf16[80,640]{1,0:T(8,128)(2,1)S(1)} collective-permute-done((bf16[80,640]{1,0:T(8,128)(2,1)S(1)}, bf16[80,640]{1,0:T(8,128)(2,1)S(1)}, u32[]{:S(2)}, u32[]{:S(2)}) %collective-permute-start.13) | collective-permute-done | bytes 102432 | tf_op jit(solution)/shard_map/ppermute | solution.py:513
  53.5 0.1 collective-permute-start.14
  53.6 1.4 %collective-permute-done.14.other_ref = f32[80,640]{1,0:T(8,128)S(1)} collective-permute-done((f32[80,640]{1,0:T(8,128)S(1)}, f32[80,640]{1,0:T(8,128)S(1)}, u32[]{:S(2)}, u32[]{:S(2)}) %collective-permute-start.14) | collective-permute-done | bytes 204832 | tf_op jit(solution)/shard_map/ppermute | solution.py:513
  55.0 0.8 %shard_map.131 = (f32[3,64,512]{2,1,0:T(8,128)}, f32[10,64]{1,0:T(8,128)}, f32[1,64]{1,0:T(1,128)}, f32[1,64]{1,0:T(1,128)}) custom-call(f32[80,640]{1,0:T(8,128)S(1)} %shard_map.130.own_ref, f32[80,640]{1,0:T(8,128)S(1)} %collective-permute-done.14.other_ref), custom_call_target="tpu_custom_call" | custom-call | tf_op jit(solution)/shard_map/pallas_call | solution.py:498
  (3 shorter events, 0.1 us)
Async XLA Ops:
  0.6 5.0 %collective-permute-start = (bf16[32,384]{1,0:T(8,128)(2,1)}, bf16[32,384]{1,0:T(8,128)(2,1)S(1)}, u32[]{:S(2)}, u32[]{:S(2)}) collective-permute-start(bf16[32,384]{1,0:T(8,128)(2,1)} %wave_hbm.1), channel_id=1, source_target_pairs={{0,1},{1,0},{2,3},{3,2},{4,5},{5,4},{6,7},{7,6},{8,9},{9,8},{10,11... | collective-permute-start | bytes 73736 | tf_op jit(solution)/shard_map/ppermute | solution.py:513
  3.6 5.4 %collective-permute-start.1 = (bf16[32,384]{1,0:T(8,128)(2,1)}, bf16[32,384]{1,0:T(8,128)(2,1)S(1)}, u32[]{:S(2)}, u32[]{:S(2)}) collective-permute-start(bf16[32,384]{1,0:T(8,128)(2,1)} %wave_hbm.1), channel_id=1, source_target_pairs={{0,2},{1,3},{2,0},{3,1},{4,6},{5,7},{6,4},{7,5},{8,10},{9,11},{10,... | collective-permute-start | bytes 73736 | tf_op jit(solution)/shard_map/ppermute | solution.py:513
  5.7 3.9 %collective-permute-start.2 = (bf16[32,384]{1,0:T(8,128)(2,1)S(1)}, bf16[32,384]{1,0:T(8,128)(2,1)S(1)}, u32[]{:S(2)}, u32[]{:S(2)}) collective-permute-start(bf16[32,384]{1,0:T(8,128)(2,1)S(1)} %collective-permute-done.refs_1_), channel_id=1, source_target_pairs={{0,2},{1,3},{2,0},{3,1},{4,6},{5,7},{6,4},{7,5},{8,10},{9,11},{10,... | collective-permute-start | bytes 73736 | tf_op jit(solution)/shard_map/ppermute | solution.py:513
  9.7 4.8 %collective-permute-start.3 = (bf16[16,384]{1,0:T(8,128)(2,1)S(1)}, bf16[16,384]{1,0:T(8,128)(2,1)S(1)}, u32[]{:S(2)}, u32[]{:S(2)}) collective-permute-start(bf16[16,384]{1,0:T(8,128)(2,1)S(1)} %get-tuple-element.51), channel_id=1, source_target_pairs={{0,4},{1,5},{2,6},{3,7},{4,0},{5,1},{6,2},{7,3},{8,12},{9,13},{10,... | collective-permute-start | bytes 36872 | tf_op jit(solution)/shard_map/ppermute | solution.py:513
  24.6 2.7 %collective-permute-start.4 = (bf16[512,512]{1,0:T(8,128)(2,1)S(1)}, bf16[512,512]{1,0:T(8,128)(2,1)S(1)}, u32[]{:S(2)}, u32[]{:S(2)}) collective-permute-start(bf16[512,512]{1,0:T(8,128)(2,1)S(1)} %get-tuple-element.59), channel_id=1, source_target_pairs={{0,8},{8,0},{16,24},{24,16},{1,9},{9,1},{17,25},{25,17},{2,10},{10... | collective-permute-start | bytes 1572872 | tf_op jit(solution)/shard_map/ppermute | solution.py:513
  25.6 1.7 %collective-permute-start.5 = (bf16[512,256]{1,0:T(8,128)(2,1)S(1)}, bf16[512,256]{1,0:T(8,128)(2,1)S(1)}, u32[]{:S(2)}, u32[]{:S(2)}) collective-permute-start(bf16[512,256]{1,0:T(8,128)(2,1)S(1)} %get-tuple-element.61), channel_id=1, source_target_pairs={{0,8},{8,0},{16,24},{24,16},{1,9},{9,1},{17,25},{25,17},{2,10},{10... | collective-permute-start | bytes 786440 | tf_op jit(solution)/shard_map/ppermute | solution.py:513
  27.4 11.8 %collective-permute-start.6 = (bf16[128,768]{1,0:T(8,128)(2,1)S(1)}, bf16[128,768]{1,0:T(8,128)(2,1)S(1)}, u32[]{:S(2)}, u32[]{:S(2)}) collective-permute-start(bf16[128,768]{1,0:T(8,128)(2,1)S(1)} %get-tuple-element.63), channel_id=1, source_target_pairs={{0,1},{1,0},{2,3},{3,2},{4,5},{5,4},{6,7},{7,6},{8,9},{9,8},{10,11... | collective-permute-start | bytes 589832 | tf_op jit(solution)/shard_map/ppermute | solution.py:513
  29.3 10.0 %collective-permute-start.7 = (bf16[128,768]{1,0:T(8,128)(2,1)S(1)}, bf16[128,768]{1,0:T(8,128)(2,1)S(1)}, u32[]{:S(2)}, u32[]{:S(2)}) collective-permute-start(bf16[128,768]{1,0:T(8,128)(2,1)S(1)} %get-tuple-element.64), channel_id=1, source_target_pairs={{0,2},{1,3},{2,0},{3,1},{4,6},{5,7},{6,4},{7,5},{8,10},{9,11},{10,... | collective-permute-start | bytes 589832 | tf_op jit(solution)/shard_map/ppermute | solution.py:513
  30.9 11.5 %collective-permute-start.8 = (bf16[128,768]{1,0:T(8,128)(2,1)S(1)}, bf16[128,768]{1,0:T(8,128)(2,1)S(1)}, u32[]{:S(2)}, u32[]{:S(2)}) collective-permute-start(bf16[128,768]{1,0:T(8,128)(2,1)S(1)} %get-tuple-element.78), channel_id=1, source_target_pairs={{0,3},{1,2},{2,1},{3,0},{4,7},{5,6},{6,5},{7,4},{8,11},{9,10},{10,... | collective-permute-start | bytes 589832 | tf_op jit(solution)/shard_map/ppermute | solution.py:513
  35.9 4.7 %collective-permute-start.10 = (f32[16,128]{1,0:T(8,128)S(1)}, f32[16,128]{1,0:T(8,128)S(1)}, u32[]{:S(2)}, u32[]{:S(2)}) collective-permute-start(f32[16,128]{1,0:T(8,128)S(1)} %get-tuple-element.81), channel_id=1, source_target_pairs={{0,2},{1,3},{2,0},{3,1},{4,6},{5,7},{6,4},{7,5},{8,10},{9,11},{10,... | collective-permute-start | bytes 24584 | tf_op jit(solution)/shard_map/ppermute | solution.py:513
  37.9 4.5 %collective-permute-start.11 = (f32[16,128]{1,0:T(8,128)S(1)}, f32[16,128]{1,0:T(8,128)S(1)}, u32[]{:S(2)}, u32[]{:S(2)}) collective-permute-start(f32[16,128]{1,0:T(8,128)S(1)} %get-tuple-element.82), channel_id=1, source_target_pairs={{0,3},{1,2},{2,1},{3,0},{4,7},{5,6},{6,5},{7,4},{8,11},{9,10},{10,... | collective-permute-start | bytes 24584 | tf_op jit(solution)/shard_map/ppermute | solution.py:513
  39.3 3.7 %collective-permute-start.9 = (f32[16,128]{1,0:T(8,128)S(1)}, f32[16,128]{1,0:T(8,128)S(1)}, u32[]{:S(2)}, u32[]{:S(2)}) collective-permute-start(f32[16,128]{1,0:T(8,128)S(1)} %get-tuple-element.80), channel_id=1, source_target_pairs={{0,1},{1,0},{2,3},{3,2},{4,5},{5,4},{6,7},{7,6},{8,9},{9,8},{10,11... | collective-permute-start | bytes 24584 | tf_op jit(solution)/shard_map/ppermute | solution.py:513
  43.1 5.6 %collective-permute-start.12 = (bf16[80,640]{1,0:T(8,128)(2,1)S(1)}, bf16[80,640]{1,0:T(8,128)(2,1)S(1)}, u32[]{:S(2)}, u32[]{:S(2)}) collective-permute-start(bf16[80,640]{1,0:T(8,128)(2,1)S(1)} %get-tuple-element.84), channel_id=1, source_target_pairs={{0,4},{1,5},{2,6},{3,7},{4,0},{5,1},{6,2},{7,3},{8,12},{9,13},{10,... | collective-permute-start | bytes 307208 | tf_op jit(solution)/shard_map/ppermute | solution.py:513
  48.8 4.7 %collective-permute-start.13 = (bf16[80,640]{1,0:T(8,128)(2,1)S(1)}, bf16[80,640]{1,0:T(8,128)(2,1)S(1)}, u32[]{:S(2)}, u32[]{:S(2)}) collective-permute-start(bf16[80,640]{1,0:T(8,128)(2,1)S(1)} %shard_map.129.mine_ref), channel_id=1, source_target_pairs={{0,16},{8,24},{16,0},{24,8},{1,17},{9,25},{17,1},{25,9},{2,18},{10... | collective-permute-start | bytes 307208 | tf_op jit(solution)/shard_map/ppermute | solution.py:513
  53.5 1.5 %collective-permute-start.14 = (f32[80,640]{1,0:T(8,128)S(1)}, f32[80,640]{1,0:T(8,128)S(1)}, u32[]{:S(2)}, u32[]{:S(2)}) collective-permute-start(f32[80,640]{1,0:T(8,128)S(1)} %shard_map.130.own_ref), channel_id=1, source_target_pairs={{0,8},{8,0},{16,24},{24,16},{1,9},{9,1},{17,25},{25,17},{2,10},{10... | collective-permute-start | bytes 614408 | tf_op jit(solution)/shard_map/ppermute | solution.py:513

commit v7 on v6

--- a/solution.py
+++ b/solution.py
@@ -116,7 +116,7 @@
     bias_hbm,
     w_hbm,
     cot_hbm,
-    feat_out,
+    feat_ref,
     even_ref,
     odd_ref,
     pre0,
@@ -136,9 +136,7 @@
     shift_ref,
     bias_ref,
     cot_ref,
-    feat_ref,
     sems,
-    out_sem,
 ):
     waiting = copies((gain_hbm, bias_hbm, w_hbm, cot_hbm), (gain_ref, bias_ref, w_ref, cot_ref), sems)
     rows, samp = valid_ref.shape[0], near_ref.shape[1]
@@ -244,12 +242,7 @@
                 feat_ref[u, :, lanes] = gelu.astype(BF16)
                 grad_ref[u + 1, :, lanes] = grad.astype(BF16)
 
-    def leave(h, used):
-        frames = pl.ds(h * half, used)
-        pltpu.make_async_copy(feat_ref.at[frames], feat_out.at[frames], out_sem).start()
-
     def turn(h, used):
-        leave(h, used)
         turned = grad_ref[pl.ds(h * half + 1, used)].reshape(used * rows, chans).T
         start = h * span
         cols = pl.ds(start if isinstance(start, int) else pl.multiple_of(start, span), used * rows)
@@ -291,24 +284,22 @@
     pre1[...] = fresh[...]
     activate1(last, frames1 - last * half, True)
     turn(last, frames1 - last * half)
-    pltpu.make_async_copy(feat_ref, feat_out, out_sem).wait()
-
-
-def outer_kernel(skips, *refs):
-    acts, (grad_t_ref, keep_ref, send_ref) = refs[:-3], refs[-3:]
-    frames = grad_t_ref.shape[1] // acts[0].shape[1]
-    rows, chans = acts[0].shape[1:]
+
+
+def outer_kernel(skip, act_ref, grad_t_ref, keep_ref, send_ref):
+    rows, chans = act_ref.shape[1:]
+    frames = grad_t_ref.shape[1] // rows
     half = chans // 2
     core = lax.rem(lax.axis_index("grp"), 2)
-    turned = grad_t_ref[...]
-    for tap, (ref, skip) in enumerate(zip(acts, skips)):
-        for side, out_ref in ((1 - core, send_ref), (core, keep_ref)):
-            lanes = pl.ds(pl.multiple_of(side * half, half), half)
-            value = dot(turned, ref[skip : skip + frames, :, lanes].reshape(frames * rows, half))
-            out_ref[:, tap * half : (tap + 1) * half] = value.astype(out_ref.dtype)
-
-
-def input_kernel(grad_ref, w_ref, even_slope, odd_slope, after_ref, even_ref, odd_ref):
+    for side, out_ref in ((1 - core, send_ref), (core, keep_ref)):
+        lanes = pl.ds(pl.multiple_of(side * half, half), half)
+        acts = act_ref[skip : skip + frames, :, lanes].reshape(frames * rows, half)
+        out_ref[...] = dot(grad_t_ref[...], acts).astype(out_ref.dtype)
+
+
+def input_kernel(grad_ref, w_ref, even_slope, odd_slope, after_ref, feat_ref, even_ref, odd_ref, feat_out, sem):
+    leaving = pltpu.make_async_copy(feat_ref, feat_out, sem)
+    leaving.start()
     evens, rows, chans = even_ref.shape
     odds = odd_ref.shape[0]
     first = grad_ref[1 : evens + 1].reshape(evens * rows, chans)
@@ -317,6 +308,7 @@
     even_ref[...] = total.reshape(even_ref.shape) * even_slope[:evens]
     second = grad_ref[1 : odds + 1].reshape(odds * rows, chans)
     odd_ref[...] = cols_both(second, w_ref[1]).reshape(odd_ref.shape) * odd_slope[:odds]
+    leaving.wait()
 
 
 def backward_kernel(
@@ -411,14 +403,16 @@
         ref[...] = quarters[jnp.bitwise_xor(place, offset)]
 
 
-def plane_kernel(keep0, got0, keep1, got1, own_ref, *send_refs):
-    size = own_ref.shape[0]
-    edge = keep0.shape[1]
+def plane_kernel(second, *refs):
+    keeps, others, outs = refs[:second], refs[second : 2 * second], refs[2 * second :]
+    size = outs[0].shape[0]
+    half = keeps[0].shape[1]
     place = lax.rem(lax.axis_index("dev"), 4)
-    for offset, out_ref in enumerate((own_ref, *send_refs)):
+    for offset, out_ref in enumerate(outs):
         lines = pl.ds(pl.multiple_of(jnp.bitwise_xor(place, offset) * size, size), size)
-        out_ref[:, :edge] = (keep0[lines, :] + got0[lines, :].astype(F32)).astype(out_ref.dtype)
-        out_ref[:, edge:] = (keep1[lines, :] + got1[lines, :].astype(F32)).astype(out_ref.dtype)
+        for tap, (keep_ref, got_ref) in enumerate(zip(keeps, others)):
+            value = keep_ref[lines, :] + got_ref[lines, :].astype(F32)
+            out_ref[:, tap * half : (tap + 1) * half] = value.astype(out_ref.dtype)
 
 
 def part_kernel(own_ref, got1, got2, small_ref, sum_ref, total_ref):
@@ -528,8 +522,9 @@
     dev_bits = members.bit_length() - 1
     grp_bits = groups_of.bit_length() - 1
 
-    offsets, waves = [0], [wave]
-    for bit in range(dev_bits - 1):
+    offsets = [0, 1, 2, 3]
+    waves = [wave] + [swap(wave, "dev", offset) for offset in offsets[1:]]
+    for bit in range(2, dev_bits - 1):
         offsets += [offset | (1 << bit) for offset in offsets]
         waves += [swap(held, "dev", 1 << bit) for held in waves]
     lens = lengths.reshape(1, members * rows)
@@ -569,7 +564,7 @@
     feat, even, odd, pre0, even_slope, odd_slope, mean, inv, patch, grad, grad_t, gain_in, w_in = call(
         functools.partial(forward_kernel, frames0, frames1, taps, places),
         [
-            ((frames1, rows, chans), BF16, "hbm"),
+            ((frames1, rows, chans), BF16),
             ((pad_frames + 1, rows, chans), BF16),
             ((pad_frames, rows, chans), BF16),
             ((groups, rows, GROUP * chans), F32),
@@ -592,40 +587,35 @@
             ((rows, chans), F32),
             (bias.shape, F32),
             (cot_t.shape, BF16),
-            (cot_t.shape, BF16),
             pltpu.SemaphoreType.DMA((4,)),
-            pltpu.SemaphoreType.DMA,
         ],
         outside=(4, 5, 6, 7),
     )
     half = chans // 2
     wide = taps_second * half
-    keep0, send0 = call(
-        functools.partial(outer_kernel, (0, 0)),
-        [((chans, 2 * half), F32), ((chans, 2 * half), BF16)],
-        [even, odd, grad_t],
-        flops=1 << 30,
-    )
-    got0 = swap(send0, "grp", 1)
-    keep1, send1 = call(
-        functools.partial(outer_kernel, (1,)),
-        [((chans, half), F32), ((chans, half), BF16)],
-        [even, grad_t],
-        flops=1 << 29,
-    )
-    got1 = swap(send1, "grp", 1)
+    keeps, others = [], []
+    for acts, skip in ((even, 0), (odd, 0), (even, 1)):
+        keep, send = call(
+            functools.partial(outer_kernel, skip),
+            [((chans, half), F32), ((chans, half), BF16)],
+            [acts, grad_t],
+            flops=1 << 29,
+        )
+        keeps.append(keep)
+        others.append(swap(send, "grp", 1))
     quarter = chans // 4
     own, *sends = call(
-        plane_kernel,
+        functools.partial(plane_kernel, taps_second),
         [((quarter, wide), F32)] + [((quarter, wide), BF16)] * 3,
-        [keep0, got0, keep1, got1],
+        [*keeps, *others],
     )
     gots = [swap(part, "dev", offset) for offset, part in enumerate(sends, 1)]
     evens, odds = (frames0 + 1) // 2, frames0 // 2
-    lift_even, lift_odd = call(
+    lift_even, lift_odd, features = call(
         input_kernel,
-        [((evens, rows, chans), F32), ((odds, rows, chans), F32)],
-        [grad, w_in, even_slope, odd_slope, own],
+        [((evens, rows, chans), F32), ((odds, rows, chans), F32), ((frames1, rows, chans), BF16, "hbm")],
+        [grad, w_in, even_slope, odd_slope, own, feat],
+        scratch=[pltpu.SemaphoreType.DMA],
         flops=1 << 30,
     )
     small, *smalls = call(
@@ -673,7 +663,7 @@
         [send, swap(send, "grp", 1)],
     )
     return (
-        feat.transpose(1, 0, 2),
+        features.transpose(1, 0, 2),
         grad_second.transpose(0, 2, 1),
         grad_first,
         grad_gain.reshape(size),

time: 56.1 us -> 56.5 us (level)
  waiting for transfers between devices: 14.8 us -> 18.1 us
  starting transfers between devices: 21.9 us -> 19.3 us
    ppermute x15 -> x16, waiting for transfers between devices: 14.8 us -> 18.1 us  [swap(): return lax.ppermute(value, axis, [(i, i ^ offset) for i in range(size)])]
    ppermute x15 -> x16, starting transfers between devices: 21.9 us -> 19.3 us  [swap(): return lax.ppermute(value, axis, [(i, i ^ offset) for i in range(size)])]
    pallas_call x13 -> x14, Pallas kernels: 18.4 us -> 18.1 us  [call(): pl.pallas_call(kernel, out_shape=[jax.ShapeDtypeStruct(out[0], out[1]) if...]
  transfers between devices with their start and end apart: 15 -> 16, of which waited for: 10 -> 12; matrix products, arithmetic and copies ran while one was open for 0% -> 0% of each run, Pallas kernels for 13% -> 11%
where the time goes in v7:
time: 56.5 us; the launch traced here: 56.3 us
  starting transfers between devices  19.3 us (34%)
  Pallas kernels  18.1 us (32%)
  waiting for transfers between devices  18.1 us (32%)
  between operations  0.74 us (1%)
    ppermute x16, starting transfers between devices, swap(): return lax.ppermute(value, axis, [(i, i ^ offset) for i in range(size)])  19.3 us
    ppermute x16, waiting for transfers between devices, swap(): return lax.ppermute(value, axis, [(i, i ^ offset) for i in range(size)])  18.1 us
    pallas_call x14, Pallas kernels, call(): pl.pallas_call(kernel, out_shape=[jax.ShapeDtypeStruct(out[0], out[1]) if...  18.1 us
  transfers between devices with their start and end apart: 16, of which 12 were waited for; matrix products, arithmetic and copies ran while one was open for 0% of the time, Pallas kernels for 11%

profile of v7, /device:TPU:0, one launch (start us, length us, event | category | flops | bytes accessed | tf_op | source)
XLA Modules:
  0.0 56.3 jit_solution(16366859525691183651)
XLA Ops:
  0.6 3.0 %collective-permute-start = (bf16[32,384]{1,0:T(8,128)(2,1)}, bf16[32,384]{1,0:T(8,128)(2,1)S(1)}, u32[]{:S(2)}, u32[]{:S(2)}) collective-permute-start(bf16[32,384]{1,0:T(8,128)(2,1)} %wave_hbm.1), channel_id=1, source_target_pairs={{0,1},{1,0},{2,3},{3,2},{4,5},{5,4},{6,7},{7,6},{8,9},{9,8},{10,11... | collective-permute-start | bytes 73736 | tf_op jit(solution)/shard_map/ppermute | solution.py:507
  3.6 1.5 %collective-permute-start.2 = (bf16[32,384]{1,0:T(8,128)(2,1)}, bf16[32,384]{1,0:T(8,128)(2,1)S(1)}, u32[]{:S(2)}, u32[]{:S(2)}) collective-permute-start(bf16[32,384]{1,0:T(8,128)(2,1)} %wave_hbm.1), channel_id=1, source_target_pairs={{0,3},{1,2},{2,1},{3,0},{4,7},{5,6},{6,5},{7,4},{8,11},{9,10},{10,... | collective-permute-start | bytes 73736 | tf_op jit(solution)/shard_map/ppermute | solution.py:507
  5.2 0.0 collective-permute-start.1
  5.2 1.3 %shard_map.119 = (s32[32,128]{1,0:T(8,128)S(1)}, bf16[128,4096]{1,0:T(8,128)(2,1)S(1)}, bf16[16,256]{1,0:T(8,128)(2,1)S(1)}, bf16[16,256]{1,0:T(8,128)(2,1)S(1)}, bf16[32,384]{1,0:T(8,128)(2,1)S(1)}) custom-call(s32[8,32]{1,0:T(8,128)} %order_hbm.1, s32[1,256]{1,0:T(1,128)} %bitcast.11, bf16[10,512]{1,0:T(8,128)(2,1)} %w_hbm.2, bf16[32,384]{1,0:T(8,128)(2,1)} %wave_hbm.1), custom_call_target="tpu_custom_call" | custom-call | tf_op jit(solution)/shard_map/pallas_call | solution.py:492
  6.5 0.0 collective-permute-done.refs_1_
  6.5 2.2 %collective-permute-done.2.refs_3_ = bf16[32,384]{1,0:T(8,128)(2,1)S(1)} collective-permute-done((bf16[32,384]{1,0:T(8,128)(2,1)}, bf16[32,384]{1,0:T(8,128)(2,1)S(1)}, u32[]{:S(2)}, u32[]{:S(2)}) %collective-permute-start.2) | collective-permute-done | bytes 24608 | tf_op jit(solution)/shard_map/ppermute | solution.py:507
  8.7 0.5 collective-permute-done.1.refs_2_
  9.2 0.2 shard_map.120
  9.4 2.6 %collective-permute-start.3 = (bf16[16,384]{1,0:T(8,128)(2,1)S(1)}, bf16[16,384]{1,0:T(8,128)(2,1)S(1)}, u32[]{:S(2)}, u32[]{:S(2)}) collective-permute-start(bf16[16,384]{1,0:T(8,128)(2,1)S(1)} %get-tuple-element.54), channel_id=1, source_target_pairs={{0,4},{1,5},{2,6},{3,7},{4,0},{5,1},{6,2},{7,3},{8,12},{9,13},{10,... | collective-permute-start | bytes 36872 | tf_op jit(solution)/shard_map/ppermute | solution.py:507
  12.1 2.0 %collective-permute-done.3.far_ref = bf16[16,384]{1,0:T(8,128)(2,1)S(1)} collective-permute-done((bf16[16,384]{1,0:T(8,128)(2,1)S(1)}, bf16[16,384]{1,0:T(8,128)(2,1)S(1)}, u32[]{:S(2)}, u32[]{:S(2)}) %collective-permute-start.3) | collective-permute-done | bytes 12320 | tf_op jit(solution)/shard_map/ppermute | solution.py:507
  14.1 8.0 %shard_map.121 = (bf16[37,32,512]{2,1,0:T(8,128)(2,1)S(1)}, bf16[41,32,512]{2,1,0:T(8,128)(2,1)S(1)}, bf16[40,32,512]{2,1,0:T(8,128)(2,1)S(1)}, f32[10,32,4096]{...) custom-call(bf16[16,384]{1,0:T(8,128)(2,1)S(1)} %get-tuple-element.5, ...), custom_call_target="tpu_custom_call" | custom-call | tf_op jit(solution)/shard_map/pallas_call | solution.py:492
  22.1 0.9 %shard_map.124 = (f32[512,256]{1,0:T(8,128)S(1)}, bf16[512,256]{1,0:T(8,128)(2,1)S(1)}) custom-call(bf16[41,32,512]{2,1,0:T(8,128)(2,1)S(1)} %get-tuple-element.61.act_ref, bf16[512,1280]{1,0:T(8,128)(2,1)S(1)} %get-tuple-element.62.grad_t_ref), custom_call_target="tpu_custom_call" | custom-call | flops 536870912 | tf_op jit(solution)/shard_map/pallas_call | solution.py:492
  23.0 0.9 %shard_map.122 = (f32[512,256]{1,0:T(8,128)S(1)}, bf16[512,256]{1,0:T(8,128)(2,1)S(1)}) custom-call(bf16[41,32,512]{2,1,0:T(8,128)(2,1)S(1)} %get-tuple-element.61.act_ref, bf16[512,1280]{1,0:T(8,128)(2,1)S(1)} %get-tuple-element.62.grad_t_ref), custom_call_target="tpu_custom_call" | custom-call | flops 536870912 | tf_op jit(solution)/shard_map/pallas_call | solution.py:492
  23.8 0.9 %shard_map.123 = (f32[512,256]{1,0:T(8,128)S(1)}, bf16[512,256]{1,0:T(8,128)(2,1)S(1)}) custom-call(bf16[40,32,512]{2,1,0:T(8,128)(2,1)S(1)} %get-tuple-element.64.act_ref, bf16[512,1280]{1,0:T(8,128)(2,1)S(1)} %get-tuple-element.62.grad_t_ref), custom_call_target="tpu_custom_call" | custom-call | flops 536870912 | tf_op jit(solution)/shard_map/pallas_call | solution.py:492
  24.7 0.1 collective-permute-start.5
  24.8 0.5 collective-permute-start.6
  25.3 0.1 collective-permute-start.4
  25.3 0.9 %collective-permute-done.5.refs_4_ = bf16[512,256]{1,0:T(8,128)(2,1)S(1)} collective-permute-done((bf16[512,256]{1,0:T(8,128)(2,1)S(1)}, bf16[512,256]{1,0:T(8,128)(2,1)S(1)}, u32[]{:S(2)}, u32[]{:S(2)}) %collective-permute-start.5) | collective-permute-done | bytes 262176 | tf_op jit(solution)/shard_map/ppermute | solution.py:507
  26.3 0.4 collective-permute-done.6.refs_5_
  26.7 0.4 collective-permute-done.4.refs_3_
  27.0 0.1 shard_map.125
  27.2 1.6 %collective-permute-start.7 = (bf16[128,768]{1,0:T(8,128)(2,1)S(1)}, bf16[128,768]{1,0:T(8,128)(2,1)S(1)}, u32[]{:S(2)}, u32[]{:S(2)}) collective-permute-start(bf16[128,768]{1,0:T(8,128)(2,1)S(1)} %get-tuple-element.73), channel_id=1, source_target_pairs={{0,1},{1,0},{2,3},{3,2},{4,5},{5,4},{6,7},{7,6},{8,9},{9,8},{10,11... | collective-permute-start | bytes 589832 | tf_op jit(solution)/shard_map/ppermute | solution.py:507
  28.8 0.4 collective-permute-start.8
  29.2 1.5 %collective-permute-start.9 = (bf16[128,768]{1,0:T(8,128)(2,1)S(1)}, bf16[128,768]{1,0:T(8,128)(2,1)S(1)}, u32[]{:S(2)}, u32[]{:S(2)}) collective-permute-start(bf16[128,768]{1,0:T(8,128)(2,1)S(1)} %get-tuple-element.84), channel_id=1, source_target_pairs={{0,3},{1,2},{2,1},{3,0},{4,7},{5,6},{6,5},{7,4},{8,11},{9,10},{10,... | collective-permute-start | bytes 589832 | tf_op jit(solution)/shard_map/ppermute | solution.py:507
  30.7 2.2 %shard_map.126 = (f32[38,32,512]{2,1,0:T(8,128)S(1)}, f32[37,32,512]{2,1,0:T(8,128)S(1)}, bf16[37,32,512]{2,1,0:T(8,128)(2,1)}) custom-call(bf16[39,32,512]{2,1,0:T(8,128)(2,1)S(1)} %get-tuple-element.57.grad_ref, bf16[3,512,512]{2,1,0:T(8,128)(2,1)S(1)} %get-tuple-element.58.w_ref, f32[40,32,512]{2,1,0:T(8,128)S(1)} %get-tuple-element.59.even_slope, ...), custom_call_target="tpu_custom_call" | custom-call | flops 1073741824 | tf_op jit(solution)/shard_map/pallas_call | solution.py:492
  33.0 2.7 %shard_map.127 = (f32[16,128]{1,0:T(8,128)S(1)}, f32[16,128]{1,0:T(8,128)S(1)}, f32[16,128]{1,0:T(8,128)S(1)}, f32[16,128]{1,0:T(8,128)S(1)}) custom-call(s32[32,128]{1,0:T(8,128)S(1)} %get-tuple-element.55.valid_ref, f32[10,32,4096]{2,1,0:T(8,128)S(1)} %get-tuple-element.75.pre0, f32[32,512]{1,0:T(8,128)S(1)} %get-tuple-element.76.mean_ref, ...), custom_call_target="tpu_custom_call" | custom-call | flops 4294967296 | tf_op jit(solution)/shard_map/pallas_call | solution.py:492
  35.7 1.0 %collective-permute-start.11 = (f32[16,128]{1,0:T(8,128)S(1)}, f32[16,128]{1,0:T(8,128)S(1)}, u32[]{:S(2)}, u32[]{:S(2)}) collective-permute-start(f32[16,128]{1,0:T(8,128)S(1)} %get-tuple-element.87), channel_id=1, source_target_pairs={{0,2},{1,3},{2,0},{3,1},{4,6},{5,7},{6,4},{7,5},{8,10},{9,11},{10,... | collective-permute-start | bytes 24584 | tf_op jit(solution)/shard_map/ppermute | solution.py:507
  36.7 2.0 %collective-permute-start.12 = (f32[16,128]{1,0:T(8,128)S(1)}, f32[16,128]{1,0:T(8,128)S(1)}, u32[]{:S(2)}, u32[]{:S(2)}) collective-permute-start(f32[16,128]{1,0:T(8,128)S(1)} %get-tuple-element.88), channel_id=1, source_target_pairs={{0,3},{1,2},{2,1},{3,0},{4,7},{5,6},{6,5},{7,4},{8,11},{9,10},{10,... | collective-permute-start | bytes 24584 | tf_op jit(solution)/shard_map/ppermute | solution.py:507
  38.7 0.0 collective-permute-done.7.got1
  38.7 0.0 collective-permute-done.8.got2
  38.7 0.1 shard_map.128
  38.8 0.6 %collective-permute-start.10 = (f32[16,128]{1,0:T(8,128)S(1)}, f32[16,128]{1,0:T(8,128)S(1)}, u32[]{:S(2)}, u32[]{:S(2)}) collective-permute-start(f32[16,128]{1,0:T(8,128)S(1)} %get-tuple-element.86), channel_id=1, source_target_pairs={{0,1},{1,0},{2,3},{3,2},{4,5},{5,4},{6,7},{7,6},{8,9},{9,8},{10,11... | collective-permute-start | bytes 24584 | tf_op jit(solution)/shard_map/ppermute | solution.py:507
  39.4 0.5 collective-permute-done.11.small2
  39.9 1.3 %collective-permute-done.12.small3 = f32[16,128]{1,0:T(8,128)S(1)} collective-permute-done((f32[16,128]{1,0:T(8,128)S(1)}, f32[16,128]{1,0:T(8,128)S(1)}, u32[]{:S(2)}, u32[]{:S(2)}) %collective-permute-start.12) | collective-permute-done | bytes 8224 | tf_op jit(solution)/shard_map/ppermute | solution.py:507
  41.2 0.0 collective-permute-done.9.got3
  41.2 1.3 %collective-permute-done.10.small1 = f32[16,128]{1,0:T(8,128)S(1)} collective-permute-done((f32[16,128]{1,0:T(8,128)S(1)}, f32[16,128]{1,0:T(8,128)S(1)}, u32[]{:S(2)}, u32[]{:S(2)}) %collective-permute-start.10) | collective-permute-done | bytes 8224 | tf_op jit(solution)/shard_map/ppermute | solution.py:507
  42.5 2.6 %collective-permute-start.13 = (bf16[80,640]{1,0:T(8,128)(2,1)S(1)}, bf16[80,640]{1,0:T(8,128)(2,1)S(1)}, u32[]{:S(2)}, u32[]{:S(2)}) collective-permute-start(bf16[80,640]{1,0:T(8,128)(2,1)S(1)} %get-tuple-element.90), channel_id=1, source_target_pairs={{0,4},{1,5},{2,6},{3,7},{4,0},{5,1},{6,2},{7,3},{8,12},{9,13},{10,... | collective-permute-start | bytes 307208 | tf_op jit(solution)/shard_map/ppermute | solution.py:507
  45.2 4.0 %collective-permute-done.13.got_ref = bf16[80,640]{1,0:T(8,128)(2,1)S(1)} collective-permute-done((bf16[80,640]{1,0:T(8,128)(2,1)S(1)}, bf16[80,640]{1,0:T(8,128)(2,1)S(1)}, u32[]{:S(2)}, u32[]{:S(2)}) %collective-permute-start.13) | collective-permute-done | bytes 102432 | tf_op jit(solution)/shard_map/ppermute | solution.py:507
  49.2 1.6 %collective-permute-start.14 = (bf16[80,640]{1,0:T(8,128)(2,1)S(1)}, bf16[80,640]{1,0:T(8,128)(2,1)S(1)}, u32[]{:S(2)}, u32[]{:S(2)}) collective-permute-start(bf16[80,640]{1,0:T(8,128)(2,1)S(1)} %shard_map.130.mine_ref), channel_id=1, source_target_pairs={{0,16},{8,24},{16,0},{24,8},{1,17},{9,25},{17,1},{25,9},{2,18},{10... | collective-permute-start | bytes 307208 | tf_op jit(solution)/shard_map/ppermute | solution.py:507
  50.7 3.1 %collective-permute-done.14.got_ref = bf16[80,640]{1,0:T(8,128)(2,1)S(1)} collective-permute-done((bf16[80,640]{1,0:T(8,128)(2,1)S(1)}, bf16[80,640]{1,0:T(8,128)(2,1)S(1)}, u32[]{:S(2)}, u32[]{:S(2)}) %collective-permute-start.14) | collective-permute-done | bytes 102432 | tf_op jit(solution)/shard_map/ppermute | solution.py:507
  53.9 0.1 collective-permute-start.15
  54.0 1.4 %collective-permute-done.15.other_ref = f32[80,640]{1,0:T(8,128)S(1)} collective-permute-done((f32[80,640]{1,0:T(8,128)S(1)}, f32[80,640]{1,0:T(8,128)S(1)}, u32[]{:S(2)}, u32[]{:S(2)}) %collective-permute-start.15) | collective-permute-done | bytes 204832 | tf_op jit(solution)/shard_map/ppermute | solution.py:507
  55.4 0.8 %shard_map.132 = (f32[3,64,512]{2,1,0:T(8,128)}, f32[10,64]{1,0:T(8,128)}, f32[1,64]{1,0:T(1,128)}, f32[1,64]{1,0:T(1,128)}) custom-call(f32[80,640]{1,0:T(8,128)S(1)} %shard_map.131.own_ref, f32[80,640]{1,0:T(8,128)S(1)} %collective-permute-done.15.other_ref), custom_call_target="tpu_custom_call" | custom-call | tf_op jit(solution)/shard_map/pallas_call | solution.py:492
  (3 shorter events, 0.1 us)
Async XLA Ops:
  0.6 5.9 %collective-permute-start = (bf16[32,384]{1,0:T(8,128)(2,1)}, bf16[32,384]{1,0:T(8,128)(2,1)S(1)}, u32[]{:S(2)}, u32[]{:S(2)}) collective-permute-start(bf16[32,384]{1,0:T(8,128)(2,1)} %wave_hbm.1), channel_id=1, source_target_pairs={{0,1},{1,0},{2,3},{3,2},{4,5},{5,4},{6,7},{7,6},{8,9},{9,8},{10,11... | collective-permute-start | bytes 73736 | tf_op jit(solution)/shard_map/ppermute | solution.py:507
  3.6 5.1 %collective-permute-start.2 = (bf16[32,384]{1,0:T(8,128)(2,1)}, bf16[32,384]{1,0:T(8,128)(2,1)S(1)}, u32[]{:S(2)}, u32[]{:S(2)}) collective-permute-start(bf16[32,384]{1,0:T(8,128)(2,1)} %wave_hbm.1), channel_id=1, source_target_pairs={{0,3},{1,2},{2,1},{3,0},{4,7},{5,6},{6,5},{7,4},{8,11},{9,10},{10,... | collective-permute-start | bytes 73736 | tf_op jit(solution)/shard_map/ppermute | solution.py:507
  5.2 4.0 %collective-permute-start.1 = (bf16[32,384]{1,0:T(8,128)(2,1)}, bf16[32,384]{1,0:T(8,128)(2,1)S(1)}, u32[]{:S(2)}, u32[]{:S(2)}) collective-permute-start(bf16[32,384]{1,0:T(8,128)(2,1)} %wave_hbm.1), channel_id=1, source_target_pairs={{0,2},{1,3},{2,0},{3,1},{4,6},{5,7},{6,4},{7,5},{8,10},{9,11},{10,... | collective-permute-start | bytes 73736 | tf_op jit(solution)/shard_map/ppermute | solution.py:507
  9.4 4.6 %collective-permute-start.3 = (bf16[16,384]{1,0:T(8,128)(2,1)S(1)}, bf16[16,384]{1,0:T(8,128)(2,1)S(1)}, u32[]{:S(2)}, u32[]{:S(2)}) collective-permute-start(bf16[16,384]{1,0:T(8,128)(2,1)S(1)} %get-tuple-element.54), channel_id=1, source_target_pairs={{0,4},{1,5},{2,6},{3,7},{4,0},{5,1},{6,2},{7,3},{8,12},{9,13},{10,... | collective-permute-start | bytes 36872 | tf_op jit(solution)/shard_map/ppermute | solution.py:507
  24.7 1.6 %collective-permute-start.5 = (bf16[512,256]{1,0:T(8,128)(2,1)S(1)}, bf16[512,256]{1,0:T(8,128)(2,1)S(1)}, u32[]{:S(2)}, u32[]{:S(2)}) collective-permute-start(bf16[512,256]{1,0:T(8,128)(2,1)S(1)} %get-tuple-element.68), channel_id=1, source_target_pairs={{0,8},{8,0},{16,24},{24,16},{1,9},{9,1},{17,25},{25,17},{2,10},{10... | collective-permute-start | bytes 786440 | tf_op jit(solution)/shard_map/ppermute | solution.py:507
  24.8 1.9 %collective-permute-start.6 = (bf16[512,256]{1,0:T(8,128)(2,1)S(1)}, bf16[512,256]{1,0:T(8,128)(2,1)S(1)}, u32[]{:S(2)}, u32[]{:S(2)}) collective-permute-start(bf16[512,256]{1,0:T(8,128)(2,1)S(1)} %get-tuple-element.69), channel_id=1, source_target_pairs={{0,8},{8,0},{16,24},{24,16},{1,9},{9,1},{17,25},{25,17},{2,10},{10... | collective-permute-start | bytes 786440 | tf_op jit(solution)/shard_map/ppermute | solution.py:507
  25.3 1.8 %collective-permute-start.4 = (bf16[512,256]{1,0:T(8,128)(2,1)S(1)}, bf16[512,256]{1,0:T(8,128)(2,1)S(1)}, u32[]{:S(2)}, u32[]{:S(2)}) collective-permute-start(bf16[512,256]{1,0:T(8,128)(2,1)S(1)} %get-tuple-element.67), channel_id=1, source_target_pairs={{0,8},{8,0},{16,24},{24,16},{1,9},{9,1},{17,25},{25,17},{2,10},{10... | collective-permute-start | bytes 786440 | tf_op jit(solution)/shard_map/ppermute | solution.py:507
  27.2 11.5 %collective-permute-start.7 = (bf16[128,768]{1,0:T(8,128)(2,1)S(1)}, bf16[128,768]{1,0:T(8,128)(2,1)S(1)}, u32[]{:S(2)}, u32[]{:S(2)}) collective-permute-start(bf16[128,768]{1,0:T(8,128)(2,1)S(1)} %get-tuple-element.73), channel_id=1, source_target_pairs={{0,1},{1,0},{2,3},{3,2},{4,5},{5,4},{6,7},{7,6},{8,9},{9,8},{10,11... | collective-permute-start | bytes 589832 | tf_op jit(solution)/shard_map/ppermute | solution.py:507
  28.8 10.0 %collective-permute-start.8 = (bf16[128,768]{1,0:T(8,128)(2,1)S(1)}, bf16[128,768]{1,0:T(8,128)(2,1)S(1)}, u32[]{:S(2)}, u32[]{:S(2)}) collective-permute-start(bf16[128,768]{1,0:T(8,128)(2,1)S(1)} %get-tuple-element.74), channel_id=1, source_target_pairs={{0,2},{1,3},{2,0},{3,1},{4,6},{5,7},{6,4},{7,5},{8,10},{9,11},{10,... | collective-permute-start | bytes 589832 | tf_op jit(solution)/shard_map/ppermute | solution.py:507
  29.2 12.0 %collective-permute-start.9 = (bf16[128,768]{1,0:T(8,128)(2,1)S(1)}, bf16[128,768]{1,0:T(8,128)(2,1)S(1)}, u32[]{:S(2)}, u32[]{:S(2)}) collective-permute-start(bf16[128,768]{1,0:T(8,128)(2,1)S(1)} %get-tuple-element.84), channel_id=1, source_target_pairs={{0,3},{1,2},{2,1},{3,0},{4,7},{5,6},{6,5},{7,4},{8,11},{9,10},{10,... | collective-permute-start | bytes 589832 | tf_op jit(solution)/shard_map/ppermute | solution.py:507
  35.7 4.2 %collective-permute-start.11 = (f32[16,128]{1,0:T(8,128)S(1)}, f32[16,128]{1,0:T(8,128)S(1)}, u32[]{:S(2)}, u32[]{:S(2)}) collective-permute-start(f32[16,128]{1,0:T(8,128)S(1)} %get-tuple-element.87), channel_id=1, source_target_pairs={{0,2},{1,3},{2,0},{3,1},{4,6},{5,7},{6,4},{7,5},{8,10},{9,11},{10,... | collective-permute-start | bytes 24584 | tf_op jit(solution)/shard_map/ppermute | solution.py:507
  36.7 4.5 %collective-permute-start.12 = (f32[16,128]{1,0:T(8,128)S(1)}, f32[16,128]{1,0:T(8,128)S(1)}, u32[]{:S(2)}, u32[]{:S(2)}) collective-permute-start(f32[16,128]{1,0:T(8,128)S(1)} %get-tuple-element.88), channel_id=1, source_target_pairs={{0,3},{1,2},{2,1},{3,0},{4,7},{5,6},{6,5},{7,4},{8,11},{9,10},{10,... | collective-permute-start | bytes 24584 | tf_op jit(solution)/shard_map/ppermute | solution.py:507
  38.8 3.7 %collective-permute-start.10 = (f32[16,128]{1,0:T(8,128)S(1)}, f32[16,128]{1,0:T(8,128)S(1)}, u32[]{:S(2)}, u32[]{:S(2)}) collective-permute-start(f32[16,128]{1,0:T(8,128)S(1)} %get-tuple-element.86), channel_id=1, source_target_pairs={{0,1},{1,0},{2,3},{3,2},{4,5},{5,4},{6,7},{7,6},{8,9},{9,8},{10,11... | collective-permute-start | bytes 24584 | tf_op jit(solution)/shard_map/ppermute | solution.py:507
  42.5 6.6 %collective-permute-start.13 = (bf16[80,640]{1,0:T(8,128)(2,1)S(1)}, bf16[80,640]{1,0:T(8,128)(2,1)S(1)}, u32[]{:S(2)}, u32[]{:S(2)}) collective-permute-start(bf16[80,640]{1,0:T(8,128)(2,1)S(1)} %get-tuple-element.90), channel_id=1, source_target_pairs={{0,4},{1,5},{2,6},{3,7},{4,0},{5,1},{6,2},{7,3},{8,12},{9,13},{10,... | collective-permute-start | bytes 307208 | tf_op jit(solution)/shard_map/ppermute | solution.py:507
  49.2 4.7 %collective-permute-start.14 = (bf16[80,640]{1,0:T(8,128)(2,1)S(1)}, bf16[80,640]{1,0:T(8,128)(2,1)S(1)}, u32[]{:S(2)}, u32[]{:S(2)}) collective-permute-start(bf16[80,640]{1,0:T(8,128)(2,1)S(1)} %shard_map.130.mine_ref), channel_id=1, source_target_pairs={{0,16},{8,24},{16,0},{24,8},{1,17},{9,25},{17,1},{25,9},{2,18},{10... | collective-permute-start | bytes 307208 | tf_op jit(solution)/shard_map/ppermute | solution.py:507
  53.9 1.5 %collective-permute-start.15 = (f32[80,640]{1,0:T(8,128)S(1)}, f32[80,640]{1,0:T(8,128)S(1)}, u32[]{:S(2)}, u32[]{:S(2)}) collective-permute-start(f32[80,640]{1,0:T(8,128)S(1)} %shard_map.131.own_ref), channel_id=1, source_target_pairs={{0,8},{8,0},{16,24},{24,16},{1,9},{9,1},{17,25},{25,17},{2,10},{10... | collective-permute-start | bytes 614408 | tf_op jit(solution)/shard_map/ppermute | solution.py:507

commit v8 on v7

--- a/solution.py
+++ b/solution.py
@@ -286,15 +286,17 @@
     turn(last, frames1 - last * half)
 
 
-def outer_kernel(skip, act_ref, grad_t_ref, keep_ref, send_ref):
-    rows, chans = act_ref.shape[1:]
+def outer_kernel(skips, *refs):
+    acts, (grad_t_ref, keep_ref, send_ref) = refs[:-3], refs[-3:]
+    rows, chans = acts[0].shape[1:]
     frames = grad_t_ref.shape[1] // rows
     half = chans // 2
     core = lax.rem(lax.axis_index("grp"), 2)
-    for side, out_ref in ((1 - core, send_ref), (core, keep_ref)):
-        lanes = pl.ds(pl.multiple_of(side * half, half), half)
-        acts = act_ref[skip : skip + frames, :, lanes].reshape(frames * rows, half)
-        out_ref[...] = dot(grad_t_ref[...], acts).astype(out_ref.dtype)
+    for tap, (act_ref, skip) in enumerate(zip(acts, skips)):
+        for side, out_ref in ((1 - core, send_ref), (core, keep_ref)):
+            lanes = pl.ds(pl.multiple_of(side * half, half), half)
+            value = dot(grad_t_ref[...], act_ref[skip : skip + frames, :, lanes].reshape(frames * rows, half))
+            out_ref[:, tap * half : (tap + 1) * half] = value.astype(out_ref.dtype)
 
 
 def input_kernel(grad_ref, w_ref, even_slope, odd_slope, after_ref, feat_ref, even_ref, odd_ref, feat_out, sem):
@@ -322,10 +324,7 @@
     even_ref,
     odd_ref,
     gain_ref,
-    mine_ref,
-    send1,
-    send2,
-    send3,
+    small_ref,
     dpre0,
     spread,
     out_ref,
@@ -399,20 +398,25 @@
         columns = [slice(first, first + size) for first in range(place * size, chans, 4 * size)]
         quarters[place] = jnp.concatenate([out_ref[:, part] for part in columns], axis=1)
     place = lax.rem(lax.axis_index("dev"), 4)
-    for offset, ref in enumerate((mine_ref, send1, send2, send3)):
-        ref[...] = quarters[jnp.bitwise_xor(place, offset)]
-
-
-def plane_kernel(second, *refs):
-    keeps, others, outs = refs[:second], refs[second : 2 * second], refs[2 * second :]
+    for offset in range(4):
+        small_ref[offset * 16 : (offset + 1) * 16] = quarters[jnp.bitwise_xor(place, offset)]
+
+
+def core_kernel(mine_ref, got_ref, *out_refs):
+    for place, ref in enumerate(out_refs):
+        lines = slice(place * 16, (place + 1) * 16)
+        ref[...] = mine_ref[lines] + got_ref[lines]
+
+
+def plane_kernel(*refs):
+    keeps, others, outs = refs[:2], refs[2:4], refs[4:]
     size = outs[0].shape[0]
-    half = keeps[0].shape[1]
+    edge = keeps[0].shape[1]
     place = lax.rem(lax.axis_index("dev"), 4)
     for offset, out_ref in enumerate(outs):
         lines = pl.ds(pl.multiple_of(jnp.bitwise_xor(place, offset) * size, size), size)
-        for tap, (keep_ref, got_ref) in enumerate(zip(keeps, others)):
-            value = keep_ref[lines, :] + got_ref[lines, :].astype(F32)
-            out_ref[:, tap * half : (tap + 1) * half] = value.astype(out_ref.dtype)
+        for lanes, keep_ref, got_ref in zip((slice(0, edge), slice(edge, None)), keeps, others):
+            out_ref[:, lanes] = (keep_ref[lines, :] + got_ref[lines, :].astype(F32)).astype(out_ref.dtype)
 
 
 def part_kernel(own_ref, got1, got2, small_ref, sum_ref, total_ref):
@@ -476,7 +480,7 @@
         for tap in range(second):
             lanes = pl.ds(pl.multiple_of(side * half, half), half)
             out_ref[tap, :, lanes] = value[:, tap * half : (tap + 1) * half]
-    total = own_ref[size:, -128:] + other_ref[size:, -128:]
+    total = jnp.where(core == 1, own_ref[size:, -128:], other_ref[size:, -128:])
     value = total[:, :size]
     for place in range(1, 128 // size):
         mine = lax.axis_index("dev") // 4 == place
@@ -505,6 +509,16 @@
 def swap(value, axis, offset):
     size = lax.axis_size(axis)
     return lax.ppermute(value, axis, [(i, i ^ offset) for i in range(size)])
+
+
+def second_swap(value, offset):
+    members = lax.axis_size("dev")
+    pairs = [
+        (grp * members + dev, grp * members + (dev ^ offset))
+        for grp in range(1, lax.axis_size("grp"), 2)
+        for dev in range(members)
+    ]
+    return lax.ppermute(value, ("grp", "dev"), pairs)
 
 
 def shards(wave, lengths, order, w_first, norm_gain, norm_bias, w_second, cot):
@@ -594,18 +608,16 @@
     half = chans // 2
     wide = taps_second * half
     keeps, others = [], []
-    for acts, skip in ((even, 0), (odd, 0), (even, 1)):
+    for acts, skips in (((even, odd), (0, 0)), ((even,), (1,))):
+        shape = (chans, len(acts) * half)
         keep, send = call(
-            functools.partial(outer_kernel, skip),
-            [((chans, half), F32), ((chans, half), BF16)],
-            [acts, grad_t],
-            flops=1 << 29,
+            functools.partial(outer_kernel, skips), [(shape, F32), (shape, BF16)], [*acts, grad_t], flops=len(acts) << 29
         )
         keeps.append(keep)
         others.append(swap(send, "grp", 1))
     quarter = chans // 4
     own, *sends = call(
-        functools.partial(plane_kernel, taps_second),
+        plane_kernel,
         [((quarter, wide), F32)] + [((quarter, wide), BF16)] * 3,
         [*keeps, *others],
     )
@@ -618,9 +630,9 @@
         scratch=[pltpu.SemaphoreType.DMA],
         flops=1 << 30,
     )
-    small, *smalls = call(
+    parts = call(
         functools.partial(backward_kernel, frames0, taps),
-        [((16, quarter), F32)] * 4,
+        [((64, quarter), F32)],
         [valid, pre0, mean, inv, patch, lift_even, lift_odd, gain_in],
         scratch=[
             ((groups, rows, GROUP * width), BF16),
@@ -629,12 +641,13 @@
             ((4, 16, quarter), F32),
         ],
         flops=1 << 32,
-    )
-    small3, small2 = swap(smalls[2], "dev", 3), swap(smalls[1], "dev", 2)
+    )[0]
+    small, *smalls = call(core_kernel, [((16, quarter), F32)] * 4, [parts, swap(parts, "grp", 1)])
+    small3, small2 = second_swap(smalls[2], 3), second_swap(smalls[1], 2)
     own, first = call(
         part_kernel, [((quarter, wide), F32), (small.shape, F32)], [own, gots[0], gots[1], smalls[0]]
     )
-    small1 = swap(first, "dev", 1)
+    small1 = second_swap(first, 1)
     size = quarter // 2
     keep, send = call(
         functools.partial(gather_kernel, dev_bits - 1),

time: 56.5 us -> 58.4 us (1.034)
  starting transfers between devices: 19.3 us -> 23.4 us
  waiting for transfers between devices: 18.1 us -> 16.1 us
    ppermute x16 -> x13, starting transfers between devices: 19.3 us -> 21.4 us  [swap(): return lax.ppermute(value, axis, [(i, i ^ offset) for i in range(size)])]
    ppermute x16 -> x13, waiting for transfers between devices: 18.1 us -> 16.1 us  [swap(): return lax.ppermute(value, axis, [(i, i ^ offset) for i in range(size)])]
    ppermute x0 -> x3, starting transfers between devices: none -> 1.97 us  [second_swap(): return lax.ppermute(value, ('grp', 'dev'), pairs)]
  transfers between devices with their start and end apart: 16 -> 16, of which waited for: 12 -> 9; matrix products, arithmetic and copies ran while one was open for 0% -> 0% of each run, Pallas kernels for 11% -> 12%
where the time goes in v8:
time: 58.4 us; the launch traced here: 58.2 us
  starting transfers between devices  23.4 us (40%)
  Pallas kernels  17.9 us (31%)
  waiting for transfers between devices  16.1 us (28%)
  between operations  0.8 us (1%)
    ppermute x13, starting transfers between devices, swap(): return lax.ppermute(value, axis, [(i, i ^ offset) for i in range(size)])  21.4 us
    pallas_call x14, Pallas kernels, call(): pl.pallas_call(kernel, out_shape=[jax.ShapeDtypeStruct(out[0], out[1]) if...  17.9 us
    ppermute x13, waiting for transfers between devices, swap(): return lax.ppermute(value, axis, [(i, i ^ offset) for i in range(size)])  16.1 us
    ppermute x3, starting transfers between devices, second_swap(): return lax.ppermute(value, ('grp', 'dev'), pairs)  1.97 us
  transfers between devices with their start and end apart: 16, of which 9 were waited for; matrix products, arithmetic and copies ran while one was open for 0% of the time, Pallas kernels for 12%

profile of v8, /device:TPU:0, one launch (start us, length us, event | category | flops | bytes accessed | tf_op | source)
XLA Modules:
  0.0 58.2 jit_solution(15863292893335188562)
XLA Ops:
  0.6 3.0 %collective-permute-start = (bf16[32,384]{1,0:T(8,128)(2,1)}, bf16[32,384]{1,0:T(8,128)(2,1)S(1)}, u32[]{:S(2)}, u32[]{:S(2)}) collective-permute-start(bf16[32,384]{1,0:T(8,128)(2,1)} %wave_hbm.1), channel_id=1, source_target_pairs={{0,1},{1,0},{2,3},{3,2},{4,5},{5,4},{6,7},{7,6},{8,9},{9,8},{10,11... | collective-permute-start | bytes 73736 | tf_op jit(solution)/shard_map/ppermute | solution.py:511
  3.6 1.5 %collective-permute-start.2 = (bf16[32,384]{1,0:T(8,128)(2,1)}, bf16[32,384]{1,0:T(8,128)(2,1)S(1)}, u32[]{:S(2)}, u32[]{:S(2)}) collective-permute-start(bf16[32,384]{1,0:T(8,128)(2,1)} %wave_hbm.1), channel_id=1, source_target_pairs={{0,3},{1,2},{2,1},{3,0},{4,7},{5,6},{6,5},{7,4},{8,11},{9,10},{10,... | collective-permute-start | bytes 73736 | tf_op jit(solution)/shard_map/ppermute | solution.py:511
  5.2 0.0 collective-permute-start.1
  5.2 1.3 %shard_map.119 = (s32[32,128]{1,0:T(8,128)S(1)}, bf16[128,4096]{1,0:T(8,128)(2,1)S(1)}, bf16[16,256]{1,0:T(8,128)(2,1)S(1)}, bf16[16,256]{1,0:T(8,128)(2,1)S(1)}, bf16[32,384]{1,0:T(8,128)(2,1)S(1)}) custom-call(s32[8,32]{1,0:T(8,128)} %order_hbm.1, s32[1,256]{1,0:T(1,128)} %bitcast.11, bf16[10,512]{1,0:T(8,128)(2,1)} %w_hbm.2, bf16[32,384]{1,0:T(8,128)(2,1)} %wave_hbm.1), custom_call_target="tpu_custom_call" | custom-call | tf_op jit(solution)/shard_map/pallas_call | solution.py:496
  6.5 0.0 collective-permute-done.refs_1_
  6.5 2.2 %collective-permute-done.2.refs_3_ = bf16[32,384]{1,0:T(8,128)(2,1)S(1)} collective-permute-done((bf16[32,384]{1,0:T(8,128)(2,1)}, bf16[32,384]{1,0:T(8,128)(2,1)S(1)}, u32[]{:S(2)}, u32[]{:S(2)}) %collective-permute-start.2) | collective-permute-done | bytes 24608 | tf_op jit(solution)/shard_map/ppermute | solution.py:511
  8.7 0.5 collective-permute-done.1.refs_2_
  9.2 0.2 shard_map.120
  9.4 2.6 %collective-permute-start.3 = (bf16[16,384]{1,0:T(8,128)(2,1)S(1)}, bf16[16,384]{1,0:T(8,128)(2,1)S(1)}, u32[]{:S(2)}, u32[]{:S(2)}) collective-permute-start(bf16[16,384]{1,0:T(8,128)(2,1)S(1)} %get-tuple-element.52), channel_id=1, source_target_pairs={{0,4},{1,5},{2,6},{3,7},{4,0},{5,1},{6,2},{7,3},{8,12},{9,13},{10,... | collective-permute-start | bytes 36872 | tf_op jit(solution)/shard_map/ppermute | solution.py:511
  12.1 2.0 %collective-permute-done.3.far_ref = bf16[16,384]{1,0:T(8,128)(2,1)S(1)} collective-permute-done((bf16[16,384]{1,0:T(8,128)(2,1)S(1)}, bf16[16,384]{1,0:T(8,128)(2,1)S(1)}, u32[]{:S(2)}, u32[]{:S(2)}) %collective-permute-start.3) | collective-permute-done | bytes 12320 | tf_op jit(solution)/shard_map/ppermute | solution.py:511
  14.1 8.0 %shard_map.121 = (bf16[37,32,512]{2,1,0:T(8,128)(2,1)S(1)}, bf16[41,32,512]{2,1,0:T(8,128)(2,1)S(1)}, bf16[40,32,512]{2,1,0:T(8,128)(2,1)S(1)}, f32[10,32,4096]{...) custom-call(bf16[16,384]{1,0:T(8,128)(2,1)S(1)} %get-tuple-element.5, ...), custom_call_target="tpu_custom_call" | custom-call | tf_op jit(solution)/shard_map/pallas_call | solution.py:496
  22.1 1.5 %shard_map.122 = (f32[512,512]{1,0:T(8,128)S(1)}, bf16[512,512]{1,0:T(8,128)(2,1)S(1)}) custom-call(bf16[41,32,512]{2,1,0:T(8,128)(2,1)S(1)} %get-tuple-element.59.refs_0_, bf16[40,32,512]{2,1,0:T(8,128)(2,1)S(1)} %get-tuple-element.60.refs_1_, bf16[512,1280]{1,0:T(8,128)(2,1)S(1)} %get-tuple-element.61.refs_2_.refs_1_), custom_call_target="tpu_custom_call" | custom-call | flops 1073741824 | tf_op jit(solution)/shard_map/pallas_call | solution.py:496
  23.6 0.1 collective-permute-start.4
  23.7 0.9 %shard_map.123 = (f32[512,256]{1,0:T(8,128)S(1)}, bf16[512,256]{1,0:T(8,128)(2,1)S(1)}) custom-call(bf16[41,32,512]{2,1,0:T(8,128)(2,1)S(1)} %get-tuple-element.59.refs_0_, bf16[512,1280]{1,0:T(8,128)(2,1)S(1)} %get-tuple-element.61.refs_2_.refs_1_), custom_call_target="tpu_custom_call" | custom-call | flops 536870912 | tf_op jit(solution)/shard_map/pallas_call | solution.py:496
  24.6 0.5 collective-permute-start.5
  25.1 1.2 %collective-permute-done.5.refs_3_ = bf16[512,256]{1,0:T(8,128)(2,1)S(1)} collective-permute-done((bf16[512,256]{1,0:T(8,128)(2,1)S(1)}, bf16[512,256]{1,0:T(8,128)(2,1)S(1)}, u32[]{:S(2)}, u32[]{:S(2)}) %collective-permute-start.5) | collective-permute-done | bytes 262176 | tf_op jit(solution)/shard_map/ppermute | solution.py:511
  26.3 0.0 collective-permute-done.4.refs_2_
  26.3 0.1 shard_map.124
  26.4 1.6 %collective-permute-start.6 = (bf16[128,768]{1,0:T(8,128)(2,1)S(1)}, bf16[128,768]{1,0:T(8,128)(2,1)S(1)}, u32[]{:S(2)}, u32[]{:S(2)}) collective-permute-start(bf16[128,768]{1,0:T(8,128)(2,1)S(1)} %get-tuple-element.69), channel_id=1, source_target_pairs={{0,1},{1,0},{2,3},{3,2},{4,5},{5,4},{6,7},{7,6},{8,9},{9,8},{10,11... | collective-permute-start | bytes 589832 | tf_op jit(solution)/shard_map/ppermute | solution.py:511
  28.0 0.4 collective-permute-start.7
  28.4 1.5 %collective-permute-start.9 = (bf16[128,768]{1,0:T(8,128)(2,1)S(1)}, bf16[128,768]{1,0:T(8,128)(2,1)S(1)}, u32[]{:S(2)}, u32[]{:S(2)}) collective-permute-start(bf16[128,768]{1,0:T(8,128)(2,1)S(1)} %get-tuple-element.80), channel_id=1, source_target_pairs={{0,3},{1,2},{2,1},{3,0},{4,7},{5,6},{6,5},{7,4},{8,11},{9,10},{10,... | collective-permute-start | bytes 589832 | tf_op jit(solution)/shard_map/ppermute | solution.py:511
  30.0 2.2 %shard_map.125 = (f32[38,32,512]{2,1,0:T(8,128)S(1)}, f32[37,32,512]{2,1,0:T(8,128)S(1)}, bf16[37,32,512]{2,1,0:T(8,128)(2,1)}) custom-call(bf16[39,32,512]{2,1,0:T(8,128)(2,1)S(1)} %get-tuple-element.55.grad_ref, bf16[3,512,512]{2,1,0:T(8,128)(2,1)S(1)} %get-tuple-element.56.w_ref, f32[40,32,512]{2,1,0:T(8,128)S(1)} %get-tuple-element.57.even_slope, ...), custom_call_target="tpu_custom_call" | custom-call | flops 1073741824 | tf_op jit(solution)/shard_map/pallas_call | solution.py:496
  32.2 2.7 %shard_map.126.mine_ref = f32[64,128]{1,0:T(8,128)S(1)} custom-call(s32[32,128]{1,0:T(8,128)S(1)} %get-tuple-element.53.valid_ref, f32[10,32,4096]{2,1,0:T(8,128)S(1)} %get-tuple-element.71.pre0, f32[32,512]{1,0:T(8,128)S(1)} %get-tuple-element.72.mean_ref, f32[32,512]{1,0:T(8,128)S(1)} %get-tuple-element.73.inv_ref, ...), custom_call_target="tpu_custom_call" | custom-call | flops 4294967296 | tf_op jit(solution)/shard_map/pallas_call | solution.py:496
  34.9 0.1 collective-permute-start.8
  35.0 1.2 %collective-permute-done.8.got_ref = f32[64,128]{1,0:T(8,128)S(1)} collective-permute-done((f32[64,128]{1,0:T(8,128)S(1)}, f32[64,128]{1,0:T(8,128)S(1)}, u32[]{:S(2)}, u32[]{:S(2)}) %collective-permute-start.8) | collective-permute-done | bytes 32800 | tf_op jit(solution)/shard_map/ppermute | solution.py:511
  36.2 0.7 %collective-permute-start.11 = (f32[16,128]{1,0:T(8,128)S(1)}, f32[16,128]{1,0:T(8,128)S(1)}, u32[]{:S(2)}, u32[]{:S(2)}) collective-permute-start(f32[16,128]{1,0:T(8,128)S(1)} %get-tuple-element.83), channel_id=1, source_target_pairs={{8,10},{9,11},{10,8},{11,9},{12,14},{13,15},{14,12},{15,13},{24,26... | collective-permute-start | bytes 24584 | tf_op jit(solution)/shard_map/ppermute | solution.py:521
  36.9 0.7 %collective-permute-start.12 = (f32[16,128]{1,0:T(8,128)S(1)}, f32[16,128]{1,0:T(8,128)S(1)}, u32[]{:S(2)}, u32[]{:S(2)}) collective-permute-start(f32[16,128]{1,0:T(8,128)S(1)} %get-tuple-element.84), channel_id=1, source_target_pairs={{8,11},{9,10},{10,9},{11,8},{12,15},{13,14},{14,13},{15,12},{24,27... | collective-permute-start | bytes 24584 | tf_op jit(solution)/shard_map/ppermute | solution.py:521
  37.5 0.0 collective-permute-done.6.got1
  37.5 0.0 collective-permute-done.7.got2
  37.6 0.1 shard_map.128
  37.6 0.7 %collective-permute-start.10 = (f32[16,128]{1,0:T(8,128)S(1)}, f32[16,128]{1,0:T(8,128)S(1)}, u32[]{:S(2)}, u32[]{:S(2)}) collective-permute-start(f32[16,128]{1,0:T(8,128)S(1)} %get-tuple-element.82), channel_id=1, source_target_pairs={{8,9},{9,8},{10,11},{11,10},{12,13},{13,12},{14,15},{15,14},{24,25... | collective-permute-start | bytes 24584 | tf_op jit(solution)/shard_map/ppermute | solution.py:521
  38.3 0.0 collective-permute-done.11.small2
  38.3 0.0 collective-permute-done.12.small3
  38.3 0.7 %collective-permute-done.9.got3 = bf16[128,768]{1,0:T(8,128)(2,1)S(1)} collective-permute-done((bf16[128,768]{1,0:T(8,128)(2,1)S(1)}, bf16[128,768]{1,0:T(8,128)(2,1)S(1)}, u32[]{:S(2)}, u32[]{:S(2)}) %collective-permute-start.9) | collective-permute-done | bytes 196640 | tf_op jit(solution)/shard_map/ppermute | solution.py:511
  39.1 0.0 collective-permute-done.10.small1
  39.1 2.7 %collective-permute-start.13 = (bf16[80,640]{1,0:T(8,128)(2,1)S(1)}, bf16[80,640]{1,0:T(8,128)(2,1)S(1)}, u32[]{:S(2)}, u32[]{:S(2)}) collective-permute-start(bf16[80,640]{1,0:T(8,128)(2,1)S(1)} %get-tuple-element.86), channel_id=1, source_target_pairs={{0,4},{1,5},{2,6},{3,7},{4,0},{5,1},{6,2},{7,3},{8,12},{9,13},{10,... | collective-permute-start | bytes 307208 | tf_op jit(solution)/shard_map/ppermute | solution.py:511
  41.8 4.1 %collective-permute-done.13.got_ref = bf16[80,640]{1,0:T(8,128)(2,1)S(1)} collective-permute-done((bf16[80,640]{1,0:T(8,128)(2,1)S(1)}, bf16[80,640]{1,0:T(8,128)(2,1)S(1)}, u32[]{:S(2)}, u32[]{:S(2)}) %collective-permute-start.13) | collective-permute-done | bytes 102432 | tf_op jit(solution)/shard_map/ppermute | solution.py:511
  45.9 1.6 %collective-permute-start.14 = (bf16[80,640]{1,0:T(8,128)(2,1)S(1)}, bf16[80,640]{1,0:T(8,128)(2,1)S(1)}, u32[]{:S(2)}, u32[]{:S(2)}) collective-permute-start(bf16[80,640]{1,0:T(8,128)(2,1)S(1)} %shard_map.130.mine_ref), channel_id=1, source_target_pairs={{0,16},{8,24},{16,0},{24,8},{1,17},{9,25},{17,1},{25,9},{2,18},{10... | collective-permute-start | bytes 307208 | tf_op jit(solution)/shard_map/ppermute | solution.py:511
  47.4 3.1 %collective-permute-done.14.got_ref = bf16[80,640]{1,0:T(8,128)(2,1)S(1)} collective-permute-done((bf16[80,640]{1,0:T(8,128)(2,1)S(1)}, bf16[80,640]{1,0:T(8,128)(2,1)S(1)}, u32[]{:S(2)}, u32[]{:S(2)}) %collective-permute-start.14) | collective-permute-done | bytes 102432 | tf_op jit(solution)/shard_map/ppermute | solution.py:511
  50.6 5.7 %collective-permute-start.15 = (f32[80,640]{1,0:T(8,128)S(1)}, f32[80,640]{1,0:T(8,128)S(1)}, u32[]{:S(2)}, u32[]{:S(2)}) collective-permute-start(f32[80,640]{1,0:T(8,128)S(1)} %shard_map.131.own_ref), channel_id=1, source_target_pairs={{0,8},{8,0},{16,24},{24,16},{1,9},{9,1},{17,25},{25,17},{2,10},{10... | collective-permute-start | bytes 614408 | tf_op jit(solution)/shard_map/ppermute | solution.py:511
  56.3 1.1 %collective-permute-done.15.other_ref = f32[80,640]{1,0:T(8,128)S(1)} collective-permute-done((f32[80,640]{1,0:T(8,128)S(1)}, f32[80,640]{1,0:T(8,128)S(1)}, u32[]{:S(2)}, u32[]{:S(2)}) %collective-permute-start.15) | collective-permute-done | bytes 204832 | tf_op jit(solution)/shard_map/ppermute | solution.py:511
  57.4 0.8 %shard_map.132 = (f32[3,64,512]{2,1,0:T(8,128)}, f32[10,64]{1,0:T(8,128)}, f32[1,64]{1,0:T(1,128)}, f32[1,64]{1,0:T(1,128)}) custom-call(f32[80,640]{1,0:T(8,128)S(1)} %shard_map.131.own_ref, f32[80,640]{1,0:T(8,128)S(1)} %collective-permute-done.15.other_ref), custom_call_target="tpu_custom_call" | custom-call | tf_op jit(solution)/shard_map/pallas_call | solution.py:496
  (4 shorter events, 0.1 us)
Async XLA Ops:
  0.6 5.9 %collective-permute-start = (bf16[32,384]{1,0:T(8,128)(2,1)}, bf16[32,384]{1,0:T(8,128)(2,1)S(1)}, u32[]{:S(2)}, u32[]{:S(2)}) collective-permute-start(bf16[32,384]{1,0:T(8,128)(2,1)} %wave_hbm.1), channel_id=1, source_target_pairs={{0,1},{1,0},{2,3},{3,2},{4,5},{5,4},{6,7},{7,6},{8,9},{9,8},{10,11... | collective-permute-start | bytes 73736 | tf_op jit(solution)/shard_map/ppermute | solution.py:511
  3.6 5.1 %collective-permute-start.2 = (bf16[32,384]{1,0:T(8,128)(2,1)}, bf16[32,384]{1,0:T(8,128)(2,1)S(1)}, u32[]{:S(2)}, u32[]{:S(2)}) collective-permute-start(bf16[32,384]{1,0:T(8,128)(2,1)} %wave_hbm.1), channel_id=1, source_target_pairs={{0,3},{1,2},{2,1},{3,0},{4,7},{5,6},{6,5},{7,4},{8,11},{9,10},{10,... | collective-permute-start | bytes 73736 | tf_op jit(solution)/shard_map/ppermute | solution.py:511
  5.2 4.0 %collective-permute-start.1 = (bf16[32,384]{1,0:T(8,128)(2,1)}, bf16[32,384]{1,0:T(8,128)(2,1)S(1)}, u32[]{:S(2)}, u32[]{:S(2)}) collective-permute-start(bf16[32,384]{1,0:T(8,128)(2,1)} %wave_hbm.1), channel_id=1, source_target_pairs={{0,2},{1,3},{2,0},{3,1},{4,6},{5,7},{6,4},{7,5},{8,10},{9,11},{10,... | collective-permute-start | bytes 73736 | tf_op jit(solution)/shard_map/ppermute | solution.py:511
  9.4 4.6 %collective-permute-start.3 = (bf16[16,384]{1,0:T(8,128)(2,1)S(1)}, bf16[16,384]{1,0:T(8,128)(2,1)S(1)}, u32[]{:S(2)}, u32[]{:S(2)}) collective-permute-start(bf16[16,384]{1,0:T(8,128)(2,1)S(1)} %get-tuple-element.52), channel_id=1, source_target_pairs={{0,4},{1,5},{2,6},{3,7},{4,0},{5,1},{6,2},{7,3},{8,12},{9,13},{10,... | collective-permute-start | bytes 36872 | tf_op jit(solution)/shard_map/ppermute | solution.py:511
  23.6 2.7 %collective-permute-start.4 = (bf16[512,512]{1,0:T(8,128)(2,1)S(1)}, bf16[512,512]{1,0:T(8,128)(2,1)S(1)}, u32[]{:S(2)}, u32[]{:S(2)}) collective-permute-start(bf16[512,512]{1,0:T(8,128)(2,1)S(1)} %get-tuple-element.64), channel_id=1, source_target_pairs={{0,8},{8,0},{16,24},{24,16},{1,9},{9,1},{17,25},{25,17},{2,10},{10... | collective-permute-start | bytes 1572872 | tf_op jit(solution)/shard_map/ppermute | solution.py:511
  24.6 1.7 %collective-permute-start.5 = (bf16[512,256]{1,0:T(8,128)(2,1)S(1)}, bf16[512,256]{1,0:T(8,128)(2,1)S(1)}, u32[]{:S(2)}, u32[]{:S(2)}) collective-permute-start(bf16[512,256]{1,0:T(8,128)(2,1)S(1)} %get-tuple-element.65), channel_id=1, source_target_pairs={{0,8},{8,0},{16,24},{24,16},{1,9},{9,1},{17,25},{25,17},{2,10},{10... | collective-permute-start | bytes 786440 | tf_op jit(solution)/shard_map/ppermute | solution.py:511
  26.4 11.1 %collective-permute-start.6 = (bf16[128,768]{1,0:T(8,128)(2,1)S(1)}, bf16[128,768]{1,0:T(8,128)(2,1)S(1)}, u32[]{:S(2)}, u32[]{:S(2)}) collective-permute-start(bf16[128,768]{1,0:T(8,128)(2,1)S(1)} %get-tuple-element.69), channel_id=1, source_target_pairs={{0,1},{1,0},{2,3},{3,2},{4,5},{5,4},{6,7},{7,6},{8,9},{9,8},{10,11... | collective-permute-start | bytes 589832 | tf_op jit(solution)/shard_map/ppermute | solution.py:511
  28.0 9.5 %collective-permute-start.7 = (bf16[128,768]{1,0:T(8,128)(2,1)S(1)}, bf16[128,768]{1,0:T(8,128)(2,1)S(1)}, u32[]{:S(2)}, u32[]{:S(2)}) collective-permute-start(bf16[128,768]{1,0:T(8,128)(2,1)S(1)} %get-tuple-element.70), channel_id=1, source_target_pairs={{0,2},{1,3},{2,0},{3,1},{4,6},{5,7},{6,4},{7,5},{8,10},{9,11},{10,... | collective-permute-start | bytes 589832 | tf_op jit(solution)/shard_map/ppermute | solution.py:511
  28.4 10.6 %collective-permute-start.9 = (bf16[128,768]{1,0:T(8,128)(2,1)S(1)}, bf16[128,768]{1,0:T(8,128)(2,1)S(1)}, u32[]{:S(2)}, u32[]{:S(2)}) collective-permute-start(bf16[128,768]{1,0:T(8,128)(2,1)S(1)} %get-tuple-element.80), channel_id=1, source_target_pairs={{0,3},{1,2},{2,1},{3,0},{4,7},{5,6},{6,5},{7,4},{8,11},{9,10},{10,... | collective-permute-start | bytes 589832 | tf_op jit(solution)/shard_map/ppermute | solution.py:511
  34.9 1.3 %collective-permute-start.8 = (f32[64,128]{1,0:T(8,128)S(1)}, f32[64,128]{1,0:T(8,128)S(1)}, u32[]{:S(2)}, u32[]{:S(2)}) collective-permute-start(f32[64,128]{1,0:T(8,128)S(1)} %shard_map.126.mine_ref), channel_id=1, source_target_pairs={{0,8},{8,0},{16,24},{24,16},{1,9},{9,1},{17,25},{25,17},{2,10},{10... | collective-permute-start | bytes 98312 | tf_op jit(solution)/shard_map/ppermute | solution.py:511
  36.2 2.1 %collective-permute-start.11 = (f32[16,128]{1,0:T(8,128)S(1)}, f32[16,128]{1,0:T(8,128)S(1)}, u32[]{:S(2)}, u32[]{:S(2)}) collective-permute-start(f32[16,128]{1,0:T(8,128)S(1)} %get-tuple-element.83), channel_id=1, source_target_pairs={{8,10},{9,11},{10,8},{11,9},{12,14},{13,15},{14,12},{15,13},{24,26... | collective-permute-start | bytes 24584 | tf_op jit(solution)/shard_map/ppermute | solution.py:521
  36.9 1.4 %collective-permute-start.12 = (f32[16,128]{1,0:T(8,128)S(1)}, f32[16,128]{1,0:T(8,128)S(1)}, u32[]{:S(2)}, u32[]{:S(2)}) collective-permute-start(f32[16,128]{1,0:T(8,128)S(1)} %get-tuple-element.84), channel_id=1, source_target_pairs={{8,11},{9,10},{10,9},{11,8},{12,15},{13,14},{14,13},{15,12},{24,27... | collective-permute-start | bytes 24584 | tf_op jit(solution)/shard_map/ppermute | solution.py:521
  37.6 1.4 %collective-permute-start.10 = (f32[16,128]{1,0:T(8,128)S(1)}, f32[16,128]{1,0:T(8,128)S(1)}, u32[]{:S(2)}, u32[]{:S(2)}) collective-permute-start(f32[16,128]{1,0:T(8,128)S(1)} %get-tuple-element.82), channel_id=1, source_target_pairs={{8,9},{9,8},{10,11},{11,10},{12,13},{13,12},{14,15},{15,14},{24,25... | collective-permute-start | bytes 24584 | tf_op jit(solution)/shard_map/ppermute | solution.py:521
  39.1 6.7 %collective-permute-start.13 = (bf16[80,640]{1,0:T(8,128)(2,1)S(1)}, bf16[80,640]{1,0:T(8,128)(2,1)S(1)}, u32[]{:S(2)}, u32[]{:S(2)}) collective-permute-start(bf16[80,640]{1,0:T(8,128)(2,1)S(1)} %get-tuple-element.86), channel_id=1, source_target_pairs={{0,4},{1,5},{2,6},{3,7},{4,0},{5,1},{6,2},{7,3},{8,12},{9,13},{10,... | collective-permute-start | bytes 307208 | tf_op jit(solution)/shard_map/ppermute | solution.py:511
  45.9 4.7 %collective-permute-start.14 = (bf16[80,640]{1,0:T(8,128)(2,1)S(1)}, bf16[80,640]{1,0:T(8,128)(2,1)S(1)}, u32[]{:S(2)}, u32[]{:S(2)}) collective-permute-start(bf16[80,640]{1,0:T(8,128)(2,1)S(1)} %shard_map.130.mine_ref), channel_id=1, source_target_pairs={{0,16},{8,24},{16,0},{24,8},{1,17},{9,25},{17,1},{25,9},{2,18},{10... | collective-permute-start | bytes 307208 | tf_op jit(solution)/shard_map/ppermute | solution.py:511
  50.6 6.7 %collective-permute-start.15 = (f32[80,640]{1,0:T(8,128)S(1)}, f32[80,640]{1,0:T(8,128)S(1)}, u32[]{:S(2)}, u32[]{:S(2)}) collective-permute-start(f32[80,640]{1,0:T(8,128)S(1)} %shard_map.131.own_ref), channel_id=1, source_target_pairs={{0,8},{8,0},{16,24},{24,16},{1,9},{9,1},{17,25},{25,17},{2,10},{10... | collective-permute-start | bytes 614408 | tf_op jit(solution)/shard_map/ppermute | solution.py:511

commit v9 on v8

--- a/solution.py
+++ b/solution.py
@@ -514,8 +514,8 @@
 def second_swap(value, offset):
     members = lax.axis_size("dev")
     pairs = [
-        (grp * members + dev, grp * members + (dev ^ offset))
-        for grp in range(1, lax.axis_size("grp"), 2)
+        (grp * members + dev, grp * members + (dev ^ (offset if grp % 2 else 0)))
+        for grp in range(lax.axis_size("grp"))
         for dev in range(members)
     ]
     return lax.ppermute(value, ("grp", "dev"), pairs)

time: 58.4 us -> 58.4 us (level)
  no operation moved by 1% of the time
where the time goes in v9:
time: 58.4 us; the launch traced here: 58.2 us
  starting transfers between devices  23.4 us (40%)
  Pallas kernels  17.9 us (31%)
  waiting for transfers between devices  16.1 us (28%)
  between operations  0.8 us (1%)
    ppermute x13, starting transfers between devices, swap(): return lax.ppermute(value, axis, [(i, i ^ offset) for i in range(size)])  21.4 us
    pallas_call x14, Pallas kernels, call(): pl.pallas_call(kernel, out_shape=[jax.ShapeDtypeStruct(out[0], out[1]) if...  17.9 us
    ppermute x13, waiting for transfers between devices, swap(): return lax.ppermute(value, axis, [(i, i ^ offset) for i in range(size)])  16.1 us
    ppermute x3, starting transfers between devices, second_swap(): return lax.ppermute(value, ('grp', 'dev'), pairs)  1.97 us
  transfers between devices with their start and end apart: 16, of which 9 were waited for; matrix products, arithmetic and copies ran while one was open for 0% of the time, Pallas kernels for 12%

profile of v9, /device:TPU:0, one launch (start us, length us, event | category | flops | bytes accessed | tf_op | source)
XLA Modules:
  0.0 58.2 jit_solution(17625405817882067192)
XLA Ops:
  0.6 3.0 %collective-permute-start = (bf16[32,384]{1,0:T(8,128)(2,1)}, bf16[32,384]{1,0:T(8,128)(2,1)S(1)}, u32[]{:S(2)}, u32[]{:S(2)}) collective-permute-start(bf16[32,384]{1,0:T(8,128)(2,1)} %wave_hbm.1), channel_id=1, source_target_pairs={{0,1},{1,0},{2,3},{3,2},{4,5},{5,4},{6,7},{7,6},{8,9},{9,8},{10,11... | collective-permute-start | bytes 73736 | tf_op jit(solution)/shard_map/ppermute | solution.py:511
  3.6 1.5 %collective-permute-start.2 = (bf16[32,384]{1,0:T(8,128)(2,1)}, bf16[32,384]{1,0:T(8,128)(2,1)S(1)}, u32[]{:S(2)}, u32[]{:S(2)}) collective-permute-start(bf16[32,384]{1,0:T(8,128)(2,1)} %wave_hbm.1), channel_id=1, source_target_pairs={{0,3},{1,2},{2,1},{3,0},{4,7},{5,6},{6,5},{7,4},{8,11},{9,10},{10,... | collective-permute-start | bytes 73736 | tf_op jit(solution)/shard_map/ppermute | solution.py:511
  5.2 0.0 collective-permute-start.1
  5.2 1.3 %shard_map.119 = (s32[32,128]{1,0:T(8,128)S(1)}, bf16[128,4096]{1,0:T(8,128)(2,1)S(1)}, bf16[16,256]{1,0:T(8,128)(2,1)S(1)}, bf16[16,256]{1,0:T(8,128)(2,1)S(1)}, bf16[32,384]{1,0:T(8,128)(2,1)S(1)}) custom-call(s32[8,32]{1,0:T(8,128)} %order_hbm.1, s32[1,256]{1,0:T(1,128)} %bitcast.11, bf16[10,512]{1,0:T(8,128)(2,1)} %w_hbm.2, bf16[32,384]{1,0:T(8,128)(2,1)} %wave_hbm.1), custom_call_target="tpu_custom_call" | custom-call | tf_op jit(solution)/shard_map/pallas_call | solution.py:496
  6.5 0.0 collective-permute-done.refs_1_
  6.5 2.2 %collective-permute-done.2.refs_3_ = bf16[32,384]{1,0:T(8,128)(2,1)S(1)} collective-permute-done((bf16[32,384]{1,0:T(8,128)(2,1)}, bf16[32,384]{1,0:T(8,128)(2,1)S(1)}, u32[]{:S(2)}, u32[]{:S(2)}) %collective-permute-start.2) | collective-permute-done | bytes 24608 | tf_op jit(solution)/shard_map/ppermute | solution.py:511
  8.7 0.5 collective-permute-done.1.refs_2_
  9.2 0.2 shard_map.120
  9.4 2.6 %collective-permute-start.3 = (bf16[16,384]{1,0:T(8,128)(2,1)S(1)}, bf16[16,384]{1,0:T(8,128)(2,1)S(1)}, u32[]{:S(2)}, u32[]{:S(2)}) collective-permute-start(bf16[16,384]{1,0:T(8,128)(2,1)S(1)} %get-tuple-element.52), channel_id=1, source_target_pairs={{0,4},{1,5},{2,6},{3,7},{4,0},{5,1},{6,2},{7,3},{8,12},{9,13},{10,... | collective-permute-start | bytes 36872 | tf_op jit(solution)/shard_map/ppermute | solution.py:511
  12.1 2.0 %collective-permute-done.3.far_ref = bf16[16,384]{1,0:T(8,128)(2,1)S(1)} collective-permute-done((bf16[16,384]{1,0:T(8,128)(2,1)S(1)}, bf16[16,384]{1,0:T(8,128)(2,1)S(1)}, u32[]{:S(2)}, u32[]{:S(2)}) %collective-permute-start.3) | collective-permute-done | bytes 12320 | tf_op jit(solution)/shard_map/ppermute | solution.py:511
  14.1 8.0 %shard_map.121 = (bf16[37,32,512]{2,1,0:T(8,128)(2,1)S(1)}, bf16[41,32,512]{2,1,0:T(8,128)(2,1)S(1)}, bf16[40,32,512]{2,1,0:T(8,128)(2,1)S(1)}, f32[10,32,4096]{...) custom-call(bf16[16,384]{1,0:T(8,128)(2,1)S(1)} %get-tuple-element.5, ...), custom_call_target="tpu_custom_call" | custom-call | tf_op jit(solution)/shard_map/pallas_call | solution.py:496
  22.1 1.5 %shard_map.122 = (f32[512,512]{1,0:T(8,128)S(1)}, bf16[512,512]{1,0:T(8,128)(2,1)S(1)}) custom-call(bf16[41,32,512]{2,1,0:T(8,128)(2,1)S(1)} %get-tuple-element.59.refs_0_, bf16[40,32,512]{2,1,0:T(8,128)(2,1)S(1)} %get-tuple-element.60.refs_1_, bf16[512,1280]{1,0:T(8,128)(2,1)S(1)} %get-tuple-element.61.refs_2_.refs_1_), custom_call_target="tpu_custom_call" | custom-call | flops 1073741824 | tf_op jit(solution)/shard_map/pallas_call | solution.py:496
  23.6 0.1 collective-permute-start.4
  23.7 0.9 %shard_map.123 = (f32[512,256]{1,0:T(8,128)S(1)}, bf16[512,256]{1,0:T(8,128)(2,1)S(1)}) custom-call(bf16[41,32,512]{2,1,0:T(8,128)(2,1)S(1)} %get-tuple-element.59.refs_0_, bf16[512,1280]{1,0:T(8,128)(2,1)S(1)} %get-tuple-element.61.refs_2_.refs_1_), custom_call_target="tpu_custom_call" | custom-call | flops 536870912 | tf_op jit(solution)/shard_map/pallas_call | solution.py:496
  24.6 0.5 collective-permute-start.5
  25.1 1.2 %collective-permute-done.5.refs_3_ = bf16[512,256]{1,0:T(8,128)(2,1)S(1)} collective-permute-done((bf16[512,256]{1,0:T(8,128)(2,1)S(1)}, bf16[512,256]{1,0:T(8,128)(2,1)S(1)}, u32[]{:S(2)}, u32[]{:S(2)}) %collective-permute-start.5) | collective-permute-done | bytes 262176 | tf_op jit(solution)/shard_map/ppermute | solution.py:511
  26.3 0.0 collective-permute-done.4.refs_2_
  26.3 0.1 shard_map.124
  26.4 1.6 %collective-permute-start.6 = (bf16[128,768]{1,0:T(8,128)(2,1)S(1)}, bf16[128,768]{1,0:T(8,128)(2,1)S(1)}, u32[]{:S(2)}, u32[]{:S(2)}) collective-permute-start(bf16[128,768]{1,0:T(8,128)(2,1)S(1)} %get-tuple-element.69), channel_id=1, source_target_pairs={{0,1},{1,0},{2,3},{3,2},{4,5},{5,4},{6,7},{7,6},{8,9},{9,8},{10,11... | collective-permute-start | bytes 589832 | tf_op jit(solution)/shard_map/ppermute | solution.py:511
  28.0 0.4 collective-permute-start.7
  28.4 1.5 %collective-permute-start.9 = (bf16[128,768]{1,0:T(8,128)(2,1)S(1)}, bf16[128,768]{1,0:T(8,128)(2,1)S(1)}, u32[]{:S(2)}, u32[]{:S(2)}) collective-permute-start(bf16[128,768]{1,0:T(8,128)(2,1)S(1)} %get-tuple-element.80), channel_id=1, source_target_pairs={{0,3},{1,2},{2,1},{3,0},{4,7},{5,6},{6,5},{7,4},{8,11},{9,10},{10,... | collective-permute-start | bytes 589832 | tf_op jit(solution)/shard_map/ppermute | solution.py:511
  30.0 2.2 %shard_map.125 = (f32[38,32,512]{2,1,0:T(8,128)S(1)}, f32[37,32,512]{2,1,0:T(8,128)S(1)}, bf16[37,32,512]{2,1,0:T(8,128)(2,1)}) custom-call(bf16[39,32,512]{2,1,0:T(8,128)(2,1)S(1)} %get-tuple-element.55.grad_ref, bf16[3,512,512]{2,1,0:T(8,128)(2,1)S(1)} %get-tuple-element.56.w_ref, f32[40,32,512]{2,1,0:T(8,128)S(1)} %get-tuple-element.57.even_slope, ...), custom_call_target="tpu_custom_call" | custom-call | flops 1073741824 | tf_op jit(solution)/shard_map/pallas_call | solution.py:496
  32.2 2.7 %shard_map.126.mine_ref = f32[64,128]{1,0:T(8,128)S(1)} custom-call(s32[32,128]{1,0:T(8,128)S(1)} %get-tuple-element.53.valid_ref, f32[10,32,4096]{2,1,0:T(8,128)S(1)} %get-tuple-element.71.pre0, f32[32,512]{1,0:T(8,128)S(1)} %get-tuple-element.72.mean_ref, f32[32,512]{1,0:T(8,128)S(1)} %get-tuple-element.73.inv_ref, ...), custom_call_target="tpu_custom_call" | custom-call | flops 4294967296 | tf_op jit(solution)/shard_map/pallas_call | solution.py:496
  34.9 0.1 collective-permute-start.8
  35.0 1.2 %collective-permute-done.8.got_ref = f32[64,128]{1,0:T(8,128)S(1)} collective-permute-done((f32[64,128]{1,0:T(8,128)S(1)}, f32[64,128]{1,0:T(8,128)S(1)}, u32[]{:S(2)}, u32[]{:S(2)}) %collective-permute-start.8) | collective-permute-done | bytes 32800 | tf_op jit(solution)/shard_map/ppermute | solution.py:511
  36.2 0.7 %collective-permute-start.11 = (f32[16,128]{1,0:T(8,128)S(1)}, f32[16,128]{1,0:T(8,128)S(1)}, u32[]{:S(2)}, u32[]{:S(2)}) collective-permute-start(f32[16,128]{1,0:T(8,128)S(1)} %get-tuple-element.83), channel_id=1, source_target_pairs={{0,0},{1,1},{2,2},{3,3},{4,4},{5,5},{6,6},{7,7},{8,10},{9,11},{10,... | collective-permute-start | bytes 24584 | tf_op jit(solution)/shard_map/ppermute | solution.py:521
  36.9 0.7 %collective-permute-start.12 = (f32[16,128]{1,0:T(8,128)S(1)}, f32[16,128]{1,0:T(8,128)S(1)}, u32[]{:S(2)}, u32[]{:S(2)}) collective-permute-start(f32[16,128]{1,0:T(8,128)S(1)} %get-tuple-element.84), channel_id=1, source_target_pairs={{0,0},{1,1},{2,2},{3,3},{4,4},{5,5},{6,6},{7,7},{8,11},{9,10},{10,... | collective-permute-start | bytes 24584 | tf_op jit(solution)/shard_map/ppermute | solution.py:521
  37.5 0.0 collective-permute-done.6.got1
  37.5 0.0 collective-permute-done.7.got2
  37.6 0.1 shard_map.128
  37.6 0.7 %collective-permute-start.10 = (f32[16,128]{1,0:T(8,128)S(1)}, f32[16,128]{1,0:T(8,128)S(1)}, u32[]{:S(2)}, u32[]{:S(2)}) collective-permute-start(f32[16,128]{1,0:T(8,128)S(1)} %get-tuple-element.82), channel_id=1, source_target_pairs={{0,0},{1,1},{2,2},{3,3},{4,4},{5,5},{6,6},{7,7},{8,9},{9,8},{10,11... | collective-permute-start | bytes 24584 | tf_op jit(solution)/shard_map/ppermute | solution.py:521
  38.3 0.0 collective-permute-done.11.small2
  38.3 0.0 collective-permute-done.12.small3
  38.3 0.7 %collective-permute-done.9.got3 = bf16[128,768]{1,0:T(8,128)(2,1)S(1)} collective-permute-done((bf16[128,768]{1,0:T(8,128)(2,1)S(1)}, bf16[128,768]{1,0:T(8,128)(2,1)S(1)}, u32[]{:S(2)}, u32[]{:S(2)}) %collective-permute-start.9) | collective-permute-done | bytes 196640 | tf_op jit(solution)/shard_map/ppermute | solution.py:511
  39.1 0.0 collective-permute-done.10.small1
  39.1 2.7 %collective-permute-start.13 = (bf16[80,640]{1,0:T(8,128)(2,1)S(1)}, bf16[80,640]{1,0:T(8,128)(2,1)S(1)}, u32[]{:S(2)}, u32[]{:S(2)}) collective-permute-start(bf16[80,640]{1,0:T(8,128)(2,1)S(1)} %get-tuple-element.86), channel_id=1, source_target_pairs={{0,4},{1,5},{2,6},{3,7},{4,0},{5,1},{6,2},{7,3},{8,12},{9,13},{10,... | collective-permute-start | bytes 307208 | tf_op jit(solution)/shard_map/ppermute | solution.py:511
  41.8 4.1 %collective-permute-done.13.got_ref = bf16[80,640]{1,0:T(8,128)(2,1)S(1)} collective-permute-done((bf16[80,640]{1,0:T(8,128)(2,1)S(1)}, bf16[80,640]{1,0:T(8,128)(2,1)S(1)}, u32[]{:S(2)}, u32[]{:S(2)}) %collective-permute-start.13) | collective-permute-done | bytes 102432 | tf_op jit(solution)/shard_map/ppermute | solution.py:511
  45.9 1.6 %collective-permute-start.14 = (bf16[80,640]{1,0:T(8,128)(2,1)S(1)}, bf16[80,640]{1,0:T(8,128)(2,1)S(1)}, u32[]{:S(2)}, u32[]{:S(2)}) collective-permute-start(bf16[80,640]{1,0:T(8,128)(2,1)S(1)} %shard_map.130.mine_ref), channel_id=1, source_target_pairs={{0,16},{8,24},{16,0},{24,8},{1,17},{9,25},{17,1},{25,9},{2,18},{10... | collective-permute-start | bytes 307208 | tf_op jit(solution)/shard_map/ppermute | solution.py:511
  47.4 3.1 %collective-permute-done.14.got_ref = bf16[80,640]{1,0:T(8,128)(2,1)S(1)} collective-permute-done((bf16[80,640]{1,0:T(8,128)(2,1)S(1)}, bf16[80,640]{1,0:T(8,128)(2,1)S(1)}, u32[]{:S(2)}, u32[]{:S(2)}) %collective-permute-start.14) | collective-permute-done | bytes 102432 | tf_op jit(solution)/shard_map/ppermute | solution.py:511
  50.6 5.7 %collective-permute-start.15 = (f32[80,640]{1,0:T(8,128)S(1)}, f32[80,640]{1,0:T(8,128)S(1)}, u32[]{:S(2)}, u32[]{:S(2)}) collective-permute-start(f32[80,640]{1,0:T(8,128)S(1)} %shard_map.131.own_ref), channel_id=1, source_target_pairs={{0,8},{8,0},{16,24},{24,16},{1,9},{9,1},{17,25},{25,17},{2,10},{10... | collective-permute-start | bytes 614408 | tf_op jit(solution)/shard_map/ppermute | solution.py:511
  56.3 1.1 %collective-permute-done.15.other_ref = f32[80,640]{1,0:T(8,128)S(1)} collective-permute-done((f32[80,640]{1,0:T(8,128)S(1)}, f32[80,640]{1,0:T(8,128)S(1)}, u32[]{:S(2)}, u32[]{:S(2)}) %collective-permute-start.15) | collective-permute-done | bytes 204832 | tf_op jit(solution)/shard_map/ppermute | solution.py:511
  57.4 0.8 %shard_map.132 = (f32[3,64,512]{2,1,0:T(8,128)}, f32[10,64]{1,0:T(8,128)}, f32[1,64]{1,0:T(1,128)}, f32[1,64]{1,0:T(1,128)}) custom-call(f32[80,640]{1,0:T(8,128)S(1)} %shard_map.131.own_ref, f32[80,640]{1,0:T(8,128)S(1)} %collective-permute-done.15.other_ref), custom_call_target="tpu_custom_call" | custom-call | tf_op jit(solution)/shard_map/pallas_call | solution.py:496
  (4 shorter events, 0.1 us)
Async XLA Ops:
  0.6 5.9 %collective-permute-start = (bf16[32,384]{1,0:T(8,128)(2,1)}, bf16[32,384]{1,0:T(8,128)(2,1)S(1)}, u32[]{:S(2)}, u32[]{:S(2)}) collective-permute-start(bf16[32,384]{1,0:T(8,128)(2,1)} %wave_hbm.1), channel_id=1, source_target_pairs={{0,1},{1,0},{2,3},{3,2},{4,5},{5,4},{6,7},{7,6},{8,9},{9,8},{10,11... | collective-permute-start | bytes 73736 | tf_op jit(solution)/shard_map/ppermute | solution.py:511
  3.6 5.1 %collective-permute-start.2 = (bf16[32,384]{1,0:T(8,128)(2,1)}, bf16[32,384]{1,0:T(8,128)(2,1)S(1)}, u32[]{:S(2)}, u32[]{:S(2)}) collective-permute-start(bf16[32,384]{1,0:T(8,128)(2,1)} %wave_hbm.1), channel_id=1, source_target_pairs={{0,3},{1,2},{2,1},{3,0},{4,7},{5,6},{6,5},{7,4},{8,11},{9,10},{10,... | collective-permute-start | bytes 73736 | tf_op jit(solution)/shard_map/ppermute | solution.py:511
  5.2 4.0 %collective-permute-start.1 = (bf16[32,384]{1,0:T(8,128)(2,1)}, bf16[32,384]{1,0:T(8,128)(2,1)S(1)}, u32[]{:S(2)}, u32[]{:S(2)}) collective-permute-start(bf16[32,384]{1,0:T(8,128)(2,1)} %wave_hbm.1), channel_id=1, source_target_pairs={{0,2},{1,3},{2,0},{3,1},{4,6},{5,7},{6,4},{7,5},{8,10},{9,11},{10,... | collective-permute-start | bytes 73736 | tf_op jit(solution)/shard_map/ppermute | solution.py:511
  9.4 4.6 %collective-permute-start.3 = (bf16[16,384]{1,0:T(8,128)(2,1)S(1)}, bf16[16,384]{1,0:T(8,128)(2,1)S(1)}, u32[]{:S(2)}, u32[]{:S(2)}) collective-permute-start(bf16[16,384]{1,0:T(8,128)(2,1)S(1)} %get-tuple-element.52), channel_id=1, source_target_pairs={{0,4},{1,5},{2,6},{3,7},{4,0},{5,1},{6,2},{7,3},{8,12},{9,13},{10,... | collective-permute-start | bytes 36872 | tf_op jit(solution)/shard_map/ppermute | solution.py:511
  23.6 2.7 %collective-permute-start.4 = (bf16[512,512]{1,0:T(8,128)(2,1)S(1)}, bf16[512,512]{1,0:T(8,128)(2,1)S(1)}, u32[]{:S(2)}, u32[]{:S(2)}) collective-permute-start(bf16[512,512]{1,0:T(8,128)(2,1)S(1)} %get-tuple-element.64), channel_id=1, source_target_pairs={{0,8},{8,0},{16,24},{24,16},{1,9},{9,1},{17,25},{25,17},{2,10},{10... | collective-permute-start | bytes 1572872 | tf_op jit(solution)/shard_map/ppermute | solution.py:511
  24.6 1.7 %collective-permute-start.5 = (bf16[512,256]{1,0:T(8,128)(2,1)S(1)}, bf16[512,256]{1,0:T(8,128)(2,1)S(1)}, u32[]{:S(2)}, u32[]{:S(2)}) collective-permute-start(bf16[512,256]{1,0:T(8,128)(2,1)S(1)} %get-tuple-element.65), channel_id=1, source_target_pairs={{0,8},{8,0},{16,24},{24,16},{1,9},{9,1},{17,25},{25,17},{2,10},{10... | collective-permute-start | bytes 786440 | tf_op jit(solution)/shard_map/ppermute | solution.py:511
  26.4 11.1 %collective-permute-start.6 = (bf16[128,768]{1,0:T(8,128)(2,1)S(1)}, bf16[128,768]{1,0:T(8,128)(2,1)S(1)}, u32[]{:S(2)}, u32[]{:S(2)}) collective-permute-start(bf16[128,768]{1,0:T(8,128)(2,1)S(1)} %get-tuple-element.69), channel_id=1, source_target_pairs={{0,1},{1,0},{2,3},{3,2},{4,5},{5,4},{6,7},{7,6},{8,9},{9,8},{10,11... | collective-permute-start | bytes 589832 | tf_op jit(solution)/shard_map/ppermute | solution.py:511
  28.0 9.5 %collective-permute-start.7 = (bf16[128,768]{1,0:T(8,128)(2,1)S(1)}, bf16[128,768]{1,0:T(8,128)(2,1)S(1)}, u32[]{:S(2)}, u32[]{:S(2)}) collective-permute-start(bf16[128,768]{1,0:T(8,128)(2,1)S(1)} %get-tuple-element.70), channel_id=1, source_target_pairs={{0,2},{1,3},{2,0},{3,1},{4,6},{5,7},{6,4},{7,5},{8,10},{9,11},{10,... | collective-permute-start | bytes 589832 | tf_op jit(solution)/shard_map/ppermute | solution.py:511
  28.4 10.6 %collective-permute-start.9 = (bf16[128,768]{1,0:T(8,128)(2,1)S(1)}, bf16[128,768]{1,0:T(8,128)(2,1)S(1)}, u32[]{:S(2)}, u32[]{:S(2)}) collective-permute-start(bf16[128,768]{1,0:T(8,128)(2,1)S(1)} %get-tuple-element.80), channel_id=1, source_target_pairs={{0,3},{1,2},{2,1},{3,0},{4,7},{5,6},{6,5},{7,4},{8,11},{9,10},{10,... | collective-permute-start | bytes 589832 | tf_op jit(solution)/shard_map/ppermute | solution.py:511
  34.9 1.3 %collective-permute-start.8 = (f32[64,128]{1,0:T(8,128)S(1)}, f32[64,128]{1,0:T(8,128)S(1)}, u32[]{:S(2)}, u32[]{:S(2)}) collective-permute-start(f32[64,128]{1,0:T(8,128)S(1)} %shard_map.126.mine_ref), channel_id=1, source_target_pairs={{0,8},{8,0},{16,24},{24,16},{1,9},{9,1},{17,25},{25,17},{2,10},{10... | collective-permute-start | bytes 98312 | tf_op jit(solution)/shard_map/ppermute | solution.py:511
  36.2 2.1 %collective-permute-start.11 = (f32[16,128]{1,0:T(8,128)S(1)}, f32[16,128]{1,0:T(8,128)S(1)}, u32[]{:S(2)}, u32[]{:S(2)}) collective-permute-start(f32[16,128]{1,0:T(8,128)S(1)} %get-tuple-element.83), channel_id=1, source_target_pairs={{0,0},{1,1},{2,2},{3,3},{4,4},{5,5},{6,6},{7,7},{8,10},{9,11},{10,... | collective-permute-start | bytes 24584 | tf_op jit(solution)/shard_map/ppermute | solution.py:521
  36.9 1.4 %collective-permute-start.12 = (f32[16,128]{1,0:T(8,128)S(1)}, f32[16,128]{1,0:T(8,128)S(1)}, u32[]{:S(2)}, u32[]{:S(2)}) collective-permute-start(f32[16,128]{1,0:T(8,128)S(1)} %get-tuple-element.84), channel_id=1, source_target_pairs={{0,0},{1,1},{2,2},{3,3},{4,4},{5,5},{6,6},{7,7},{8,11},{9,10},{10,... | collective-permute-start | bytes 24584 | tf_op jit(solution)/shard_map/ppermute | solution.py:521
  37.6 1.4 %collective-permute-start.10 = (f32[16,128]{1,0:T(8,128)S(1)}, f32[16,128]{1,0:T(8,128)S(1)}, u32[]{:S(2)}, u32[]{:S(2)}) collective-permute-start(f32[16,128]{1,0:T(8,128)S(1)} %get-tuple-element.82), channel_id=1, source_target_pairs={{0,0},{1,1},{2,2},{3,3},{4,4},{5,5},{6,6},{7,7},{8,9},{9,8},{10,11... | collective-permute-start | bytes 24584 | tf_op jit(solution)/shard_map/ppermute | solution.py:521
  39.1 6.7 %collective-permute-start.13 = (bf16[80,640]{1,0:T(8,128)(2,1)S(1)}, bf16[80,640]{1,0:T(8,128)(2,1)S(1)}, u32[]{:S(2)}, u32[]{:S(2)}) collective-permute-start(bf16[80,640]{1,0:T(8,128)(2,1)S(1)} %get-tuple-element.86), channel_id=1, source_target_pairs={{0,4},{1,5},{2,6},{3,7},{4,0},{5,1},{6,2},{7,3},{8,12},{9,13},{10,... | collective-permute-start | bytes 307208 | tf_op jit(solution)/shard_map/ppermute | solution.py:511
  45.9 4.7 %collective-permute-start.14 = (bf16[80,640]{1,0:T(8,128)(2,1)S(1)}, bf16[80,640]{1,0:T(8,128)(2,1)S(1)}, u32[]{:S(2)}, u32[]{:S(2)}) collective-permute-start(bf16[80,640]{1,0:T(8,128)(2,1)S(1)} %shard_map.130.mine_ref), channel_id=1, source_target_pairs={{0,16},{8,24},{16,0},{24,8},{1,17},{9,25},{17,1},{25,9},{2,18},{10... | collective-permute-start | bytes 307208 | tf_op jit(solution)/shard_map/ppermute | solution.py:511
  50.6 6.7 %collective-permute-start.15 = (f32[80,640]{1,0:T(8,128)S(1)}, f32[80,640]{1,0:T(8,128)S(1)}, u32[]{:S(2)}, u32[]{:S(2)}) collective-permute-start(f32[80,640]{1,0:T(8,128)S(1)} %shard_map.131.own_ref), channel_id=1, source_target_pairs={{0,8},{8,0},{16,24},{24,16},{1,9},{9,1},{17,25},{25,17},{2,10},{10... | collective-permute-start | bytes 614408 | tf_op jit(solution)/shard_map/ppermute | solution.py:511

commit v10 on v9

--- a/solution.py
+++ b/solution.py
@@ -402,12 +402,6 @@
         small_ref[offset * 16 : (offset + 1) * 16] = quarters[jnp.bitwise_xor(place, offset)]
 
 
-def core_kernel(mine_ref, got_ref, *out_refs):
-    for place, ref in enumerate(out_refs):
-        lines = slice(place * 16, (place + 1) * 16)
-        ref[...] = mine_ref[lines] + got_ref[lines]
-
-
 def plane_kernel(*refs):
     keeps, others, outs = refs[:2], refs[2:4], refs[4:]
     size = outs[0].shape[0]
@@ -417,11 +411,6 @@
         lines = pl.ds(pl.multiple_of(jnp.bitwise_xor(place, offset) * size, size), size)
         for lanes, keep_ref, got_ref in zip((slice(0, edge), slice(edge, None)), keeps, others):
             out_ref[:, lanes] = (keep_ref[lines, :] + got_ref[lines, :].astype(F32)).astype(out_ref.dtype)
-
-
-def part_kernel(own_ref, got1, got2, small_ref, sum_ref, total_ref):
-    sum_ref[...] = own_ref[...] + (got1[...].astype(F32) + got2[...].astype(F32))
-    total_ref[...] = small_ref[...]
 
 
 def packed(size, wide):
@@ -449,13 +438,17 @@
     return jnp.concatenate([whole, jnp.concatenate(pieces, axis=0)], axis=1)
 
 
-def gather_kernel(bit, own_ref, got3, small0, small1, small2, small3, keep_ref, send_ref):
+def gather_kernel(bit, own_ref, got1, got2, got3, parts_ref, parts_got, keep_ref, send_ref, *small_refs):
     half = own_ref.shape[0] // 2
     side = lax.rem(lax.shift_right_logical(lax.axis_index("dev"), bit), 2)
-    total = (small0[...] + small1[...]) + (small2[...] + small3[...])
+    empty = jnp.zeros((16, 128), F32)
     for index, ref in ((1 - side, send_ref), (side, keep_ref)):
         lines = pl.ds(pl.multiple_of(index * half, half), half)
-        write_packed(ref, own_ref[lines, :] + got3[lines, :].astype(F32), total)
+        terms = got1[lines, :].astype(F32) + got2[lines, :].astype(F32) + got3[lines, :].astype(F32)
+        write_packed(ref, own_ref[lines, :] + terms, empty)
+    for place, ref in enumerate(small_refs):
+        lines = slice(place * 16, (place + 1) * 16)
+        ref[...] = parts_ref[lines] + parts_got[lines]
 
 
 def halve_kernel(bit, keep_ref, got_ref, next_ref, send_ref):
@@ -467,8 +460,19 @@
         write_packed(ref, read_packed(keep_ref, first, half) + read_packed(got_ref, first, half), small)
 
 
+def round_kernel(keep_ref, got_ref, small0, small1, small2, small3, send_ref, total_ref):
+    send_ref[...] = (keep_ref[...] + got_ref[...].astype(F32)).astype(BF16)
+    total_ref[...] = (small0[...] + small1[...]) + (small2[...] + small3[...])
+
+
 def add_kernel(mine_ref, got_ref, out_ref):
     out_ref[...] = (mine_ref[...].astype(F32) + got_ref[...].astype(F32)).astype(out_ref.dtype)
+
+
+def last_add_kernel(mine_ref, got_ref, small_ref, small_got, out_ref):
+    size, lanes = out_ref.shape[0] - 16, out_ref.shape[1] - 128
+    out_ref[...] = mine_ref[...].astype(F32) + got_ref[...].astype(F32)
+    out_ref[size:, lanes:] = small_ref[...] + small_got[...]
 
 
 def join_kernel(taps, own_ref, other_ref, out_ref, first_ref, gain_ref, bias_ref):
@@ -480,7 +484,7 @@
         for tap in range(second):
             lanes = pl.ds(pl.multiple_of(side * half, half), half)
             out_ref[tap, :, lanes] = value[:, tap * half : (tap + 1) * half]
-    total = jnp.where(core == 1, own_ref[size:, -128:], other_ref[size:, -128:])
+    total = own_ref[size:, -128:] + other_ref[size:, -128:]
     value = total[:, :size]
     for place in range(1, 128 // size):
         mine = lax.axis_index("dev") // 4 == place
@@ -509,16 +513,6 @@
 def swap(value, axis, offset):
     size = lax.axis_size(axis)
     return lax.ppermute(value, axis, [(i, i ^ offset) for i in range(size)])
-
-
-def second_swap(value, offset):
-    members = lax.axis_size("dev")
-    pairs = [
-        (grp * members + dev, grp * members + (dev ^ (offset if grp % 2 else 0)))
-        for grp in range(lax.axis_size("grp"))
-        for dev in range(members)
-    ]
-    return lax.ppermute(value, ("grp", "dev"), pairs)
 
 
 def shards(wave, lengths, order, w_first, norm_gain, norm_bias, w_second, cot):
@@ -642,29 +636,33 @@
         ],
         flops=1 << 32,
     )[0]
-    small, *smalls = call(core_kernel, [((16, quarter), F32)] * 4, [parts, swap(parts, "grp", 1)])
-    small3, small2 = second_swap(smalls[2], 3), second_swap(smalls[1], 2)
-    own, first = call(
-        part_kernel, [((quarter, wide), F32), (small.shape, F32)], [own, gots[0], gots[1], smalls[0]]
-    )
-    small1 = second_swap(first, 1)
+    for bit in range(1, grp_bits - 1):
+        parts = parts + swap(parts, "grp", 1 << bit)
     size = quarter // 2
-    keep, send = call(
+    keep, send, small, *smalls = call(
         functools.partial(gather_kernel, dev_bits - 1),
-        [(packed(size, wide), F32), (packed(size, wide), BF16)],
-        [own, gots[2], small, small1, small2, small3],
-    )
+        [(packed(size, wide), F32), (packed(size, wide), BF16)] + [((16, quarter), F32)] * 4,
+        [own, *gots, parts, swap(parts, "grp", groups_of // 2)],
+    )
+    got = swap(send, "dev", members // 2)
+    smalls = [swap(part, "dev", offset) for offset, part in enumerate(smalls, 1)]
     for bit in range(dev_bits - 1, 2, -1):
         size //= 2
         keep, send = call(
             functools.partial(halve_kernel, bit - 1),
             [(packed(size, wide), F32), (packed(size, wide), BF16)],
-            [keep, swap(send, "dev", 1 << bit)],
+            [keep, got],
         )
-    send = call(add_kernel, [(packed(size, wide), BF16)], [keep, swap(send, "dev", 4)])[0]
-    for bit in range(1, grp_bits):
-        kind = F32 if bit == grp_bits - 1 else BF16
-        send = call(add_kernel, [(packed(size, wide), kind)], [send, swap(send, "grp", 1 << bit)])[0]
+        got = swap(send, "dev", 1 << (bit - 1))
+    send, small = call(round_kernel, [(packed(size, wide), BF16), (small.shape, F32)], [keep, got, small, *smalls])
+    for bit in range(3, dev_bits):
+        small = small + swap(small, "dev", 1 << bit)
+    small_got = swap(small, "dev", 4)
+    for bit in range(1, grp_bits - 1):
+        send = call(add_kernel, [(packed(size, wide), BF16)], [send, swap(send, "grp", 1 << bit)])[0]
+    send = call(
+        last_add_kernel, [(packed(size, wide), F32)], [send, swap(send, "grp", groups_of // 2), small, small_got]
+    )[0]
     grad_second, grad_first, grad_gain, grad_bias = call(
         functools.partial(join_kernel, taps),
         [

time: 58.4 us -> 57.1 us (0.978)
  starting transfers between devices: 23.4 us -> 21.1 us
  waiting for transfers between devices: 16.1 us -> 17.1 us
    ppermute x3 -> x0, starting transfers between devices: 1.97 us -> none  [second_swap(): return lax.ppermute(value, ('grp', 'dev'), pairs)]
    ppermute x13 -> x17, waiting for transfers between devices: 16.1 us -> 17.1 us  [swap(): return lax.ppermute(value, axis, [(i, i ^ offset) for i in range(size)])]
    ppermute x13 -> x17, starting transfers between devices: 21.4 us -> 21.1 us  [swap(): return lax.ppermute(value, axis, [(i, i ^ offset) for i in range(size)])]
    pallas_call x14 -> x12, Pallas kernels: 17.9 us -> 17.9 us  [call(): pl.pallas_call(kernel, out_shape=[jax.ShapeDtypeStruct(out[0], out[1]) if...]
  transfers between devices with their start and end apart: 16 -> 17, of which waited for: 9 -> 11; matrix products, arithmetic and copies ran while one was open for 0% -> 0% of each run, Pallas kernels for 12% -> 12%
where the time goes in v10:
time: 57.1 us; the launch traced here: 56.9 us
  starting transfers between devices  21.1 us (37%)
  Pallas kernels  17.9 us (31%)
  waiting for transfers between devices  17.1 us (30%)
  between operations  0.73 us (1%)
    ppermute x17, starting transfers between devices, swap(): return lax.ppermute(value, axis, [(i, i ^ offset) for i in range(size)])  21.1 us
    pallas_call x12, Pallas kernels, call(): pl.pallas_call(kernel, out_shape=[jax.ShapeDtypeStruct(out[0], out[1]) if...  17.9 us
    ppermute x17, waiting for transfers between devices, swap(): return lax.ppermute(value, axis, [(i, i ^ offset) for i in range(size)])  17.1 us
  transfers between devices with their start and end apart: 17, of which 11 were waited for; matrix products, arithmetic and copies ran while one was open for 0% of the time, Pallas kernels for 12%

profile of v10, /device:TPU:0, one launch (start us, length us, event | category | flops | bytes accessed | tf_op | source)
XLA Modules:
  0.0 56.9 jit_solution(10467823819286218816)
XLA Ops:
  0.6 3.0 %collective-permute-start = (bf16[32,384]{1,0:T(8,128)(2,1)}, bf16[32,384]{1,0:T(8,128)(2,1)S(1)}, u32[]{:S(2)}, u32[]{:S(2)}) collective-permute-start(bf16[32,384]{1,0:T(8,128)(2,1)} %wave_hbm.1), channel_id=1, source_target_pairs={{0,1},{1,0},{2,3},{3,2},{4,5},{5,4},{6,7},{7,6},{8,9},{9,8},{10,11... | collective-permute-start | bytes 73736 | tf_op jit(solution)/shard_map/ppermute | solution.py:515
  3.6 1.5 %collective-permute-start.2 = (bf16[32,384]{1,0:T(8,128)(2,1)}, bf16[32,384]{1,0:T(8,128)(2,1)S(1)}, u32[]{:S(2)}, u32[]{:S(2)}) collective-permute-start(bf16[32,384]{1,0:T(8,128)(2,1)} %wave_hbm.1), channel_id=1, source_target_pairs={{0,3},{1,2},{2,1},{3,0},{4,7},{5,6},{6,5},{7,4},{8,11},{9,10},{10,... | collective-permute-start | bytes 73736 | tf_op jit(solution)/shard_map/ppermute | solution.py:515
  5.2 0.0 collective-permute-start.1
  5.2 1.3 %shard_map.119 = (s32[32,128]{1,0:T(8,128)S(1)}, bf16[128,4096]{1,0:T(8,128)(2,1)S(1)}, bf16[16,256]{1,0:T(8,128)(2,1)S(1)}, bf16[16,256]{1,0:T(8,128)(2,1)S(1)}, bf16[32,384]{1,0:T(8,128)(2,1)S(1)}) custom-call(s32[8,32]{1,0:T(8,128)} %order_hbm.1, s32[1,256]{1,0:T(1,128)} %bitcast.11, bf16[10,512]{1,0:T(8,128)(2,1)} %w_hbm.2, bf16[32,384]{1,0:T(8,128)(2,1)} %wave_hbm.1), custom_call_target="tpu_custom_call" | custom-call | tf_op jit(solution)/shard_map/pallas_call | solution.py:500
  6.5 0.0 collective-permute-done.refs_1_
  6.5 2.2 %collective-permute-done.2.refs_3_ = bf16[32,384]{1,0:T(8,128)(2,1)S(1)} collective-permute-done((bf16[32,384]{1,0:T(8,128)(2,1)}, bf16[32,384]{1,0:T(8,128)(2,1)S(1)}, u32[]{:S(2)}, u32[]{:S(2)}) %collective-permute-start.2) | collective-permute-done | bytes 24608 | tf_op jit(solution)/shard_map/ppermute | solution.py:515
  8.7 0.5 collective-permute-done.1.refs_2_
  9.2 0.2 shard_map.120
  9.4 2.6 %collective-permute-start.3 = (bf16[16,384]{1,0:T(8,128)(2,1)S(1)}, bf16[16,384]{1,0:T(8,128)(2,1)S(1)}, u32[]{:S(2)}, u32[]{:S(2)}) collective-permute-start(bf16[16,384]{1,0:T(8,128)(2,1)S(1)} %get-tuple-element.52), channel_id=1, source_target_pairs={{0,4},{1,5},{2,6},{3,7},{4,0},{5,1},{6,2},{7,3},{8,12},{9,13},{10,... | collective-permute-start | bytes 36872 | tf_op jit(solution)/shard_map/ppermute | solution.py:515
  12.1 2.0 %collective-permute-done.3.far_ref = bf16[16,384]{1,0:T(8,128)(2,1)S(1)} collective-permute-done((bf16[16,384]{1,0:T(8,128)(2,1)S(1)}, bf16[16,384]{1,0:T(8,128)(2,1)S(1)}, u32[]{:S(2)}, u32[]{:S(2)}) %collective-permute-start.3) | collective-permute-done | bytes 12320 | tf_op jit(solution)/shard_map/ppermute | solution.py:515
  14.1 8.0 %shard_map.121 = (bf16[37,32,512]{2,1,0:T(8,128)(2,1)S(1)}, bf16[41,32,512]{2,1,0:T(8,128)(2,1)S(1)}, bf16[40,32,512]{2,1,0:T(8,128)(2,1)S(1)}, f32[10,32,4096]{...) custom-call(bf16[16,384]{1,0:T(8,128)(2,1)S(1)} %get-tuple-element.5, ...), custom_call_target="tpu_custom_call" | custom-call | tf_op jit(solution)/shard_map/pallas_call | solution.py:500
  22.1 1.5 %shard_map.122 = (f32[512,512]{1,0:T(8,128)S(1)}, bf16[512,512]{1,0:T(8,128)(2,1)S(1)}) custom-call(bf16[41,32,512]{2,1,0:T(8,128)(2,1)S(1)} %get-tuple-element.59.refs_0_, bf16[40,32,512]{2,1,0:T(8,128)(2,1)S(1)} %get-tuple-element.60.refs_1_, bf16[512,1280]{1,0:T(8,128)(2,1)S(1)} %get-tuple-element.61.refs_2_.refs_1_), custom_call_target="tpu_custom_call" | custom-call | flops 1073741824 | tf_op jit(solution)/shard_map/pallas_call | solution.py:500
  23.6 0.1 collective-permute-start.4
  23.7 0.9 %shard_map.123 = (f32[512,256]{1,0:T(8,128)S(1)}, bf16[512,256]{1,0:T(8,128)(2,1)S(1)}) custom-call(bf16[41,32,512]{2,1,0:T(8,128)(2,1)S(1)} %get-tuple-element.59.refs_0_, bf16[512,1280]{1,0:T(8,128)(2,1)S(1)} %get-tuple-element.61.refs_2_.refs_1_), custom_call_target="tpu_custom_call" | custom-call | flops 536870912 | tf_op jit(solution)/shard_map/pallas_call | solution.py:500
  24.6 0.5 collective-permute-start.5
  25.1 1.2 %collective-permute-done.5.refs_3_ = bf16[512,256]{1,0:T(8,128)(2,1)S(1)} collective-permute-done((bf16[512,256]{1,0:T(8,128)(2,1)S(1)}, bf16[512,256]{1,0:T(8,128)(2,1)S(1)}, u32[]{:S(2)}, u32[]{:S(2)}) %collective-permute-start.5) | collective-permute-done | bytes 262176 | tf_op jit(solution)/shard_map/ppermute | solution.py:515
  26.3 0.0 collective-permute-done.4.refs_2_
  26.3 0.1 shard_map.124
  26.4 1.6 %collective-permute-start.6 = (bf16[128,768]{1,0:T(8,128)(2,1)S(1)}, bf16[128,768]{1,0:T(8,128)(2,1)S(1)}, u32[]{:S(2)}, u32[]{:S(2)}) collective-permute-start(bf16[128,768]{1,0:T(8,128)(2,1)S(1)} %get-tuple-element.69), channel_id=1, source_target_pairs={{0,1},{1,0},{2,3},{3,2},{4,5},{5,4},{6,7},{7,6},{8,9},{9,8},{10,11... | collective-permute-start | bytes 589832 | tf_op jit(solution)/shard_map/ppermute | solution.py:515
  28.0 0.4 collective-permute-start.7
  28.4 1.5 %collective-permute-start.8 = (bf16[128,768]{1,0:T(8,128)(2,1)S(1)}, bf16[128,768]{1,0:T(8,128)(2,1)S(1)}, u32[]{:S(2)}, u32[]{:S(2)}) collective-permute-start(bf16[128,768]{1,0:T(8,128)(2,1)S(1)} %get-tuple-element.71), channel_id=1, source_target_pairs={{0,3},{1,2},{2,1},{3,0},{4,7},{5,6},{6,5},{7,4},{8,11},{9,10},{10,... | collective-permute-start | bytes 589832 | tf_op jit(solution)/shard_map/ppermute | solution.py:515
  30.0 2.2 %shard_map.125 = (f32[38,32,512]{2,1,0:T(8,128)S(1)}, f32[37,32,512]{2,1,0:T(8,128)S(1)}, bf16[37,32,512]{2,1,0:T(8,128)(2,1)}) custom-call(bf16[39,32,512]{2,1,0:T(8,128)(2,1)S(1)} %get-tuple-element.55.grad_ref, bf16[3,512,512]{2,1,0:T(8,128)(2,1)S(1)} %get-tuple-element.56.w_ref, f32[40,32,512]{2,1,0:T(8,128)S(1)} %get-tuple-element.57.even_slope, ...), custom_call_target="tpu_custom_call" | custom-call | flops 1073741824 | tf_op jit(solution)/shard_map/pallas_call | solution.py:500
  32.2 2.7 %shard_map.126.parts_ref = f32[64,128]{1,0:T(8,128)S(1)} custom-call(s32[32,128]{1,0:T(8,128)S(1)} %get-tuple-element.53.valid_ref, f32[10,32,4096]{2,1,0:T(8,128)S(1)} %get-tuple-element.72.pre0, f32[32,512]{1,0:T(8,128)S(1)} %get-tuple-element.73.mean_ref, f32[32,512]{1,0:T(8,128)S(1)} %get-tuple-element.74.inv_ref, ...), custom_call_target="tpu_custom_call" | custom-call | flops 4294967296 | tf_op jit(solution)/shard_map/pallas_call | solution.py:500
  34.9 1.6 %collective-permute-start.9 = (f32[64,128]{1,0:T(8,128)S(1)}, f32[64,128]{1,0:T(8,128)S(1)}, u32[]{:S(2)}, u32[]{:S(2)}) collective-permute-start(f32[64,128]{1,0:T(8,128)S(1)} %shard_map.126.parts_ref), channel_id=1, source_target_pairs={{0,16},{8,24},{16,0},{24,8},{1,17},{9,25},{17,1},{25,9},{2,18},{10... | collective-permute-start | bytes 98312 | tf_op jit(solution)/shard_map/ppermute | solution.py:515
  36.5 2.4 %collective-permute-done.9.parts_got = f32[64,128]{1,0:T(8,128)S(1)} collective-permute-done((f32[64,128]{1,0:T(8,128)S(1)}, f32[64,128]{1,0:T(8,128)S(1)}, u32[]{:S(2)}, u32[]{:S(2)}) %collective-permute-start.9) | collective-permute-done | bytes 32800 | tf_op jit(solution)/shard_map/ppermute | solution.py:515
  38.9 0.0 collective-permute-done.6.got1
  38.9 0.0 collective-permute-done.7.got2
  38.9 0.1 collective-permute-done.8.got3
  39.1 0.1 shard_map.127
  39.2 2.7 %collective-permute-start.10 = (bf16[80,640]{1,0:T(8,128)(2,1)S(1)}, bf16[80,640]{1,0:T(8,128)(2,1)S(1)}, u32[]{:S(2)}, u32[]{:S(2)}) collective-permute-start(bf16[80,640]{1,0:T(8,128)(2,1)S(1)} %get-tuple-element.80), channel_id=1, source_target_pairs={{0,4},{1,5},{2,6},{3,7},{4,0},{5,1},{6,2},{7,3},{8,12},{9,13},{10,... | collective-permute-start | bytes 307208 | tf_op jit(solution)/shard_map/ppermute | solution.py:515
  41.8 1.5 %collective-permute-start.11 = (f32[16,128]{1,0:T(8,128)S(1)}, f32[16,128]{1,0:T(8,128)S(1)}, u32[]{:S(2)}, u32[]{:S(2)}) collective-permute-start(f32[16,128]{1,0:T(8,128)S(1)} %get-tuple-element.82), channel_id=1, source_target_pairs={{0,1},{1,0},{2,3},{3,2},{4,5},{5,4},{6,7},{7,6},{8,9},{9,8},{10,11... | collective-permute-start | bytes 24584 | tf_op jit(solution)/shard_map/ppermute | solution.py:515
  43.3 0.5 collective-permute-start.12
  43.8 1.5 %collective-permute-start.13 = (f32[16,128]{1,0:T(8,128)S(1)}, f32[16,128]{1,0:T(8,128)S(1)}, u32[]{:S(2)}, u32[]{:S(2)}) collective-permute-start(f32[16,128]{1,0:T(8,128)S(1)} %get-tuple-element.84), channel_id=1, source_target_pairs={{0,3},{1,2},{2,1},{3,0},{4,7},{5,6},{6,5},{7,4},{8,11},{9,10},{10,... | collective-permute-start | bytes 24584 | tf_op jit(solution)/shard_map/ppermute | solution.py:515
  45.3 0.2 collective-permute-done.11.small1
  45.5 1.5 %collective-permute-done.12.small2 = f32[16,128]{1,0:T(8,128)S(1)} collective-permute-done((f32[16,128]{1,0:T(8,128)S(1)}, f32[16,128]{1,0:T(8,128)S(1)}, u32[]{:S(2)}, u32[]{:S(2)}) %collective-permute-start.12) | collective-permute-done | bytes 8224 | tf_op jit(solution)/shard_map/ppermute | solution.py:515
  47.0 1.4 %collective-permute-done.13.small3 = f32[16,128]{1,0:T(8,128)S(1)} collective-permute-done((f32[16,128]{1,0:T(8,128)S(1)}, f32[16,128]{1,0:T(8,128)S(1)}, u32[]{:S(2)}, u32[]{:S(2)}) %collective-permute-start.13) | collective-permute-done | bytes 8224 | tf_op jit(solution)/shard_map/ppermute | solution.py:515
  48.3 0.0 collective-permute-done.10.got_ref
  48.3 1.6 %collective-permute-start.14 = (bf16[80,640]{1,0:T(8,128)(2,1)S(1)}, bf16[80,640]{1,0:T(8,128)(2,1)S(1)}, u32[]{:S(2)}, u32[]{:S(2)}) collective-permute-start(bf16[80,640]{1,0:T(8,128)(2,1)S(1)} %get-tuple-element.85.mine_ref), channel_id=1, source_target_pairs={{0,16},{8,24},{16,0},{24,8},{1,17},{9,25},{17,1},{25,9},{2,18},{10... | collective-permute-start | bytes 307208 | tf_op jit(solution)/shard_map/ppermute | solution.py:515
  49.9 0.3 collective-permute-start.15
  50.3 4.2 %collective-permute-done.15.small_got = f32[16,128]{1,0:T(8,128)S(1)} collective-permute-done((f32[16,128]{1,0:T(8,128)S(1)}, f32[16,128]{1,0:T(8,128)S(1)}, u32[]{:S(2)}, u32[]{:S(2)}) %collective-permute-start.15) | collective-permute-done | bytes 8224 | tf_op jit(solution)/shard_map/ppermute | solution.py:515
  54.5 0.0 collective-permute-done.14.got_ref
  54.5 0.1 collective-permute-start.16
  54.6 1.4 %collective-permute-done.16.other_ref = f32[80,640]{1,0:T(8,128)S(1)} collective-permute-done((f32[80,640]{1,0:T(8,128)S(1)}, f32[80,640]{1,0:T(8,128)S(1)}, u32[]{:S(2)}, u32[]{:S(2)}) %collective-permute-start.16) | collective-permute-done | bytes 204832 | tf_op jit(solution)/shard_map/ppermute | solution.py:515
  56.0 0.8 %shard_map.130 = (f32[3,64,512]{2,1,0:T(8,128)}, f32[10,64]{1,0:T(8,128)}, f32[1,64]{1,0:T(1,128)}, f32[1,64]{1,0:T(1,128)}) custom-call(f32[80,640]{1,0:T(8,128)S(1)} %shard_map.129.own_ref, f32[80,640]{1,0:T(8,128)S(1)} %collective-permute-done.16.other_ref), custom_call_target="tpu_custom_call" | custom-call | tf_op jit(solution)/shard_map/pallas_call | solution.py:500
  (2 shorter events, 0.1 us)
Async XLA Ops:
  0.6 5.9 %collective-permute-start = (bf16[32,384]{1,0:T(8,128)(2,1)}, bf16[32,384]{1,0:T(8,128)(2,1)S(1)}, u32[]{:S(2)}, u32[]{:S(2)}) collective-permute-start(bf16[32,384]{1,0:T(8,128)(2,1)} %wave_hbm.1), channel_id=1, source_target_pairs={{0,1},{1,0},{2,3},{3,2},{4,5},{5,4},{6,7},{7,6},{8,9},{9,8},{10,11... | collective-permute-start | bytes 73736 | tf_op jit(solution)/shard_map/ppermute | solution.py:515
  3.6 5.1 %collective-permute-start.2 = (bf16[32,384]{1,0:T(8,128)(2,1)}, bf16[32,384]{1,0:T(8,128)(2,1)S(1)}, u32[]{:S(2)}, u32[]{:S(2)}) collective-permute-start(bf16[32,384]{1,0:T(8,128)(2,1)} %wave_hbm.1), channel_id=1, source_target_pairs={{0,3},{1,2},{2,1},{3,0},{4,7},{5,6},{6,5},{7,4},{8,11},{9,10},{10,... | collective-permute-start | bytes 73736 | tf_op jit(solution)/shard_map/ppermute | solution.py:515
  5.2 4.0 %collective-permute-start.1 = (bf16[32,384]{1,0:T(8,128)(2,1)}, bf16[32,384]{1,0:T(8,128)(2,1)S(1)}, u32[]{:S(2)}, u32[]{:S(2)}) collective-permute-start(bf16[32,384]{1,0:T(8,128)(2,1)} %wave_hbm.1), channel_id=1, source_target_pairs={{0,2},{1,3},{2,0},{3,1},{4,6},{5,7},{6,4},{7,5},{8,10},{9,11},{10,... | collective-permute-start | bytes 73736 | tf_op jit(solution)/shard_map/ppermute | solution.py:515
  9.4 4.6 %collective-permute-start.3 = (bf16[16,384]{1,0:T(8,128)(2,1)S(1)}, bf16[16,384]{1,0:T(8,128)(2,1)S(1)}, u32[]{:S(2)}, u32[]{:S(2)}) collective-permute-start(bf16[16,384]{1,0:T(8,128)(2,1)S(1)} %get-tuple-element.52), channel_id=1, source_target_pairs={{0,4},{1,5},{2,6},{3,7},{4,0},{5,1},{6,2},{7,3},{8,12},{9,13},{10,... | collective-permute-start | bytes 36872 | tf_op jit(solution)/shard_map/ppermute | solution.py:515
  23.6 2.7 %collective-permute-start.4 = (bf16[512,512]{1,0:T(8,128)(2,1)S(1)}, bf16[512,512]{1,0:T(8,128)(2,1)S(1)}, u32[]{:S(2)}, u32[]{:S(2)}) collective-permute-start(bf16[512,512]{1,0:T(8,128)(2,1)S(1)} %get-tuple-element.64), channel_id=1, source_target_pairs={{0,8},{8,0},{16,24},{24,16},{1,9},{9,1},{17,25},{25,17},{2,10},{10... | collective-permute-start | bytes 1572872 | tf_op jit(solution)/shard_map/ppermute | solution.py:515
  24.6 1.7 %collective-permute-start.5 = (bf16[512,256]{1,0:T(8,128)(2,1)S(1)}, bf16[512,256]{1,0:T(8,128)(2,1)S(1)}, u32[]{:S(2)}, u32[]{:S(2)}) collective-permute-start(bf16[512,256]{1,0:T(8,128)(2,1)S(1)} %get-tuple-element.65), channel_id=1, source_target_pairs={{0,8},{8,0},{16,24},{24,16},{1,9},{9,1},{17,25},{25,17},{2,10},{10... | collective-permute-start | bytes 786440 | tf_op jit(solution)/shard_map/ppermute | solution.py:515
  26.4 12.5 %collective-permute-start.6 = (bf16[128,768]{1,0:T(8,128)(2,1)S(1)}, bf16[128,768]{1,0:T(8,128)(2,1)S(1)}, u32[]{:S(2)}, u32[]{:S(2)}) collective-permute-start(bf16[128,768]{1,0:T(8,128)(2,1)S(1)} %get-tuple-element.69), channel_id=1, source_target_pairs={{0,1},{1,0},{2,3},{3,2},{4,5},{5,4},{6,7},{7,6},{8,9},{9,8},{10,11... | collective-permute-start | bytes 589832 | tf_op jit(solution)/shard_map/ppermute | solution.py:515
  28.0 10.9 %collective-permute-start.7 = (bf16[128,768]{1,0:T(8,128)(2,1)S(1)}, bf16[128,768]{1,0:T(8,128)(2,1)S(1)}, u32[]{:S(2)}, u32[]{:S(2)}) collective-permute-start(bf16[128,768]{1,0:T(8,128)(2,1)S(1)} %get-tuple-element.70), channel_id=1, source_target_pairs={{0,2},{1,3},{2,0},{3,1},{4,6},{5,7},{6,4},{7,5},{8,10},{9,11},{10,... | collective-permute-start | bytes 589832 | tf_op jit(solution)/shard_map/ppermute | solution.py:515
  28.4 10.6 %collective-permute-start.8 = (bf16[128,768]{1,0:T(8,128)(2,1)S(1)}, bf16[128,768]{1,0:T(8,128)(2,1)S(1)}, u32[]{:S(2)}, u32[]{:S(2)}) collective-permute-start(bf16[128,768]{1,0:T(8,128)(2,1)S(1)} %get-tuple-element.71), channel_id=1, source_target_pairs={{0,3},{1,2},{2,1},{3,0},{4,7},{5,6},{6,5},{7,4},{8,11},{9,10},{10,... | collective-permute-start | bytes 589832 | tf_op jit(solution)/shard_map/ppermute | solution.py:515
  34.9 4.0 %collective-permute-start.9 = (f32[64,128]{1,0:T(8,128)S(1)}, f32[64,128]{1,0:T(8,128)S(1)}, u32[]{:S(2)}, u32[]{:S(2)}) collective-permute-start(f32[64,128]{1,0:T(8,128)S(1)} %shard_map.126.parts_ref), channel_id=1, source_target_pairs={{0,16},{8,24},{16,0},{24,8},{1,17},{9,25},{17,1},{25,9},{2,18},{10... | collective-permute-start | bytes 98312 | tf_op jit(solution)/shard_map/ppermute | solution.py:515
  39.2 9.2 %collective-permute-start.10 = (bf16[80,640]{1,0:T(8,128)(2,1)S(1)}, bf16[80,640]{1,0:T(8,128)(2,1)S(1)}, u32[]{:S(2)}, u32[]{:S(2)}) collective-permute-start(bf16[80,640]{1,0:T(8,128)(2,1)S(1)} %get-tuple-element.80), channel_id=1, source_target_pairs={{0,4},{1,5},{2,6},{3,7},{4,0},{5,1},{6,2},{7,3},{8,12},{9,13},{10,... | collective-permute-start | bytes 307208 | tf_op jit(solution)/shard_map/ppermute | solution.py:515
  41.8 3.7 %collective-permute-start.11 = (f32[16,128]{1,0:T(8,128)S(1)}, f32[16,128]{1,0:T(8,128)S(1)}, u32[]{:S(2)}, u32[]{:S(2)}) collective-permute-start(f32[16,128]{1,0:T(8,128)S(1)} %get-tuple-element.82), channel_id=1, source_target_pairs={{0,1},{1,0},{2,3},{3,2},{4,5},{5,4},{6,7},{7,6},{8,9},{9,8},{10,11... | collective-permute-start | bytes 24584 | tf_op jit(solution)/shard_map/ppermute | solution.py:515
  43.3 3.7 %collective-permute-start.12 = (f32[16,128]{1,0:T(8,128)S(1)}, f32[16,128]{1,0:T(8,128)S(1)}, u32[]{:S(2)}, u32[]{:S(2)}) collective-permute-start(f32[16,128]{1,0:T(8,128)S(1)} %get-tuple-element.83), channel_id=1, source_target_pairs={{0,2},{1,3},{2,0},{3,1},{4,6},{5,7},{6,4},{7,5},{8,10},{9,11},{10,... | collective-permute-start | bytes 24584 | tf_op jit(solution)/shard_map/ppermute | solution.py:515
  43.8 4.5 %collective-permute-start.13 = (f32[16,128]{1,0:T(8,128)S(1)}, f32[16,128]{1,0:T(8,128)S(1)}, u32[]{:S(2)}, u32[]{:S(2)}) collective-permute-start(f32[16,128]{1,0:T(8,128)S(1)} %get-tuple-element.84), channel_id=1, source_target_pairs={{0,3},{1,2},{2,1},{3,0},{4,7},{5,6},{6,5},{7,4},{8,11},{9,10},{10,... | collective-permute-start | bytes 24584 | tf_op jit(solution)/shard_map/ppermute | solution.py:515
  48.3 6.1 %collective-permute-start.14 = (bf16[80,640]{1,0:T(8,128)(2,1)S(1)}, bf16[80,640]{1,0:T(8,128)(2,1)S(1)}, u32[]{:S(2)}, u32[]{:S(2)}) collective-permute-start(bf16[80,640]{1,0:T(8,128)(2,1)S(1)} %get-tuple-element.85.mine_ref), channel_id=1, source_target_pairs={{0,16},{8,24},{16,0},{24,8},{1,17},{9,25},{17,1},{25,9},{2,18},{10... | collective-permute-start | bytes 307208 | tf_op jit(solution)/shard_map/ppermute | solution.py:515
  49.9 4.5 %collective-permute-start.15 = (f32[16,128]{1,0:T(8,128)S(1)}, f32[16,128]{1,0:T(8,128)S(1)}, u32[]{:S(2)}, u32[]{:S(2)}) collective-permute-start(f32[16,128]{1,0:T(8,128)S(1)} %get-tuple-element.86.small_ref), channel_id=1, source_target_pairs={{0,4},{1,5},{2,6},{3,7},{4,0},{5,1},{6,2},{7,3},{8,12},{9,13},{10,... | collective-permute-start | bytes 24584 | tf_op jit(solution)/shard_map/ppermute | solution.py:515
  54.5 1.5 %collective-permute-start.16 = (f32[80,640]{1,0:T(8,128)S(1)}, f32[80,640]{1,0:T(8,128)S(1)}, u32[]{:S(2)}, u32[]{:S(2)}) collective-permute-start(f32[80,640]{1,0:T(8,128)S(1)} %shard_map.129.own_ref), channel_id=1, source_target_pairs={{0,8},{8,0},{16,24},{24,16},{1,9},{9,1},{17,25},{25,17},{2,10},{10... | collective-permute-start | bytes 614408 | tf_op jit(solution)/shard_map/ppermute | solution.py:515

commit v11 on v7

--- a/solution.py
+++ b/solution.py
@@ -286,18 +286,20 @@
     turn(last, frames1 - last * half)
 
 
-def outer_kernel(skip, act_ref, grad_t_ref, keep_ref, send_ref):
-    rows, chans = act_ref.shape[1:]
+def outer_kernel(skips, *refs):
+    acts, (grad_t_ref, keep_ref, send_ref) = refs[:-3], refs[-3:]
+    rows, chans = acts[0].shape[1:]
     frames = grad_t_ref.shape[1] // rows
     half = chans // 2
     core = lax.rem(lax.axis_index("grp"), 2)
-    for side, out_ref in ((1 - core, send_ref), (core, keep_ref)):
-        lanes = pl.ds(pl.multiple_of(side * half, half), half)
-        acts = act_ref[skip : skip + frames, :, lanes].reshape(frames * rows, half)
-        out_ref[...] = dot(grad_t_ref[...], acts).astype(out_ref.dtype)
-
-
-def input_kernel(grad_ref, w_ref, even_slope, odd_slope, after_ref, feat_ref, even_ref, odd_ref, feat_out, sem):
+    for tap, (act_ref, skip) in enumerate(zip(acts, skips)):
+        for side, out_ref in ((1 - core, send_ref), (core, keep_ref)):
+            lanes = pl.ds(pl.multiple_of(side * half, half), half)
+            value = dot(grad_t_ref[...], act_ref[skip : skip + frames, :, lanes].reshape(frames * rows, half))
+            out_ref[:, tap * half : (tap + 1) * half] = value.astype(out_ref.dtype)
+
+
+def input_kernel(grad_ref, w_ref, even_slope, odd_slope, feat_ref, even_ref, odd_ref, feat_out, sem):
     leaving = pltpu.make_async_copy(feat_ref, feat_out, sem)
     leaving.start()
     evens, rows, chans = even_ref.shape
@@ -403,16 +405,15 @@
         ref[...] = quarters[jnp.bitwise_xor(place, offset)]
 
 
-def plane_kernel(second, *refs):
-    keeps, others, outs = refs[:second], refs[second : 2 * second], refs[2 * second :]
+def plane_kernel(*refs):
+    keeps, others, outs = refs[:2], refs[2:4], refs[5:]
     size = outs[0].shape[0]
-    half = keeps[0].shape[1]
+    edge = keeps[0].shape[1]
     place = lax.rem(lax.axis_index("dev"), 4)
     for offset, out_ref in enumerate(outs):
         lines = pl.ds(pl.multiple_of(jnp.bitwise_xor(place, offset) * size, size), size)
-        for tap, (keep_ref, got_ref) in enumerate(zip(keeps, others)):
-            value = keep_ref[lines, :] + got_ref[lines, :].astype(F32)
-            out_ref[:, tap * half : (tap + 1) * half] = value.astype(out_ref.dtype)
+        for lanes, keep_ref, got_ref in zip((slice(0, edge), slice(edge, None)), keeps, others):
+            out_ref[:, lanes] = (keep_ref[lines, :] + got_ref[lines, :].astype(F32)).astype(out_ref.dtype)
 
 
 def part_kernel(own_ref, got1, got2, small_ref, sum_ref, total_ref):
@@ -594,30 +595,28 @@
     half = chans // 2
     wide = taps_second * half
     keeps, others = [], []
-    for acts, skip in ((even, 0), (odd, 0), (even, 1)):
+    for acts, skips in (((even, odd), (0, 0)), ((even,), (1,))):
+        shape = (chans, len(acts) * half)
         keep, send = call(
-            functools.partial(outer_kernel, skip),
-            [((chans, half), F32), ((chans, half), BF16)],
-            [acts, grad_t],
-            flops=1 << 29,
+            functools.partial(outer_kernel, skips), [(shape, F32), (shape, BF16)], [*acts, grad_t], flops=len(acts) << 29
         )
         keeps.append(keep)
         others.append(swap(send, "grp", 1))
-    quarter = chans // 4
-    own, *sends = call(
-        functools.partial(plane_kernel, taps_second),
-        [((quarter, wide), F32)] + [((quarter, wide), BF16)] * 3,
-        [*keeps, *others],
-    )
-    gots = [swap(part, "dev", offset) for offset, part in enumerate(sends, 1)]
     evens, odds = (frames0 + 1) // 2, frames0 // 2
     lift_even, lift_odd, features = call(
         input_kernel,
         [((evens, rows, chans), F32), ((odds, rows, chans), F32), ((frames1, rows, chans), BF16, "hbm")],
-        [grad, w_in, even_slope, odd_slope, own, feat],
+        [grad, w_in, even_slope, odd_slope, feat],
         scratch=[pltpu.SemaphoreType.DMA],
         flops=1 << 30,
     )
+    quarter = chans // 4
+    own, *sends = call(
+        plane_kernel,
+        [((quarter, wide), F32)] + [((quarter, wide), BF16)] * 3,
+        [*keeps, *others, lift_odd],
+    )
+    gots = [swap(part, "dev", offset) for offset, part in enumerate(sends, 1)]
     small, *smalls = call(
         functools.partial(backward_kernel, frames0, taps),
         [((16, quarter), F32)] * 4,

time: 56.5 us -> 54.7 us (0.968)
  waiting for transfers between devices: 18.1 us -> 16.4 us
    ppermute x16 -> x15, waiting for transfers between devices: 18.1 us -> 16.4 us  [swap(): return lax.ppermute(value, axis, [(i, i ^ offset) for i in range(size)])]
    pallas_call x14 -> x13, Pallas kernels: 18.1 us -> 18 us  [call(): pl.pallas_call(kernel, out_shape=[jax.ShapeDtypeStruct(out[0], out[1]) if...]
    ppermute x16 -> x15, starting transfers between devices: 19.3 us -> 19.3 us  [swap(): return lax.ppermute(value, axis, [(i, i ^ offset) for i in range(size)])]
  transfers between devices with their start and end apart: 16 -> 15, of which waited for: 12 -> 8; matrix products, arithmetic and copies ran while one was open for 0% -> 0% of each run, Pallas kernels for 11% -> 13%
where the time goes in v11:
time: 54.7 us; the launch traced here: 54.5 us
  starting transfers between devices  19.3 us (35%)
  Pallas kernels  18 us (33%)
  waiting for transfers between devices  16.4 us (30%)
  between operations  0.75 us (1%)
    ppermute x15, starting transfers between devices, swap(): return lax.ppermute(value, axis, [(i, i ^ offset) for i in range(size)])  19.3 us
    pallas_call x13, Pallas kernels, call(): pl.pallas_call(kernel, out_shape=[jax.ShapeDtypeStruct(out[0], out[1]) if...  18 us
    ppermute x15, waiting for transfers between devices, swap(): return lax.ppermute(value, axis, [(i, i ^ offset) for i in range(size)])  16.4 us
  transfers between devices with their start and end apart: 15, of which 8 were waited for; matrix products, arithmetic and copies ran while one was open for 0% of the time, Pallas kernels for 13%

profile of v11, /device:TPU:0, one launch (start us, length us, event | category | flops | bytes accessed | tf_op | source)
XLA Modules:
  0.0 54.5 jit_solution(2013254473239395521)
XLA Ops:
  0.6 3.0 %collective-permute-start = (bf16[32,384]{1,0:T(8,128)(2,1)}, bf16[32,384]{1,0:T(8,128)(2,1)S(1)}, u32[]{:S(2)}, u32[]{:S(2)}) collective-permute-start(bf16[32,384]{1,0:T(8,128)(2,1)} %wave_hbm.1), channel_id=1, source_target_pairs={{0,1},{1,0},{2,3},{3,2},{4,5},{5,4},{6,7},{7,6},{8,9},{9,8},{10,11... | collective-permute-start | bytes 73736 | tf_op jit(solution)/shard_map/ppermute | solution.py:508
  3.6 1.5 %collective-permute-start.2 = (bf16[32,384]{1,0:T(8,128)(2,1)}, bf16[32,384]{1,0:T(8,128)(2,1)S(1)}, u32[]{:S(2)}, u32[]{:S(2)}) collective-permute-start(bf16[32,384]{1,0:T(8,128)(2,1)} %wave_hbm.1), channel_id=1, source_target_pairs={{0,3},{1,2},{2,1},{3,0},{4,7},{5,6},{6,5},{7,4},{8,11},{9,10},{10,... | collective-permute-start | bytes 73736 | tf_op jit(solution)/shard_map/ppermute | solution.py:508
  5.2 0.0 collective-permute-start.1
  5.2 1.3 %shard_map.119 = (s32[32,128]{1,0:T(8,128)S(1)}, bf16[128,4096]{1,0:T(8,128)(2,1)S(1)}, bf16[16,256]{1,0:T(8,128)(2,1)S(1)}, bf16[16,256]{1,0:T(8,128)(2,1)S(1)}, bf16[32,384]{1,0:T(8,128)(2,1)S(1)}) custom-call(s32[8,32]{1,0:T(8,128)} %order_hbm.1, s32[1,256]{1,0:T(1,128)} %bitcast.11, bf16[10,512]{1,0:T(8,128)(2,1)} %w_hbm.2, bf16[32,384]{1,0:T(8,128)(2,1)} %wave_hbm.1), custom_call_target="tpu_custom_call" | custom-call | tf_op jit(solution)/shard_map/pallas_call | solution.py:493
  6.5 0.0 collective-permute-done.refs_1_
  6.5 2.2 %collective-permute-done.2.refs_3_ = bf16[32,384]{1,0:T(8,128)(2,1)S(1)} collective-permute-done((bf16[32,384]{1,0:T(8,128)(2,1)}, bf16[32,384]{1,0:T(8,128)(2,1)S(1)}, u32[]{:S(2)}, u32[]{:S(2)}) %collective-permute-start.2) | collective-permute-done | bytes 24608 | tf_op jit(solution)/shard_map/ppermute | solution.py:508
  8.7 0.5 collective-permute-done.1.refs_2_
  9.2 0.2 shard_map.120
  9.4 2.6 %collective-permute-start.3 = (bf16[16,384]{1,0:T(8,128)(2,1)S(1)}, bf16[16,384]{1,0:T(8,128)(2,1)S(1)}, u32[]{:S(2)}, u32[]{:S(2)}) collective-permute-start(bf16[16,384]{1,0:T(8,128)(2,1)S(1)} %get-tuple-element.52), channel_id=1, source_target_pairs={{0,4},{1,5},{2,6},{3,7},{4,0},{5,1},{6,2},{7,3},{8,12},{9,13},{10,... | collective-permute-start | bytes 36872 | tf_op jit(solution)/shard_map/ppermute | solution.py:508
  12.1 2.0 %collective-permute-done.3.far_ref = bf16[16,384]{1,0:T(8,128)(2,1)S(1)} collective-permute-done((bf16[16,384]{1,0:T(8,128)(2,1)S(1)}, bf16[16,384]{1,0:T(8,128)(2,1)S(1)}, u32[]{:S(2)}, u32[]{:S(2)}) %collective-permute-start.3) | collective-permute-done | bytes 12320 | tf_op jit(solution)/shard_map/ppermute | solution.py:508
  14.1 8.0 %shard_map.121 = (bf16[37,32,512]{2,1,0:T(8,128)(2,1)S(1)}, bf16[41,32,512]{2,1,0:T(8,128)(2,1)S(1)}, bf16[40,32,512]{2,1,0:T(8,128)(2,1)S(1)}, f32[10,32,4096]{...) custom-call(bf16[16,384]{1,0:T(8,128)(2,1)S(1)} %get-tuple-element.5, ...), custom_call_target="tpu_custom_call" | custom-call | tf_op jit(solution)/shard_map/pallas_call | solution.py:493
  22.1 1.5 %shard_map.123 = (f32[512,512]{1,0:T(8,128)S(1)}, bf16[512,512]{1,0:T(8,128)(2,1)S(1)}) custom-call(bf16[41,32,512]{2,1,0:T(8,128)(2,1)S(1)} %get-tuple-element.61.refs_0_, bf16[40,32,512]{2,1,0:T(8,128)(2,1)S(1)} %get-tuple-element.62.refs_1_, bf16[512,1280]{1,0:T(8,128)(2,1)S(1)} %get-tuple-element.63.refs_2_.refs_1_), custom_call_target="tpu_custom_call" | custom-call | flops 1073741824 | tf_op jit(solution)/shard_map/pallas_call | solution.py:493
  23.6 0.1 collective-permute-start.4
  23.7 0.9 %shard_map.124 = (f32[512,256]{1,0:T(8,128)S(1)}, bf16[512,256]{1,0:T(8,128)(2,1)S(1)}) custom-call(bf16[41,32,512]{2,1,0:T(8,128)(2,1)S(1)} %get-tuple-element.61.refs_0_, bf16[512,1280]{1,0:T(8,128)(2,1)S(1)} %get-tuple-element.63.refs_2_.refs_1_), custom_call_target="tpu_custom_call" | custom-call | flops 536870912 | tf_op jit(solution)/shard_map/pallas_call | solution.py:493
  24.6 0.5 %collective-permute-start.5 = (bf16[512,256]{1,0:T(8,128)(2,1)S(1)}, bf16[512,256]{1,0:T(8,128)(2,1)S(1)}, u32[]{:S(2)}, u32[]{:S(2)}) collective-permute-start(bf16[512,256]{1,0:T(8,128)(2,1)S(1)} %get-tuple-element.67), channel_id=1, source_target_pairs={{0,8},{8,0},{16,24},{24,16},{1,9},{9,1},{17,25},{25,17},{2,10},{10... | collective-permute-start | bytes 786440 | tf_op jit(solution)/shard_map/ppermute | solution.py:508
  25.1 2.2 %shard_map.122 = (f32[38,32,512]{2,1,0:T(8,128)S(1)}, f32[37,32,512]{2,1,0:T(8,128)S(1)}, bf16[37,32,512]{2,1,0:T(8,128)(2,1)}) custom-call(bf16[39,32,512]{2,1,0:T(8,128)(2,1)S(1)} %get-tuple-element.55.grad_ref, bf16[3,512,512]{2,1,0:T(8,128)(2,1)S(1)} %get-tuple-element.56.w_ref, f32[40,32,512]{2,1,0:T(8,128)S(1)} %get-tuple-element.57.even_slope, ...), custom_call_target="tpu_custom_call" | custom-call | flops 1073741824 | tf_op jit(solution)/shard_map/pallas_call | solution.py:493
  27.4 0.0 collective-permute-done.5.refs_3_
  27.4 0.0 collective-permute-done.4.refs_2_
  27.4 0.1 shard_map.125
  27.5 1.6 %collective-permute-start.6 = (bf16[128,768]{1,0:T(8,128)(2,1)S(1)}, bf16[128,768]{1,0:T(8,128)(2,1)S(1)}, u32[]{:S(2)}, u32[]{:S(2)}) collective-permute-start(bf16[128,768]{1,0:T(8,128)(2,1)S(1)} %get-tuple-element.70), channel_id=1, source_target_pairs={{0,1},{1,0},{2,3},{3,2},{4,5},{5,4},{6,7},{7,6},{8,9},{9,8},{10,11... | collective-permute-start | bytes 589832 | tf_op jit(solution)/shard_map/ppermute | solution.py:508
  29.1 0.4 collective-permute-start.7
  29.5 1.5 %collective-permute-start.8 = (bf16[128,768]{1,0:T(8,128)(2,1)S(1)}, bf16[128,768]{1,0:T(8,128)(2,1)S(1)}, u32[]{:S(2)}, u32[]{:S(2)}) collective-permute-start(bf16[128,768]{1,0:T(8,128)(2,1)S(1)} %get-tuple-element.80), channel_id=1, source_target_pairs={{0,3},{1,2},{2,1},{3,0},{4,7},{5,6},{6,5},{7,4},{8,11},{9,10},{10,... | collective-permute-start | bytes 589832 | tf_op jit(solution)/shard_map/ppermute | solution.py:508
  31.1 2.8 %shard_map.126 = (f32[16,128]{1,0:T(8,128)S(1)}, f32[16,128]{1,0:T(8,128)S(1)}, f32[16,128]{1,0:T(8,128)S(1)}, f32[16,128]{1,0:T(8,128)S(1)}) custom-call(s32[32,128]{1,0:T(8,128)S(1)} %get-tuple-element.53.valid_ref, f32[10,32,4096]{2,1,0:T(8,128)S(1)} %get-tuple-element.72.pre0, f32[32,512]{1,0:T(8,128)S(1)} %get-tuple-element.73.mean_ref, ...), custom_call_target="tpu_custom_call" | custom-call | flops 4294967296 | tf_op jit(solution)/shard_map/pallas_call | solution.py:493
  33.9 1.0 %collective-permute-start.10 = (f32[16,128]{1,0:T(8,128)S(1)}, f32[16,128]{1,0:T(8,128)S(1)}, u32[]{:S(2)}, u32[]{:S(2)}) collective-permute-start(f32[16,128]{1,0:T(8,128)S(1)} %get-tuple-element.83), channel_id=1, source_target_pairs={{0,2},{1,3},{2,0},{3,1},{4,6},{5,7},{6,4},{7,5},{8,10},{9,11},{10,... | collective-permute-start | bytes 24584 | tf_op jit(solution)/shard_map/ppermute | solution.py:508
  34.9 2.0 %collective-permute-start.11 = (f32[16,128]{1,0:T(8,128)S(1)}, f32[16,128]{1,0:T(8,128)S(1)}, u32[]{:S(2)}, u32[]{:S(2)}) collective-permute-start(f32[16,128]{1,0:T(8,128)S(1)} %get-tuple-element.84), channel_id=1, source_target_pairs={{0,3},{1,2},{2,1},{3,0},{4,7},{5,6},{6,5},{7,4},{8,11},{9,10},{10,... | collective-permute-start | bytes 24584 | tf_op jit(solution)/shard_map/ppermute | solution.py:508
  37.0 0.0 collective-permute-done.6.got1
  37.0 0.0 collective-permute-done.7.got2
  37.0 0.1 shard_map.127
  37.0 0.6 %collective-permute-start.9 = (f32[16,128]{1,0:T(8,128)S(1)}, f32[16,128]{1,0:T(8,128)S(1)}, u32[]{:S(2)}, u32[]{:S(2)}) collective-permute-start(f32[16,128]{1,0:T(8,128)S(1)} %get-tuple-element.82), channel_id=1, source_target_pairs={{0,1},{1,0},{2,3},{3,2},{4,5},{5,4},{6,7},{7,6},{8,9},{9,8},{10,11... | collective-permute-start | bytes 24584 | tf_op jit(solution)/shard_map/ppermute | solution.py:508
  37.6 2.5 %collective-permute-done.10.small2 = f32[16,128]{1,0:T(8,128)S(1)} collective-permute-done((f32[16,128]{1,0:T(8,128)S(1)}, f32[16,128]{1,0:T(8,128)S(1)}, u32[]{:S(2)}, u32[]{:S(2)}) %collective-permute-start.10) | collective-permute-done | bytes 8224 | tf_op jit(solution)/shard_map/ppermute | solution.py:508
  40.1 0.0 collective-permute-done.11.small3
  40.2 0.0 collective-permute-done.8.got3
  40.2 0.6 %collective-permute-done.9.small1 = f32[16,128]{1,0:T(8,128)S(1)} collective-permute-done((f32[16,128]{1,0:T(8,128)S(1)}, f32[16,128]{1,0:T(8,128)S(1)}, u32[]{:S(2)}, u32[]{:S(2)}) %collective-permute-start.9) | collective-permute-done | bytes 8224 | tf_op jit(solution)/shard_map/ppermute | solution.py:508
  40.8 0.1 shard_map.128
  40.8 2.6 %collective-permute-start.12 = (bf16[80,640]{1,0:T(8,128)(2,1)S(1)}, bf16[80,640]{1,0:T(8,128)(2,1)S(1)}, u32[]{:S(2)}, u32[]{:S(2)}) collective-permute-start(bf16[80,640]{1,0:T(8,128)(2,1)S(1)} %get-tuple-element.86), channel_id=1, source_target_pairs={{0,4},{1,5},{2,6},{3,7},{4,0},{5,1},{6,2},{7,3},{8,12},{9,13},{10,... | collective-permute-start | bytes 307208 | tf_op jit(solution)/shard_map/ppermute | solution.py:508
  43.4 4.0 %collective-permute-done.12.got_ref = bf16[80,640]{1,0:T(8,128)(2,1)S(1)} collective-permute-done((bf16[80,640]{1,0:T(8,128)(2,1)S(1)}, bf16[80,640]{1,0:T(8,128)(2,1)S(1)}, u32[]{:S(2)}, u32[]{:S(2)}) %collective-permute-start.12) | collective-permute-done | bytes 102432 | tf_op jit(solution)/shard_map/ppermute | solution.py:508
  47.4 1.6 %collective-permute-start.13 = (bf16[80,640]{1,0:T(8,128)(2,1)S(1)}, bf16[80,640]{1,0:T(8,128)(2,1)S(1)}, u32[]{:S(2)}, u32[]{:S(2)}) collective-permute-start(bf16[80,640]{1,0:T(8,128)(2,1)S(1)} %shard_map.129.mine_ref), channel_id=1, source_target_pairs={{0,16},{8,24},{16,0},{24,8},{1,17},{9,25},{17,1},{25,9},{2,18},{10... | collective-permute-start | bytes 307208 | tf_op jit(solution)/shard_map/ppermute | solution.py:508
  49.0 3.1 %collective-permute-done.13.got_ref = bf16[80,640]{1,0:T(8,128)(2,1)S(1)} collective-permute-done((bf16[80,640]{1,0:T(8,128)(2,1)S(1)}, bf16[80,640]{1,0:T(8,128)(2,1)S(1)}, u32[]{:S(2)}, u32[]{:S(2)}) %collective-permute-start.13) | collective-permute-done | bytes 102432 | tf_op jit(solution)/shard_map/ppermute | solution.py:508
  52.2 0.1 collective-permute-start.14
  52.3 1.4 %collective-permute-done.14.other_ref = f32[80,640]{1,0:T(8,128)S(1)} collective-permute-done((f32[80,640]{1,0:T(8,128)S(1)}, f32[80,640]{1,0:T(8,128)S(1)}, u32[]{:S(2)}, u32[]{:S(2)}) %collective-permute-start.14) | collective-permute-done | bytes 204832 | tf_op jit(solution)/shard_map/ppermute | solution.py:508
  53.7 0.8 %shard_map.131 = (f32[3,64,512]{2,1,0:T(8,128)}, f32[10,64]{1,0:T(8,128)}, f32[1,64]{1,0:T(1,128)}, f32[1,64]{1,0:T(1,128)}) custom-call(f32[80,640]{1,0:T(8,128)S(1)} %shard_map.130.own_ref, f32[80,640]{1,0:T(8,128)S(1)} %collective-permute-done.14.other_ref), custom_call_target="tpu_custom_call" | custom-call | tf_op jit(solution)/shard_map/pallas_call | solution.py:493
  (2 shorter events, 0.0 us)
Async XLA Ops:
  0.6 5.9 %collective-permute-start = (bf16[32,384]{1,0:T(8,128)(2,1)}, bf16[32,384]{1,0:T(8,128)(2,1)S(1)}, u32[]{:S(2)}, u32[]{:S(2)}) collective-permute-start(bf16[32,384]{1,0:T(8,128)(2,1)} %wave_hbm.1), channel_id=1, source_target_pairs={{0,1},{1,0},{2,3},{3,2},{4,5},{5,4},{6,7},{7,6},{8,9},{9,8},{10,11... | collective-permute-start | bytes 73736 | tf_op jit(solution)/shard_map/ppermute | solution.py:508
  3.6 5.1 %collective-permute-start.2 = (bf16[32,384]{1,0:T(8,128)(2,1)}, bf16[32,384]{1,0:T(8,128)(2,1)S(1)}, u32[]{:S(2)}, u32[]{:S(2)}) collective-permute-start(bf16[32,384]{1,0:T(8,128)(2,1)} %wave_hbm.1), channel_id=1, source_target_pairs={{0,3},{1,2},{2,1},{3,0},{4,7},{5,6},{6,5},{7,4},{8,11},{9,10},{10,... | collective-permute-start | bytes 73736 | tf_op jit(solution)/shard_map/ppermute | solution.py:508
  5.2 4.0 %collective-permute-start.1 = (bf16[32,384]{1,0:T(8,128)(2,1)}, bf16[32,384]{1,0:T(8,128)(2,1)S(1)}, u32[]{:S(2)}, u32[]{:S(2)}) collective-permute-start(bf16[32,384]{1,0:T(8,128)(2,1)} %wave_hbm.1), channel_id=1, source_target_pairs={{0,2},{1,3},{2,0},{3,1},{4,6},{5,7},{6,4},{7,5},{8,10},{9,11},{10,... | collective-permute-start | bytes 73736 | tf_op jit(solution)/shard_map/ppermute | solution.py:508
  9.4 4.6 %collective-permute-start.3 = (bf16[16,384]{1,0:T(8,128)(2,1)S(1)}, bf16[16,384]{1,0:T(8,128)(2,1)S(1)}, u32[]{:S(2)}, u32[]{:S(2)}) collective-permute-start(bf16[16,384]{1,0:T(8,128)(2,1)S(1)} %get-tuple-element.52), channel_id=1, source_target_pairs={{0,4},{1,5},{2,6},{3,7},{4,0},{5,1},{6,2},{7,3},{8,12},{9,13},{10,... | collective-permute-start | bytes 36872 | tf_op jit(solution)/shard_map/ppermute | solution.py:508
  23.6 3.7 %collective-permute-start.4 = (bf16[512,512]{1,0:T(8,128)(2,1)S(1)}, bf16[512,512]{1,0:T(8,128)(2,1)S(1)}, u32[]{:S(2)}, u32[]{:S(2)}) collective-permute-start(bf16[512,512]{1,0:T(8,128)(2,1)S(1)} %get-tuple-element.66), channel_id=1, source_target_pairs={{0,8},{8,0},{16,24},{24,16},{1,9},{9,1},{17,25},{25,17},{2,10},{10... | collective-permute-start | bytes 1572872 | tf_op jit(solution)/shard_map/ppermute | solution.py:508
  24.6 2.8 %collective-permute-start.5 = (bf16[512,256]{1,0:T(8,128)(2,1)S(1)}, bf16[512,256]{1,0:T(8,128)(2,1)S(1)}, u32[]{:S(2)}, u32[]{:S(2)}) collective-permute-start(bf16[512,256]{1,0:T(8,128)(2,1)S(1)} %get-tuple-element.67), channel_id=1, source_target_pairs={{0,8},{8,0},{16,24},{24,16},{1,9},{9,1},{17,25},{25,17},{2,10},{10... | collective-permute-start | bytes 786440 | tf_op jit(solution)/shard_map/ppermute | solution.py:508
  27.5 9.4 %collective-permute-start.6 = (bf16[128,768]{1,0:T(8,128)(2,1)S(1)}, bf16[128,768]{1,0:T(8,128)(2,1)S(1)}, u32[]{:S(2)}, u32[]{:S(2)}) collective-permute-start(bf16[128,768]{1,0:T(8,128)(2,1)S(1)} %get-tuple-element.70), channel_id=1, source_target_pairs={{0,1},{1,0},{2,3},{3,2},{4,5},{5,4},{6,7},{7,6},{8,9},{9,8},{10,11... | collective-permute-start | bytes 589832 | tf_op jit(solution)/shard_map/ppermute | solution.py:508
  29.1 7.9 %collective-permute-start.7 = (bf16[128,768]{1,0:T(8,128)(2,1)S(1)}, bf16[128,768]{1,0:T(8,128)(2,1)S(1)}, u32[]{:S(2)}, u32[]{:S(2)}) collective-permute-start(bf16[128,768]{1,0:T(8,128)(2,1)S(1)} %get-tuple-element.71), channel_id=1, source_target_pairs={{0,2},{1,3},{2,0},{3,1},{4,6},{5,7},{6,4},{7,5},{8,10},{9,11},{10,... | collective-permute-start | bytes 589832 | tf_op jit(solution)/shard_map/ppermute | solution.py:508
  29.5 10.6 %collective-permute-start.8 = (bf16[128,768]{1,0:T(8,128)(2,1)S(1)}, bf16[128,768]{1,0:T(8,128)(2,1)S(1)}, u32[]{:S(2)}, u32[]{:S(2)}) collective-permute-start(bf16[128,768]{1,0:T(8,128)(2,1)S(1)} %get-tuple-element.80), channel_id=1, source_target_pairs={{0,3},{1,2},{2,1},{3,0},{4,7},{5,6},{6,5},{7,4},{8,11},{9,10},{10,... | collective-permute-start | bytes 589832 | tf_op jit(solution)/shard_map/ppermute | solution.py:508
  33.9 6.2 %collective-permute-start.10 = (f32[16,128]{1,0:T(8,128)S(1)}, f32[16,128]{1,0:T(8,128)S(1)}, u32[]{:S(2)}, u32[]{:S(2)}) collective-permute-start(f32[16,128]{1,0:T(8,128)S(1)} %get-tuple-element.83), channel_id=1, source_target_pairs={{0,2},{1,3},{2,0},{3,1},{4,6},{5,7},{6,4},{7,5},{8,10},{9,11},{10,... | collective-permute-start | bytes 24584 | tf_op jit(solution)/shard_map/ppermute | solution.py:508
  34.9 5.2 %collective-permute-start.11 = (f32[16,128]{1,0:T(8,128)S(1)}, f32[16,128]{1,0:T(8,128)S(1)}, u32[]{:S(2)}, u32[]{:S(2)}) collective-permute-start(f32[16,128]{1,0:T(8,128)S(1)} %get-tuple-element.84), channel_id=1, source_target_pairs={{0,3},{1,2},{2,1},{3,0},{4,7},{5,6},{6,5},{7,4},{8,11},{9,10},{10,... | collective-permute-start | bytes 24584 | tf_op jit(solution)/shard_map/ppermute | solution.py:508
  37.0 3.7 %collective-permute-start.9 = (f32[16,128]{1,0:T(8,128)S(1)}, f32[16,128]{1,0:T(8,128)S(1)}, u32[]{:S(2)}, u32[]{:S(2)}) collective-permute-start(f32[16,128]{1,0:T(8,128)S(1)} %get-tuple-element.82), channel_id=1, source_target_pairs={{0,1},{1,0},{2,3},{3,2},{4,5},{5,4},{6,7},{7,6},{8,9},{9,8},{10,11... | collective-permute-start | bytes 24584 | tf_op jit(solution)/shard_map/ppermute | solution.py:508
  40.8 6.6 %collective-permute-start.12 = (bf16[80,640]{1,0:T(8,128)(2,1)S(1)}, bf16[80,640]{1,0:T(8,128)(2,1)S(1)}, u32[]{:S(2)}, u32[]{:S(2)}) collective-permute-start(bf16[80,640]{1,0:T(8,128)(2,1)S(1)} %get-tuple-element.86), channel_id=1, source_target_pairs={{0,4},{1,5},{2,6},{3,7},{4,0},{5,1},{6,2},{7,3},{8,12},{9,13},{10,... | collective-permute-start | bytes 307208 | tf_op jit(solution)/shard_map/ppermute | solution.py:508
  47.4 4.7 %collective-permute-start.13 = (bf16[80,640]{1,0:T(8,128)(2,1)S(1)}, bf16[80,640]{1,0:T(8,128)(2,1)S(1)}, u32[]{:S(2)}, u32[]{:S(2)}) collective-permute-start(bf16[80,640]{1,0:T(8,128)(2,1)S(1)} %shard_map.129.mine_ref), channel_id=1, source_target_pairs={{0,16},{8,24},{16,0},{24,8},{1,17},{9,25},{17,1},{25,9},{2,18},{10... | collective-permute-start | bytes 307208 | tf_op jit(solution)/shard_map/ppermute | solution.py:508
  52.2 1.5 %collective-permute-start.14 = (f32[80,640]{1,0:T(8,128)S(1)}, f32[80,640]{1,0:T(8,128)S(1)}, u32[]{:S(2)}, u32[]{:S(2)}) collective-permute-start(f32[80,640]{1,0:T(8,128)S(1)} %shard_map.130.own_ref), channel_id=1, source_target_pairs={{0,8},{8,0},{16,24},{24,16},{1,9},{9,1},{17,25},{25,17},{2,10},{10... | collective-permute-start | bytes 614408 | tf_op jit(solution)/shard_map/ppermute | solution.py:508

commit v12 on v9

--- a/solution.py
+++ b/solution.py
@@ -402,26 +402,18 @@
         small_ref[offset * 16 : (offset + 1) * 16] = quarters[jnp.bitwise_xor(place, offset)]
 
 
-def core_kernel(mine_ref, got_ref, *out_refs):
-    for place, ref in enumerate(out_refs):
-        lines = slice(place * 16, (place + 1) * 16)
-        ref[...] = mine_ref[lines] + got_ref[lines]
-
-
-def plane_kernel(*refs):
-    keeps, others, outs = refs[:2], refs[2:4], refs[4:]
+def plane_kernel(keep_ref, got_ref, *refs):
+    small_ref, outs = (None, refs) if len(refs) == 4 else (refs[0], refs[2:])
     size = outs[0].shape[0]
-    edge = keeps[0].shape[1]
     place = lax.rem(lax.axis_index("dev"), 4)
     for offset, out_ref in enumerate(outs):
         lines = pl.ds(pl.multiple_of(jnp.bitwise_xor(place, offset) * size, size), size)
-        for lanes, keep_ref, got_ref in zip((slice(0, edge), slice(edge, None)), keeps, others):
-            out_ref[:, lanes] = (keep_ref[lines, :] + got_ref[lines, :].astype(F32)).astype(out_ref.dtype)
-
-
-def part_kernel(own_ref, got1, got2, small_ref, sum_ref, total_ref):
-    sum_ref[...] = own_ref[...] + (got1[...].astype(F32) + got2[...].astype(F32))
-    total_ref[...] = small_ref[...]
+        out_ref[:size] = (keep_ref[lines, :] + got_ref[lines, :].astype(F32)).astype(out_ref.dtype)
+        if small_ref is not None and offset:
+            value = small_ref[offset * 16 : (offset + 1) * 16]
+            high = value.astype(BF16)
+            out_ref[size:, :128] = high
+            out_ref[size:, 128:] = (value - high.astype(F32)).astype(BF16)
 
 
 def packed(size, wide):
@@ -449,13 +441,21 @@
     return jnp.concatenate([whole, jnp.concatenate(pieces, axis=0)], axis=1)
 
 
-def gather_kernel(bit, own_ref, got3, small0, small1, small2, small3, keep_ref, send_ref):
-    half = own_ref.shape[0] // 2
+def sum_kernel(own_ref, got1, got2, got3, sum_ref):
+    sum_ref[...] = own_ref[...] + (got1[...].astype(F32) + got2[...].astype(F32) + got3[...].astype(F32))
+
+
+def gather_kernel(bit, sum_ref, own_ref, got1, got2, got3, small_ref, keep_ref, send_ref):
+    size, edge = sum_ref.shape
+    half = size // 2
     side = lax.rem(lax.shift_right_logical(lax.axis_index("dev"), bit), 2)
-    total = (small0[...] + small1[...]) + (small2[...] + small3[...])
+    small = small_ref[:16]
+    for ref in (got1, got2, got3):
+        small += ref[size:, :128].astype(F32) + ref[size:, 128:].astype(F32)
     for index, ref in ((1 - side, send_ref), (side, keep_ref)):
         lines = pl.ds(pl.multiple_of(index * half, half), half)
-        write_packed(ref, own_ref[lines, :] + got3[lines, :].astype(F32), total)
+        late = got1[lines, :].astype(F32) + got2[lines, :].astype(F32) + got3[lines, :].astype(F32)
+        write_packed(ref, jnp.concatenate([sum_ref[lines, :], own_ref[lines, :] + late], axis=1), small)
 
 
 def halve_kernel(bit, keep_ref, got_ref, next_ref, send_ref):
@@ -480,7 +480,7 @@
         for tap in range(second):
             lanes = pl.ds(pl.multiple_of(side * half, half), half)
             out_ref[tap, :, lanes] = value[:, tap * half : (tap + 1) * half]
-    total = jnp.where(core == 1, own_ref[size:, -128:], other_ref[size:, -128:])
+    total = own_ref[size:, -128:] + other_ref[size:, -128:]
     value = total[:, :size]
     for place in range(1, 128 // size):
         mine = lax.axis_index("dev") // 4 == place
@@ -509,16 +509,6 @@
 def swap(value, axis, offset):
     size = lax.axis_size(axis)
     return lax.ppermute(value, axis, [(i, i ^ offset) for i in range(size)])
-
-
-def second_swap(value, offset):
-    members = lax.axis_size("dev")
-    pairs = [
-        (grp * members + dev, grp * members + (dev ^ (offset if grp % 2 else 0)))
-        for grp in range(lax.axis_size("grp"))
-        for dev in range(members)
-    ]
-    return lax.ppermute(value, ("grp", "dev"), pairs)
 
 
 def shards(wave, lengths, order, w_first, norm_gain, norm_bias, w_second, cot):
@@ -616,21 +606,18 @@
         keeps.append(keep)
         others.append(swap(send, "grp", 1))
     quarter = chans // 4
-    own, *sends = call(
-        plane_kernel,
-        [((quarter, wide), F32)] + [((quarter, wide), BF16)] * 3,
-        [*keeps, *others],
-    )
-    gots = [swap(part, "dev", offset) for offset, part in enumerate(sends, 1)]
+    shape = (quarter, 2 * half)
+    own0, *sends = call(plane_kernel, [(shape, F32)] + [(shape, BF16)] * 3, [keeps[0], others[0]])
+    gots0 = [swap(part, "dev", offset) for offset, part in enumerate(sends, 1)]
     evens, odds = (frames0 + 1) // 2, frames0 // 2
     lift_even, lift_odd, features = call(
         input_kernel,
         [((evens, rows, chans), F32), ((odds, rows, chans), F32), ((frames1, rows, chans), BF16, "hbm")],
-        [grad, w_in, even_slope, odd_slope, own, feat],
+        [grad, w_in, even_slope, odd_slope, own0, feat],
         scratch=[pltpu.SemaphoreType.DMA],
         flops=1 << 30,
     )
-    parts = call(
+    small = call(
         functools.partial(backward_kernel, frames0, taps),
         [((64, quarter), F32)],
         [valid, pre0, mean, inv, patch, lift_even, lift_odd, gain_in],
@@ -642,17 +629,18 @@
         ],
         flops=1 << 32,
     )[0]
-    small, *smalls = call(core_kernel, [((16, quarter), F32)] * 4, [parts, swap(parts, "grp", 1)])
-    small3, small2 = second_swap(smalls[2], 3), second_swap(smalls[1], 2)
-    own, first = call(
-        part_kernel, [((quarter, wide), F32), (small.shape, F32)], [own, gots[0], gots[1], smalls[0]]
-    )
-    small1 = second_swap(first, 1)
+    sum0 = call(sum_kernel, [(shape, F32)], [own0, *gots0])[0]
+    own1, *sends = call(
+        plane_kernel,
+        [((quarter, half), F32)] + [((quarter + 16, half), BF16)] * 3,
+        [keeps[1], others[1], small, sum0],
+    )
+    gots1 = [swap(part, "dev", offset) for offset, part in enumerate(sends, 1)]
     size = quarter // 2
     keep, send = call(
         functools.partial(gather_kernel, dev_bits - 1),
         [(packed(size, wide), F32), (packed(size, wide), BF16)],
-        [own, gots[2], small, small1, small2, small3],
+        [sum0, own1, *gots1, small],
     )
     for bit in range(dev_bits - 1, 2, -1):
         size //= 2

time: 58.4 us -> 55.7 us (0.954)
  starting transfers between devices: 23.4 us -> 19.4 us
  waiting for transfers between devices: 16.1 us -> 17.4 us
    ppermute x13 -> x15, starting transfers between devices: 21.4 us -> 19.4 us  [swap(): return lax.ppermute(value, axis, [(i, i ^ offset) for i in range(size)])]
    ppermute x3 -> x0, starting transfers between devices: 1.97 us -> none  [second_swap(): return lax.ppermute(value, ('grp', 'dev'), pairs)]
    ppermute x13 -> x15, waiting for transfers between devices: 16.1 us -> 17.4 us  [swap(): return lax.ppermute(value, axis, [(i, i ^ offset) for i in range(size)])]
  transfers between devices with their start and end apart: 16 -> 15, of which waited for: 9 -> 11; matrix products, arithmetic and copies ran while one was open for 0% -> 0% of each run, Pallas kernels for 12% -> 13%
where the time goes in v12:
time: 55.7 us; the launch traced here: 55.5 us
  starting transfers between devices  19.4 us (35%)
  Pallas kernels  18 us (32%)
  waiting for transfers between devices  17.4 us (31%)
  between operations  0.76 us (1%)
    ppermute x15, starting transfers between devices, swap(): return lax.ppermute(value, axis, [(i, i ^ offset) for i in range(size)])  19.4 us
    pallas_call x14, Pallas kernels, call(): pl.pallas_call(kernel, out_shape=[jax.ShapeDtypeStruct(out[0], out[1]) if...  18 us
    ppermute x15, waiting for transfers between devices, swap(): return lax.ppermute(value, axis, [(i, i ^ offset) for i in range(size)])  17.4 us
  transfers between devices with their start and end apart: 15, of which 11 were waited for; matrix products, arithmetic and copies ran while one was open for 0% of the time, Pallas kernels for 13%

profile of v12, /device:TPU:0, one launch (start us, length us, event | category | flops | bytes accessed | tf_op | source)
XLA Modules:
  0.0 55.5 jit_solution(4374184094928963306)
XLA Ops:
  0.6 3.0 %collective-permute-start = (bf16[32,384]{1,0:T(8,128)(2,1)}, bf16[32,384]{1,0:T(8,128)(2,1)S(1)}, u32[]{:S(2)}, u32[]{:S(2)}) collective-permute-start(bf16[32,384]{1,0:T(8,128)(2,1)} %wave_hbm.1), channel_id=1, source_target_pairs={{0,1},{1,0},{2,3},{3,2},{4,5},{5,4},{6,7},{7,6},{8,9},{9,8},{10,11... | collective-permute-start | bytes 73736 | tf_op jit(solution)/shard_map/ppermute | solution.py:511
  3.6 1.5 %collective-permute-start.2 = (bf16[32,384]{1,0:T(8,128)(2,1)}, bf16[32,384]{1,0:T(8,128)(2,1)S(1)}, u32[]{:S(2)}, u32[]{:S(2)}) collective-permute-start(bf16[32,384]{1,0:T(8,128)(2,1)} %wave_hbm.1), channel_id=1, source_target_pairs={{0,3},{1,2},{2,1},{3,0},{4,7},{5,6},{6,5},{7,4},{8,11},{9,10},{10,... | collective-permute-start | bytes 73736 | tf_op jit(solution)/shard_map/ppermute | solution.py:511
  5.2 0.0 collective-permute-start.1
  5.2 1.3 %shard_map.119 = (s32[32,128]{1,0:T(8,128)S(1)}, bf16[128,4096]{1,0:T(8,128)(2,1)S(1)}, bf16[16,256]{1,0:T(8,128)(2,1)S(1)}, bf16[16,256]{1,0:T(8,128)(2,1)S(1)}, bf16[32,384]{1,0:T(8,128)(2,1)S(1)}) custom-call(s32[8,32]{1,0:T(8,128)} %order_hbm.1, s32[1,256]{1,0:T(1,128)} %bitcast.11, bf16[10,512]{1,0:T(8,128)(2,1)} %w_hbm.2, bf16[32,384]{1,0:T(8,128)(2,1)} %wave_hbm.1), custom_call_target="tpu_custom_call" | custom-call | tf_op jit(solution)/shard_map/pallas_call | solution.py:496
  6.5 0.0 collective-permute-done.refs_1_
  6.5 2.2 %collective-permute-done.2.refs_3_ = bf16[32,384]{1,0:T(8,128)(2,1)S(1)} collective-permute-done((bf16[32,384]{1,0:T(8,128)(2,1)}, bf16[32,384]{1,0:T(8,128)(2,1)S(1)}, u32[]{:S(2)}, u32[]{:S(2)}) %collective-permute-start.2) | collective-permute-done | bytes 24608 | tf_op jit(solution)/shard_map/ppermute | solution.py:511
  8.7 0.5 collective-permute-done.1.refs_2_
  9.2 0.2 shard_map.120
  9.4 2.6 %collective-permute-start.3 = (bf16[16,384]{1,0:T(8,128)(2,1)S(1)}, bf16[16,384]{1,0:T(8,128)(2,1)S(1)}, u32[]{:S(2)}, u32[]{:S(2)}) collective-permute-start(bf16[16,384]{1,0:T(8,128)(2,1)S(1)} %get-tuple-element.50), channel_id=1, source_target_pairs={{0,4},{1,5},{2,6},{3,7},{4,0},{5,1},{6,2},{7,3},{8,12},{9,13},{10,... | collective-permute-start | bytes 36872 | tf_op jit(solution)/shard_map/ppermute | solution.py:511
  12.1 2.0 %collective-permute-done.3.far_ref = bf16[16,384]{1,0:T(8,128)(2,1)S(1)} collective-permute-done((bf16[16,384]{1,0:T(8,128)(2,1)S(1)}, bf16[16,384]{1,0:T(8,128)(2,1)S(1)}, u32[]{:S(2)}, u32[]{:S(2)}) %collective-permute-start.3) | collective-permute-done | bytes 12320 | tf_op jit(solution)/shard_map/ppermute | solution.py:511
  14.1 8.0 %shard_map.121 = (bf16[37,32,512]{2,1,0:T(8,128)(2,1)S(1)}, bf16[41,32,512]{2,1,0:T(8,128)(2,1)S(1)}, bf16[40,32,512]{2,1,0:T(8,128)(2,1)S(1)}, f32[10,32,4096]{...) custom-call(bf16[16,384]{1,0:T(8,128)(2,1)S(1)} %get-tuple-element.4, ...), custom_call_target="tpu_custom_call" | custom-call | tf_op jit(solution)/shard_map/pallas_call | solution.py:496
  22.1 1.5 %shard_map.122 = (f32[512,512]{1,0:T(8,128)S(1)}, bf16[512,512]{1,0:T(8,128)(2,1)S(1)}) custom-call(bf16[41,32,512]{2,1,0:T(8,128)(2,1)S(1)} %get-tuple-element.57.refs_0_, bf16[40,32,512]{2,1,0:T(8,128)(2,1)S(1)} %get-tuple-element.58.refs_1_, bf16[512,1280]{1,0:T(8,128)(2,1)S(1)} %get-tuple-element.59.refs_2_.refs_1_), custom_call_target="tpu_custom_call" | custom-call | flops 1073741824 | tf_op jit(solution)/shard_map/pallas_call | solution.py:496
  23.6 0.1 collective-permute-start.4
  23.7 0.9 %shard_map.126 = (f32[512,256]{1,0:T(8,128)S(1)}, bf16[512,256]{1,0:T(8,128)(2,1)S(1)}) custom-call(bf16[41,32,512]{2,1,0:T(8,128)(2,1)S(1)} %get-tuple-element.57.refs_0_, bf16[512,1280]{1,0:T(8,128)(2,1)S(1)} %get-tuple-element.59.refs_2_.refs_1_), custom_call_target="tpu_custom_call" | custom-call | flops 536870912 | tf_op jit(solution)/shard_map/pallas_call | solution.py:496
  24.6 0.5 collective-permute-start.8
  25.1 0.5 collective-permute-done.4.got_ref
  25.6 0.1 shard_map.123
  25.7 1.6 %collective-permute-start.5 = (bf16[128,512]{1,0:T(8,128)(2,1)S(1)}, bf16[128,512]{1,0:T(8,128)(2,1)S(1)}, u32[]{:S(2)}, u32[]{:S(2)}) collective-permute-start(bf16[128,512]{1,0:T(8,128)(2,1)S(1)} %get-tuple-element.65), channel_id=1, source_target_pairs={{0,1},{1,0},{2,3},{3,2},{4,5},{5,4},{6,7},{7,6},{8,9},{9,8},{10,11... | collective-permute-start | bytes 393224 | tf_op jit(solution)/shard_map/ppermute | solution.py:511
  27.3 0.4 collective-permute-start.6
  27.7 1.5 %collective-permute-start.7 = (bf16[128,512]{1,0:T(8,128)(2,1)S(1)}, bf16[128,512]{1,0:T(8,128)(2,1)S(1)}, u32[]{:S(2)}, u32[]{:S(2)}) collective-permute-start(bf16[128,512]{1,0:T(8,128)(2,1)S(1)} %get-tuple-element.67), channel_id=1, source_target_pairs={{0,3},{1,2},{2,1},{3,0},{4,7},{5,6},{6,5},{7,4},{8,11},{9,10},{10,... | collective-permute-start | bytes 393224 | tf_op jit(solution)/shard_map/ppermute | solution.py:511
  29.3 2.2 %shard_map.124 = (f32[38,32,512]{2,1,0:T(8,128)S(1)}, f32[37,32,512]{2,1,0:T(8,128)S(1)}, bf16[37,32,512]{2,1,0:T(8,128)(2,1)}) custom-call(bf16[39,32,512]{2,1,0:T(8,128)(2,1)S(1)} %get-tuple-element.53.grad_ref, bf16[3,512,512]{2,1,0:T(8,128)(2,1)S(1)} %get-tuple-element.54.w_ref, f32[40,32,512]{2,1,0:T(8,128)S(1)} %get-tuple-element.55.even_slope, ...), custom_call_target="tpu_custom_call" | custom-call | flops 1073741824 | tf_op jit(solution)/shard_map/pallas_call | solution.py:496
  31.5 2.8 %shard_map.127.refs_0_.small_ref = f32[64,128]{1,0:T(8,128)S(1)} custom-call(s32[32,128]{1,0:T(8,128)S(1)} %get-tuple-element.51.valid_ref, f32[10,32,4096]{2,1,0:T(8,128)S(1)} %get-tuple-element.70.pre0, f32[32,512]{1,0:T(8,128)S(1)} %get-tuple-element.71.mean_ref, f32[32,512]{1,0:T(8,128)S(1)} %get-tuple-element.72.inv_ref, ...), custom_call_target="tpu_custom_call" | custom-call | flops 4294967296 | tf_op jit(solution)/shard_map/pallas_call | solution.py:496
  34.3 0.0 collective-permute-done.5.got1
  34.3 0.0 collective-permute-done.6.got2
  34.3 1.0 %collective-permute-done.7.got3 = bf16[128,512]{1,0:T(8,128)(2,1)S(1)} collective-permute-done((bf16[128,512]{1,0:T(8,128)(2,1)S(1)}, bf16[128,512]{1,0:T(8,128)(2,1)S(1)}, u32[]{:S(2)}, u32[]{:S(2)}) %collective-permute-start.7) | collective-permute-done | bytes 131104 | tf_op jit(solution)/shard_map/ppermute | solution.py:511
  35.3 0.1 shard_map.125.refs_1_.sum_ref
  35.4 0.0 collective-permute-done.8.got_ref
  35.4 0.1 shard_map.128
  35.4 1.6 %collective-permute-start.9 = (bf16[144,256]{1,0:T(8,128)(2,1)S(1)}, bf16[144,256]{1,0:T(8,128)(2,1)S(1)}, u32[]{:S(2)}, u32[]{:S(2)}) collective-permute-start(bf16[144,256]{1,0:T(8,128)(2,1)S(1)} %get-tuple-element.78), channel_id=1, source_target_pairs={{0,1},{1,0},{2,3},{3,2},{4,5},{5,4},{6,7},{7,6},{8,9},{9,8},{10,11... | collective-permute-start | bytes 221192 | tf_op jit(solution)/shard_map/ppermute | solution.py:511
  37.0 0.4 collective-permute-start.10
  37.5 1.5 %collective-permute-start.11 = (bf16[144,256]{1,0:T(8,128)(2,1)S(1)}, bf16[144,256]{1,0:T(8,128)(2,1)S(1)}, u32[]{:S(2)}, u32[]{:S(2)}) collective-permute-start(bf16[144,256]{1,0:T(8,128)(2,1)S(1)} %get-tuple-element.80), channel_id=1, source_target_pairs={{0,3},{1,2},{2,1},{3,0},{4,7},{5,6},{6,5},{7,4},{8,11},{9,10},{10,... | collective-permute-start | bytes 221192 | tf_op jit(solution)/shard_map/ppermute | solution.py:511
  39.0 1.7 %collective-permute-done.9.got1 = bf16[144,256]{1,0:T(8,128)(2,1)S(1)} collective-permute-done((bf16[144,256]{1,0:T(8,128)(2,1)S(1)}, bf16[144,256]{1,0:T(8,128)(2,1)S(1)}, u32[]{:S(2)}, u32[]{:S(2)}) %collective-permute-start.9) | collective-permute-done | bytes 73760 | tf_op jit(solution)/shard_map/ppermute | solution.py:511
  40.6 0.7 %collective-permute-done.10.got2 = bf16[144,256]{1,0:T(8,128)(2,1)S(1)} collective-permute-done((bf16[144,256]{1,0:T(8,128)(2,1)S(1)}, bf16[144,256]{1,0:T(8,128)(2,1)S(1)}, u32[]{:S(2)}, u32[]{:S(2)}) %collective-permute-start.10) | collective-permute-done | bytes 73760 | tf_op jit(solution)/shard_map/ppermute | solution.py:511
  41.4 1.3 %collective-permute-done.11.got3 = bf16[144,256]{1,0:T(8,128)(2,1)S(1)} collective-permute-done((bf16[144,256]{1,0:T(8,128)(2,1)S(1)}, bf16[144,256]{1,0:T(8,128)(2,1)S(1)}, u32[]{:S(2)}, u32[]{:S(2)}) %collective-permute-start.11) | collective-permute-done | bytes 73760 | tf_op jit(solution)/shard_map/ppermute | solution.py:511
  42.8 2.8 %collective-permute-start.12 = (bf16[80,640]{1,0:T(8,128)(2,1)S(1)}, bf16[80,640]{1,0:T(8,128)(2,1)S(1)}, u32[]{:S(2)}, u32[]{:S(2)}) collective-permute-start(bf16[80,640]{1,0:T(8,128)(2,1)S(1)} %get-tuple-element.82), channel_id=1, source_target_pairs={{0,4},{1,5},{2,6},{3,7},{4,0},{5,1},{6,2},{7,3},{8,12},{9,13},{10,... | collective-permute-start | bytes 307208 | tf_op jit(solution)/shard_map/ppermute | solution.py:511
  45.5 2.9 %collective-permute-done.12.got_ref = bf16[80,640]{1,0:T(8,128)(2,1)S(1)} collective-permute-done((bf16[80,640]{1,0:T(8,128)(2,1)S(1)}, bf16[80,640]{1,0:T(8,128)(2,1)S(1)}, u32[]{:S(2)}, u32[]{:S(2)}) %collective-permute-start.12) | collective-permute-done | bytes 102432 | tf_op jit(solution)/shard_map/ppermute | solution.py:511
  48.4 1.6 %collective-permute-start.13 = (bf16[80,640]{1,0:T(8,128)(2,1)S(1)}, bf16[80,640]{1,0:T(8,128)(2,1)S(1)}, u32[]{:S(2)}, u32[]{:S(2)}) collective-permute-start(bf16[80,640]{1,0:T(8,128)(2,1)S(1)} %shard_map.130.mine_ref), channel_id=1, source_target_pairs={{0,16},{8,24},{16,0},{24,8},{1,17},{9,25},{17,1},{25,9},{2,18},{10... | collective-permute-start | bytes 307208 | tf_op jit(solution)/shard_map/ppermute | solution.py:511
  50.0 3.1 %collective-permute-done.13.got_ref = bf16[80,640]{1,0:T(8,128)(2,1)S(1)} collective-permute-done((bf16[80,640]{1,0:T(8,128)(2,1)S(1)}, bf16[80,640]{1,0:T(8,128)(2,1)S(1)}, u32[]{:S(2)}, u32[]{:S(2)}) %collective-permute-start.13) | collective-permute-done | bytes 102432 | tf_op jit(solution)/shard_map/ppermute | solution.py:511
  53.2 0.1 collective-permute-start.14
  53.2 1.4 %collective-permute-done.14.other_ref = f32[80,640]{1,0:T(8,128)S(1)} collective-permute-done((f32[80,640]{1,0:T(8,128)S(1)}, f32[80,640]{1,0:T(8,128)S(1)}, u32[]{:S(2)}, u32[]{:S(2)}) %collective-permute-start.14) | collective-permute-done | bytes 204832 | tf_op jit(solution)/shard_map/ppermute | solution.py:511
  54.7 0.8 %shard_map.132 = (f32[3,64,512]{2,1,0:T(8,128)}, f32[10,64]{1,0:T(8,128)}, f32[1,64]{1,0:T(1,128)}, f32[1,64]{1,0:T(1,128)}) custom-call(f32[80,640]{1,0:T(8,128)S(1)} %shard_map.131.own_ref, f32[80,640]{1,0:T(8,128)S(1)} %collective-permute-done.14.other_ref), custom_call_target="tpu_custom_call" | custom-call | tf_op jit(solution)/shard_map/pallas_call | solution.py:496
  (3 shorter events, 0.1 us)
Async XLA Ops:
  0.6 5.9 %collective-permute-start = (bf16[32,384]{1,0:T(8,128)(2,1)}, bf16[32,384]{1,0:T(8,128)(2,1)S(1)}, u32[]{:S(2)}, u32[]{:S(2)}) collective-permute-start(bf16[32,384]{1,0:T(8,128)(2,1)} %wave_hbm.1), channel_id=1, source_target_pairs={{0,1},{1,0},{2,3},{3,2},{4,5},{5,4},{6,7},{7,6},{8,9},{9,8},{10,11... | collective-permute-start | bytes 73736 | tf_op jit(solution)/shard_map/ppermute | solution.py:511
  3.6 5.1 %collective-permute-start.2 = (bf16[32,384]{1,0:T(8,128)(2,1)}, bf16[32,384]{1,0:T(8,128)(2,1)S(1)}, u32[]{:S(2)}, u32[]{:S(2)}) collective-permute-start(bf16[32,384]{1,0:T(8,128)(2,1)} %wave_hbm.1), channel_id=1, source_target_pairs={{0,3},{1,2},{2,1},{3,0},{4,7},{5,6},{6,5},{7,4},{8,11},{9,10},{10,... | collective-permute-start | bytes 73736 | tf_op jit(solution)/shard_map/ppermute | solution.py:511
  5.2 4.0 %collective-permute-start.1 = (bf16[32,384]{1,0:T(8,128)(2,1)}, bf16[32,384]{1,0:T(8,128)(2,1)S(1)}, u32[]{:S(2)}, u32[]{:S(2)}) collective-permute-start(bf16[32,384]{1,0:T(8,128)(2,1)} %wave_hbm.1), channel_id=1, source_target_pairs={{0,2},{1,3},{2,0},{3,1},{4,6},{5,7},{6,4},{7,5},{8,10},{9,11},{10,... | collective-permute-start | bytes 73736 | tf_op jit(solution)/shard_map/ppermute | solution.py:511
  9.4 4.6 %collective-permute-start.3 = (bf16[16,384]{1,0:T(8,128)(2,1)S(1)}, bf16[16,384]{1,0:T(8,128)(2,1)S(1)}, u32[]{:S(2)}, u32[]{:S(2)}) collective-permute-start(bf16[16,384]{1,0:T(8,128)(2,1)S(1)} %get-tuple-element.50), channel_id=1, source_target_pairs={{0,4},{1,5},{2,6},{3,7},{4,0},{5,1},{6,2},{7,3},{8,12},{9,13},{10,... | collective-permute-start | bytes 36872 | tf_op jit(solution)/shard_map/ppermute | solution.py:511
  23.6 2.0 %collective-permute-start.4 = (bf16[512,512]{1,0:T(8,128)(2,1)S(1)}, bf16[512,512]{1,0:T(8,128)(2,1)S(1)}, u32[]{:S(2)}, u32[]{:S(2)}) collective-permute-start(bf16[512,512]{1,0:T(8,128)(2,1)S(1)} %get-tuple-element.61), channel_id=1, source_target_pairs={{0,8},{8,0},{16,24},{24,16},{1,9},{9,1},{17,25},{25,17},{2,10},{10... | collective-permute-start | bytes 1572872 | tf_op jit(solution)/shard_map/ppermute | solution.py:511
  24.6 10.8 %collective-permute-start.8 = (bf16[512,256]{1,0:T(8,128)(2,1)S(1)}, bf16[512,256]{1,0:T(8,128)(2,1)S(1)}, u32[]{:S(2)}, u32[]{:S(2)}) collective-permute-start(bf16[512,256]{1,0:T(8,128)(2,1)S(1)} %get-tuple-element.69), channel_id=1, source_target_pairs={{0,8},{8,0},{16,24},{24,16},{1,9},{9,1},{17,25},{25,17},{2,10},{10... | collective-permute-start | bytes 786440 | tf_op jit(solution)/shard_map/ppermute | solution.py:511
  25.7 8.6 %collective-permute-start.5 = (bf16[128,512]{1,0:T(8,128)(2,1)S(1)}, bf16[128,512]{1,0:T(8,128)(2,1)S(1)}, u32[]{:S(2)}, u32[]{:S(2)}) collective-permute-start(bf16[128,512]{1,0:T(8,128)(2,1)S(1)} %get-tuple-element.65), channel_id=1, source_target_pairs={{0,1},{1,0},{2,3},{3,2},{4,5},{5,4},{6,7},{7,6},{8,9},{9,8},{10,11... | collective-permute-start | bytes 393224 | tf_op jit(solution)/shard_map/ppermute | solution.py:511
  27.3 7.0 %collective-permute-start.6 = (bf16[128,512]{1,0:T(8,128)(2,1)S(1)}, bf16[128,512]{1,0:T(8,128)(2,1)S(1)}, u32[]{:S(2)}, u32[]{:S(2)}) collective-permute-start(bf16[128,512]{1,0:T(8,128)(2,1)S(1)} %get-tuple-element.66), channel_id=1, source_target_pairs={{0,2},{1,3},{2,0},{3,1},{4,6},{5,7},{6,4},{7,5},{8,10},{9,11},{10,... | collective-permute-start | bytes 393224 | tf_op jit(solution)/shard_map/ppermute | solution.py:511
  27.7 7.6 %collective-permute-start.7 = (bf16[128,512]{1,0:T(8,128)(2,1)S(1)}, bf16[128,512]{1,0:T(8,128)(2,1)S(1)}, u32[]{:S(2)}, u32[]{:S(2)}) collective-permute-start(bf16[128,512]{1,0:T(8,128)(2,1)S(1)} %get-tuple-element.67), channel_id=1, source_target_pairs={{0,3},{1,2},{2,1},{3,0},{4,7},{5,6},{6,5},{7,4},{8,11},{9,10},{10,... | collective-permute-start | bytes 393224 | tf_op jit(solution)/shard_map/ppermute | solution.py:511
  35.4 5.2 %collective-permute-start.9 = (bf16[144,256]{1,0:T(8,128)(2,1)S(1)}, bf16[144,256]{1,0:T(8,128)(2,1)S(1)}, u32[]{:S(2)}, u32[]{:S(2)}) collective-permute-start(bf16[144,256]{1,0:T(8,128)(2,1)S(1)} %get-tuple-element.78), channel_id=1, source_target_pairs={{0,1},{1,0},{2,3},{3,2},{4,5},{5,4},{6,7},{7,6},{8,9},{9,8},{10,11... | collective-permute-start | bytes 221192 | tf_op jit(solution)/shard_map/ppermute | solution.py:511
  37.0 4.4 %collective-permute-start.10 = (bf16[144,256]{1,0:T(8,128)(2,1)S(1)}, bf16[144,256]{1,0:T(8,128)(2,1)S(1)}, u32[]{:S(2)}, u32[]{:S(2)}) collective-permute-start(bf16[144,256]{1,0:T(8,128)(2,1)S(1)} %get-tuple-element.79), channel_id=1, source_target_pairs={{0,2},{1,3},{2,0},{3,1},{4,6},{5,7},{6,4},{7,5},{8,10},{9,11},{10,... | collective-permute-start | bytes 221192 | tf_op jit(solution)/shard_map/ppermute | solution.py:511
  37.5 5.3 %collective-permute-start.11 = (bf16[144,256]{1,0:T(8,128)(2,1)S(1)}, bf16[144,256]{1,0:T(8,128)(2,1)S(1)}, u32[]{:S(2)}, u32[]{:S(2)}) collective-permute-start(bf16[144,256]{1,0:T(8,128)(2,1)S(1)} %get-tuple-element.80), channel_id=1, source_target_pairs={{0,3},{1,2},{2,1},{3,0},{4,7},{5,6},{6,5},{7,4},{8,11},{9,10},{10,... | collective-permute-start | bytes 221192 | tf_op jit(solution)/shard_map/ppermute | solution.py:511
  42.8 5.6 %collective-permute-start.12 = (bf16[80,640]{1,0:T(8,128)(2,1)S(1)}, bf16[80,640]{1,0:T(8,128)(2,1)S(1)}, u32[]{:S(2)}, u32[]{:S(2)}) collective-permute-start(bf16[80,640]{1,0:T(8,128)(2,1)S(1)} %get-tuple-element.82), channel_id=1, source_target_pairs={{0,4},{1,5},{2,6},{3,7},{4,0},{5,1},{6,2},{7,3},{8,12},{9,13},{10,... | collective-permute-start | bytes 307208 | tf_op jit(solution)/shard_map/ppermute | solution.py:511
  48.4 4.7 %collective-permute-start.13 = (bf16[80,640]{1,0:T(8,128)(2,1)S(1)}, bf16[80,640]{1,0:T(8,128)(2,1)S(1)}, u32[]{:S(2)}, u32[]{:S(2)}) collective-permute-start(bf16[80,640]{1,0:T(8,128)(2,1)S(1)} %shard_map.130.mine_ref), channel_id=1, source_target_pairs={{0,16},{8,24},{16,0},{24,8},{1,17},{9,25},{17,1},{25,9},{2,18},{10... | collective-permute-start | bytes 307208 | tf_op jit(solution)/shard_map/ppermute | solution.py:511
  53.2 1.5 %collective-permute-start.14 = (f32[80,640]{1,0:T(8,128)S(1)}, f32[80,640]{1,0:T(8,128)S(1)}, u32[]{:S(2)}, u32[]{:S(2)}) collective-permute-start(f32[80,640]{1,0:T(8,128)S(1)} %shard_map.131.own_ref), channel_id=1, source_target_pairs={{0,8},{8,0},{16,24},{24,16},{1,9},{9,1},{17,25},{25,17},{2,10},{10... | collective-permute-start | bytes 614408 | tf_op jit(solution)/shard_map/ppermute | solution.py:511

commit v13 on v11

--- a/solution.py
+++ b/solution.py
@@ -129,9 +129,8 @@
     grad_t_ref,
     gain_ref,
     w_ref,
-    stage,
-    fresh,
-    pre1,
+    fresh0,
+    fresh1,
     scale_ref,
     shift_ref,
     bias_ref,
@@ -199,91 +198,72 @@
         scale_ref[:, lanes] = scale
         shift_ref[:, lanes] = bias_ref[:, lanes] - mean * scale
 
-    half = GROUP // 2
-    span = half * rows
-    frames_of = even_ref.shape[0] - 1
-    even_ref[frames_of:] = jnp.zeros((1,) + even_ref.shape[1:], BF16)
-    grad_ref[0] = jnp.zeros(grad_ref.shape[1:], BF16)
-    grad_ref[frames1 + 1] = jnp.zeros(grad_ref.shape[1:], BF16)
-    grad_t_ref[:, frames1 // half * span :] = jnp.zeros((chans, grad_t_ref.shape[1] - frames1 // half * span), BF16)
+    half = GROUP
+    evens, odds = (frames0 + 1) // 2, frames0 // 2
     min_valid1 = (min_valid - 3) // 2 + 1
     valid1 = lax.shift_right_arithmetic(valid - 3, 1) + 1
     slab = chans // len(places)
-
-    def unstage(g):
-        for f in range(GROUP):
-            (odd_ref if f % 2 else even_ref)[g * half + f // 2] = stage[f]
-
-    def activate0(g, masked, used=GROUP):
-        for f in range(used):
+    steps = -(-frames1 // half)
+
+    def used_in(step):
+        return min(half, frames1 - step * half)
+
+    def activate0(step):
+        for t in range(step * 2 * half, min((step + 1) * 2 * half, frames0)):
             for lanes in parts:
-                gelu, slope = gelu_and_slope(frame(g, f, lanes) * scale_ref[:, lanes] + shift_ref[:, lanes])
-                t = g * GROUP + f
-                slope_ref = odd_slope if f % 2 else even_slope
-                slope_ref[g * half + f // 2, :, lanes] = masked_to(slope, t, masked)
-                stage[f, :, lanes] = masked_to(gelu, t, masked).astype(BF16)
-
-    def convolve(h, used):
-        first = h * half
+                gelu, slope = gelu_and_slope(
+                    frame(t // GROUP, t % GROUP, lanes) * scale_ref[:, lanes] + shift_ref[:, lanes]
+                )
+                act_ref, slope_ref = (odd_ref, odd_slope) if t % 2 else (even_ref, even_slope)
+                slope_ref[t // 2, :, lanes] = masked_to(slope, t, t >= min_valid)
+                act_ref[t // 2, :, lanes] = masked_to(gelu, t, t >= min_valid).astype(BF16)
+
+    def convolve(step, out_ref):
+        first, used = step * half, used_in(step)
         for lanes in parts:
-            total = dot(even_ref[pl.ds(first, used)].reshape(used * rows, chans), w_ref[0, :, lanes])
-            total += dot(odd_ref[pl.ds(first, used)].reshape(used * rows, chans), w_ref[1, :, lanes])
-            total += dot(even_ref[pl.ds(first + 1, used)].reshape(used * rows, chans), w_ref[2, :, lanes])
-            fresh[:used, :, lanes] = total.reshape(used, rows, width)
-
-    def activate1(h, used, masked):
-        for j in range(used):
-            u = h * half + j
+            total = dot(even_ref[first : first + used].reshape(used * rows, chans), w_ref[0, :, lanes])
+            total += dot(odd_ref[first : first + used].reshape(used * rows, chans), w_ref[1, :, lanes])
+            total += dot(even_ref[first + 1 : first + used + 1].reshape(used * rows, chans), w_ref[2, :, lanes])
+            out_ref[:used, :, lanes] = total.reshape(used, rows, width)
+
+    def activate1(step, in_ref):
+        for j in range(used_in(step)):
+            u = step * half + j
             for lanes in parts:
-                gelu, slope = gelu_and_slope(pre1[j, :, lanes])
+                gelu, slope = gelu_and_slope(in_ref[j, :, lanes])
                 grad = cot_ref[u, :, lanes].astype(F32) * slope
-                if masked:
+                if u >= min_valid1:
                     gelu, grad = jnp.where(valid1 > u, gelu, 0.0), jnp.where(valid1 > u, grad, 0.0)
                 feat_ref[u, :, lanes] = gelu.astype(BF16)
                 grad_ref[u + 1, :, lanes] = grad.astype(BF16)
 
-    def turn(h, used):
-        turned = grad_ref[pl.ds(h * half + 1, used)].reshape(used * rows, chans).T
-        start = h * span
-        cols = pl.ds(start if isinstance(start, int) else pl.multiple_of(start, span), used * rows)
+    def turn(step):
+        first, size = step * half, used_in(step) * rows
+        turned = grad_ref[first + 1 : first + 1 + used_in(step)].reshape(size, chans).T
         for place, source in enumerate(places):
-            grad_t_ref[place * slab : (place + 1) * slab, cols] = turned[source * slab : (source + 1) * slab]
-
-    def fill(g, carry):
-        unstage(jnp.maximum(g - 1, 0))
-        activate0(g, False)
-        return carry
-
-    def steady(masked, g, carry, used=GROUP):
-        unstage(g - 1)
-        pre1[...] = fresh[...]
-        convolve(g - 2, half)
-        activate1(g - 3, half, masked)
-        activate0(g, masked, used)
-        turn(g - 3, half)
-        return carry
-
-    stage[...] = jnp.zeros(stage.shape, BF16)
-    lax.fori_loop(0, 3, fill, 0)
-    waiting[2].wait()
-    waiting[3].wait()
-    convolve(0, half)
-    lax.fori_loop(3, free_groups, functools.partial(steady, False), 0)
-    lax.fori_loop(free_groups, full_groups, functools.partial(steady, True), 0)
-    rest = frames0 - full_groups * GROUP
-    if rest:
-        steady(True, full_groups, 0, rest)
-        stage[rest:] = jnp.zeros((GROUP - rest,) + stage.shape[1:], BF16)
-    unstage(groups - 1)
-    last = frames1 // half
-    for h in range(groups - 2, last + 1):
-        pre1[...] = fresh[...]
-        convolve(h, min(half, frames1 - h * half))
-        activate1(h - 1, half, True)
-        turn(h - 1, half)
-    pre1[...] = fresh[...]
-    activate1(last, frames1 - last * half, True)
-    turn(last, frames1 - last * half)
+            grad_t_ref[place * slab : (place + 1) * slab, first * rows : first * rows + size] = turned[
+                source * slab : (source + 1) * slab
+            ]
+
+    for ref, used in ((even_ref, evens), (odd_ref, odds)):
+        ref[used:] = jnp.zeros((ref.shape[0] - used,) + ref.shape[1:], BF16)
+    grad_ref[0] = jnp.zeros(grad_ref.shape[1:], BF16)
+    grad_ref[frames1 + 1] = jnp.zeros(grad_ref.shape[1:], BF16)
+    full = frames1 * rows // 128 * 128
+    grad_t_ref[:, full:] = jnp.zeros((chans, grad_t_ref.shape[1] - full), BF16)
+    fresh = (fresh0, fresh1)
+    for step in range(steps + 3):
+        if step == 2:
+            waiting[2].wait()
+            waiting[3].wait()
+        if 0 <= step - 2 < steps:
+            convolve(step - 2, fresh[step % 2])
+        if 0 <= step - 3 < steps:
+            activate1(step - 3, fresh[(step - 1) % 2])
+        if step < -(-frames0 // (2 * half)):
+            activate0(step)
+        if 0 <= step - 3 < steps:
+            turn(step - 3)
 
 
 def outer_kernel(skips, *refs):
@@ -581,9 +561,8 @@
         ],
         [near, far, valid, band, gain, bias, w_second, cot_t],
         scratch=[
-            ((GROUP, rows, chans), BF16),
-            ((GROUP // 2, rows, chans), F32),
-            ((GROUP // 2, rows, chans), F32),
+            ((GROUP, rows, chans), F32),
+            ((GROUP, rows, chans), F32),
             ((rows, chans), F32),
             ((rows, chans), F32),
             (bias.shape, F32),

time: 54.7 us -> 53.8 us (0.984)
  Pallas kernels: 18 us -> 17.1 us
    pallas_call x13, Pallas kernels: 18 us -> 17.1 us  [call(): pl.pallas_call(kernel, out_shape=[jax.ShapeDtypeStruct(out[0], out[1]) if...]
where the time goes in v13:
time: 53.8 us; the launch traced here: 53.6 us
  starting transfers between devices  19.3 us (36%)
  Pallas kernels  17.1 us (32%)
  waiting for transfers between devices  16.4 us (30%)
  between operations  0.75 us (1%)
    ppermute x15, starting transfers between devices, swap(): return lax.ppermute(value, axis, [(i, i ^ offset) for i in range(size)])  19.3 us
    pallas_call x13, Pallas kernels, call(): pl.pallas_call(kernel, out_shape=[jax.ShapeDtypeStruct(out[0], out[1]) if...  17.1 us
    ppermute x15, waiting for transfers between devices, swap(): return lax.ppermute(value, axis, [(i, i ^ offset) for i in range(size)])  16.4 us
  transfers between devices with their start and end apart: 15, of which 8 were waited for; matrix products, arithmetic and copies ran while one was open for 0% of the time, Pallas kernels for 13%

profile of v13, /device:TPU:0, one launch (start us, length us, event | category | flops | bytes accessed | tf_op | source)
XLA Modules:
  0.0 53.6 jit_solution(4960544894515099149)
XLA Ops:
  0.6 3.0 %collective-permute-start = (bf16[32,384]{1,0:T(8,128)(2,1)}, bf16[32,384]{1,0:T(8,128)(2,1)S(1)}, u32[]{:S(2)}, u32[]{:S(2)}) collective-permute-start(bf16[32,384]{1,0:T(8,128)(2,1)} %wave_hbm.1), channel_id=1, source_target_pairs={{0,1},{1,0},{2,3},{3,2},{4,5},{5,4},{6,7},{7,6},{8,9},{9,8},{10,11... | collective-permute-start | bytes 73736 | tf_op jit(solution)/shard_map/ppermute | solution.py:488
  3.6 1.5 %collective-permute-start.2 = (bf16[32,384]{1,0:T(8,128)(2,1)}, bf16[32,384]{1,0:T(8,128)(2,1)S(1)}, u32[]{:S(2)}, u32[]{:S(2)}) collective-permute-start(bf16[32,384]{1,0:T(8,128)(2,1)} %wave_hbm.1), channel_id=1, source_target_pairs={{0,3},{1,2},{2,1},{3,0},{4,7},{5,6},{6,5},{7,4},{8,11},{9,10},{10,... | collective-permute-start | bytes 73736 | tf_op jit(solution)/shard_map/ppermute | solution.py:488
  5.2 0.0 collective-permute-start.1
  5.2 1.3 %shard_map.119 = (s32[32,128]{1,0:T(8,128)S(1)}, bf16[128,4096]{1,0:T(8,128)(2,1)S(1)}, bf16[16,256]{1,0:T(8,128)(2,1)S(1)}, bf16[16,256]{1,0:T(8,128)(2,1)S(1)}, bf16[32,384]{1,0:T(8,128)(2,1)S(1)}) custom-call(s32[8,32]{1,0:T(8,128)} %order_hbm.1, s32[1,256]{1,0:T(1,128)} %bitcast.11, bf16[10,512]{1,0:T(8,128)(2,1)} %w_hbm.2, bf16[32,384]{1,0:T(8,128)(2,1)} %wave_hbm.1), custom_call_target="tpu_custom_call" | custom-call | tf_op jit(solution)/shard_map/pallas_call | solution.py:473
  6.5 0.0 collective-permute-done.refs_1_
  6.5 2.2 %collective-permute-done.2.refs_3_ = bf16[32,384]{1,0:T(8,128)(2,1)S(1)} collective-permute-done((bf16[32,384]{1,0:T(8,128)(2,1)}, bf16[32,384]{1,0:T(8,128)(2,1)S(1)}, u32[]{:S(2)}, u32[]{:S(2)}) %collective-permute-start.2) | collective-permute-done | bytes 24608 | tf_op jit(solution)/shard_map/ppermute | solution.py:488
  8.7 0.5 collective-permute-done.1.refs_2_
  9.2 0.2 shard_map.120
  9.4 2.6 %collective-permute-start.3 = (bf16[16,384]{1,0:T(8,128)(2,1)S(1)}, bf16[16,384]{1,0:T(8,128)(2,1)S(1)}, u32[]{:S(2)}, u32[]{:S(2)}) collective-permute-start(bf16[16,384]{1,0:T(8,128)(2,1)S(1)} %get-tuple-element.52), channel_id=1, source_target_pairs={{0,4},{1,5},{2,6},{3,7},{4,0},{5,1},{6,2},{7,3},{8,12},{9,13},{10,... | collective-permute-start | bytes 36872 | tf_op jit(solution)/shard_map/ppermute | solution.py:488
  12.1 2.0 %collective-permute-done.3.far_ref = bf16[16,384]{1,0:T(8,128)(2,1)S(1)} collective-permute-done((bf16[16,384]{1,0:T(8,128)(2,1)S(1)}, bf16[16,384]{1,0:T(8,128)(2,1)S(1)}, u32[]{:S(2)}, u32[]{:S(2)}) %collective-permute-start.3) | collective-permute-done | bytes 12320 | tf_op jit(solution)/shard_map/ppermute | solution.py:488
  14.1 7.1 %shard_map.121 = (bf16[37,32,512]{2,1,0:T(8,128)(2,1)S(1)}, bf16[41,32,512]{2,1,0:T(8,128)(2,1)S(1)}, bf16[40,32,512]{2,1,0:T(8,128)(2,1)S(1)}, f32[10,32,4096]{...) custom-call(bf16[16,384]{1,0:T(8,128)(2,1)S(1)} %get-tuple-element.5, ...), custom_call_target="tpu_custom_call" | custom-call | tf_op jit(solution)/shard_map/pallas_call | solution.py:473
  21.1 1.5 %shard_map.123 = (f32[512,512]{1,0:T(8,128)S(1)}, bf16[512,512]{1,0:T(8,128)(2,1)S(1)}) custom-call(bf16[41,32,512]{2,1,0:T(8,128)(2,1)S(1)} %get-tuple-element.61.refs_0_, bf16[40,32,512]{2,1,0:T(8,128)(2,1)S(1)} %get-tuple-element.62.refs_1_, bf16[512,1280]{1,0:T(8,128)(2,1)S(1)} %get-tuple-element.63.refs_2_.refs_1_), custom_call_target="tpu_custom_call" | custom-call | flops 1073741824 | tf_op jit(solution)/shard_map/pallas_call | solution.py:473
  22.7 0.1 collective-permute-start.4
  22.8 0.9 %shard_map.124 = (f32[512,256]{1,0:T(8,128)S(1)}, bf16[512,256]{1,0:T(8,128)(2,1)S(1)}) custom-call(bf16[41,32,512]{2,1,0:T(8,128)(2,1)S(1)} %get-tuple-element.61.refs_0_, bf16[512,1280]{1,0:T(8,128)(2,1)S(1)} %get-tuple-element.63.refs_2_.refs_1_), custom_call_target="tpu_custom_call" | custom-call | flops 536870912 | tf_op jit(solution)/shard_map/pallas_call | solution.py:473
  23.6 0.5 %collective-permute-start.5 = (bf16[512,256]{1,0:T(8,128)(2,1)S(1)}, bf16[512,256]{1,0:T(8,128)(2,1)S(1)}, u32[]{:S(2)}, u32[]{:S(2)}) collective-permute-start(bf16[512,256]{1,0:T(8,128)(2,1)S(1)} %get-tuple-element.67), channel_id=1, source_target_pairs={{0,8},{8,0},{16,24},{24,16},{1,9},{9,1},{17,25},{25,17},{2,10},{10... | collective-permute-start | bytes 786440 | tf_op jit(solution)/shard_map/ppermute | solution.py:488
  24.2 2.2 %shard_map.122 = (f32[38,32,512]{2,1,0:T(8,128)S(1)}, f32[37,32,512]{2,1,0:T(8,128)S(1)}, bf16[37,32,512]{2,1,0:T(8,128)(2,1)}) custom-call(bf16[39,32,512]{2,1,0:T(8,128)(2,1)S(1)} %get-tuple-element.55.grad_ref, bf16[3,512,512]{2,1,0:T(8,128)(2,1)S(1)} %get-tuple-element.56.w_ref, f32[40,32,512]{2,1,0:T(8,128)S(1)} %get-tuple-element.57.even_slope, ...), custom_call_target="tpu_custom_call" | custom-call | flops 1073741824 | tf_op jit(solution)/shard_map/pallas_call | solution.py:473
  26.4 0.0 collective-permute-done.5.refs_3_
  26.4 0.0 collective-permute-done.4.refs_2_
  26.4 0.1 shard_map.125
  26.6 1.6 %collective-permute-start.6 = (bf16[128,768]{1,0:T(8,128)(2,1)S(1)}, bf16[128,768]{1,0:T(8,128)(2,1)S(1)}, u32[]{:S(2)}, u32[]{:S(2)}) collective-permute-start(bf16[128,768]{1,0:T(8,128)(2,1)S(1)} %get-tuple-element.70), channel_id=1, source_target_pairs={{0,1},{1,0},{2,3},{3,2},{4,5},{5,4},{6,7},{7,6},{8,9},{9,8},{10,11... | collective-permute-start | bytes 589832 | tf_op jit(solution)/shard_map/ppermute | solution.py:488
  28.1 0.4 collective-permute-start.7
  28.6 1.6 %collective-permute-start.8 = (bf16[128,768]{1,0:T(8,128)(2,1)S(1)}, bf16[128,768]{1,0:T(8,128)(2,1)S(1)}, u32[]{:S(2)}, u32[]{:S(2)}) collective-permute-start(bf16[128,768]{1,0:T(8,128)(2,1)S(1)} %get-tuple-element.80), channel_id=1, source_target_pairs={{0,3},{1,2},{2,1},{3,0},{4,7},{5,6},{6,5},{7,4},{8,11},{9,10},{10,... | collective-permute-start | bytes 589832 | tf_op jit(solution)/shard_map/ppermute | solution.py:488
  30.1 2.8 %shard_map.126 = (f32[16,128]{1,0:T(8,128)S(1)}, f32[16,128]{1,0:T(8,128)S(1)}, f32[16,128]{1,0:T(8,128)S(1)}, f32[16,128]{1,0:T(8,128)S(1)}) custom-call(s32[32,128]{1,0:T(8,128)S(1)} %get-tuple-element.53.valid_ref, f32[10,32,4096]{2,1,0:T(8,128)S(1)} %get-tuple-element.72.pre0, f32[32,512]{1,0:T(8,128)S(1)} %get-tuple-element.73.mean_ref, ...), custom_call_target="tpu_custom_call" | custom-call | flops 4294967296 | tf_op jit(solution)/shard_map/pallas_call | solution.py:473
  33.0 1.0 %collective-permute-start.10 = (f32[16,128]{1,0:T(8,128)S(1)}, f32[16,128]{1,0:T(8,128)S(1)}, u32[]{:S(2)}, u32[]{:S(2)}) collective-permute-start(f32[16,128]{1,0:T(8,128)S(1)} %get-tuple-element.83), channel_id=1, source_target_pairs={{0,2},{1,3},{2,0},{3,1},{4,6},{5,7},{6,4},{7,5},{8,10},{9,11},{10,... | collective-permute-start | bytes 24584 | tf_op jit(solution)/shard_map/ppermute | solution.py:488
  34.0 2.0 %collective-permute-start.11 = (f32[16,128]{1,0:T(8,128)S(1)}, f32[16,128]{1,0:T(8,128)S(1)}, u32[]{:S(2)}, u32[]{:S(2)}) collective-permute-start(f32[16,128]{1,0:T(8,128)S(1)} %get-tuple-element.84), channel_id=1, source_target_pairs={{0,3},{1,2},{2,1},{3,0},{4,7},{5,6},{6,5},{7,4},{8,11},{9,10},{10,... | collective-permute-start | bytes 24584 | tf_op jit(solution)/shard_map/ppermute | solution.py:488
  36.0 0.0 collective-permute-done.6.got1
  36.0 0.0 collective-permute-done.7.got2
  36.0 0.1 shard_map.127
  36.1 0.6 %collective-permute-start.9 = (f32[16,128]{1,0:T(8,128)S(1)}, f32[16,128]{1,0:T(8,128)S(1)}, u32[]{:S(2)}, u32[]{:S(2)}) collective-permute-start(f32[16,128]{1,0:T(8,128)S(1)} %get-tuple-element.82), channel_id=1, source_target_pairs={{0,1},{1,0},{2,3},{3,2},{4,5},{5,4},{6,7},{7,6},{8,9},{9,8},{10,11... | collective-permute-start | bytes 24584 | tf_op jit(solution)/shard_map/ppermute | solution.py:488
  36.7 2.5 %collective-permute-done.10.small2 = f32[16,128]{1,0:T(8,128)S(1)} collective-permute-done((f32[16,128]{1,0:T(8,128)S(1)}, f32[16,128]{1,0:T(8,128)S(1)}, u32[]{:S(2)}, u32[]{:S(2)}) %collective-permute-start.10) | collective-permute-done | bytes 8224 | tf_op jit(solution)/shard_map/ppermute | solution.py:488
  39.2 0.0 collective-permute-done.11.small3
  39.2 0.0 collective-permute-done.8.got3
  39.2 0.6 %collective-permute-done.9.small1 = f32[16,128]{1,0:T(8,128)S(1)} collective-permute-done((f32[16,128]{1,0:T(8,128)S(1)}, f32[16,128]{1,0:T(8,128)S(1)}, u32[]{:S(2)}, u32[]{:S(2)}) %collective-permute-start.9) | collective-permute-done | bytes 8224 | tf_op jit(solution)/shard_map/ppermute | solution.py:488
  39.8 0.1 shard_map.128
  39.8 2.6 %collective-permute-start.12 = (bf16[80,640]{1,0:T(8,128)(2,1)S(1)}, bf16[80,640]{1,0:T(8,128)(2,1)S(1)}, u32[]{:S(2)}, u32[]{:S(2)}) collective-permute-start(bf16[80,640]{1,0:T(8,128)(2,1)S(1)} %get-tuple-element.86), channel_id=1, source_target_pairs={{0,4},{1,5},{2,6},{3,7},{4,0},{5,1},{6,2},{7,3},{8,12},{9,13},{10,... | collective-permute-start | bytes 307208 | tf_op jit(solution)/shard_map/ppermute | solution.py:488
  42.5 4.0 %collective-permute-done.12.got_ref = bf16[80,640]{1,0:T(8,128)(2,1)S(1)} collective-permute-done((bf16[80,640]{1,0:T(8,128)(2,1)S(1)}, bf16[80,640]{1,0:T(8,128)(2,1)S(1)}, u32[]{:S(2)}, u32[]{:S(2)}) %collective-permute-start.12) | collective-permute-done | bytes 102432 | tf_op jit(solution)/shard_map/ppermute | solution.py:488
  46.5 1.6 %collective-permute-start.13 = (bf16[80,640]{1,0:T(8,128)(2,1)S(1)}, bf16[80,640]{1,0:T(8,128)(2,1)S(1)}, u32[]{:S(2)}, u32[]{:S(2)}) collective-permute-start(bf16[80,640]{1,0:T(8,128)(2,1)S(1)} %shard_map.129.mine_ref), channel_id=1, source_target_pairs={{0,16},{8,24},{16,0},{24,8},{1,17},{9,25},{17,1},{25,9},{2,18},{10... | collective-permute-start | bytes 307208 | tf_op jit(solution)/shard_map/ppermute | solution.py:488
  48.1 3.1 %collective-permute-done.13.got_ref = bf16[80,640]{1,0:T(8,128)(2,1)S(1)} collective-permute-done((bf16[80,640]{1,0:T(8,128)(2,1)S(1)}, bf16[80,640]{1,0:T(8,128)(2,1)S(1)}, u32[]{:S(2)}, u32[]{:S(2)}) %collective-permute-start.13) | collective-permute-done | bytes 102432 | tf_op jit(solution)/shard_map/ppermute | solution.py:488
  51.2 0.1 collective-permute-start.14
  51.3 1.4 %collective-permute-done.14.other_ref = f32[80,640]{1,0:T(8,128)S(1)} collective-permute-done((f32[80,640]{1,0:T(8,128)S(1)}, f32[80,640]{1,0:T(8,128)S(1)}, u32[]{:S(2)}, u32[]{:S(2)}) %collective-permute-start.14) | collective-permute-done | bytes 204832 | tf_op jit(solution)/shard_map/ppermute | solution.py:488
  52.8 0.8 %shard_map.131 = (f32[3,64,512]{2,1,0:T(8,128)}, f32[10,64]{1,0:T(8,128)}, f32[1,64]{1,0:T(1,128)}, f32[1,64]{1,0:T(1,128)}) custom-call(f32[80,640]{1,0:T(8,128)S(1)} %shard_map.130.own_ref, f32[80,640]{1,0:T(8,128)S(1)} %collective-permute-done.14.other_ref), custom_call_target="tpu_custom_call" | custom-call | tf_op jit(solution)/shard_map/pallas_call | solution.py:473
  (2 shorter events, 0.0 us)
Async XLA Ops:
  0.6 5.9 %collective-permute-start = (bf16[32,384]{1,0:T(8,128)(2,1)}, bf16[32,384]{1,0:T(8,128)(2,1)S(1)}, u32[]{:S(2)}, u32[]{:S(2)}) collective-permute-start(bf16[32,384]{1,0:T(8,128)(2,1)} %wave_hbm.1), channel_id=1, source_target_pairs={{0,1},{1,0},{2,3},{3,2},{4,5},{5,4},{6,7},{7,6},{8,9},{9,8},{10,11... | collective-permute-start | bytes 73736 | tf_op jit(solution)/shard_map/ppermute | solution.py:488
  3.6 5.1 %collective-permute-start.2 = (bf16[32,384]{1,0:T(8,128)(2,1)}, bf16[32,384]{1,0:T(8,128)(2,1)S(1)}, u32[]{:S(2)}, u32[]{:S(2)}) collective-permute-start(bf16[32,384]{1,0:T(8,128)(2,1)} %wave_hbm.1), channel_id=1, source_target_pairs={{0,3},{1,2},{2,1},{3,0},{4,7},{5,6},{6,5},{7,4},{8,11},{9,10},{10,... | collective-permute-start | bytes 73736 | tf_op jit(solution)/shard_map/ppermute | solution.py:488
  5.2 4.0 %collective-permute-start.1 = (bf16[32,384]{1,0:T(8,128)(2,1)}, bf16[32,384]{1,0:T(8,128)(2,1)S(1)}, u32[]{:S(2)}, u32[]{:S(2)}) collective-permute-start(bf16[32,384]{1,0:T(8,128)(2,1)} %wave_hbm.1), channel_id=1, source_target_pairs={{0,2},{1,3},{2,0},{3,1},{4,6},{5,7},{6,4},{7,5},{8,10},{9,11},{10,... | collective-permute-start | bytes 73736 | tf_op jit(solution)/shard_map/ppermute | solution.py:488
  9.4 4.6 %collective-permute-start.3 = (bf16[16,384]{1,0:T(8,128)(2,1)S(1)}, bf16[16,384]{1,0:T(8,128)(2,1)S(1)}, u32[]{:S(2)}, u32[]{:S(2)}) collective-permute-start(bf16[16,384]{1,0:T(8,128)(2,1)S(1)} %get-tuple-element.52), channel_id=1, source_target_pairs={{0,4},{1,5},{2,6},{3,7},{4,0},{5,1},{6,2},{7,3},{8,12},{9,13},{10,... | collective-permute-start | bytes 36872 | tf_op jit(solution)/shard_map/ppermute | solution.py:488
  22.7 3.7 %collective-permute-start.4 = (bf16[512,512]{1,0:T(8,128)(2,1)S(1)}, bf16[512,512]{1,0:T(8,128)(2,1)S(1)}, u32[]{:S(2)}, u32[]{:S(2)}) collective-permute-start(bf16[512,512]{1,0:T(8,128)(2,1)S(1)} %get-tuple-element.66), channel_id=1, source_target_pairs={{0,8},{8,0},{16,24},{24,16},{1,9},{9,1},{17,25},{25,17},{2,10},{10... | collective-permute-start | bytes 1572872 | tf_op jit(solution)/shard_map/ppermute | solution.py:488
  23.6 2.8 %collective-permute-start.5 = (bf16[512,256]{1,0:T(8,128)(2,1)S(1)}, bf16[512,256]{1,0:T(8,128)(2,1)S(1)}, u32[]{:S(2)}, u32[]{:S(2)}) collective-permute-start(bf16[512,256]{1,0:T(8,128)(2,1)S(1)} %get-tuple-element.67), channel_id=1, source_target_pairs={{0,8},{8,0},{16,24},{24,16},{1,9},{9,1},{17,25},{25,17},{2,10},{10... | collective-permute-start | bytes 786440 | tf_op jit(solution)/shard_map/ppermute | solution.py:488
  26.6 9.4 %collective-permute-start.6 = (bf16[128,768]{1,0:T(8,128)(2,1)S(1)}, bf16[128,768]{1,0:T(8,128)(2,1)S(1)}, u32[]{:S(2)}, u32[]{:S(2)}) collective-permute-start(bf16[128,768]{1,0:T(8,128)(2,1)S(1)} %get-tuple-element.70), channel_id=1, source_target_pairs={{0,1},{1,0},{2,3},{3,2},{4,5},{5,4},{6,7},{7,6},{8,9},{9,8},{10,11... | collective-permute-start | bytes 589832 | tf_op jit(solution)/shard_map/ppermute | solution.py:488
  28.1 7.9 %collective-permute-start.7 = (bf16[128,768]{1,0:T(8,128)(2,1)S(1)}, bf16[128,768]{1,0:T(8,128)(2,1)S(1)}, u32[]{:S(2)}, u32[]{:S(2)}) collective-permute-start(bf16[128,768]{1,0:T(8,128)(2,1)S(1)} %get-tuple-element.71), channel_id=1, source_target_pairs={{0,2},{1,3},{2,0},{3,1},{4,6},{5,7},{6,4},{7,5},{8,10},{9,11},{10,... | collective-permute-start | bytes 589832 | tf_op jit(solution)/shard_map/ppermute | solution.py:488
  28.6 10.6 %collective-permute-start.8 = (bf16[128,768]{1,0:T(8,128)(2,1)S(1)}, bf16[128,768]{1,0:T(8,128)(2,1)S(1)}, u32[]{:S(2)}, u32[]{:S(2)}) collective-permute-start(bf16[128,768]{1,0:T(8,128)(2,1)S(1)} %get-tuple-element.80), channel_id=1, source_target_pairs={{0,3},{1,2},{2,1},{3,0},{4,7},{5,6},{6,5},{7,4},{8,11},{9,10},{10,... | collective-permute-start | bytes 589832 | tf_op jit(solution)/shard_map/ppermute | solution.py:488
  33.0 6.2 %collective-permute-start.10 = (f32[16,128]{1,0:T(8,128)S(1)}, f32[16,128]{1,0:T(8,128)S(1)}, u32[]{:S(2)}, u32[]{:S(2)}) collective-permute-start(f32[16,128]{1,0:T(8,128)S(1)} %get-tuple-element.83), channel_id=1, source_target_pairs={{0,2},{1,3},{2,0},{3,1},{4,6},{5,7},{6,4},{7,5},{8,10},{9,11},{10,... | collective-permute-start | bytes 24584 | tf_op jit(solution)/shard_map/ppermute | solution.py:488
  34.0 5.2 %collective-permute-start.11 = (f32[16,128]{1,0:T(8,128)S(1)}, f32[16,128]{1,0:T(8,128)S(1)}, u32[]{:S(2)}, u32[]{:S(2)}) collective-permute-start(f32[16,128]{1,0:T(8,128)S(1)} %get-tuple-element.84), channel_id=1, source_target_pairs={{0,3},{1,2},{2,1},{3,0},{4,7},{5,6},{6,5},{7,4},{8,11},{9,10},{10,... | collective-permute-start | bytes 24584 | tf_op jit(solution)/shard_map/ppermute | solution.py:488
  36.1 3.7 %collective-permute-start.9 = (f32[16,128]{1,0:T(8,128)S(1)}, f32[16,128]{1,0:T(8,128)S(1)}, u32[]{:S(2)}, u32[]{:S(2)}) collective-permute-start(f32[16,128]{1,0:T(8,128)S(1)} %get-tuple-element.82), channel_id=1, source_target_pairs={{0,1},{1,0},{2,3},{3,2},{4,5},{5,4},{6,7},{7,6},{8,9},{9,8},{10,11... | collective-permute-start | bytes 24584 | tf_op jit(solution)/shard_map/ppermute | solution.py:488
  39.8 6.6 %collective-permute-start.12 = (bf16[80,640]{1,0:T(8,128)(2,1)S(1)}, bf16[80,640]{1,0:T(8,128)(2,1)S(1)}, u32[]{:S(2)}, u32[]{:S(2)}) collective-permute-start(bf16[80,640]{1,0:T(8,128)(2,1)S(1)} %get-tuple-element.86), channel_id=1, source_target_pairs={{0,4},{1,5},{2,6},{3,7},{4,0},{5,1},{6,2},{7,3},{8,12},{9,13},{10,... | collective-permute-start | bytes 307208 | tf_op jit(solution)/shard_map/ppermute | solution.py:488
  46.5 4.7 %collective-permute-start.13 = (bf16[80,640]{1,0:T(8,128)(2,1)S(1)}, bf16[80,640]{1,0:T(8,128)(2,1)S(1)}, u32[]{:S(2)}, u32[]{:S(2)}) collective-permute-start(bf16[80,640]{1,0:T(8,128)(2,1)S(1)} %shard_map.129.mine_ref), channel_id=1, source_target_pairs={{0,16},{8,24},{16,0},{24,8},{1,17},{9,25},{17,1},{25,9},{2,18},{10... | collective-permute-start | bytes 307208 | tf_op jit(solution)/shard_map/ppermute | solution.py:488
  51.2 1.5 %collective-permute-start.14 = (f32[80,640]{1,0:T(8,128)S(1)}, f32[80,640]{1,0:T(8,128)S(1)}, u32[]{:S(2)}, u32[]{:S(2)}) collective-permute-start(f32[80,640]{1,0:T(8,128)S(1)} %shard_map.130.own_ref), channel_id=1, source_target_pairs={{0,8},{8,0},{16,24},{24,16},{1,9},{9,1},{17,25},{25,17},{2,10},{10... | collective-permute-start | bytes 614408 | tf_op jit(solution)/shard_map/ppermute | solution.py:488

commit v14 on v13

--- a/solution.py
+++ b/solution.py
@@ -19,10 +19,6 @@
     bell = jnp.exp2(value * value * (-0.5 * 1.4426950408889634))
     phi = 0.5 + 0.5 * lax.erf(value * 0.7071067811865476)
     return value * phi, phi + value * bell * 0.3989422804014327
-
-
-def rows_first(a, b):
-    return lax.dot_general(a, b, (((0,), (0,)), ((), ())), preferred_element_type=F32)
 
 
 def cols_both(a, b):
@@ -146,8 +142,6 @@
     width = LANES
     parts = [slice(first, first + width) for first in range(0, chans, width)]
     min_valid = (MIN_SAMPLES - taps) // stride + 1
-    full_groups = frames0 // GROUP
-    free_groups = min(min_valid // GROUP, full_groups)
     low_half = lax.axis_index("dev") < lax.axis_size("dev") // 2
     near, far = near_ref[...].astype(F32), far_ref[...].astype(F32)
     wave = jnp.concatenate([jnp.where(low_half, near, far), jnp.where(low_half, far, near)], axis=0).astype(BF16)
@@ -155,9 +149,6 @@
         pick = onehot(iota((samp, depth), 0) == iota((samp, depth), 1) + GROUP * stride * g)
         patch_ref[g] = dot(wave, pick).astype(BF16)
     patches = patch_ref[...].reshape(groups * rows, depth)
-    for f in range(GROUP):
-        cols = slice(f * chans, (f + 1) * chans)
-        pre0[:, :, cols] = dot(patches, band_ref[:, cols]).reshape(groups, rows, chans)
 
     valid = jnp.broadcast_to(valid_ref[:, :1], (rows, width))
     count = valid.astype(F32)
@@ -169,26 +160,23 @@
         return jnp.where(valid > t, value, 0.0) if masked else value
 
     for lanes in parts:
-
-        def over_frames(body):
-            def step(masked, g, total):
-                for f in range(GROUP):
-                    total = total + body(g, f, masked)
-                return total
-
-            total = lax.fori_loop(0, free_groups, functools.partial(step, False), jnp.zeros((rows, width), F32))
-            total = lax.fori_loop(free_groups, full_groups, functools.partial(step, True), total)
-            for f in range(frames0 - full_groups * GROUP):
-                total = total + body(full_groups, f, True)
-            return total
-
-        mean = over_frames(lambda g, f, masked: masked_to(frame(g, f, lanes), g * GROUP + f, masked)) / count
-
-        def square(g, f, masked):
-            centred = masked_to(frame(g, f, lanes) - mean, g * GROUP + f, masked)
-            return centred * centred
-
-        inv = lax.rsqrt(over_frames(square) / count + 1e-05)
+        for f in range(GROUP):
+            cols = slice(f * chans + lanes.start, f * chans + lanes.stop)
+            value = dot(patches, band_ref[:, cols]).reshape(groups, rows, width)
+            pre0[:, :, cols] = value
+            if f == 0:
+                origin = value[0]
+                shift = jnp.zeros((rows, width), F32)
+                square = jnp.zeros((rows, width), F32)
+            for g in range(groups):
+                t = g * GROUP + f
+                if 0 < t < frames0:
+                    away = masked_to(value[g] - origin, t, t >= min_valid)
+                    shift += away
+                    square += away * away
+        shift = shift / count
+        mean = origin + shift
+        inv = lax.rsqrt(jnp.maximum(square / count - shift * shift, 0.0) + 1e-05)
         mean_ref[:, lanes] = mean
         inv_ref[:, lanes] = inv
         if lanes.start == 0:
@@ -310,6 +298,7 @@
     send3,
     dpre0,
     spread,
+    turned_ref,
     out_ref,
     quarters,
 ):
@@ -320,7 +309,8 @@
     full_groups = frames0 // GROUP
     free_groups = min(((MIN_SAMPLES - taps) // stride + 1) // GROUP, full_groups)
     rest = frames0 - full_groups * GROUP
-    patches = patch_ref[...].reshape(groups * rows, depth)
+    turned = patch_ref[...].reshape(groups * rows, depth).astype(F32).T
+    turned_ref[...] = turned[: turned_ref.shape[0]].astype(BF16)
     for block in range(chans // width):
         lanes = slice(block * width, (block + 1) * width)
 
@@ -371,7 +361,7 @@
             finish(full_groups, f, True)
         if full_groups < groups:
             dpre0[full_groups, :, rest * width :] = jnp.zeros((rows, (GROUP - rest) * width), BF16)
-        spread[...] = rows_first(patches, dpre0[...].reshape(groups * rows, GROUP * width))
+        spread[...] = dot(turned_ref[...], dpre0[...].reshape(groups * rows, GROUP * width))
         total = jnp.zeros((taps, width), F32)
         for f in range(GROUP):
             total += spread[stride * f : stride * f + taps, f * width : (f + 1) * width]
@@ -596,13 +586,15 @@
         [*keeps, *others, lift_odd],
     )
     gots = [swap(part, "dev", offset) for offset, part in enumerate(sends, 1)]
+    used = -(-(stride * (GROUP - 1) + taps) // 16) * 16
     small, *smalls = call(
         functools.partial(backward_kernel, frames0, taps),
         [((16, quarter), F32)] * 4,
         [valid, pre0, mean, inv, patch, lift_even, lift_odd, gain_in],
         scratch=[
             ((groups, rows, GROUP * width), BF16),
-            ((depth, GROUP * width), F32),
+            ((used, GROUP * width), F32),
+            ((used, groups * rows), BF16),
             ((16, chans), F32),
             ((4, 16, quarter), F32),
         ],

time: 53.8 us -> 53.1 us (0.987)
  Pallas kernels: 17.1 us -> 16.3 us
    pallas_call x13, Pallas kernels: 17.1 us -> 16.3 us  [call(): pl.pallas_call(kernel, out_shape=[jax.ShapeDtypeStruct(out[0], out[1]) if...]
where the time goes in v14:
time: 53.1 us; the launch traced here: 52.9 us
  starting transfers between devices  19.3 us (36%)
  waiting for transfers between devices  16.5 us (31%)
  Pallas kernels  16.3 us (31%)
  between operations  0.75 us (1%)
    ppermute x15, starting transfers between devices, swap(): return lax.ppermute(value, axis, [(i, i ^ offset) for i in range(size)])  19.3 us
    ppermute x15, waiting for transfers between devices, swap(): return lax.ppermute(value, axis, [(i, i ^ offset) for i in range(size)])  16.5 us
    pallas_call x13, Pallas kernels, call(): pl.pallas_call(kernel, out_shape=[jax.ShapeDtypeStruct(out[0], out[1]) if...  16.3 us
  transfers between devices with their start and end apart: 15, of which 8 were waited for; matrix products, arithmetic and copies ran while one was open for 0% of the time, Pallas kernels for 13%

profile of v14, /device:TPU:0, one launch (start us, length us, event | category | flops | bytes accessed | tf_op | source)
XLA Modules:
  0.0 52.9 jit_solution(8752694591657557847)
XLA Ops:
  0.6 3.0 %collective-permute-start = (bf16[32,384]{1,0:T(8,128)(2,1)}, bf16[32,384]{1,0:T(8,128)(2,1)S(1)}, u32[]{:S(2)}, u32[]{:S(2)}) collective-permute-start(bf16[32,384]{1,0:T(8,128)(2,1)} %wave_hbm.1), channel_id=1, source_target_pairs={{0,1},{1,0},{2,3},{3,2},{4,5},{5,4},{6,7},{7,6},{8,9},{9,8},{10,11... | collective-permute-start | bytes 73736 | tf_op jit(solution)/shard_map/ppermute | solution.py:478
  3.6 1.5 %collective-permute-start.2 = (bf16[32,384]{1,0:T(8,128)(2,1)}, bf16[32,384]{1,0:T(8,128)(2,1)S(1)}, u32[]{:S(2)}, u32[]{:S(2)}) collective-permute-start(bf16[32,384]{1,0:T(8,128)(2,1)} %wave_hbm.1), channel_id=1, source_target_pairs={{0,3},{1,2},{2,1},{3,0},{4,7},{5,6},{6,5},{7,4},{8,11},{9,10},{10,... | collective-permute-start | bytes 73736 | tf_op jit(solution)/shard_map/ppermute | solution.py:478
  5.2 0.0 collective-permute-start.1
  5.2 1.3 %shard_map.119 = (s32[32,128]{1,0:T(8,128)S(1)}, bf16[128,4096]{1,0:T(8,128)(2,1)S(1)}, bf16[16,256]{1,0:T(8,128)(2,1)S(1)}, bf16[16,256]{1,0:T(8,128)(2,1)S(1)}, bf16[32,384]{1,0:T(8,128)(2,1)S(1)}) custom-call(s32[8,32]{1,0:T(8,128)} %order_hbm.1, s32[1,256]{1,0:T(1,128)} %bitcast.11, bf16[10,512]{1,0:T(8,128)(2,1)} %w_hbm.2, bf16[32,384]{1,0:T(8,128)(2,1)} %wave_hbm.1), custom_call_target="tpu_custom_call" | custom-call | tf_op jit(solution)/shard_map/pallas_call | solution.py:463
  6.5 0.0 collective-permute-done.refs_1_
  6.5 2.2 %collective-permute-done.2.refs_3_ = bf16[32,384]{1,0:T(8,128)(2,1)S(1)} collective-permute-done((bf16[32,384]{1,0:T(8,128)(2,1)}, bf16[32,384]{1,0:T(8,128)(2,1)S(1)}, u32[]{:S(2)}, u32[]{:S(2)}) %collective-permute-start.2) | collective-permute-done | bytes 24608 | tf_op jit(solution)/shard_map/ppermute | solution.py:478
  8.7 0.5 collective-permute-done.1.refs_2_
  9.2 0.2 shard_map.120
  9.4 2.6 %collective-permute-start.3 = (bf16[16,384]{1,0:T(8,128)(2,1)S(1)}, bf16[16,384]{1,0:T(8,128)(2,1)S(1)}, u32[]{:S(2)}, u32[]{:S(2)}) collective-permute-start(bf16[16,384]{1,0:T(8,128)(2,1)S(1)} %get-tuple-element.52), channel_id=1, source_target_pairs={{0,4},{1,5},{2,6},{3,7},{4,0},{5,1},{6,2},{7,3},{8,12},{9,13},{10,... | collective-permute-start | bytes 36872 | tf_op jit(solution)/shard_map/ppermute | solution.py:478
  12.1 2.0 %collective-permute-done.3.far_ref = bf16[16,384]{1,0:T(8,128)(2,1)S(1)} collective-permute-done((bf16[16,384]{1,0:T(8,128)(2,1)S(1)}, bf16[16,384]{1,0:T(8,128)(2,1)S(1)}, u32[]{:S(2)}, u32[]{:S(2)}) %collective-permute-start.3) | collective-permute-done | bytes 12320 | tf_op jit(solution)/shard_map/ppermute | solution.py:478
  14.1 6.3 %shard_map.121 = (bf16[37,32,512]{2,1,0:T(8,128)(2,1)S(1)}, bf16[41,32,512]{2,1,0:T(8,128)(2,1)S(1)}, bf16[40,32,512]{2,1,0:T(8,128)(2,1)S(1)}, f32[10,32,4096]{...) custom-call(bf16[16,384]{1,0:T(8,128)(2,1)S(1)} %get-tuple-element.5, ...), custom_call_target="tpu_custom_call" | custom-call | tf_op jit(solution)/shard_map/pallas_call | solution.py:463
  20.4 1.5 %shard_map.123 = (f32[512,512]{1,0:T(8,128)S(1)}, bf16[512,512]{1,0:T(8,128)(2,1)S(1)}) custom-call(bf16[41,32,512]{2,1,0:T(8,128)(2,1)S(1)} %get-tuple-element.61.refs_0_, bf16[40,32,512]{2,1,0:T(8,128)(2,1)S(1)} %get-tuple-element.62.refs_1_, bf16[512,1280]{1,0:T(8,128)(2,1)S(1)} %get-tuple-element.63.refs_2_.refs_1_), custom_call_target="tpu_custom_call" | custom-call | flops 1073741824 | tf_op jit(solution)/shard_map/pallas_call | solution.py:463
  21.9 0.1 collective-permute-start.4
  22.0 0.9 %shard_map.124 = (f32[512,256]{1,0:T(8,128)S(1)}, bf16[512,256]{1,0:T(8,128)(2,1)S(1)}) custom-call(bf16[41,32,512]{2,1,0:T(8,128)(2,1)S(1)} %get-tuple-element.61.refs_0_, bf16[512,1280]{1,0:T(8,128)(2,1)S(1)} %get-tuple-element.63.refs_2_.refs_1_), custom_call_target="tpu_custom_call" | custom-call | flops 536870912 | tf_op jit(solution)/shard_map/pallas_call | solution.py:463
  22.9 0.5 %collective-permute-start.5 = (bf16[512,256]{1,0:T(8,128)(2,1)S(1)}, bf16[512,256]{1,0:T(8,128)(2,1)S(1)}, u32[]{:S(2)}, u32[]{:S(2)}) collective-permute-start(bf16[512,256]{1,0:T(8,128)(2,1)S(1)} %get-tuple-element.67), channel_id=1, source_target_pairs={{0,8},{8,0},{16,24},{24,16},{1,9},{9,1},{17,25},{25,17},{2,10},{10... | collective-permute-start | bytes 786440 | tf_op jit(solution)/shard_map/ppermute | solution.py:478
  23.4 2.2 %shard_map.122 = (f32[38,32,512]{2,1,0:T(8,128)S(1)}, f32[37,32,512]{2,1,0:T(8,128)S(1)}, bf16[37,32,512]{2,1,0:T(8,128)(2,1)}) custom-call(bf16[39,32,512]{2,1,0:T(8,128)(2,1)S(1)} %get-tuple-element.55.grad_ref, bf16[3,512,512]{2,1,0:T(8,128)(2,1)S(1)} %get-tuple-element.56.w_ref, f32[40,32,512]{2,1,0:T(8,128)S(1)} %get-tuple-element.57.even_slope, ...), custom_call_target="tpu_custom_call" | custom-call | flops 1073741824 | tf_op jit(solution)/shard_map/pallas_call | solution.py:463
  25.7 0.0 collective-permute-done.5.refs_3_
  25.7 0.0 collective-permute-done.4.refs_2_
  25.7 0.1 shard_map.125
  25.8 1.6 %collective-permute-start.6 = (bf16[128,768]{1,0:T(8,128)(2,1)S(1)}, bf16[128,768]{1,0:T(8,128)(2,1)S(1)}, u32[]{:S(2)}, u32[]{:S(2)}) collective-permute-start(bf16[128,768]{1,0:T(8,128)(2,1)S(1)} %get-tuple-element.70), channel_id=1, source_target_pairs={{0,1},{1,0},{2,3},{3,2},{4,5},{5,4},{6,7},{7,6},{8,9},{9,8},{10,11... | collective-permute-start | bytes 589832 | tf_op jit(solution)/shard_map/ppermute | solution.py:478
  27.4 0.4 collective-permute-start.7
  27.8 1.6 %collective-permute-start.8 = (bf16[128,768]{1,0:T(8,128)(2,1)S(1)}, bf16[128,768]{1,0:T(8,128)(2,1)S(1)}, u32[]{:S(2)}, u32[]{:S(2)}) collective-permute-start(bf16[128,768]{1,0:T(8,128)(2,1)S(1)} %get-tuple-element.80), channel_id=1, source_target_pairs={{0,3},{1,2},{2,1},{3,0},{4,7},{5,6},{6,5},{7,4},{8,11},{9,10},{10,... | collective-permute-start | bytes 589832 | tf_op jit(solution)/shard_map/ppermute | solution.py:478
  29.4 2.7 %shard_map.126 = (f32[16,128]{1,0:T(8,128)S(1)}, f32[16,128]{1,0:T(8,128)S(1)}, f32[16,128]{1,0:T(8,128)S(1)}, f32[16,128]{1,0:T(8,128)S(1)}) custom-call(s32[32,128]{1,0:T(8,128)S(1)} %get-tuple-element.53.valid_ref, f32[10,32,4096]{2,1,0:T(8,128)S(1)} %get-tuple-element.72.pre0, f32[32,512]{1,0:T(8,128)S(1)} %get-tuple-element.73.mean_ref, ...), custom_call_target="tpu_custom_call" | custom-call | flops 4294967296 | tf_op jit(solution)/shard_map/pallas_call | solution.py:463
  32.1 1.0 %collective-permute-start.10 = (f32[16,128]{1,0:T(8,128)S(1)}, f32[16,128]{1,0:T(8,128)S(1)}, u32[]{:S(2)}, u32[]{:S(2)}) collective-permute-start(f32[16,128]{1,0:T(8,128)S(1)} %get-tuple-element.83), channel_id=1, source_target_pairs={{0,2},{1,3},{2,0},{3,1},{4,6},{5,7},{6,4},{7,5},{8,10},{9,11},{10,... | collective-permute-start | bytes 24584 | tf_op jit(solution)/shard_map/ppermute | solution.py:478
  33.1 2.0 %collective-permute-start.11 = (f32[16,128]{1,0:T(8,128)S(1)}, f32[16,128]{1,0:T(8,128)S(1)}, u32[]{:S(2)}, u32[]{:S(2)}) collective-permute-start(f32[16,128]{1,0:T(8,128)S(1)} %get-tuple-element.84), channel_id=1, source_target_pairs={{0,3},{1,2},{2,1},{3,0},{4,7},{5,6},{6,5},{7,4},{8,11},{9,10},{10,... | collective-permute-start | bytes 24584 | tf_op jit(solution)/shard_map/ppermute | solution.py:478
  35.2 0.0 collective-permute-done.6.got1
  35.2 0.0 collective-permute-done.7.got2
  35.2 0.1 shard_map.127
  35.3 0.6 %collective-permute-start.9 = (f32[16,128]{1,0:T(8,128)S(1)}, f32[16,128]{1,0:T(8,128)S(1)}, u32[]{:S(2)}, u32[]{:S(2)}) collective-permute-start(f32[16,128]{1,0:T(8,128)S(1)} %get-tuple-element.82), channel_id=1, source_target_pairs={{0,1},{1,0},{2,3},{3,2},{4,5},{5,4},{6,7},{7,6},{8,9},{9,8},{10,11... | collective-permute-start | bytes 24584 | tf_op jit(solution)/shard_map/ppermute | solution.py:478
  35.9 2.6 %collective-permute-done.10.small2 = f32[16,128]{1,0:T(8,128)S(1)} collective-permute-done((f32[16,128]{1,0:T(8,128)S(1)}, f32[16,128]{1,0:T(8,128)S(1)}, u32[]{:S(2)}, u32[]{:S(2)}) %collective-permute-start.10) | collective-permute-done | bytes 8224 | tf_op jit(solution)/shard_map/ppermute | solution.py:478
  38.4 0.0 collective-permute-done.11.small3
  38.5 0.0 collective-permute-done.8.got3
  38.5 0.5 collective-permute-done.9.small1
  39.0 0.1 shard_map.128
  39.0 2.6 %collective-permute-start.12 = (bf16[80,640]{1,0:T(8,128)(2,1)S(1)}, bf16[80,640]{1,0:T(8,128)(2,1)S(1)}, u32[]{:S(2)}, u32[]{:S(2)}) collective-permute-start(bf16[80,640]{1,0:T(8,128)(2,1)S(1)} %get-tuple-element.86), channel_id=1, source_target_pairs={{0,4},{1,5},{2,6},{3,7},{4,0},{5,1},{6,2},{7,3},{8,12},{9,13},{10,... | collective-permute-start | bytes 307208 | tf_op jit(solution)/shard_map/ppermute | solution.py:478
  41.7 4.0 %collective-permute-done.12.got_ref = bf16[80,640]{1,0:T(8,128)(2,1)S(1)} collective-permute-done((bf16[80,640]{1,0:T(8,128)(2,1)S(1)}, bf16[80,640]{1,0:T(8,128)(2,1)S(1)}, u32[]{:S(2)}, u32[]{:S(2)}) %collective-permute-start.12) | collective-permute-done | bytes 102432 | tf_op jit(solution)/shard_map/ppermute | solution.py:478
  45.7 1.6 %collective-permute-start.13 = (bf16[80,640]{1,0:T(8,128)(2,1)S(1)}, bf16[80,640]{1,0:T(8,128)(2,1)S(1)}, u32[]{:S(2)}, u32[]{:S(2)}) collective-permute-start(bf16[80,640]{1,0:T(8,128)(2,1)S(1)} %shard_map.129.mine_ref), channel_id=1, source_target_pairs={{0,16},{8,24},{16,0},{24,8},{1,17},{9,25},{17,1},{25,9},{2,18},{10... | collective-permute-start | bytes 307208 | tf_op jit(solution)/shard_map/ppermute | solution.py:478
  47.3 3.1 %collective-permute-done.13.got_ref = bf16[80,640]{1,0:T(8,128)(2,1)S(1)} collective-permute-done((bf16[80,640]{1,0:T(8,128)(2,1)S(1)}, bf16[80,640]{1,0:T(8,128)(2,1)S(1)}, u32[]{:S(2)}, u32[]{:S(2)}) %collective-permute-start.13) | collective-permute-done | bytes 102432 | tf_op jit(solution)/shard_map/ppermute | solution.py:478
  50.5 0.1 collective-permute-start.14
  50.6 1.4 %collective-permute-done.14.other_ref = f32[80,640]{1,0:T(8,128)S(1)} collective-permute-done((f32[80,640]{1,0:T(8,128)S(1)}, f32[80,640]{1,0:T(8,128)S(1)}, u32[]{:S(2)}, u32[]{:S(2)}) %collective-permute-start.14) | collective-permute-done | bytes 204832 | tf_op jit(solution)/shard_map/ppermute | solution.py:478
  52.0 0.8 %shard_map.131 = (f32[3,64,512]{2,1,0:T(8,128)}, f32[10,64]{1,0:T(8,128)}, f32[1,64]{1,0:T(1,128)}, f32[1,64]{1,0:T(1,128)}) custom-call(f32[80,640]{1,0:T(8,128)S(1)} %shard_map.130.own_ref, f32[80,640]{1,0:T(8,128)S(1)} %collective-permute-done.14.other_ref), custom_call_target="tpu_custom_call" | custom-call | tf_op jit(solution)/shard_map/pallas_call | solution.py:463
  (2 shorter events, 0.0 us)
Async XLA Ops:
  0.6 5.9 %collective-permute-start = (bf16[32,384]{1,0:T(8,128)(2,1)}, bf16[32,384]{1,0:T(8,128)(2,1)S(1)}, u32[]{:S(2)}, u32[]{:S(2)}) collective-permute-start(bf16[32,384]{1,0:T(8,128)(2,1)} %wave_hbm.1), channel_id=1, source_target_pairs={{0,1},{1,0},{2,3},{3,2},{4,5},{5,4},{6,7},{7,6},{8,9},{9,8},{10,11... | collective-permute-start | bytes 73736 | tf_op jit(solution)/shard_map/ppermute | solution.py:478
  3.6 5.1 %collective-permute-start.2 = (bf16[32,384]{1,0:T(8,128)(2,1)}, bf16[32,384]{1,0:T(8,128)(2,1)S(1)}, u32[]{:S(2)}, u32[]{:S(2)}) collective-permute-start(bf16[32,384]{1,0:T(8,128)(2,1)} %wave_hbm.1), channel_id=1, source_target_pairs={{0,3},{1,2},{2,1},{3,0},{4,7},{5,6},{6,5},{7,4},{8,11},{9,10},{10,... | collective-permute-start | bytes 73736 | tf_op jit(solution)/shard_map/ppermute | solution.py:478
  5.2 4.0 %collective-permute-start.1 = (bf16[32,384]{1,0:T(8,128)(2,1)}, bf16[32,384]{1,0:T(8,128)(2,1)S(1)}, u32[]{:S(2)}, u32[]{:S(2)}) collective-permute-start(bf16[32,384]{1,0:T(8,128)(2,1)} %wave_hbm.1), channel_id=1, source_target_pairs={{0,2},{1,3},{2,0},{3,1},{4,6},{5,7},{6,4},{7,5},{8,10},{9,11},{10,... | collective-permute-start | bytes 73736 | tf_op jit(solution)/shard_map/ppermute | solution.py:478
  9.4 4.6 %collective-permute-start.3 = (bf16[16,384]{1,0:T(8,128)(2,1)S(1)}, bf16[16,384]{1,0:T(8,128)(2,1)S(1)}, u32[]{:S(2)}, u32[]{:S(2)}) collective-permute-start(bf16[16,384]{1,0:T(8,128)(2,1)S(1)} %get-tuple-element.52), channel_id=1, source_target_pairs={{0,4},{1,5},{2,6},{3,7},{4,0},{5,1},{6,2},{7,3},{8,12},{9,13},{10,... | collective-permute-start | bytes 36872 | tf_op jit(solution)/shard_map/ppermute | solution.py:478
  21.9 3.7 %collective-permute-start.4 = (bf16[512,512]{1,0:T(8,128)(2,1)S(1)}, bf16[512,512]{1,0:T(8,128)(2,1)S(1)}, u32[]{:S(2)}, u32[]{:S(2)}) collective-permute-start(bf16[512,512]{1,0:T(8,128)(2,1)S(1)} %get-tuple-element.66), channel_id=1, source_target_pairs={{0,8},{8,0},{16,24},{24,16},{1,9},{9,1},{17,25},{25,17},{2,10},{10... | collective-permute-start | bytes 1572872 | tf_op jit(solution)/shard_map/ppermute | solution.py:478
  22.9 2.8 %collective-permute-start.5 = (bf16[512,256]{1,0:T(8,128)(2,1)S(1)}, bf16[512,256]{1,0:T(8,128)(2,1)S(1)}, u32[]{:S(2)}, u32[]{:S(2)}) collective-permute-start(bf16[512,256]{1,0:T(8,128)(2,1)S(1)} %get-tuple-element.67), channel_id=1, source_target_pairs={{0,8},{8,0},{16,24},{24,16},{1,9},{9,1},{17,25},{25,17},{2,10},{10... | collective-permute-start | bytes 786440 | tf_op jit(solution)/shard_map/ppermute | solution.py:478
  25.8 9.3 %collective-permute-start.6 = (bf16[128,768]{1,0:T(8,128)(2,1)S(1)}, bf16[128,768]{1,0:T(8,128)(2,1)S(1)}, u32[]{:S(2)}, u32[]{:S(2)}) collective-permute-start(bf16[128,768]{1,0:T(8,128)(2,1)S(1)} %get-tuple-element.70), channel_id=1, source_target_pairs={{0,1},{1,0},{2,3},{3,2},{4,5},{5,4},{6,7},{7,6},{8,9},{9,8},{10,11... | collective-permute-start | bytes 589832 | tf_op jit(solution)/shard_map/ppermute | solution.py:478
  27.4 7.8 %collective-permute-start.7 = (bf16[128,768]{1,0:T(8,128)(2,1)S(1)}, bf16[128,768]{1,0:T(8,128)(2,1)S(1)}, u32[]{:S(2)}, u32[]{:S(2)}) collective-permute-start(bf16[128,768]{1,0:T(8,128)(2,1)S(1)} %get-tuple-element.71), channel_id=1, source_target_pairs={{0,2},{1,3},{2,0},{3,1},{4,6},{5,7},{6,4},{7,5},{8,10},{9,11},{10,... | collective-permute-start | bytes 589832 | tf_op jit(solution)/shard_map/ppermute | solution.py:478
  27.8 10.6 %collective-permute-start.8 = (bf16[128,768]{1,0:T(8,128)(2,1)S(1)}, bf16[128,768]{1,0:T(8,128)(2,1)S(1)}, u32[]{:S(2)}, u32[]{:S(2)}) collective-permute-start(bf16[128,768]{1,0:T(8,128)(2,1)S(1)} %get-tuple-element.80), channel_id=1, source_target_pairs={{0,3},{1,2},{2,1},{3,0},{4,7},{5,6},{6,5},{7,4},{8,11},{9,10},{10,... | collective-permute-start | bytes 589832 | tf_op jit(solution)/shard_map/ppermute | solution.py:478
  32.1 6.3 %collective-permute-start.10 = (f32[16,128]{1,0:T(8,128)S(1)}, f32[16,128]{1,0:T(8,128)S(1)}, u32[]{:S(2)}, u32[]{:S(2)}) collective-permute-start(f32[16,128]{1,0:T(8,128)S(1)} %get-tuple-element.83), channel_id=1, source_target_pairs={{0,2},{1,3},{2,0},{3,1},{4,6},{5,7},{6,4},{7,5},{8,10},{9,11},{10,... | collective-permute-start | bytes 24584 | tf_op jit(solution)/shard_map/ppermute | solution.py:478
  33.1 5.4 %collective-permute-start.11 = (f32[16,128]{1,0:T(8,128)S(1)}, f32[16,128]{1,0:T(8,128)S(1)}, u32[]{:S(2)}, u32[]{:S(2)}) collective-permute-start(f32[16,128]{1,0:T(8,128)S(1)} %get-tuple-element.84), channel_id=1, source_target_pairs={{0,3},{1,2},{2,1},{3,0},{4,7},{5,6},{6,5},{7,4},{8,11},{9,10},{10,... | collective-permute-start | bytes 24584 | tf_op jit(solution)/shard_map/ppermute | solution.py:478
  35.3 3.7 %collective-permute-start.9 = (f32[16,128]{1,0:T(8,128)S(1)}, f32[16,128]{1,0:T(8,128)S(1)}, u32[]{:S(2)}, u32[]{:S(2)}) collective-permute-start(f32[16,128]{1,0:T(8,128)S(1)} %get-tuple-element.82), channel_id=1, source_target_pairs={{0,1},{1,0},{2,3},{3,2},{4,5},{5,4},{6,7},{7,6},{8,9},{9,8},{10,11... | collective-permute-start | bytes 24584 | tf_op jit(solution)/shard_map/ppermute | solution.py:478
  39.0 6.7 %collective-permute-start.12 = (bf16[80,640]{1,0:T(8,128)(2,1)S(1)}, bf16[80,640]{1,0:T(8,128)(2,1)S(1)}, u32[]{:S(2)}, u32[]{:S(2)}) collective-permute-start(bf16[80,640]{1,0:T(8,128)(2,1)S(1)} %get-tuple-element.86), channel_id=1, source_target_pairs={{0,4},{1,5},{2,6},{3,7},{4,0},{5,1},{6,2},{7,3},{8,12},{9,13},{10,... | collective-permute-start | bytes 307208 | tf_op jit(solution)/shard_map/ppermute | solution.py:478
  45.7 4.7 %collective-permute-start.13 = (bf16[80,640]{1,0:T(8,128)(2,1)S(1)}, bf16[80,640]{1,0:T(8,128)(2,1)S(1)}, u32[]{:S(2)}, u32[]{:S(2)}) collective-permute-start(bf16[80,640]{1,0:T(8,128)(2,1)S(1)} %shard_map.129.mine_ref), channel_id=1, source_target_pairs={{0,16},{8,24},{16,0},{24,8},{1,17},{9,25},{17,1},{25,9},{2,18},{10... | collective-permute-start | bytes 307208 | tf_op jit(solution)/shard_map/ppermute | solution.py:478
  50.5 1.5 %collective-permute-start.14 = (f32[80,640]{1,0:T(8,128)S(1)}, f32[80,640]{1,0:T(8,128)S(1)}, u32[]{:S(2)}, u32[]{:S(2)}) collective-permute-start(f32[80,640]{1,0:T(8,128)S(1)} %shard_map.130.own_ref), channel_id=1, source_target_pairs={{0,8},{8,0},{16,24},{24,16},{1,9},{9,1},{17,25},{25,17},{2,10},{10... | collective-permute-start | bytes 614408 | tf_op jit(solution)/shard_map/ppermute | solution.py:478

commit v15 on v14

--- a/solution.py
+++ b/solution.py
@@ -267,17 +267,20 @@
             out_ref[:, tap * half : (tap + 1) * half] = value.astype(out_ref.dtype)
 
 
-def input_kernel(grad_ref, w_ref, even_slope, odd_slope, feat_ref, even_ref, odd_ref, feat_out, sem):
+def odd_input_kernel(grad_ref, w_ref, slope_ref, lift_ref):
+    odds, rows, chans = lift_ref.shape
+    second = grad_ref[1 : odds + 1].reshape(odds * rows, chans)
+    lift_ref[...] = cols_both(second, w_ref[1]).reshape(lift_ref.shape) * slope_ref[:odds]
+
+
+def even_input_kernel(grad_ref, w_ref, slope_ref, after_ref, feat_ref, lift_ref, feat_out, sem):
     leaving = pltpu.make_async_copy(feat_ref, feat_out, sem)
     leaving.start()
-    evens, rows, chans = even_ref.shape
-    odds = odd_ref.shape[0]
+    evens, rows, chans = lift_ref.shape
     first = grad_ref[1 : evens + 1].reshape(evens * rows, chans)
     third = grad_ref[0:evens].reshape(evens * rows, chans)
     total = cols_both(first, w_ref[0]) + cols_both(third, w_ref[2])
-    even_ref[...] = total.reshape(even_ref.shape) * even_slope[:evens]
-    second = grad_ref[1 : odds + 1].reshape(odds * rows, chans)
-    odd_ref[...] = cols_both(second, w_ref[1]).reshape(odd_ref.shape) * odd_slope[:odds]
+    lift_ref[...] = total.reshape(lift_ref.shape) * slope_ref[:evens]
     leaving.wait()
 
 
@@ -305,67 +308,58 @@
     groups, rows, depth = patch_ref.shape
     chans = gain_ref.shape[1]
     stride = taps // 2
-    width = dpre0.shape[2] // GROUP
-    full_groups = frames0 // GROUP
-    free_groups = min(((MIN_SAMPLES - taps) // stride + 1) // GROUP, full_groups)
-    rest = frames0 - full_groups * GROUP
+    width = dpre0.shape[3] // GROUP
     turned = patch_ref[...].reshape(groups * rows, depth).astype(F32).T
     turned_ref[...] = turned[: turned_ref.shape[0]].astype(BF16)
-    for block in range(chans // width):
-        lanes = slice(block * width, (block + 1) * width)
-
-        def frame(g, f):
-            return pre0[g, :, f * chans + block * width : f * chans + (block + 1) * width]
-
-        def lift(g, f):
-            return (odd_ref if f % 2 else even_ref)[g * (GROUP // 2) + f // 2, :, lanes]
-
-        def sums(g, f, carry):
-            bias_sum, gain_sum = carry
-            return bias_sum + lift(g, f), gain_sum + lift(g, f) * frame(g, f)
-
-        def add(g, carry):
-            for f in range(GROUP):
-                carry = sums(g, f, carry)
-            return carry
-
-        zero = jnp.zeros((rows, width), F32)
-        carry = lax.fori_loop(0, full_groups, add, (zero, zero))
-        for f in range(rest):
-            carry = sums(full_groups, f, carry)
-        bias_sum, gain_sum = carry
+    valid = jnp.broadcast_to(valid_ref[:, :1], (rows, width))
+    count = valid.astype(F32)
+    min_valid = (MIN_SAMPLES - taps) // stride + 1
+    parts = [slice(first, first + width) for first in range(0, chans, width)]
+
+    def frame(t, lanes):
+        start = t % GROUP * chans
+        return pre0[t // GROUP, :, start + lanes.start : start + lanes.stop]
+
+    def lift(t, lanes):
+        return (odd_ref if t % 2 else even_ref)[t // 2, :, lanes]
+
+    def sums(lanes):
+        bias_sum = gain_sum = jnp.zeros((rows, width), F32)
+        for t in range(frames0):
+            bias_sum += lift(t, lanes)
+            gain_sum += lift(t, lanes) * frame(t, lanes)
         mean, inv = mean_ref[:, lanes], inv_ref[:, lanes]
         gain_sum = (gain_sum - mean * bias_sum) * inv
         out_ref[taps : taps + 1, lanes] = jnp.sum(gain_sum, axis=0, keepdims=True)
         out_ref[taps + 1 : taps + 2, lanes] = jnp.sum(bias_sum, axis=0, keepdims=True)
-        valid = jnp.broadcast_to(valid_ref[:, :1], (rows, width))
-        count = valid.astype(F32)
         scale = inv * gain_ref[:, lanes]
         slant = scale * inv * gain_sum / count
-        level = scale * bias_sum / count - mean * slant
-
-        def finish(g, f, masked):
-            value = scale * lift(g, f) - frame(g, f) * slant - level
-            if masked:
-                value = jnp.where(valid > g * GROUP + f, value, 0.0)
-            dpre0[g, :, f * width : (f + 1) * width] = value.astype(BF16)
-
-        def whole(masked, g, carry):
-            for f in range(GROUP):
-                finish(g, f, masked)
-            return carry
-
-        lax.fori_loop(0, free_groups, functools.partial(whole, False), 0)
-        lax.fori_loop(free_groups, full_groups, functools.partial(whole, True), 0)
-        for f in range(rest):
-            finish(full_groups, f, True)
-        if full_groups < groups:
-            dpre0[full_groups, :, rest * width :] = jnp.zeros((rows, (GROUP - rest) * width), BF16)
-        spread[...] = dot(turned_ref[...], dpre0[...].reshape(groups * rows, GROUP * width))
+        return scale, slant, scale * bias_sum / count - mean * slant
+
+    def gradients(block, lanes, scale, slant, level):
+        for t in range(frames0):
+            value = scale * lift(t, lanes) - frame(t, lanes) * slant - level
+            if t >= min_valid:
+                value = jnp.where(valid > t, value, 0.0)
+            f = t % GROUP
+            dpre0[block, t // GROUP, :, f * width : (f + 1) * width] = value.astype(BF16)
+        rest = frames0 - frames0 // GROUP * GROUP
+        if rest:
+            dpre0[block, groups - 1, :, rest * width :] = jnp.zeros((rows, (GROUP - rest) * width), BF16)
+
+    def taps_of(block, lanes):
+        spread[block] = dot(turned_ref[...], dpre0[block].reshape(groups * rows, GROUP * width))
         total = jnp.zeros((taps, width), F32)
         for f in range(GROUP):
-            total += spread[stride * f : stride * f + taps, f * width : (f + 1) * width]
+            total += spread[block, stride * f : stride * f + taps, f * width : (f + 1) * width]
         out_ref[:taps, lanes] = total
+
+    terms = sums(parts[0])
+    for block, lanes in enumerate(parts):
+        gradients(block, lanes, *terms)
+        if block + 1 < len(parts):
+            terms = sums(parts[block + 1])
+        taps_of(block, lanes)
     size = chans // lax.axis_size("dev")
     for place in range(4):
         columns = [slice(first, first + size) for first in range(place * size, chans, 4 * size)]
@@ -572,13 +566,7 @@
         keeps.append(keep)
         others.append(swap(send, "grp", 1))
     evens, odds = (frames0 + 1) // 2, frames0 // 2
-    lift_even, lift_odd, features = call(
-        input_kernel,
-        [((evens, rows, chans), F32), ((odds, rows, chans), F32), ((frames1, rows, chans), BF16, "hbm")],
-        [grad, w_in, even_slope, odd_slope, feat],
-        scratch=[pltpu.SemaphoreType.DMA],
-        flops=1 << 30,
-    )
+    lift_odd = call(odd_input_kernel, [((odds, rows, chans), F32)], [grad, w_in, odd_slope], flops=1 << 29)[0]
     quarter = chans // 4
     own, *sends = call(
         plane_kernel,
@@ -586,14 +574,21 @@
         [*keeps, *others, lift_odd],
     )
     gots = [swap(part, "dev", offset) for offset, part in enumerate(sends, 1)]
+    lift_even, features = call(
+        even_input_kernel,
+        [((evens, rows, chans), F32), ((frames1, rows, chans), BF16, "hbm")],
+        [grad, w_in, even_slope, own, feat],
+        scratch=[pltpu.SemaphoreType.DMA],
+        flops=1 << 30,
+    )
     used = -(-(stride * (GROUP - 1) + taps) // 16) * 16
     small, *smalls = call(
         functools.partial(backward_kernel, frames0, taps),
         [((16, quarter), F32)] * 4,
         [valid, pre0, mean, inv, patch, lift_even, lift_odd, gain_in],
         scratch=[
-            ((groups, rows, GROUP * width), BF16),
-            ((used, GROUP * width), F32),
+            ((chans // width, groups, rows, GROUP * width), BF16),
+            ((chans // width, used, GROUP * width), F32),
             ((used, groups * rows), BF16),
             ((16, chans), F32),
             ((4, 16, quarter), F32),

time: 53.1 us -> 53.1 us (level)
  Pallas kernels: 16.3 us -> 15.7 us
    pallas_call x13 -> x14, Pallas kernels: 16.3 us -> 15.7 us  [call(): pl.pallas_call(kernel, out_shape=[jax.ShapeDtypeStruct(out[0], out[1]) if...]
  transfers between devices with their start and end apart: 15 -> 15, of which waited for: 8 -> 10; matrix products, arithmetic and copies ran while one was open for 0% -> 0% of each run, Pallas kernels for 13% -> 12%
where the time goes in v15:
time: 53.1 us; the launch traced here: 52.9 us
  starting transfers between devices  19.5 us (37%)
  waiting for transfers between devices  17 us (32%)
  Pallas kernels  15.7 us (30%)
  between operations  0.73 us (1%)
    ppermute x15, starting transfers between devices, swap(): return lax.ppermute(value, axis, [(i, i ^ offset) for i in range(size)])  19.5 us
    ppermute x15, waiting for transfers between devices, swap(): return lax.ppermute(value, axis, [(i, i ^ offset) for i in range(size)])  17 us
    pallas_call x14, Pallas kernels, call(): pl.pallas_call(kernel, out_shape=[jax.ShapeDtypeStruct(out[0], out[1]) if...  15.7 us
  transfers between devices with their start and end apart: 15, of which 10 were waited for; matrix products, arithmetic and copies ran while one was open for 0% of the time, Pallas kernels for 12%

profile of v15, /device:TPU:0, one launch (start us, length us, event | category | flops | bytes accessed | tf_op | source)
XLA Modules:
  0.0 52.9 jit_solution(5634078741918407046)
XLA Ops:
  0.6 3.0 %collective-permute-start = (bf16[32,384]{1,0:T(8,128)(2,1)}, bf16[32,384]{1,0:T(8,128)(2,1)S(1)}, u32[]{:S(2)}, u32[]{:S(2)}) collective-permute-start(bf16[32,384]{1,0:T(8,128)(2,1)} %wave_hbm.1), channel_id=1, source_target_pairs={{0,1},{1,0},{2,3},{3,2},{4,5},{5,4},{6,7},{7,6},{8,9},{9,8},{10,11... | collective-permute-start | bytes 73736 | tf_op jit(solution)/shard_map/ppermute | solution.py:472
  3.6 1.6 %collective-permute-start.1 = (bf16[32,384]{1,0:T(8,128)(2,1)}, bf16[32,384]{1,0:T(8,128)(2,1)S(1)}, u32[]{:S(2)}, u32[]{:S(2)}) collective-permute-start(bf16[32,384]{1,0:T(8,128)(2,1)} %wave_hbm.1), channel_id=1, source_target_pairs={{0,2},{1,3},{2,0},{3,1},{4,6},{5,7},{6,4},{7,5},{8,10},{9,11},{10,... | collective-permute-start | bytes 73736 | tf_op jit(solution)/shard_map/ppermute | solution.py:472
  5.2 0.0 collective-permute-start.2
  5.2 1.3 %shard_map.119 = (s32[32,128]{1,0:T(8,128)S(1)}, bf16[128,4096]{1,0:T(8,128)(2,1)S(1)}, bf16[16,256]{1,0:T(8,128)(2,1)S(1)}, bf16[16,256]{1,0:T(8,128)(2,1)S(1)}, bf16[32,384]{1,0:T(8,128)(2,1)S(1)}) custom-call(s32[8,32]{1,0:T(8,128)} %order_hbm.1, s32[1,256]{1,0:T(1,128)} %bitcast.11, bf16[10,512]{1,0:T(8,128)(2,1)} %w_hbm.2, bf16[32,384]{1,0:T(8,128)(2,1)} %wave_hbm.1), custom_call_target="tpu_custom_call" | custom-call | tf_op jit(solution)/shard_map/pallas_call | solution.py:457
  6.5 0.0 collective-permute-done.refs_1_
  6.5 1.3 %collective-permute-done.1.refs_2_ = bf16[32,384]{1,0:T(8,128)(2,1)S(1)} collective-permute-done((bf16[32,384]{1,0:T(8,128)(2,1)}, bf16[32,384]{1,0:T(8,128)(2,1)S(1)}, u32[]{:S(2)}, u32[]{:S(2)}) %collective-permute-start.1) | collective-permute-done | bytes 24608 | tf_op jit(solution)/shard_map/ppermute | solution.py:472
  7.8 2.4 %collective-permute-done.2.refs_3_ = bf16[32,384]{1,0:T(8,128)(2,1)S(1)} collective-permute-done((bf16[32,384]{1,0:T(8,128)(2,1)}, bf16[32,384]{1,0:T(8,128)(2,1)S(1)}, u32[]{:S(2)}, u32[]{:S(2)}) %collective-permute-start.2) | collective-permute-done | bytes 24608 | tf_op jit(solution)/shard_map/ppermute | solution.py:472
  10.2 0.2 shard_map.120
  10.3 2.8 %collective-permute-start.3 = (bf16[16,384]{1,0:T(8,128)(2,1)S(1)}, bf16[16,384]{1,0:T(8,128)(2,1)S(1)}, u32[]{:S(2)}, u32[]{:S(2)}) collective-permute-start(bf16[16,384]{1,0:T(8,128)(2,1)S(1)} %get-tuple-element.51), channel_id=1, source_target_pairs={{0,4},{1,5},{2,6},{3,7},{4,0},{5,1},{6,2},{7,3},{8,12},{9,13},{10,... | collective-permute-start | bytes 36872 | tf_op jit(solution)/shard_map/ppermute | solution.py:472
  13.1 1.9 %collective-permute-done.3.far_ref = bf16[16,384]{1,0:T(8,128)(2,1)S(1)} collective-permute-done((bf16[16,384]{1,0:T(8,128)(2,1)S(1)}, bf16[16,384]{1,0:T(8,128)(2,1)S(1)}, u32[]{:S(2)}, u32[]{:S(2)}) %collective-permute-start.3) | collective-permute-done | bytes 12320 | tf_op jit(solution)/shard_map/ppermute | solution.py:472
  15.0 6.3 %shard_map.121 = (bf16[37,32,512]{2,1,0:T(8,128)(2,1)S(1)}, bf16[41,32,512]{2,1,0:T(8,128)(2,1)S(1)}, bf16[40,32,512]{2,1,0:T(8,128)(2,1)S(1)}, f32[10,32,4096]{...) custom-call(bf16[16,384]{1,0:T(8,128)(2,1)S(1)} %get-tuple-element.5, ...), custom_call_target="tpu_custom_call" | custom-call | tf_op jit(solution)/shard_map/pallas_call | solution.py:457
  21.3 1.5 %shard_map.122 = (f32[512,512]{1,0:T(8,128)S(1)}, bf16[512,512]{1,0:T(8,128)(2,1)S(1)}) custom-call(bf16[41,32,512]{2,1,0:T(8,128)(2,1)S(1)} %get-tuple-element.57.refs_0_, bf16[40,32,512]{2,1,0:T(8,128)(2,1)S(1)} %get-tuple-element.58.refs_1_, bf16[512,1280]{1,0:T(8,128)(2,1)S(1)} %get-tuple-element.59.refs_2_.refs_1_), custom_call_target="tpu_custom_call" | custom-call | flops 1073741824 | tf_op jit(solution)/shard_map/pallas_call | solution.py:457
  22.9 0.1 collective-permute-start.4
  23.0 0.9 %shard_map.123 = (f32[512,256]{1,0:T(8,128)S(1)}, bf16[512,256]{1,0:T(8,128)(2,1)S(1)}) custom-call(bf16[41,32,512]{2,1,0:T(8,128)(2,1)S(1)} %get-tuple-element.57.refs_0_, bf16[512,1280]{1,0:T(8,128)(2,1)S(1)} %get-tuple-element.59.refs_2_.refs_1_), custom_call_target="tpu_custom_call" | custom-call | flops 536870912 | tf_op jit(solution)/shard_map/pallas_call | solution.py:457
  23.8 0.5 %collective-permute-start.5 = (bf16[512,256]{1,0:T(8,128)(2,1)S(1)}, bf16[512,256]{1,0:T(8,128)(2,1)S(1)}, u32[]{:S(2)}, u32[]{:S(2)}) collective-permute-start(bf16[512,256]{1,0:T(8,128)(2,1)S(1)} %get-tuple-element.63), channel_id=1, source_target_pairs={{0,8},{8,0},{16,24},{24,16},{1,9},{9,1},{17,25},{25,17},{2,10},{10... | collective-permute-start | bytes 786440 | tf_op jit(solution)/shard_map/ppermute | solution.py:472
  24.4 0.8 %shard_map.124.refs_4_.odd_ref = f32[37,32,512]{2,1,0:T(8,128)S(1)} custom-call(bf16[39,32,512]{2,1,0:T(8,128)(2,1)S(1)} %get-tuple-element.54.grad_ref, bf16[3,512,512]{2,1,0:T(8,128)(2,1)S(1)} %get-tuple-element.55.w_ref, f32[40,32,512]{2,1,0:T(8,128)S(1)} %get-tuple-element.64.slope_ref), custom_call_target="tpu_custom_call" | custom-call | flops 536870912 | tf_op jit(solution)/shard_map/pallas_call | solution.py:457
  25.2 0.3 collective-permute-done.5.refs_3_
  25.5 0.0 collective-permute-done.4.refs_2_
  25.5 0.1 shard_map.125
  25.7 0.6 %collective-permute-start.6 = (bf16[128,768]{1,0:T(8,128)(2,1)S(1)}, bf16[128,768]{1,0:T(8,128)(2,1)S(1)}, u32[]{:S(2)}, u32[]{:S(2)}) collective-permute-start(bf16[128,768]{1,0:T(8,128)(2,1)S(1)} %get-tuple-element.68), channel_id=1, source_target_pairs={{0,1},{1,0},{2,3},{3,2},{4,5},{5,4},{6,7},{7,6},{8,9},{9,8},{10,11... | collective-permute-start | bytes 589832 | tf_op jit(solution)/shard_map/ppermute | solution.py:472
  26.3 0.3 collective-permute-start.7
  26.6 2.7 %collective-permute-start.8 = (bf16[128,768]{1,0:T(8,128)(2,1)S(1)}, bf16[128,768]{1,0:T(8,128)(2,1)S(1)}, u32[]{:S(2)}, u32[]{:S(2)}) collective-permute-start(bf16[128,768]{1,0:T(8,128)(2,1)S(1)} %get-tuple-element.78), channel_id=1, source_target_pairs={{0,3},{1,2},{2,1},{3,0},{4,7},{5,6},{6,5},{7,4},{8,11},{9,10},{10,... | collective-permute-start | bytes 589832 | tf_op jit(solution)/shard_map/ppermute | solution.py:472
  29.2 1.5 %shard_map.126 = (f32[38,32,512]{2,1,0:T(8,128)S(1)}, bf16[37,32,512]{2,1,0:T(8,128)(2,1)}) custom-call(bf16[39,32,512]{2,1,0:T(8,128)(2,1)S(1)} %get-tuple-element.54.grad_ref, bf16[3,512,512]{2,1,0:T(8,128)(2,1)S(1)} %get-tuple-element.55.w_ref, f32[40,32,512]{2,1,0:T(8,128)S(1)} %get-tuple-element.56.slope_ref, ...), custom_call_target="tpu_custom_call" | custom-call | flops 1073741824 | tf_op jit(solution)/shard_map/pallas_call | solution.py:457
  30.8 2.0 %shard_map.127 = (f32[16,128]{1,0:T(8,128)S(1)}, f32[16,128]{1,0:T(8,128)S(1)}, f32[16,128]{1,0:T(8,128)S(1)}, f32[16,128]{1,0:T(8,128)S(1)}) custom-call(s32[32,128]{1,0:T(8,128)S(1)} %get-tuple-element.52.valid_ref, f32[10,32,4096]{2,1,0:T(8,128)S(1)} %get-tuple-element.70.pre0, f32[32,512]{1,0:T(8,128)S(1)} %get-tuple-element.71.mean_ref, ...), custom_call_target="tpu_custom_call" | custom-call | flops 4294967296 | tf_op jit(solution)/shard_map/pallas_call | solution.py:457
  32.8 0.5 collective-permute-start.10
  33.3 1.5 %collective-permute-start.11 = (f32[16,128]{1,0:T(8,128)S(1)}, f32[16,128]{1,0:T(8,128)S(1)}, u32[]{:S(2)}, u32[]{:S(2)}) collective-permute-start(f32[16,128]{1,0:T(8,128)S(1)} %get-tuple-element.82), channel_id=1, source_target_pairs={{0,3},{1,2},{2,1},{3,0},{4,7},{5,6},{6,5},{7,4},{8,11},{9,10},{10,... | collective-permute-start | bytes 24584 | tf_op jit(solution)/shard_map/ppermute | solution.py:472
  34.9 0.0 collective-permute-done.6.got1
  34.9 0.0 collective-permute-done.7.got2
  34.9 0.1 shard_map.128
  34.9 1.6 %collective-permute-start.9 = (f32[16,128]{1,0:T(8,128)S(1)}, f32[16,128]{1,0:T(8,128)S(1)}, u32[]{:S(2)}, u32[]{:S(2)}) collective-permute-start(f32[16,128]{1,0:T(8,128)S(1)} %get-tuple-element.80), channel_id=1, source_target_pairs={{0,1},{1,0},{2,3},{3,2},{4,5},{5,4},{6,7},{7,6},{8,9},{9,8},{10,11... | collective-permute-start | bytes 24584 | tf_op jit(solution)/shard_map/ppermute | solution.py:472
  36.5 1.1 %collective-permute-done.10.small2 = f32[16,128]{1,0:T(8,128)S(1)} collective-permute-done((f32[16,128]{1,0:T(8,128)S(1)}, f32[16,128]{1,0:T(8,128)S(1)}, u32[]{:S(2)}, u32[]{:S(2)}) %collective-permute-start.10) | collective-permute-done | bytes 8224 | tf_op jit(solution)/shard_map/ppermute | solution.py:472
  37.6 1.0 %collective-permute-done.11.small3 = f32[16,128]{1,0:T(8,128)S(1)} collective-permute-done((f32[16,128]{1,0:T(8,128)S(1)}, f32[16,128]{1,0:T(8,128)S(1)}, u32[]{:S(2)}, u32[]{:S(2)}) %collective-permute-start.11) | collective-permute-done | bytes 8224 | tf_op jit(solution)/shard_map/ppermute | solution.py:472
  38.7 0.0 collective-permute-done.8.got3
  38.7 0.1 collective-permute-done.9.small1
  38.7 0.1 shard_map.129
  38.8 2.7 %collective-permute-start.12 = (bf16[80,640]{1,0:T(8,128)(2,1)S(1)}, bf16[80,640]{1,0:T(8,128)(2,1)S(1)}, u32[]{:S(2)}, u32[]{:S(2)}) collective-permute-start(bf16[80,640]{1,0:T(8,128)(2,1)S(1)} %get-tuple-element.84), channel_id=1, source_target_pairs={{0,4},{1,5},{2,6},{3,7},{4,0},{5,1},{6,2},{7,3},{8,12},{9,13},{10,... | collective-permute-start | bytes 307208 | tf_op jit(solution)/shard_map/ppermute | solution.py:472
  41.5 4.3 %collective-permute-done.12.got_ref = bf16[80,640]{1,0:T(8,128)(2,1)S(1)} collective-permute-done((bf16[80,640]{1,0:T(8,128)(2,1)S(1)}, bf16[80,640]{1,0:T(8,128)(2,1)S(1)}, u32[]{:S(2)}, u32[]{:S(2)}) %collective-permute-start.12) | collective-permute-done | bytes 102432 | tf_op jit(solution)/shard_map/ppermute | solution.py:472
  45.8 1.6 %collective-permute-start.13 = (bf16[80,640]{1,0:T(8,128)(2,1)S(1)}, bf16[80,640]{1,0:T(8,128)(2,1)S(1)}, u32[]{:S(2)}, u32[]{:S(2)}) collective-permute-start(bf16[80,640]{1,0:T(8,128)(2,1)S(1)} %shard_map.130.mine_ref), channel_id=1, source_target_pairs={{0,16},{8,24},{16,0},{24,8},{1,17},{9,25},{17,1},{25,9},{2,18},{10... | collective-permute-start | bytes 307208 | tf_op jit(solution)/shard_map/ppermute | solution.py:472
  47.4 3.1 %collective-permute-done.13.got_ref = bf16[80,640]{1,0:T(8,128)(2,1)S(1)} collective-permute-done((bf16[80,640]{1,0:T(8,128)(2,1)S(1)}, bf16[80,640]{1,0:T(8,128)(2,1)S(1)}, u32[]{:S(2)}, u32[]{:S(2)}) %collective-permute-start.13) | collective-permute-done | bytes 102432 | tf_op jit(solution)/shard_map/ppermute | solution.py:472
  50.6 0.1 collective-permute-start.14
  50.6 1.4 %collective-permute-done.14.other_ref = f32[80,640]{1,0:T(8,128)S(1)} collective-permute-done((f32[80,640]{1,0:T(8,128)S(1)}, f32[80,640]{1,0:T(8,128)S(1)}, u32[]{:S(2)}, u32[]{:S(2)}) %collective-permute-start.14) | collective-permute-done | bytes 204832 | tf_op jit(solution)/shard_map/ppermute | solution.py:472
  52.1 0.8 %shard_map.132 = (f32[3,64,512]{2,1,0:T(8,128)}, f32[10,64]{1,0:T(8,128)}, f32[1,64]{1,0:T(1,128)}, f32[1,64]{1,0:T(1,128)}) custom-call(f32[80,640]{1,0:T(8,128)S(1)} %shard_map.131.own_ref, f32[80,640]{1,0:T(8,128)S(1)} %collective-permute-done.14.other_ref), custom_call_target="tpu_custom_call" | custom-call | tf_op jit(solution)/shard_map/pallas_call | solution.py:457
  (2 shorter events, 0.0 us)
Async XLA Ops:
  0.6 5.8 %collective-permute-start = (bf16[32,384]{1,0:T(8,128)(2,1)}, bf16[32,384]{1,0:T(8,128)(2,1)S(1)}, u32[]{:S(2)}, u32[]{:S(2)}) collective-permute-start(bf16[32,384]{1,0:T(8,128)(2,1)} %wave_hbm.1), channel_id=1, source_target_pairs={{0,1},{1,0},{2,3},{3,2},{4,5},{5,4},{6,7},{7,6},{8,9},{9,8},{10,11... | collective-permute-start | bytes 73736 | tf_op jit(solution)/shard_map/ppermute | solution.py:472
  3.6 4.2 %collective-permute-start.1 = (bf16[32,384]{1,0:T(8,128)(2,1)}, bf16[32,384]{1,0:T(8,128)(2,1)S(1)}, u32[]{:S(2)}, u32[]{:S(2)}) collective-permute-start(bf16[32,384]{1,0:T(8,128)(2,1)} %wave_hbm.1), channel_id=1, source_target_pairs={{0,2},{1,3},{2,0},{3,1},{4,6},{5,7},{6,4},{7,5},{8,10},{9,11},{10,... | collective-permute-start | bytes 73736 | tf_op jit(solution)/shard_map/ppermute | solution.py:472
  5.2 4.9 %collective-permute-start.2 = (bf16[32,384]{1,0:T(8,128)(2,1)}, bf16[32,384]{1,0:T(8,128)(2,1)S(1)}, u32[]{:S(2)}, u32[]{:S(2)}) collective-permute-start(bf16[32,384]{1,0:T(8,128)(2,1)} %wave_hbm.1), channel_id=1, source_target_pairs={{0,3},{1,2},{2,1},{3,0},{4,7},{5,6},{6,5},{7,4},{8,11},{9,10},{10,... | collective-permute-start | bytes 73736 | tf_op jit(solution)/shard_map/ppermute | solution.py:472
  10.3 4.7 %collective-permute-start.3 = (bf16[16,384]{1,0:T(8,128)(2,1)S(1)}, bf16[16,384]{1,0:T(8,128)(2,1)S(1)}, u32[]{:S(2)}, u32[]{:S(2)}) collective-permute-start(bf16[16,384]{1,0:T(8,128)(2,1)S(1)} %get-tuple-element.51), channel_id=1, source_target_pairs={{0,4},{1,5},{2,6},{3,7},{4,0},{5,1},{6,2},{7,3},{8,12},{9,13},{10,... | collective-permute-start | bytes 36872 | tf_op jit(solution)/shard_map/ppermute | solution.py:472
  22.9 2.7 %collective-permute-start.4 = (bf16[512,512]{1,0:T(8,128)(2,1)S(1)}, bf16[512,512]{1,0:T(8,128)(2,1)S(1)}, u32[]{:S(2)}, u32[]{:S(2)}) collective-permute-start(bf16[512,512]{1,0:T(8,128)(2,1)S(1)} %get-tuple-element.62), channel_id=1, source_target_pairs={{0,8},{8,0},{16,24},{24,16},{1,9},{9,1},{17,25},{25,17},{2,10},{10... | collective-permute-start | bytes 1572872 | tf_op jit(solution)/shard_map/ppermute | solution.py:472
  23.8 1.7 %collective-permute-start.5 = (bf16[512,256]{1,0:T(8,128)(2,1)S(1)}, bf16[512,256]{1,0:T(8,128)(2,1)S(1)}, u32[]{:S(2)}, u32[]{:S(2)}) collective-permute-start(bf16[512,256]{1,0:T(8,128)(2,1)S(1)} %get-tuple-element.63), channel_id=1, source_target_pairs={{0,8},{8,0},{16,24},{24,16},{1,9},{9,1},{17,25},{25,17},{2,10},{10... | collective-permute-start | bytes 786440 | tf_op jit(solution)/shard_map/ppermute | solution.py:472
  25.7 9.2 %collective-permute-start.6 = (bf16[128,768]{1,0:T(8,128)(2,1)S(1)}, bf16[128,768]{1,0:T(8,128)(2,1)S(1)}, u32[]{:S(2)}, u32[]{:S(2)}) collective-permute-start(bf16[128,768]{1,0:T(8,128)(2,1)S(1)} %get-tuple-element.68), channel_id=1, source_target_pairs={{0,1},{1,0},{2,3},{3,2},{4,5},{5,4},{6,7},{7,6},{8,9},{9,8},{10,11... | collective-permute-start | bytes 589832 | tf_op jit(solution)/shard_map/ppermute | solution.py:472
  26.3 8.6 %collective-permute-start.7 = (bf16[128,768]{1,0:T(8,128)(2,1)S(1)}, bf16[128,768]{1,0:T(8,128)(2,1)S(1)}, u32[]{:S(2)}, u32[]{:S(2)}) collective-permute-start(bf16[128,768]{1,0:T(8,128)(2,1)S(1)} %get-tuple-element.69), channel_id=1, source_target_pairs={{0,2},{1,3},{2,0},{3,1},{4,6},{5,7},{6,4},{7,5},{8,10},{9,11},{10,... | collective-permute-start | bytes 589832 | tf_op jit(solution)/shard_map/ppermute | solution.py:472
  26.6 12.1 %collective-permute-start.8 = (bf16[128,768]{1,0:T(8,128)(2,1)S(1)}, bf16[128,768]{1,0:T(8,128)(2,1)S(1)}, u32[]{:S(2)}, u32[]{:S(2)}) collective-permute-start(bf16[128,768]{1,0:T(8,128)(2,1)S(1)} %get-tuple-element.78), channel_id=1, source_target_pairs={{0,3},{1,2},{2,1},{3,0},{4,7},{5,6},{6,5},{7,4},{8,11},{9,10},{10,... | collective-permute-start | bytes 589832 | tf_op jit(solution)/shard_map/ppermute | solution.py:472
  32.8 4.8 %collective-permute-start.10 = (f32[16,128]{1,0:T(8,128)S(1)}, f32[16,128]{1,0:T(8,128)S(1)}, u32[]{:S(2)}, u32[]{:S(2)}) collective-permute-start(f32[16,128]{1,0:T(8,128)S(1)} %get-tuple-element.81), channel_id=1, source_target_pairs={{0,2},{1,3},{2,0},{3,1},{4,6},{5,7},{6,4},{7,5},{8,10},{9,11},{10,... | collective-permute-start | bytes 24584 | tf_op jit(solution)/shard_map/ppermute | solution.py:472
  33.3 5.4 %collective-permute-start.11 = (f32[16,128]{1,0:T(8,128)S(1)}, f32[16,128]{1,0:T(8,128)S(1)}, u32[]{:S(2)}, u32[]{:S(2)}) collective-permute-start(f32[16,128]{1,0:T(8,128)S(1)} %get-tuple-element.82), channel_id=1, source_target_pairs={{0,3},{1,2},{2,1},{3,0},{4,7},{5,6},{6,5},{7,4},{8,11},{9,10},{10,... | collective-permute-start | bytes 24584 | tf_op jit(solution)/shard_map/ppermute | solution.py:472
  34.9 3.8 %collective-permute-start.9 = (f32[16,128]{1,0:T(8,128)S(1)}, f32[16,128]{1,0:T(8,128)S(1)}, u32[]{:S(2)}, u32[]{:S(2)}) collective-permute-start(f32[16,128]{1,0:T(8,128)S(1)} %get-tuple-element.80), channel_id=1, source_target_pairs={{0,1},{1,0},{2,3},{3,2},{4,5},{5,4},{6,7},{7,6},{8,9},{9,8},{10,11... | collective-permute-start | bytes 24584 | tf_op jit(solution)/shard_map/ppermute | solution.py:472
  38.8 7.0 %collective-permute-start.12 = (bf16[80,640]{1,0:T(8,128)(2,1)S(1)}, bf16[80,640]{1,0:T(8,128)(2,1)S(1)}, u32[]{:S(2)}, u32[]{:S(2)}) collective-permute-start(bf16[80,640]{1,0:T(8,128)(2,1)S(1)} %get-tuple-element.84), channel_id=1, source_target_pairs={{0,4},{1,5},{2,6},{3,7},{4,0},{5,1},{6,2},{7,3},{8,12},{9,13},{10,... | collective-permute-start | bytes 307208 | tf_op jit(solution)/shard_map/ppermute | solution.py:472
  45.8 4.7 %collective-permute-start.13 = (bf16[80,640]{1,0:T(8,128)(2,1)S(1)}, bf16[80,640]{1,0:T(8,128)(2,1)S(1)}, u32[]{:S(2)}, u32[]{:S(2)}) collective-permute-start(bf16[80,640]{1,0:T(8,128)(2,1)S(1)} %shard_map.130.mine_ref), channel_id=1, source_target_pairs={{0,16},{8,24},{16,0},{24,8},{1,17},{9,25},{17,1},{25,9},{2,18},{10... | collective-permute-start | bytes 307208 | tf_op jit(solution)/shard_map/ppermute | solution.py:472
  50.6 1.5 %collective-permute-start.14 = (f32[80,640]{1,0:T(8,128)S(1)}, f32[80,640]{1,0:T(8,128)S(1)}, u32[]{:S(2)}, u32[]{:S(2)}) collective-permute-start(f32[80,640]{1,0:T(8,128)S(1)} %shard_map.131.own_ref), channel_id=1, source_target_pairs={{0,8},{8,0},{16,24},{24,16},{1,9},{9,1},{17,25},{25,17},{2,10},{10... | collective-permute-start | bytes 614408 | tf_op jit(solution)/shard_map/ppermute | solution.py:472

commit v16 on v15

--- a/solution.py
+++ b/solution.py
@@ -55,6 +55,7 @@
     near_ref,
     far_ref,
     own_ref,
+    spread_ref,
     order_ref,
     len_ref,
     w_ref,
@@ -86,6 +87,11 @@
     for f in range(GROUP):
         spread = onehot(iota((depth, taps), 0) == iota((depth, taps), 1) + stride * f)
         band_ref[:, f * chans : (f + 1) * chans] = dot(spread, w_ref[...]).astype(BF16)
+    samp = spread_ref.shape[0]
+    for first in range(0, spread_ref.shape[1], depth):
+        group = first // depth
+        picked = iota((samp, depth), 0) == iota((samp, depth), 1) + GROUP * stride * group
+        spread_ref[:, first : first + depth] = onehot(picked)
 
 
 def pick_kernel(offsets, near_ref, far_ref, *refs):
@@ -108,6 +114,7 @@
     far_ref,
     valid_ref,
     band_ref,
+    spread_ref,
     gain_hbm,
     bias_hbm,
     w_hbm,
@@ -145,9 +152,9 @@
     low_half = lax.axis_index("dev") < lax.axis_size("dev") // 2
     near, far = near_ref[...].astype(F32), far_ref[...].astype(F32)
     wave = jnp.concatenate([jnp.where(low_half, near, far), jnp.where(low_half, far, near)], axis=0).astype(BF16)
+    spread_out = dot(wave, spread_ref[...]).astype(BF16)
     for g in range(groups):
-        pick = onehot(iota((samp, depth), 0) == iota((samp, depth), 1) + GROUP * stride * g)
-        patch_ref[g] = dot(wave, pick).astype(BF16)
+        patch_ref[g] = spread_out[:, g * depth : (g + 1) * depth]
     patches = patch_ref[...].reshape(groups * rows, depth)
 
     valid = jnp.broadcast_to(valid_ref[:, :1], (rows, width))
@@ -267,20 +274,17 @@
             out_ref[:, tap * half : (tap + 1) * half] = value.astype(out_ref.dtype)
 
 
-def odd_input_kernel(grad_ref, w_ref, slope_ref, lift_ref):
-    odds, rows, chans = lift_ref.shape
-    second = grad_ref[1 : odds + 1].reshape(odds * rows, chans)
-    lift_ref[...] = cols_both(second, w_ref[1]).reshape(lift_ref.shape) * slope_ref[:odds]
-
-
-def even_input_kernel(grad_ref, w_ref, slope_ref, after_ref, feat_ref, lift_ref, feat_out, sem):
+def input_kernel(grad_ref, w_ref, even_slope, odd_slope, feat_ref, even_ref, odd_ref, feat_out, sem):
     leaving = pltpu.make_async_copy(feat_ref, feat_out, sem)
     leaving.start()
-    evens, rows, chans = lift_ref.shape
+    evens, rows, chans = even_ref.shape
+    odds = odd_ref.shape[0]
     first = grad_ref[1 : evens + 1].reshape(evens * rows, chans)
     third = grad_ref[0:evens].reshape(evens * rows, chans)
     total = cols_both(first, w_ref[0]) + cols_both(third, w_ref[2])
-    lift_ref[...] = total.reshape(lift_ref.shape) * slope_ref[:evens]
+    even_ref[...] = total.reshape(even_ref.shape) * even_slope[:evens]
+    second = grad_ref[1 : odds + 1].reshape(odds * rows, chans)
+    odd_ref[...] = cols_both(second, w_ref[1]).reshape(odd_ref.shape) * odd_slope[:odds]
     leaving.wait()
 
 
@@ -494,7 +498,7 @@
         waves += [swap(held, "dev", 1 << bit) for held in waves]
     lens = lengths.reshape(1, members * rows)
     every = members * rows
-    valid, band, near_sel, far_sel, own_wave = call(
+    valid, band, near_sel, far_sel, own_wave, spread = call(
         functools.partial(setup_kernel, members),
         [
             ((rows, 128), jnp.int32),
@@ -502,6 +506,7 @@
             ((rows // 2, every), BF16),
             ((rows // 2, every), BF16),
             ((rows, samp), BF16),
+            ((samp, groups * depth), BF16),
         ],
         [order, lens, w_first, wave],
         scratch=[
@@ -543,7 +548,7 @@
             ((1, chans), F32),
             (w_second.shape, BF16),
         ],
-        [near, far, valid, band, gain, bias, w_second, cot_t],
+        [near, far, valid, band, spread, gain, bias, w_second, cot_t],
         scratch=[
             ((GROUP, rows, chans), F32),
             ((GROUP, rows, chans), F32),
@@ -553,7 +558,7 @@
             (cot_t.shape, BF16),
             pltpu.SemaphoreType.DMA((4,)),
         ],
-        outside=(4, 5, 6, 7),
+        outside=(5, 6, 7, 8),
     )
     half = chans // 2
     wide = taps_second * half
@@ -566,7 +571,13 @@
         keeps.append(keep)
         others.append(swap(send, "grp", 1))
     evens, odds = (frames0 + 1) // 2, frames0 // 2
-    lift_odd = call(odd_input_kernel, [((odds, rows, chans), F32)], [grad, w_in, odd_slope], flops=1 << 29)[0]
+    lift_even, lift_odd, features = call(
+        input_kernel,
+        [((evens, rows, chans), F32), ((odds, rows, chans), F32), ((frames1, rows, chans), BF16, "hbm")],
+        [grad, w_in, even_slope, odd_slope, feat],
+        scratch=[pltpu.SemaphoreType.DMA],
+        flops=1 << 30,
+    )
     quarter = chans // 4
     own, *sends = call(
         plane_kernel,
@@ -574,13 +585,6 @@
         [*keeps, *others, lift_odd],
     )
     gots = [swap(part, "dev", offset) for offset, part in enumerate(sends, 1)]
-    lift_even, features = call(
-        even_input_kernel,
-        [((evens, rows, chans), F32), ((frames1, rows, chans), BF16, "hbm")],
-        [grad, w_in, even_slope, own, feat],
-        scratch=[pltpu.SemaphoreType.DMA],
-        flops=1 << 30,
-    )
     used = -(-(stride * (GROUP - 1) + taps) // 16) * 16
     small, *smalls = call(
         functools.partial(backward_kernel, frames0, taps),

time: 53.1 us -> 53.6 us (level)
  Pallas kernels: 15.7 us -> 16.3 us
    pallas_call x14 -> x13, Pallas kernels: 15.7 us -> 16.3 us  [call(): pl.pallas_call(kernel, out_shape=[jax.ShapeDtypeStruct(out[0], out[1]) if...]
  transfers between devices with their start and end apart: 15 -> 15, of which waited for: 10 -> 9; matrix products, arithmetic and copies ran while one was open for 0% -> 0% of each run, Pallas kernels for 12% -> 13%
where the time goes in v16:
time: 53.6 us; the launch traced here: 53.4 us
  starting transfers between devices  19.3 us (36%)
  waiting for transfers between devices  17 us (32%)
  Pallas kernels  16.3 us (30%)
  between operations  0.74 us (1%)
    ppermute x15, starting transfers between devices, swap(): return lax.ppermute(value, axis, [(i, i ^ offset) for i in range(size)])  19.3 us
    ppermute x15, waiting for transfers between devices, swap(): return lax.ppermute(value, axis, [(i, i ^ offset) for i in range(size)])  17 us
    pallas_call x13, Pallas kernels, call(): pl.pallas_call(kernel, out_shape=[jax.ShapeDtypeStruct(out[0], out[1]) if...  16.3 us
  transfers between devices with their start and end apart: 15, of which 9 were waited for; matrix products, arithmetic and copies ran while one was open for 0% of the time, Pallas kernels for 13%

profile of v16, /device:TPU:0, one launch (start us, length us, event | category | flops | bytes accessed | tf_op | source)
XLA Modules:
  0.0 53.4 jit_solution(13185182615625773048)
XLA Ops:
  0.6 3.0 %collective-permute-start = (bf16[32,384]{1,0:T(8,128)(2,1)}, bf16[32,384]{1,0:T(8,128)(2,1)S(1)}, u32[]{:S(2)}, u32[]{:S(2)}) collective-permute-start(bf16[32,384]{1,0:T(8,128)(2,1)} %wave_hbm.1), channel_id=1, source_target_pairs={{0,1},{1,0},{2,3},{3,2},{4,5},{5,4},{6,7},{7,6},{8,9},{9,8},{10,11... | collective-permute-start | bytes 73736 | tf_op jit(solution)/shard_map/ppermute | solution.py:476
  3.6 1.5 %collective-permute-start.2 = (bf16[32,384]{1,0:T(8,128)(2,1)}, bf16[32,384]{1,0:T(8,128)(2,1)S(1)}, u32[]{:S(2)}, u32[]{:S(2)}) collective-permute-start(bf16[32,384]{1,0:T(8,128)(2,1)} %wave_hbm.1), channel_id=1, source_target_pairs={{0,3},{1,2},{2,1},{3,0},{4,7},{5,6},{6,5},{7,4},{8,11},{9,10},{10,... | collective-permute-start | bytes 73736 | tf_op jit(solution)/shard_map/ppermute | solution.py:476
  5.2 0.0 collective-permute-start.1
  5.2 1.4 %shard_map.119 = (s32[32,128]{1,0:T(8,128)S(1)}, bf16[128,4096]{1,0:T(8,128)(2,1)S(1)}, bf16[16,256]{1,0:T(8,128)(2,1)S(1)}, bf16[16,256]{1,0:T(8,128)(2,1)S(1)}...) custom-call(s32[8,32]{1,0:T(8,128)} %order_hbm.1, s32[1,256]{1,0:T(1,128)} %bitcast.11, ...), custom_call_target="tpu_custom_call" | custom-call | tf_op jit(solution)/shard_map/pallas_call | solution.py:461
  6.6 0.0 collective-permute-done.refs_1_
  6.6 2.1 %collective-permute-done.2.refs_3_ = bf16[32,384]{1,0:T(8,128)(2,1)S(1)} collective-permute-done((bf16[32,384]{1,0:T(8,128)(2,1)}, bf16[32,384]{1,0:T(8,128)(2,1)S(1)}, u32[]{:S(2)}, u32[]{:S(2)}) %collective-permute-start.2) | collective-permute-done | bytes 24608 | tf_op jit(solution)/shard_map/ppermute | solution.py:476
  8.7 0.5 collective-permute-done.1.refs_2_
  9.2 0.2 shard_map.120
  9.4 2.6 %collective-permute-start.3 = (bf16[16,384]{1,0:T(8,128)(2,1)S(1)}, bf16[16,384]{1,0:T(8,128)(2,1)S(1)}, u32[]{:S(2)}, u32[]{:S(2)}) collective-permute-start(bf16[16,384]{1,0:T(8,128)(2,1)S(1)} %get-tuple-element.53), channel_id=1, source_target_pairs={{0,4},{1,5},{2,6},{3,7},{4,0},{5,1},{6,2},{7,3},{8,12},{9,13},{10,... | collective-permute-start | bytes 36872 | tf_op jit(solution)/shard_map/ppermute | solution.py:476
  12.1 2.0 %collective-permute-done.3.far_ref = bf16[16,384]{1,0:T(8,128)(2,1)S(1)} collective-permute-done((bf16[16,384]{1,0:T(8,128)(2,1)S(1)}, bf16[16,384]{1,0:T(8,128)(2,1)S(1)}, u32[]{:S(2)}, u32[]{:S(2)}) %collective-permute-start.3) | collective-permute-done | bytes 12320 | tf_op jit(solution)/shard_map/ppermute | solution.py:476
  14.1 6.8 %shard_map.121 = (bf16[37,32,512]{2,1,0:T(8,128)(2,1)S(1)}, bf16[41,32,512]{2,1,0:T(8,128)(2,1)S(1)}, bf16[40,32,512]{2,1,0:T(8,128)(2,1)S(1)}, f32[10,32,4096]{...) custom-call(bf16[16,384]{1,0:T(8,128)(2,1)S(1)} %get-tuple-element.5, ...), custom_call_target="tpu_custom_call" | custom-call | tf_op jit(solution)/shard_map/pallas_call | solution.py:461
  20.9 1.5 %shard_map.123 = (f32[512,512]{1,0:T(8,128)S(1)}, bf16[512,512]{1,0:T(8,128)(2,1)S(1)}) custom-call(bf16[41,32,512]{2,1,0:T(8,128)(2,1)S(1)} %get-tuple-element.63.refs_0_, bf16[40,32,512]{2,1,0:T(8,128)(2,1)S(1)} %get-tuple-element.64.refs_1_, bf16[512,1280]{1,0:T(8,128)(2,1)S(1)} %get-tuple-element.65.refs_2_.refs_1_), custom_call_target="tpu_custom_call" | custom-call | flops 1073741824 | tf_op jit(solution)/shard_map/pallas_call | solution.py:461
  22.4 0.1 collective-permute-start.4
  22.5 0.9 %shard_map.124 = (f32[512,256]{1,0:T(8,128)S(1)}, bf16[512,256]{1,0:T(8,128)(2,1)S(1)}) custom-call(bf16[41,32,512]{2,1,0:T(8,128)(2,1)S(1)} %get-tuple-element.63.refs_0_, bf16[512,1280]{1,0:T(8,128)(2,1)S(1)} %get-tuple-element.65.refs_2_.refs_1_), custom_call_target="tpu_custom_call" | custom-call | flops 536870912 | tf_op jit(solution)/shard_map/pallas_call | solution.py:461
  23.4 0.5 %collective-permute-start.5 = (bf16[512,256]{1,0:T(8,128)(2,1)S(1)}, bf16[512,256]{1,0:T(8,128)(2,1)S(1)}, u32[]{:S(2)}, u32[]{:S(2)}) collective-permute-start(bf16[512,256]{1,0:T(8,128)(2,1)S(1)} %get-tuple-element.69), channel_id=1, source_target_pairs={{0,8},{8,0},{16,24},{24,16},{1,9},{9,1},{17,25},{25,17},{2,10},{10... | collective-permute-start | bytes 786440 | tf_op jit(solution)/shard_map/ppermute | solution.py:476
  23.9 2.2 %shard_map.122 = (f32[38,32,512]{2,1,0:T(8,128)S(1)}, f32[37,32,512]{2,1,0:T(8,128)S(1)}, bf16[37,32,512]{2,1,0:T(8,128)(2,1)}) custom-call(bf16[39,32,512]{2,1,0:T(8,128)(2,1)S(1)} %get-tuple-element.57.grad_ref, bf16[3,512,512]{2,1,0:T(8,128)(2,1)S(1)} %get-tuple-element.58.w_ref, f32[40,32,512]{2,1,0:T(8,128)S(1)} %get-tuple-element.59.even_slope, ...), custom_call_target="tpu_custom_call" | custom-call | flops 1073741824 | tf_op jit(solution)/shard_map/pallas_call | solution.py:461
  26.2 0.0 collective-permute-done.5.refs_3_
  26.2 0.0 collective-permute-done.4.refs_2_
  26.2 0.1 shard_map.125
  26.3 1.6 %collective-permute-start.6 = (bf16[128,768]{1,0:T(8,128)(2,1)S(1)}, bf16[128,768]{1,0:T(8,128)(2,1)S(1)}, u32[]{:S(2)}, u32[]{:S(2)}) collective-permute-start(bf16[128,768]{1,0:T(8,128)(2,1)S(1)} %get-tuple-element.72), channel_id=1, source_target_pairs={{0,1},{1,0},{2,3},{3,2},{4,5},{5,4},{6,7},{7,6},{8,9},{9,8},{10,11... | collective-permute-start | bytes 589832 | tf_op jit(solution)/shard_map/ppermute | solution.py:476
  27.9 0.4 collective-permute-start.7
  28.4 1.5 %collective-permute-start.8 = (bf16[128,768]{1,0:T(8,128)(2,1)S(1)}, bf16[128,768]{1,0:T(8,128)(2,1)S(1)}, u32[]{:S(2)}, u32[]{:S(2)}) collective-permute-start(bf16[128,768]{1,0:T(8,128)(2,1)S(1)} %get-tuple-element.82), channel_id=1, source_target_pairs={{0,3},{1,2},{2,1},{3,0},{4,7},{5,6},{6,5},{7,4},{8,11},{9,10},{10,... | collective-permute-start | bytes 589832 | tf_op jit(solution)/shard_map/ppermute | solution.py:476
  29.9 2.2 %shard_map.126 = (f32[16,128]{1,0:T(8,128)S(1)}, f32[16,128]{1,0:T(8,128)S(1)}, f32[16,128]{1,0:T(8,128)S(1)}, f32[16,128]{1,0:T(8,128)S(1)}) custom-call(s32[32,128]{1,0:T(8,128)S(1)} %get-tuple-element.54.valid_ref, f32[10,32,4096]{2,1,0:T(8,128)S(1)} %get-tuple-element.74.pre0, f32[32,512]{1,0:T(8,128)S(1)} %get-tuple-element.75.mean_ref, ...), custom_call_target="tpu_custom_call" | custom-call | flops 4294967296 | tf_op jit(solution)/shard_map/pallas_call | solution.py:461
  32.0 1.0 %collective-permute-start.10 = (f32[16,128]{1,0:T(8,128)S(1)}, f32[16,128]{1,0:T(8,128)S(1)}, u32[]{:S(2)}, u32[]{:S(2)}) collective-permute-start(f32[16,128]{1,0:T(8,128)S(1)} %get-tuple-element.85), channel_id=1, source_target_pairs={{0,2},{1,3},{2,0},{3,1},{4,6},{5,7},{6,4},{7,5},{8,10},{9,11},{10,... | collective-permute-start | bytes 24584 | tf_op jit(solution)/shard_map/ppermute | solution.py:476
  33.0 2.0 %collective-permute-start.11 = (f32[16,128]{1,0:T(8,128)S(1)}, f32[16,128]{1,0:T(8,128)S(1)}, u32[]{:S(2)}, u32[]{:S(2)}) collective-permute-start(f32[16,128]{1,0:T(8,128)S(1)} %get-tuple-element.86), channel_id=1, source_target_pairs={{0,3},{1,2},{2,1},{3,0},{4,7},{5,6},{6,5},{7,4},{8,11},{9,10},{10,... | collective-permute-start | bytes 24584 | tf_op jit(solution)/shard_map/ppermute | solution.py:476
  35.1 0.0 collective-permute-done.6.got1
  35.1 0.6 %collective-permute-done.7.got2 = bf16[128,768]{1,0:T(8,128)(2,1)S(1)} collective-permute-done((bf16[128,768]{1,0:T(8,128)(2,1)S(1)}, bf16[128,768]{1,0:T(8,128)(2,1)S(1)}, u32[]{:S(2)}, u32[]{:S(2)}) %collective-permute-start.7) | collective-permute-done | bytes 196640 | tf_op jit(solution)/shard_map/ppermute | solution.py:476
  35.7 0.1 shard_map.127
  35.8 0.6 %collective-permute-start.9 = (f32[16,128]{1,0:T(8,128)S(1)}, f32[16,128]{1,0:T(8,128)S(1)}, u32[]{:S(2)}, u32[]{:S(2)}) collective-permute-start(f32[16,128]{1,0:T(8,128)S(1)} %get-tuple-element.84), channel_id=1, source_target_pairs={{0,1},{1,0},{2,3},{3,2},{4,5},{5,4},{6,7},{7,6},{8,9},{9,8},{10,11... | collective-permute-start | bytes 24584 | tf_op jit(solution)/shard_map/ppermute | solution.py:476
  36.4 2.6 %collective-permute-done.10.small2 = f32[16,128]{1,0:T(8,128)S(1)} collective-permute-done((f32[16,128]{1,0:T(8,128)S(1)}, f32[16,128]{1,0:T(8,128)S(1)}, u32[]{:S(2)}, u32[]{:S(2)}) %collective-permute-start.10) | collective-permute-done | bytes 8224 | tf_op jit(solution)/shard_map/ppermute | solution.py:476
  39.0 0.0 collective-permute-done.11.small3
  39.0 0.0 collective-permute-done.8.got3
  39.0 0.5 collective-permute-done.9.small1
  39.5 0.1 shard_map.128
  39.6 2.6 %collective-permute-start.12 = (bf16[80,640]{1,0:T(8,128)(2,1)S(1)}, bf16[80,640]{1,0:T(8,128)(2,1)S(1)}, u32[]{:S(2)}, u32[]{:S(2)}) collective-permute-start(bf16[80,640]{1,0:T(8,128)(2,1)S(1)} %get-tuple-element.88), channel_id=1, source_target_pairs={{0,4},{1,5},{2,6},{3,7},{4,0},{5,1},{6,2},{7,3},{8,12},{9,13},{10,... | collective-permute-start | bytes 307208 | tf_op jit(solution)/shard_map/ppermute | solution.py:476
  42.2 4.0 %collective-permute-done.12.got_ref = bf16[80,640]{1,0:T(8,128)(2,1)S(1)} collective-permute-done((bf16[80,640]{1,0:T(8,128)(2,1)S(1)}, bf16[80,640]{1,0:T(8,128)(2,1)S(1)}, u32[]{:S(2)}, u32[]{:S(2)}) %collective-permute-start.12) | collective-permute-done | bytes 102432 | tf_op jit(solution)/shard_map/ppermute | solution.py:476
  46.2 1.6 %collective-permute-start.13 = (bf16[80,640]{1,0:T(8,128)(2,1)S(1)}, bf16[80,640]{1,0:T(8,128)(2,1)S(1)}, u32[]{:S(2)}, u32[]{:S(2)}) collective-permute-start(bf16[80,640]{1,0:T(8,128)(2,1)S(1)} %shard_map.129.mine_ref), channel_id=1, source_target_pairs={{0,16},{8,24},{16,0},{24,8},{1,17},{9,25},{17,1},{25,9},{2,18},{10... | collective-permute-start | bytes 307208 | tf_op jit(solution)/shard_map/ppermute | solution.py:476
  47.8 3.1 %collective-permute-done.13.got_ref = bf16[80,640]{1,0:T(8,128)(2,1)S(1)} collective-permute-done((bf16[80,640]{1,0:T(8,128)(2,1)S(1)}, bf16[80,640]{1,0:T(8,128)(2,1)S(1)}, u32[]{:S(2)}, u32[]{:S(2)}) %collective-permute-start.13) | collective-permute-done | bytes 102432 | tf_op jit(solution)/shard_map/ppermute | solution.py:476
  51.0 0.1 collective-permute-start.14
  51.1 1.4 %collective-permute-done.14.other_ref = f32[80,640]{1,0:T(8,128)S(1)} collective-permute-done((f32[80,640]{1,0:T(8,128)S(1)}, f32[80,640]{1,0:T(8,128)S(1)}, u32[]{:S(2)}, u32[]{:S(2)}) %collective-permute-start.14) | collective-permute-done | bytes 204832 | tf_op jit(solution)/shard_map/ppermute | solution.py:476
  52.5 0.8 %shard_map.131 = (f32[3,64,512]{2,1,0:T(8,128)}, f32[10,64]{1,0:T(8,128)}, f32[1,64]{1,0:T(1,128)}, f32[1,64]{1,0:T(1,128)}) custom-call(f32[80,640]{1,0:T(8,128)S(1)} %shard_map.130.own_ref, f32[80,640]{1,0:T(8,128)S(1)} %collective-permute-done.14.other_ref), custom_call_target="tpu_custom_call" | custom-call | tf_op jit(solution)/shard_map/pallas_call | solution.py:461
  (2 shorter events, 0.0 us)
Async XLA Ops:
  0.6 6.0 %collective-permute-start = (bf16[32,384]{1,0:T(8,128)(2,1)}, bf16[32,384]{1,0:T(8,128)(2,1)S(1)}, u32[]{:S(2)}, u32[]{:S(2)}) collective-permute-start(bf16[32,384]{1,0:T(8,128)(2,1)} %wave_hbm.1), channel_id=1, source_target_pairs={{0,1},{1,0},{2,3},{3,2},{4,5},{5,4},{6,7},{7,6},{8,9},{9,8},{10,11... | collective-permute-start | bytes 73736 | tf_op jit(solution)/shard_map/ppermute | solution.py:476
  3.6 5.1 %collective-permute-start.2 = (bf16[32,384]{1,0:T(8,128)(2,1)}, bf16[32,384]{1,0:T(8,128)(2,1)S(1)}, u32[]{:S(2)}, u32[]{:S(2)}) collective-permute-start(bf16[32,384]{1,0:T(8,128)(2,1)} %wave_hbm.1), channel_id=1, source_target_pairs={{0,3},{1,2},{2,1},{3,0},{4,7},{5,6},{6,5},{7,4},{8,11},{9,10},{10,... | collective-permute-start | bytes 73736 | tf_op jit(solution)/shard_map/ppermute | solution.py:476
  5.2 4.0 %collective-permute-start.1 = (bf16[32,384]{1,0:T(8,128)(2,1)}, bf16[32,384]{1,0:T(8,128)(2,1)S(1)}, u32[]{:S(2)}, u32[]{:S(2)}) collective-permute-start(bf16[32,384]{1,0:T(8,128)(2,1)} %wave_hbm.1), channel_id=1, source_target_pairs={{0,2},{1,3},{2,0},{3,1},{4,6},{5,7},{6,4},{7,5},{8,10},{9,11},{10,... | collective-permute-start | bytes 73736 | tf_op jit(solution)/shard_map/ppermute | solution.py:476
  9.4 4.6 %collective-permute-start.3 = (bf16[16,384]{1,0:T(8,128)(2,1)S(1)}, bf16[16,384]{1,0:T(8,128)(2,1)S(1)}, u32[]{:S(2)}, u32[]{:S(2)}) collective-permute-start(bf16[16,384]{1,0:T(8,128)(2,1)S(1)} %get-tuple-element.53), channel_id=1, source_target_pairs={{0,4},{1,5},{2,6},{3,7},{4,0},{5,1},{6,2},{7,3},{8,12},{9,13},{10,... | collective-permute-start | bytes 36872 | tf_op jit(solution)/shard_map/ppermute | solution.py:476
  22.4 3.7 %collective-permute-start.4 = (bf16[512,512]{1,0:T(8,128)(2,1)S(1)}, bf16[512,512]{1,0:T(8,128)(2,1)S(1)}, u32[]{:S(2)}, u32[]{:S(2)}) collective-permute-start(bf16[512,512]{1,0:T(8,128)(2,1)S(1)} %get-tuple-element.68), channel_id=1, source_target_pairs={{0,8},{8,0},{16,24},{24,16},{1,9},{9,1},{17,25},{25,17},{2,10},{10... | collective-permute-start | bytes 1572872 | tf_op jit(solution)/shard_map/ppermute | solution.py:476
  23.4 2.8 %collective-permute-start.5 = (bf16[512,256]{1,0:T(8,128)(2,1)S(1)}, bf16[512,256]{1,0:T(8,128)(2,1)S(1)}, u32[]{:S(2)}, u32[]{:S(2)}) collective-permute-start(bf16[512,256]{1,0:T(8,128)(2,1)S(1)} %get-tuple-element.69), channel_id=1, source_target_pairs={{0,8},{8,0},{16,24},{24,16},{1,9},{9,1},{17,25},{25,17},{2,10},{10... | collective-permute-start | bytes 786440 | tf_op jit(solution)/shard_map/ppermute | solution.py:476
  26.3 8.8 %collective-permute-start.6 = (bf16[128,768]{1,0:T(8,128)(2,1)S(1)}, bf16[128,768]{1,0:T(8,128)(2,1)S(1)}, u32[]{:S(2)}, u32[]{:S(2)}) collective-permute-start(bf16[128,768]{1,0:T(8,128)(2,1)S(1)} %get-tuple-element.72), channel_id=1, source_target_pairs={{0,1},{1,0},{2,3},{3,2},{4,5},{5,4},{6,7},{7,6},{8,9},{9,8},{10,11... | collective-permute-start | bytes 589832 | tf_op jit(solution)/shard_map/ppermute | solution.py:476
  27.9 7.8 %collective-permute-start.7 = (bf16[128,768]{1,0:T(8,128)(2,1)S(1)}, bf16[128,768]{1,0:T(8,128)(2,1)S(1)}, u32[]{:S(2)}, u32[]{:S(2)}) collective-permute-start(bf16[128,768]{1,0:T(8,128)(2,1)S(1)} %get-tuple-element.73), channel_id=1, source_target_pairs={{0,2},{1,3},{2,0},{3,1},{4,6},{5,7},{6,4},{7,5},{8,10},{9,11},{10,... | collective-permute-start | bytes 589832 | tf_op jit(solution)/shard_map/ppermute | solution.py:476
  28.4 10.6 %collective-permute-start.8 = (bf16[128,768]{1,0:T(8,128)(2,1)S(1)}, bf16[128,768]{1,0:T(8,128)(2,1)S(1)}, u32[]{:S(2)}, u32[]{:S(2)}) collective-permute-start(bf16[128,768]{1,0:T(8,128)(2,1)S(1)} %get-tuple-element.82), channel_id=1, source_target_pairs={{0,3},{1,2},{2,1},{3,0},{4,7},{5,6},{6,5},{7,4},{8,11},{9,10},{10,... | collective-permute-start | bytes 589832 | tf_op jit(solution)/shard_map/ppermute | solution.py:476
  32.0 6.9 %collective-permute-start.10 = (f32[16,128]{1,0:T(8,128)S(1)}, f32[16,128]{1,0:T(8,128)S(1)}, u32[]{:S(2)}, u32[]{:S(2)}) collective-permute-start(f32[16,128]{1,0:T(8,128)S(1)} %get-tuple-element.85), channel_id=1, source_target_pairs={{0,2},{1,3},{2,0},{3,1},{4,6},{5,7},{6,4},{7,5},{8,10},{9,11},{10,... | collective-permute-start | bytes 24584 | tf_op jit(solution)/shard_map/ppermute | solution.py:476
  33.0 5.9 %collective-permute-start.11 = (f32[16,128]{1,0:T(8,128)S(1)}, f32[16,128]{1,0:T(8,128)S(1)}, u32[]{:S(2)}, u32[]{:S(2)}) collective-permute-start(f32[16,128]{1,0:T(8,128)S(1)} %get-tuple-element.86), channel_id=1, source_target_pairs={{0,3},{1,2},{2,1},{3,0},{4,7},{5,6},{6,5},{7,4},{8,11},{9,10},{10,... | collective-permute-start | bytes 24584 | tf_op jit(solution)/shard_map/ppermute | solution.py:476
  35.8 3.7 %collective-permute-start.9 = (f32[16,128]{1,0:T(8,128)S(1)}, f32[16,128]{1,0:T(8,128)S(1)}, u32[]{:S(2)}, u32[]{:S(2)}) collective-permute-start(f32[16,128]{1,0:T(8,128)S(1)} %get-tuple-element.84), channel_id=1, source_target_pairs={{0,1},{1,0},{2,3},{3,2},{4,5},{5,4},{6,7},{7,6},{8,9},{9,8},{10,11... | collective-permute-start | bytes 24584 | tf_op jit(solution)/shard_map/ppermute | solution.py:476
  39.6 6.7 %collective-permute-start.12 = (bf16[80,640]{1,0:T(8,128)(2,1)S(1)}, bf16[80,640]{1,0:T(8,128)(2,1)S(1)}, u32[]{:S(2)}, u32[]{:S(2)}) collective-permute-start(bf16[80,640]{1,0:T(8,128)(2,1)S(1)} %get-tuple-element.88), channel_id=1, source_target_pairs={{0,4},{1,5},{2,6},{3,7},{4,0},{5,1},{6,2},{7,3},{8,12},{9,13},{10,... | collective-permute-start | bytes 307208 | tf_op jit(solution)/shard_map/ppermute | solution.py:476
  46.2 4.7 %collective-permute-start.13 = (bf16[80,640]{1,0:T(8,128)(2,1)S(1)}, bf16[80,640]{1,0:T(8,128)(2,1)S(1)}, u32[]{:S(2)}, u32[]{:S(2)}) collective-permute-start(bf16[80,640]{1,0:T(8,128)(2,1)S(1)} %shard_map.129.mine_ref), channel_id=1, source_target_pairs={{0,16},{8,24},{16,0},{24,8},{1,17},{9,25},{17,1},{25,9},{2,18},{10... | collective-permute-start | bytes 307208 | tf_op jit(solution)/shard_map/ppermute | solution.py:476
  51.0 1.5 %collective-permute-start.14 = (f32[80,640]{1,0:T(8,128)S(1)}, f32[80,640]{1,0:T(8,128)S(1)}, u32[]{:S(2)}, u32[]{:S(2)}) collective-permute-start(f32[80,640]{1,0:T(8,128)S(1)} %shard_map.130.own_ref), channel_id=1, source_target_pairs={{0,8},{8,0},{16,24},{24,16},{1,9},{9,1},{17,25},{25,17},{2,10},{10... | collective-permute-start | bytes 614408 | tf_op jit(solution)/shard_map/ppermute | solution.py:476

commit v17 on v16

--- a/solution.py
+++ b/solution.py
@@ -55,7 +55,6 @@
     near_ref,
     far_ref,
     own_ref,
-    spread_ref,
     order_ref,
     len_ref,
     w_ref,
@@ -87,11 +86,6 @@
     for f in range(GROUP):
         spread = onehot(iota((depth, taps), 0) == iota((depth, taps), 1) + stride * f)
         band_ref[:, f * chans : (f + 1) * chans] = dot(spread, w_ref[...]).astype(BF16)
-    samp = spread_ref.shape[0]
-    for first in range(0, spread_ref.shape[1], depth):
-        group = first // depth
-        picked = iota((samp, depth), 0) == iota((samp, depth), 1) + GROUP * stride * group
-        spread_ref[:, first : first + depth] = onehot(picked)
 
 
 def pick_kernel(offsets, near_ref, far_ref, *refs):
@@ -114,7 +108,6 @@
     far_ref,
     valid_ref,
     band_ref,
-    spread_ref,
     gain_hbm,
     bias_hbm,
     w_hbm,
@@ -152,9 +145,9 @@
     low_half = lax.axis_index("dev") < lax.axis_size("dev") // 2
     near, far = near_ref[...].astype(F32), far_ref[...].astype(F32)
     wave = jnp.concatenate([jnp.where(low_half, near, far), jnp.where(low_half, far, near)], axis=0).astype(BF16)
-    spread_out = dot(wave, spread_ref[...]).astype(BF16)
     for g in range(groups):
-        patch_ref[g] = spread_out[:, g * depth : (g + 1) * depth]
+        pick = onehot(iota((samp, depth), 0) == iota((samp, depth), 1) + GROUP * stride * g)
+        patch_ref[g] = dot(wave, pick).astype(BF16)
     patches = patch_ref[...].reshape(groups * rows, depth)
 
     valid = jnp.broadcast_to(valid_ref[:, :1], (rows, width))
@@ -498,7 +491,7 @@
         waves += [swap(held, "dev", 1 << bit) for held in waves]
     lens = lengths.reshape(1, members * rows)
     every = members * rows
-    valid, band, near_sel, far_sel, own_wave, spread = call(
+    valid, band, near_sel, far_sel, own_wave = call(
         functools.partial(setup_kernel, members),
         [
             ((rows, 128), jnp.int32),
@@ -506,7 +499,6 @@
             ((rows // 2, every), BF16),
             ((rows // 2, every), BF16),
             ((rows, samp), BF16),
-            ((samp, groups * depth), BF16),
         ],
         [order, lens, w_first, wave],
         scratch=[
@@ -548,7 +540,7 @@
             ((1, chans), F32),
             (w_second.shape, BF16),
         ],
-        [near, far, valid, band, spread, gain, bias, w_second, cot_t],
+        [near, far, valid, band, gain, bias, w_second, cot_t],
         scratch=[
             ((GROUP, rows, chans), F32),
             ((GROUP, rows, chans), F32),
@@ -558,7 +550,7 @@
             (cot_t.shape, BF16),
             pltpu.SemaphoreType.DMA((4,)),
         ],
-        outside=(5, 6, 7, 8),
+        outside=(4, 5, 6, 7),
     )
     half = chans // 2
     wide = taps_second * half

time: 53.6 us -> 53.1 us (level)
  Pallas kernels: 16.3 us -> 15.7 us
    pallas_call x13, Pallas kernels: 16.3 us -> 15.7 us  [call(): pl.pallas_call(kernel, out_shape=[jax.ShapeDtypeStruct(out[0], out[1]) if...]
  transfers between devices with their start and end apart: 15 -> 15, of which waited for: 9 -> 9; matrix products, arithmetic and copies ran while one was open for 0% -> 0% of each run, Pallas kernels for 13% -> 12%
where the time goes in v17:
time: 53.1 us; the launch traced here: 52.9 us
  starting transfers between devices  19.3 us (36%)
  waiting for transfers between devices  17.1 us (32%)
  Pallas kernels  15.7 us (30%)
  between operations  0.74 us (1%)
    ppermute x15, starting transfers between devices, swap(): return lax.ppermute(value, axis, [(i, i ^ offset) for i in range(size)])  19.3 us
    ppermute x15, waiting for transfers between devices, swap(): return lax.ppermute(value, axis, [(i, i ^ offset) for i in range(size)])  17.1 us
    pallas_call x13, Pallas kernels, call(): pl.pallas_call(kernel, out_shape=[jax.ShapeDtypeStruct(out[0], out[1]) if...  15.7 us
  transfers between devices with their start and end apart: 15, of which 9 were waited for; matrix products, arithmetic and copies ran while one was open for 0% of the time, Pallas kernels for 12%

profile of v17, /device:TPU:0, one launch (start us, length us, event | category | flops | bytes accessed | tf_op | source)
XLA Modules:
  0.0 52.9 jit_solution(10963124419750819590)
XLA Ops:
  0.6 3.0 %collective-permute-start = (bf16[32,384]{1,0:T(8,128)(2,1)}, bf16[32,384]{1,0:T(8,128)(2,1)S(1)}, u32[]{:S(2)}, u32[]{:S(2)}) collective-permute-start(bf16[32,384]{1,0:T(8,128)(2,1)} %wave_hbm.1), channel_id=1, source_target_pairs={{0,1},{1,0},{2,3},{3,2},{4,5},{5,4},{6,7},{7,6},{8,9},{9,8},{10,11... | collective-permute-start | bytes 73736 | tf_op jit(solution)/shard_map/ppermute | solution.py:469
  3.6 1.5 %collective-permute-start.2 = (bf16[32,384]{1,0:T(8,128)(2,1)}, bf16[32,384]{1,0:T(8,128)(2,1)S(1)}, u32[]{:S(2)}, u32[]{:S(2)}) collective-permute-start(bf16[32,384]{1,0:T(8,128)(2,1)} %wave_hbm.1), channel_id=1, source_target_pairs={{0,3},{1,2},{2,1},{3,0},{4,7},{5,6},{6,5},{7,4},{8,11},{9,10},{10,... | collective-permute-start | bytes 73736 | tf_op jit(solution)/shard_map/ppermute | solution.py:469
  5.2 0.0 collective-permute-start.1
  5.2 1.3 %shard_map.119 = (s32[32,128]{1,0:T(8,128)S(1)}, bf16[128,4096]{1,0:T(8,128)(2,1)S(1)}, bf16[16,256]{1,0:T(8,128)(2,1)S(1)}, bf16[16,256]{1,0:T(8,128)(2,1)S(1)}, bf16[32,384]{1,0:T(8,128)(2,1)S(1)}) custom-call(s32[8,32]{1,0:T(8,128)} %order_hbm.1, s32[1,256]{1,0:T(1,128)} %bitcast.11, bf16[10,512]{1,0:T(8,128)(2,1)} %w_hbm.2, bf16[32,384]{1,0:T(8,128)(2,1)} %wave_hbm.1), custom_call_target="tpu_custom_call" | custom-call | tf_op jit(solution)/shard_map/pallas_call | solution.py:454
  6.5 0.0 collective-permute-done.refs_1_
  6.5 2.2 %collective-permute-done.2.refs_3_ = bf16[32,384]{1,0:T(8,128)(2,1)S(1)} collective-permute-done((bf16[32,384]{1,0:T(8,128)(2,1)}, bf16[32,384]{1,0:T(8,128)(2,1)S(1)}, u32[]{:S(2)}, u32[]{:S(2)}) %collective-permute-start.2) | collective-permute-done | bytes 24608 | tf_op jit(solution)/shard_map/ppermute | solution.py:469
  8.7 0.5 collective-permute-done.1.refs_2_
  9.2 0.2 shard_map.120
  9.4 2.6 %collective-permute-start.3 = (bf16[16,384]{1,0:T(8,128)(2,1)S(1)}, bf16[16,384]{1,0:T(8,128)(2,1)S(1)}, u32[]{:S(2)}, u32[]{:S(2)}) collective-permute-start(bf16[16,384]{1,0:T(8,128)(2,1)S(1)} %get-tuple-element.52), channel_id=1, source_target_pairs={{0,4},{1,5},{2,6},{3,7},{4,0},{5,1},{6,2},{7,3},{8,12},{9,13},{10,... | collective-permute-start | bytes 36872 | tf_op jit(solution)/shard_map/ppermute | solution.py:469
  12.1 2.0 %collective-permute-done.3.far_ref = bf16[16,384]{1,0:T(8,128)(2,1)S(1)} collective-permute-done((bf16[16,384]{1,0:T(8,128)(2,1)S(1)}, bf16[16,384]{1,0:T(8,128)(2,1)S(1)}, u32[]{:S(2)}, u32[]{:S(2)}) %collective-permute-start.3) | collective-permute-done | bytes 12320 | tf_op jit(solution)/shard_map/ppermute | solution.py:469
  14.1 6.3 %shard_map.121 = (bf16[37,32,512]{2,1,0:T(8,128)(2,1)S(1)}, bf16[41,32,512]{2,1,0:T(8,128)(2,1)S(1)}, bf16[40,32,512]{2,1,0:T(8,128)(2,1)S(1)}, f32[10,32,4096]{...) custom-call(bf16[16,384]{1,0:T(8,128)(2,1)S(1)} %get-tuple-element.5, ...), custom_call_target="tpu_custom_call" | custom-call | tf_op jit(solution)/shard_map/pallas_call | solution.py:454
  20.4 1.5 %shard_map.123 = (f32[512,512]{1,0:T(8,128)S(1)}, bf16[512,512]{1,0:T(8,128)(2,1)S(1)}) custom-call(bf16[41,32,512]{2,1,0:T(8,128)(2,1)S(1)} %get-tuple-element.61.refs_0_, bf16[40,32,512]{2,1,0:T(8,128)(2,1)S(1)} %get-tuple-element.62.refs_1_, bf16[512,1280]{1,0:T(8,128)(2,1)S(1)} %get-tuple-element.63.refs_2_.refs_1_), custom_call_target="tpu_custom_call" | custom-call | flops 1073741824 | tf_op jit(solution)/shard_map/pallas_call | solution.py:454
  21.9 0.1 collective-permute-start.4
  22.0 0.9 %shard_map.124 = (f32[512,256]{1,0:T(8,128)S(1)}, bf16[512,256]{1,0:T(8,128)(2,1)S(1)}) custom-call(bf16[41,32,512]{2,1,0:T(8,128)(2,1)S(1)} %get-tuple-element.61.refs_0_, bf16[512,1280]{1,0:T(8,128)(2,1)S(1)} %get-tuple-element.63.refs_2_.refs_1_), custom_call_target="tpu_custom_call" | custom-call | flops 536870912 | tf_op jit(solution)/shard_map/pallas_call | solution.py:454
  22.9 0.5 %collective-permute-start.5 = (bf16[512,256]{1,0:T(8,128)(2,1)S(1)}, bf16[512,256]{1,0:T(8,128)(2,1)S(1)}, u32[]{:S(2)}, u32[]{:S(2)}) collective-permute-start(bf16[512,256]{1,0:T(8,128)(2,1)S(1)} %get-tuple-element.67), channel_id=1, source_target_pairs={{0,8},{8,0},{16,24},{24,16},{1,9},{9,1},{17,25},{25,17},{2,10},{10... | collective-permute-start | bytes 786440 | tf_op jit(solution)/shard_map/ppermute | solution.py:469
  23.4 2.2 %shard_map.122 = (f32[38,32,512]{2,1,0:T(8,128)S(1)}, f32[37,32,512]{2,1,0:T(8,128)S(1)}, bf16[37,32,512]{2,1,0:T(8,128)(2,1)}) custom-call(bf16[39,32,512]{2,1,0:T(8,128)(2,1)S(1)} %get-tuple-element.55.grad_ref, bf16[3,512,512]{2,1,0:T(8,128)(2,1)S(1)} %get-tuple-element.56.w_ref, f32[40,32,512]{2,1,0:T(8,128)S(1)} %get-tuple-element.57.even_slope, ...), custom_call_target="tpu_custom_call" | custom-call | flops 1073741824 | tf_op jit(solution)/shard_map/pallas_call | solution.py:454
  25.7 0.0 collective-permute-done.5.refs_3_
  25.7 0.0 collective-permute-done.4.refs_2_
  25.7 0.1 shard_map.125
  25.8 1.6 %collective-permute-start.6 = (bf16[128,768]{1,0:T(8,128)(2,1)S(1)}, bf16[128,768]{1,0:T(8,128)(2,1)S(1)}, u32[]{:S(2)}, u32[]{:S(2)}) collective-permute-start(bf16[128,768]{1,0:T(8,128)(2,1)S(1)} %get-tuple-element.70), channel_id=1, source_target_pairs={{0,1},{1,0},{2,3},{3,2},{4,5},{5,4},{6,7},{7,6},{8,9},{9,8},{10,11... | collective-permute-start | bytes 589832 | tf_op jit(solution)/shard_map/ppermute | solution.py:469
  27.4 0.4 collective-permute-start.7
  27.8 1.6 %collective-permute-start.8 = (bf16[128,768]{1,0:T(8,128)(2,1)S(1)}, bf16[128,768]{1,0:T(8,128)(2,1)S(1)}, u32[]{:S(2)}, u32[]{:S(2)}) collective-permute-start(bf16[128,768]{1,0:T(8,128)(2,1)S(1)} %get-tuple-element.80), channel_id=1, source_target_pairs={{0,3},{1,2},{2,1},{3,0},{4,7},{5,6},{6,5},{7,4},{8,11},{9,10},{10,... | collective-permute-start | bytes 589832 | tf_op jit(solution)/shard_map/ppermute | solution.py:469
  29.4 2.2 %shard_map.126 = (f32[16,128]{1,0:T(8,128)S(1)}, f32[16,128]{1,0:T(8,128)S(1)}, f32[16,128]{1,0:T(8,128)S(1)}, f32[16,128]{1,0:T(8,128)S(1)}) custom-call(s32[32,128]{1,0:T(8,128)S(1)} %get-tuple-element.53.valid_ref, f32[10,32,4096]{2,1,0:T(8,128)S(1)} %get-tuple-element.72.pre0, f32[32,512]{1,0:T(8,128)S(1)} %get-tuple-element.73.mean_ref, ...), custom_call_target="tpu_custom_call" | custom-call | flops 4294967296 | tf_op jit(solution)/shard_map/pallas_call | solution.py:454
  31.6 1.0 %collective-permute-start.10 = (f32[16,128]{1,0:T(8,128)S(1)}, f32[16,128]{1,0:T(8,128)S(1)}, u32[]{:S(2)}, u32[]{:S(2)}) collective-permute-start(f32[16,128]{1,0:T(8,128)S(1)} %get-tuple-element.83), channel_id=1, source_target_pairs={{0,2},{1,3},{2,0},{3,1},{4,6},{5,7},{6,4},{7,5},{8,10},{9,11},{10,... | collective-permute-start | bytes 24584 | tf_op jit(solution)/shard_map/ppermute | solution.py:469
  32.6 2.0 %collective-permute-start.11 = (f32[16,128]{1,0:T(8,128)S(1)}, f32[16,128]{1,0:T(8,128)S(1)}, u32[]{:S(2)}, u32[]{:S(2)}) collective-permute-start(f32[16,128]{1,0:T(8,128)S(1)} %get-tuple-element.84), channel_id=1, source_target_pairs={{0,3},{1,2},{2,1},{3,0},{4,7},{5,6},{6,5},{7,4},{8,11},{9,10},{10,... | collective-permute-start | bytes 24584 | tf_op jit(solution)/shard_map/ppermute | solution.py:469
  34.6 0.0 collective-permute-done.6.got1
  34.6 0.6 %collective-permute-done.7.got2 = bf16[128,768]{1,0:T(8,128)(2,1)S(1)} collective-permute-done((bf16[128,768]{1,0:T(8,128)(2,1)S(1)}, bf16[128,768]{1,0:T(8,128)(2,1)S(1)}, u32[]{:S(2)}, u32[]{:S(2)}) %collective-permute-start.7) | collective-permute-done | bytes 196640 | tf_op jit(solution)/shard_map/ppermute | solution.py:469
  35.2 0.1 shard_map.127
  35.3 0.6 %collective-permute-start.9 = (f32[16,128]{1,0:T(8,128)S(1)}, f32[16,128]{1,0:T(8,128)S(1)}, u32[]{:S(2)}, u32[]{:S(2)}) collective-permute-start(f32[16,128]{1,0:T(8,128)S(1)} %get-tuple-element.82), channel_id=1, source_target_pairs={{0,1},{1,0},{2,3},{3,2},{4,5},{5,4},{6,7},{7,6},{8,9},{9,8},{10,11... | collective-permute-start | bytes 24584 | tf_op jit(solution)/shard_map/ppermute | solution.py:469
  35.9 2.6 %collective-permute-done.10.small2 = f32[16,128]{1,0:T(8,128)S(1)} collective-permute-done((f32[16,128]{1,0:T(8,128)S(1)}, f32[16,128]{1,0:T(8,128)S(1)}, u32[]{:S(2)}, u32[]{:S(2)}) %collective-permute-start.10) | collective-permute-done | bytes 8224 | tf_op jit(solution)/shard_map/ppermute | solution.py:469
  38.4 0.0 collective-permute-done.11.small3
  38.5 0.0 collective-permute-done.8.got3
  38.5 0.5 collective-permute-done.9.small1
  39.0 0.1 shard_map.128
  39.0 2.6 %collective-permute-start.12 = (bf16[80,640]{1,0:T(8,128)(2,1)S(1)}, bf16[80,640]{1,0:T(8,128)(2,1)S(1)}, u32[]{:S(2)}, u32[]{:S(2)}) collective-permute-start(bf16[80,640]{1,0:T(8,128)(2,1)S(1)} %get-tuple-element.86), channel_id=1, source_target_pairs={{0,4},{1,5},{2,6},{3,7},{4,0},{5,1},{6,2},{7,3},{8,12},{9,13},{10,... | collective-permute-start | bytes 307208 | tf_op jit(solution)/shard_map/ppermute | solution.py:469
  41.7 4.0 %collective-permute-done.12.got_ref = bf16[80,640]{1,0:T(8,128)(2,1)S(1)} collective-permute-done((bf16[80,640]{1,0:T(8,128)(2,1)S(1)}, bf16[80,640]{1,0:T(8,128)(2,1)S(1)}, u32[]{:S(2)}, u32[]{:S(2)}) %collective-permute-start.12) | collective-permute-done | bytes 102432 | tf_op jit(solution)/shard_map/ppermute | solution.py:469
  45.7 1.6 %collective-permute-start.13 = (bf16[80,640]{1,0:T(8,128)(2,1)S(1)}, bf16[80,640]{1,0:T(8,128)(2,1)S(1)}, u32[]{:S(2)}, u32[]{:S(2)}) collective-permute-start(bf16[80,640]{1,0:T(8,128)(2,1)S(1)} %shard_map.129.mine_ref), channel_id=1, source_target_pairs={{0,16},{8,24},{16,0},{24,8},{1,17},{9,25},{17,1},{25,9},{2,18},{10... | collective-permute-start | bytes 307208 | tf_op jit(solution)/shard_map/ppermute | solution.py:469
  47.3 3.1 %collective-permute-done.13.got_ref = bf16[80,640]{1,0:T(8,128)(2,1)S(1)} collective-permute-done((bf16[80,640]{1,0:T(8,128)(2,1)S(1)}, bf16[80,640]{1,0:T(8,128)(2,1)S(1)}, u32[]{:S(2)}, u32[]{:S(2)}) %collective-permute-start.13) | collective-permute-done | bytes 102432 | tf_op jit(solution)/shard_map/ppermute | solution.py:469
  50.5 0.1 collective-permute-start.14
  50.6 1.4 %collective-permute-done.14.other_ref = f32[80,640]{1,0:T(8,128)S(1)} collective-permute-done((f32[80,640]{1,0:T(8,128)S(1)}, f32[80,640]{1,0:T(8,128)S(1)}, u32[]{:S(2)}, u32[]{:S(2)}) %collective-permute-start.14) | collective-permute-done | bytes 204832 | tf_op jit(solution)/shard_map/ppermute | solution.py:469
  52.0 0.8 %shard_map.131 = (f32[3,64,512]{2,1,0:T(8,128)}, f32[10,64]{1,0:T(8,128)}, f32[1,64]{1,0:T(1,128)}, f32[1,64]{1,0:T(1,128)}) custom-call(f32[80,640]{1,0:T(8,128)S(1)} %shard_map.130.own_ref, f32[80,640]{1,0:T(8,128)S(1)} %collective-permute-done.14.other_ref), custom_call_target="tpu_custom_call" | custom-call | tf_op jit(solution)/shard_map/pallas_call | solution.py:454
  (2 shorter events, 0.0 us)
Async XLA Ops:
  0.6 5.9 %collective-permute-start = (bf16[32,384]{1,0:T(8,128)(2,1)}, bf16[32,384]{1,0:T(8,128)(2,1)S(1)}, u32[]{:S(2)}, u32[]{:S(2)}) collective-permute-start(bf16[32,384]{1,0:T(8,128)(2,1)} %wave_hbm.1), channel_id=1, source_target_pairs={{0,1},{1,0},{2,3},{3,2},{4,5},{5,4},{6,7},{7,6},{8,9},{9,8},{10,11... | collective-permute-start | bytes 73736 | tf_op jit(solution)/shard_map/ppermute | solution.py:469
  3.6 5.1 %collective-permute-start.2 = (bf16[32,384]{1,0:T(8,128)(2,1)}, bf16[32,384]{1,0:T(8,128)(2,1)S(1)}, u32[]{:S(2)}, u32[]{:S(2)}) collective-permute-start(bf16[32,384]{1,0:T(8,128)(2,1)} %wave_hbm.1), channel_id=1, source_target_pairs={{0,3},{1,2},{2,1},{3,0},{4,7},{5,6},{6,5},{7,4},{8,11},{9,10},{10,... | collective-permute-start | bytes 73736 | tf_op jit(solution)/shard_map/ppermute | solution.py:469
  5.2 4.0 %collective-permute-start.1 = (bf16[32,384]{1,0:T(8,128)(2,1)}, bf16[32,384]{1,0:T(8,128)(2,1)S(1)}, u32[]{:S(2)}, u32[]{:S(2)}) collective-permute-start(bf16[32,384]{1,0:T(8,128)(2,1)} %wave_hbm.1), channel_id=1, source_target_pairs={{0,2},{1,3},{2,0},{3,1},{4,6},{5,7},{6,4},{7,5},{8,10},{9,11},{10,... | collective-permute-start | bytes 73736 | tf_op jit(solution)/shard_map/ppermute | solution.py:469
  9.4 4.6 %collective-permute-start.3 = (bf16[16,384]{1,0:T(8,128)(2,1)S(1)}, bf16[16,384]{1,0:T(8,128)(2,1)S(1)}, u32[]{:S(2)}, u32[]{:S(2)}) collective-permute-start(bf16[16,384]{1,0:T(8,128)(2,1)S(1)} %get-tuple-element.52), channel_id=1, source_target_pairs={{0,4},{1,5},{2,6},{3,7},{4,0},{5,1},{6,2},{7,3},{8,12},{9,13},{10,... | collective-permute-start | bytes 36872 | tf_op jit(solution)/shard_map/ppermute | solution.py:469
  21.9 3.7 %collective-permute-start.4 = (bf16[512,512]{1,0:T(8,128)(2,1)S(1)}, bf16[512,512]{1,0:T(8,128)(2,1)S(1)}, u32[]{:S(2)}, u32[]{:S(2)}) collective-permute-start(bf16[512,512]{1,0:T(8,128)(2,1)S(1)} %get-tuple-element.66), channel_id=1, source_target_pairs={{0,8},{8,0},{16,24},{24,16},{1,9},{9,1},{17,25},{25,17},{2,10},{10... | collective-permute-start | bytes 1572872 | tf_op jit(solution)/shard_map/ppermute | solution.py:469
  22.9 2.8 %collective-permute-start.5 = (bf16[512,256]{1,0:T(8,128)(2,1)S(1)}, bf16[512,256]{1,0:T(8,128)(2,1)S(1)}, u32[]{:S(2)}, u32[]{:S(2)}) collective-permute-start(bf16[512,256]{1,0:T(8,128)(2,1)S(1)} %get-tuple-element.67), channel_id=1, source_target_pairs={{0,8},{8,0},{16,24},{24,16},{1,9},{9,1},{17,25},{25,17},{2,10},{10... | collective-permute-start | bytes 786440 | tf_op jit(solution)/shard_map/ppermute | solution.py:469
  25.8 8.7 %collective-permute-start.6 = (bf16[128,768]{1,0:T(8,128)(2,1)S(1)}, bf16[128,768]{1,0:T(8,128)(2,1)S(1)}, u32[]{:S(2)}, u32[]{:S(2)}) collective-permute-start(bf16[128,768]{1,0:T(8,128)(2,1)S(1)} %get-tuple-element.70), channel_id=1, source_target_pairs={{0,1},{1,0},{2,3},{3,2},{4,5},{5,4},{6,7},{7,6},{8,9},{9,8},{10,11... | collective-permute-start | bytes 589832 | tf_op jit(solution)/shard_map/ppermute | solution.py:469
  27.4 7.8 %collective-permute-start.7 = (bf16[128,768]{1,0:T(8,128)(2,1)S(1)}, bf16[128,768]{1,0:T(8,128)(2,1)S(1)}, u32[]{:S(2)}, u32[]{:S(2)}) collective-permute-start(bf16[128,768]{1,0:T(8,128)(2,1)S(1)} %get-tuple-element.71), channel_id=1, source_target_pairs={{0,2},{1,3},{2,0},{3,1},{4,6},{5,7},{6,4},{7,5},{8,10},{9,11},{10,... | collective-permute-start | bytes 589832 | tf_op jit(solution)/shard_map/ppermute | solution.py:469
  27.8 10.6 %collective-permute-start.8 = (bf16[128,768]{1,0:T(8,128)(2,1)S(1)}, bf16[128,768]{1,0:T(8,128)(2,1)S(1)}, u32[]{:S(2)}, u32[]{:S(2)}) collective-permute-start(bf16[128,768]{1,0:T(8,128)(2,1)S(1)} %get-tuple-element.80), channel_id=1, source_target_pairs={{0,3},{1,2},{2,1},{3,0},{4,7},{5,6},{6,5},{7,4},{8,11},{9,10},{10,... | collective-permute-start | bytes 589832 | tf_op jit(solution)/shard_map/ppermute | solution.py:469
  31.6 6.9 %collective-permute-start.10 = (f32[16,128]{1,0:T(8,128)S(1)}, f32[16,128]{1,0:T(8,128)S(1)}, u32[]{:S(2)}, u32[]{:S(2)}) collective-permute-start(f32[16,128]{1,0:T(8,128)S(1)} %get-tuple-element.83), channel_id=1, source_target_pairs={{0,2},{1,3},{2,0},{3,1},{4,6},{5,7},{6,4},{7,5},{8,10},{9,11},{10,... | collective-permute-start | bytes 24584 | tf_op jit(solution)/shard_map/ppermute | solution.py:469
  32.6 5.9 %collective-permute-start.11 = (f32[16,128]{1,0:T(8,128)S(1)}, f32[16,128]{1,0:T(8,128)S(1)}, u32[]{:S(2)}, u32[]{:S(2)}) collective-permute-start(f32[16,128]{1,0:T(8,128)S(1)} %get-tuple-element.84), channel_id=1, source_target_pairs={{0,3},{1,2},{2,1},{3,0},{4,7},{5,6},{6,5},{7,4},{8,11},{9,10},{10,... | collective-permute-start | bytes 24584 | tf_op jit(solution)/shard_map/ppermute | solution.py:469
  35.3 3.7 %collective-permute-start.9 = (f32[16,128]{1,0:T(8,128)S(1)}, f32[16,128]{1,0:T(8,128)S(1)}, u32[]{:S(2)}, u32[]{:S(2)}) collective-permute-start(f32[16,128]{1,0:T(8,128)S(1)} %get-tuple-element.82), channel_id=1, source_target_pairs={{0,1},{1,0},{2,3},{3,2},{4,5},{5,4},{6,7},{7,6},{8,9},{9,8},{10,11... | collective-permute-start | bytes 24584 | tf_op jit(solution)/shard_map/ppermute | solution.py:469
  39.0 6.7 %collective-permute-start.12 = (bf16[80,640]{1,0:T(8,128)(2,1)S(1)}, bf16[80,640]{1,0:T(8,128)(2,1)S(1)}, u32[]{:S(2)}, u32[]{:S(2)}) collective-permute-start(bf16[80,640]{1,0:T(8,128)(2,1)S(1)} %get-tuple-element.86), channel_id=1, source_target_pairs={{0,4},{1,5},{2,6},{3,7},{4,0},{5,1},{6,2},{7,3},{8,12},{9,13},{10,... | collective-permute-start | bytes 307208 | tf_op jit(solution)/shard_map/ppermute | solution.py:469
  45.7 4.7 %collective-permute-start.13 = (bf16[80,640]{1,0:T(8,128)(2,1)S(1)}, bf16[80,640]{1,0:T(8,128)(2,1)S(1)}, u32[]{:S(2)}, u32[]{:S(2)}) collective-permute-start(bf16[80,640]{1,0:T(8,128)(2,1)S(1)} %shard_map.129.mine_ref), channel_id=1, source_target_pairs={{0,16},{8,24},{16,0},{24,8},{1,17},{9,25},{17,1},{25,9},{2,18},{10... | collective-permute-start | bytes 307208 | tf_op jit(solution)/shard_map/ppermute | solution.py:469
  50.5 1.5 %collective-permute-start.14 = (f32[80,640]{1,0:T(8,128)S(1)}, f32[80,640]{1,0:T(8,128)S(1)}, u32[]{:S(2)}, u32[]{:S(2)}) collective-permute-start(f32[80,640]{1,0:T(8,128)S(1)} %shard_map.130.own_ref), channel_id=1, source_target_pairs={{0,8},{8,0},{16,24},{24,16},{1,9},{9,1},{17,25},{25,17},{2,10},{10... | collective-permute-start | bytes 614408 | tf_op jit(solution)/shard_map/ppermute | solution.py:469
